TPU v7x, 32 devices: a whole 2x2x4 slice. The times are simulated.
32 devices in a mesh: groups: 2 (over x), tensor: 16 (over z, y, core).
Axes of the slice: x: 2, y: 2, z: 4, core: 2. Of those that a mesh axis runs over, the one named last changes fastest.
Arguments:
- hidden_in: bfloat16 [256, 16384], P('groups'), parts along dimension 0, may hold values from -4 to 4
- attn_gain: bfloat16 [16384], replicated, may hold values from 0.099609375 to 1.8984375
- w_query: bfloat16 [16384, 8192], P(None, 'tensor'), may hold values from -0.046875 to 0.046875
- w_keyval: bfloat16 [16384, 1024], P(None, 'tensor'), may hold values from -0.046875 to 0.046875
- cache_keys: bfloat16 [256, 1024, 512], P(('groups', 'tensor')), parts along dimension 0, may hold values from -140 to 140, as said below
- cache_values: bfloat16 [256, 1024, 512], P(('groups', 'tensor')), parts along dimension 0, may hold values from -8 to 8
- w_out: bfloat16 [8192, 16384], P('tensor'), may hold values from -0.09375 to 0.09375
- ffn_gain: bfloat16 [16384], replicated, may hold values from 0.099609375 to 1.8984375
- lengths: int32 [256], P(('groups', 'tensor')), parts along dimension 0, may hold values from 1 to 1024, as said below
- positions: int32 [256], P('groups'), parts along dimension 0, may hold values from 0 to 8191
Outputs:
- stream: bfloat16 [256, 16384], P('groups', 'tensor'), parts along dimension 0
- normed: bfloat16 [256, 16384], P('groups'), parts along dimension 0
There are 2 independent parts, one for each index of `groups`. A program takes and returns all parts, laid end to end along the dimension named above; an argument that names none is the same for every part. Nothing has to cross between parts.
Inputs may be any that keep to these rules, and one draw needn't show every extreme that they name: `lengths`: every draw has a row whose length is exactly 1024. `cache_keys`: cached keys are already rotated to their own positions.
All inputs are finite; a program needn't handle non-finite values.
Results may differ from a plain program's by a relative error of at most 0.018.
The roundings to bfloat16 on the way count: a program that leaves them out, or rounds other values in their place, can miss the bound.
Values may be sent and summed in bfloat16 or wider, within the bound.
No kernel may reach another device: no remote copies, remote signals or barrier semaphores. Data moves between devices by JAX's collectives and lax.ppermute only.
A program may use at most 192 MiB of HBM per device.

v0:
```python
import math

import jax
import jax.numpy as jnp
from jax import lax
from jax.sharding import PartitionSpec as P

HD = 128


epsilon = 1e-05
rope_theta = 500000.0


def normalize(values, gain):
    floats = values.astype(jnp.float32)
    mean_square = jnp.mean(floats * floats, axis=-1, keepdims=True)
    return (floats * lax.rsqrt(mean_square + epsilon) * gain.astype(jnp.float32)).astype(
        jnp.bfloat16
    )


def rotate(values, positions):
    half_width = values.shape[-1] // 2
    frequency = jnp.exp(
        jnp.arange(half_width, dtype=jnp.float32) * (-math.log(rope_theta) / half_width)
    )
    angles = positions.astype(jnp.float32)[:, None] * frequency[None, :]
    cosine = jnp.cos(angles)[:, None, :]
    sine_part = jnp.sin(angles)[:, None, :]
    first_half = values[..., :half_width]
    second_half = values[..., half_width:]
    return jnp.concatenate(
        [
            first_half * cosine - second_half * sine_part,
            second_half * cosine + first_half * sine_part,
        ],
        axis=-1,
    )


def attend(queries, keyval, cache_keys, cache_values, lengths, positions):
    row_count = queries.shape[0]
    key_width = keyval.shape[1] // 2
    kv_groups = key_width // HD
    span = cache_keys.shape[1]
    grouped = queries.reshape(row_count, kv_groups, -1, HD)
    new_keys = rotate(
        keyval[:, :key_width].astype(jnp.float32).reshape(row_count, kv_groups, HD), positions
    ).astype(jnp.bfloat16)
    new_values = keyval[:, key_width:].reshape(row_count, kv_groups, HD)
    old_keys = cache_keys.reshape(row_count, span, kv_groups, HD)
    old_values = cache_values.reshape(row_count, span, kv_groups, HD)
    score_scale = HD ** (-0.5)
    scores = (
        jnp.einsum("rgqd,rlgd->rgql", grouped, old_keys, preferred_element_type=jnp.float32)
        * score_scale
    )
    valid_mask = jnp.arange(span)[None, :] < lengths[:, None]
    scores = jnp.where(valid_mask[:, None, None, :], scores, -1e30)
    own_score = (
        jnp.einsum("rgqd,rgd->rgq", grouped, new_keys, preferred_element_type=jnp.float32)
        * score_scale
    )
    largest = jnp.maximum(jnp.max(scores, axis=-1), own_score)
    expsum = jnp.exp(scores - largest[..., None])
    own_exp = jnp.exp(own_score - largest)
    totals = jnp.sum(expsum, axis=-1) + own_exp
    weights = (expsum / totals[..., None]).astype(jnp.bfloat16)
    own_weight = (own_exp / totals).astype(jnp.bfloat16)
    mixed = jnp.einsum("rgql,rlgd->rgqd", weights, old_values, preferred_element_type=jnp.float32)
    mixed = (
        mixed
        + own_weight.astype(jnp.float32)[..., None] * new_values.astype(jnp.float32)[:, :, None, :]
    )
    return mixed.astype(jnp.bfloat16).reshape(row_count, -1)


def on_device(
    hidden_in,
    attn_gain,
    w_query,
    w_keyval,
    cache_keys,
    cache_values,
    w_out,
    ffn_gain,
    lengths,
    positions,
):
    row_count = hidden_in.shape[0]
    my_index = lax.axis_index("tensor")
    normed_in = normalize(hidden_in, attn_gain)
    queries = jnp.dot(normed_in, w_query, preferred_element_type=jnp.float32)
    queries = queries.reshape(row_count, queries.shape[1] // HD, HD)
    queries = rotate(queries, positions).astype(jnp.bfloat16).reshape(row_count, -1)
    keyval = jnp.dot(normed_in, w_keyval, preferred_element_type=jnp.float32).astype(jnp.bfloat16)
    row_queries, row_keyval = (
        lax.all_to_all(queries, "tensor", split_axis=0, concat_axis=1, tiled=True),
        lax.all_to_all(keyval, "tensor", split_axis=0, concat_axis=1, tiled=True),
    )
    rows_here = row_queries.shape[0]
    own_positions = lax.dynamic_slice_in_dim(positions, my_index * rows_here, rows_here)
    attended = attend(row_queries, row_keyval, cache_keys, cache_values, lengths, own_positions)
    head_rows = lax.all_to_all(attended, "tensor", split_axis=1, concat_axis=0, tiled=True)
    partial_value = jnp.dot(head_rows, w_out, preferred_element_type=jnp.float32)
    summed = lax.psum(partial_value.astype(jnp.bfloat16), "tensor").astype(jnp.float32)
    full_stream = (hidden_in.astype(jnp.float32) + summed).astype(jnp.bfloat16)
    normed = normalize(full_stream, ffn_gain)
    share_width = w_out.shape[1] // lax.axis_size("tensor")
    stream = lax.dynamic_slice_in_dim(full_stream, my_index * share_width, share_width, 1)
    return (stream, normed)


def solution(mesh):
    placed = (
        P("groups", None),
        P(),
        P(None, "tensor"),
        P(None, "tensor"),
        P(("groups", "tensor"), None, None),
        P(("groups", "tensor"), None, None),
        P("tensor", None),
        P(),
        P(("groups", "tensor")),
        P("groups"),
    )
    return jax.shard_map(
        on_device,
        mesh=mesh,
        in_specs=placed,
        out_specs=(P("groups", "tensor"), P("groups", None)),
        check_vma=False,
    )
```

profile of v0, /device:TPU:0, one launch (start us, length us, event | category | flops | bytes accessed | tf_op | source)
XLA Modules:
  0.0 204.4 jit_solution(9029187076355577960)
XLA Ops:
  7.2 0.0 copy-start
  7.2 0.0 copy-start.2
  7.2 0.9 convert_element_type.68
  8.1 3.5 %fusion.3 = f32[128]{0:T(128)S(1)} fusion(bf16[128,16384]{1,0:T(8,128)(2,1)} %param.10), kind=kLoop, calls=%fused_computation.9 | loop fusion | flops 6291328 | bytes 4194816 | tf_op jit(solution)/shard_map/reduce_sum | solution.py:17
  11.6 0.0 copy-done
  11.7 0.0 copy-done.2
  11.7 0.0 copy-start.5
  11.7 1.6 fusion.25
  13.3 0.1 copy.24
  13.4 0.7 reshape.190
  14.2 7.4 %all-to-all-start.1 = ((bf16[16,2,256]{2,1,0:T(2,128)(2,1)}), bf16[16,2,256]{2,1,0:T(2,128)(2,1)S(1)}, u32[]{:S(2)}, u32[]{:S(2)}) async-start(bf16[16,2,256]{2,1,0:T(2,128)(2,1)} %reshape.190), calls=%async_computation.1 | async-start | bytes 32768 | tf_op jit(solution)/shard_map/all_to_all | solution.py:100
  21.6 0.0 copy-done.5
  21.6 0.1 dynamic-slice_convert_fusion
  21.7 0.0 copy-start.4
  21.7 9.4 %fusion.17 = f32[128,512]{1,0:T(8,128)S(1)} fusion(bf16[16384,512]{1,0:T(8,128)(2,1)} %param.12, bf16[128,16384]{1,0:T(8,128)(2,1)} %param.10, f32[16384]{0:T(1024)S(1)} %convert_element_type.68, f32[128]{0:T(128)S(1)} %add_rsqrt_fusion.1), kind=kOutput, calls=%fused_computation.25 | convolution fusion | flops 2155872256 | bytes 21299712 | tf_op jit(solution)/shard_map/dot_general | solution.py:94
  31.1 0.1 reshape.179
  31.2 0.1 multiply_cosine_fusion.1
  31.3 0.3 multiply_cosine_fusion
  31.6 0.0 copy-done.4
  31.7 0.1 iota_compare_fusion
  31.7 0.3 subtract_convert_fusion
  32.0 0.2 pad_maximum_fusion
  32.2 0.7 convert_element_type.71
  32.9 0.0 all-to-all-done.1
  32.9 6.0 %all-to-all-start = ((bf16[16,8,512]{2,1,0:T(8,128)(2,1)}), bf16[16,8,512]{2,1,0:T(8,128)(2,1)S(1)}, u32[]{:S(2)}, u32[]{:S(2)}) async-start(bf16[16,8,512]{2,1,0:T(8,128)(2,1)} %convert_element_type.71), calls=%async_computation | async-start | bytes 262144 | tf_op jit(solution)/shard_map/all_to_all | solution.py:99
  38.9 0.0 all-reduce.2.cloned.1.call-start
  39.0 0.1 reshape.191
  39.1 0.1 all_to_all.43
  39.2 0.1 subtract_convert_fusion.1
  39.3 0.1 maximum_bitcast_fusion
  39.4 7.5 %all-to-all-done = bf16[16,8,512]{2,1,0:T(8,128)(2,1)S(1)} async-done(((bf16[16,8,512]{2,1,0:T(8,128)(2,1)}), bf16[16,8,512]{2,1,0:T(8,128)(2,1)S(1)}, u32[]{:S(2)}, u32[]{:S(2)}) %all-to-all-start) | async-done | bytes 131104 | tf_op jit(solution)/shard_map/all_to_all | solution.py:99
  46.9 0.1 reshape.180
  47.0 0.2 fusion.34
  47.2 5.8 %fusion.13 = (f32[8,4,16]{2,1,0:T(4,128)S(1)}, f32[8,4,16,1024]{3,2,1,0:T(8,128)S(1)}) fusion(pred[8,1024]{1,0:T(8,128)(4,1)S(1)} %iota_compare_fusion, bf16[8,4,16,128]{3,2,1,0:T(8,128)(2,1)S(1)} %reshape.180, bf16[8,1024,512]{2,1,0:T(8,128)(2,1)} %param.14), kind=kOutput, calls=%fused_computation.22 | convolution fusion | flops 135790080 | bytes 10627072 | tf_op jit(solution)/shard_map/rgqd,rlgd->rgql/dot_general | solution.py:56
  53.0 0.6 fusion.14
  53.6 4.9 %fusion.22 = bf16[8,4,16,128]{3,2,1,0:T(8,128)(2,1)S(1)} fusion(f32[8,4,16,1024]{3,2,1,0:T(8,128)S(1)} %get-tuple-element.17, f32[8,4,16]{2,1,0:T(4,128)S(1)} %get-tuple-element.7, f32[8,4,16]{2,1,0:T(4,128)S(1)} %multiply_maximum_fusion, pred[8,1024]{1,0:T(8,128)(4,1)S(1)} %iota_compare_fusion, f32[8,4,128]{2,1,0:T(4,128)S(1)} %copy.27, ...), kind=kOutput, calls=%fused_computation.27 | convolution fusion | flops 137035776 | bytes 10647552 | tf_op jit(solution)/shard_map/rgql,rlgd->rgqd/dot_general | solution.py:71
  58.5 0.1 all_to_all.44
  58.6 0.1 copy.28
  58.7 10.5 %all_to_all.51 = bf16[8,16,512]{2,0,1:T(8,128)(2,1)S(1)} all-to-all(bf16[8,16,512]{2,0,1:T(8,128)(2,1)S(1)} %copy.28), channel_id=1, replica_groups=mesh['groups'=2,'tensor'=16] {'tensor'}, dimensions={1} | all-to-all | bytes 262144 | tf_op jit(solution)/shard_map/all_to_all | solution.py:105
  69.2 10.1 %convolution_convert_fusion = bf16[128,16384]{1,0:T(8,128)(2,1)} fusion(bf16[512,16384]{1,0:T(8,128)(2,1)} %param.16, bf16[8,16,512]{2,0,1:T(8,128)(2,1)S(1)} %all_to_all.51), kind=kOutput, calls=%fused_computation | convolution fusion | flops 2149580800 | bytes 21102592 | tf_op jit(solution)/shard_map/dot_general | solution.py:106
  79.3 0.0 copy-start.3
  79.3 0.0 all-reduce.2.cloned.1.call-update
  79.3 0.7 copy-done.3
  80.1 108.6 %all-reduce.2.cloned.1.call-done = bf16[128,16384]{1,0:T(8,128)(2,1)} async-done(((bf16[128,16384]{1,0:T(8,128)(2,1)}), bf16[128,16384]{1,0:T(8,128)(2,1)}) %all-reduce.2.cloned.1.call-update) | async-done | bytes 4194320 | tf_op jit(solution)/shard_map/psum | solution.py:107
  188.7 5.0 %fusion = (f32[128]{0:T(128)S(1)}, bf16[128,16384]{1,0:T(8,128)(2,1)S(1)}) fusion(bf16[128,16384]{1,0:T(8,128)(2,1)} %all-reduce.2.cloned.1.call-done, bf16[128,16384]{1,0:T(8,128)(2,1)} %param.10), kind=kLoop, calls=%fused_computation.6 | loop fusion | flops 14679936 | bytes 12583424 | tf_op jit(solution)/shard_map/reduce_sum | solution.py:17
  193.7 0.0 copy-start.1
  193.7 0.7 constant_dynamic-slice_fusion
  194.5 3.1 %fusion.2 = bf16[128,16384]{1,0:T(8,128)(2,1)} fusion(bf16[128,16384]{1,0:T(8,128)(2,1)S(1)} %get-tuple-element.3, f32[16384]{0:T(1024)S(1)} %convert_element_type.84, f32[128]{0:T(128)S(1)} %add_rsqrt_fusion), kind=kLoop, calls=%fused_computation.8 | loop fusion | flops 8388608 | bytes 8454656 | tf_op jit(solution)/shard_map/convert_element_type | solution.py:18
  197.6 0.0 copy-done.1
  (11 shorter events, 0.1 us)
Async XLA Ops:
  7.2 4.5 %copy-start = (bf16[16384,64]{0,1:T(8,128)(2,1)S(1)}, bf16[16384,64]{0,1:T(8,128)(2,1)}, u32[]{:S(2)}) copy-start(bf16[16384,64]{0,1:T(8,128)(2,1)} %param.13) | copy-start | bytes 6291460
  7.2 4.5 %copy-start.2 = (bf16[128,16384]{1,0:T(8,128)(2,1)S(1)}, bf16[128,16384]{1,0:T(8,128)(2,1)}, u32[]{:S(2)}) copy-start(bf16[128,16384]{1,0:T(8,128)(2,1)} %param.10) | copy-start | bytes 12582916
  11.7 9.9 %copy-start.5 = (s32[128]{0:T(128)S(1)}, s32[128]{0:T(128)}, u32[]{:S(2)}) copy-start(s32[128]{0:T(128)} %param.19) | copy-start | bytes 1540
  14.2 18.8 %all-to-all-start.1 = ((bf16[16,2,256]{2,1,0:T(2,128)(2,1)}), bf16[16,2,256]{2,1,0:T(2,128)(2,1)S(1)}, u32[]{:S(2)}, u32[]{:S(2)}) async-start(bf16[16,2,256]{2,1,0:T(2,128)(2,1)} %reshape.190), calls=%async_computation.1 | async-start | bytes 32768 | tf_op jit(solution)/shard_map/all_to_all | solution.py:100
  21.7 10.0 %copy-start.4 = (s32[8]{0:T(128)S(1)}, s32[8]{0:T(128)}, u32[]{:S(2)}) copy-start(s32[8]{0:T(128)} %param.18) | copy-start | bytes 100
  32.9 13.9 %all-to-all-start = ((bf16[16,8,512]{2,1,0:T(8,128)(2,1)}), bf16[16,8,512]{2,1,0:T(8,128)(2,1)S(1)}, u32[]{:S(2)}, u32[]{:S(2)}) async-start(bf16[16,8,512]{2,1,0:T(8,128)(2,1)} %convert_element_type.71), calls=%async_computation | async-start | bytes 262144 | tf_op jit(solution)/shard_map/all_to_all | solution.py:99
  38.9 149.7 %all-reduce.2.cloned.1.call-start = ((), (), s32[]{:S(2)}) async-start(), calls=%async_computation.3 | async-start | bytes 8388608 | tf_op jit(solution)/shard_map/psum | solution.py:107
  79.3 0.8 copy-start.3
  193.7 3.9 %copy-start.1 = (bf16[16384,64]{0,1:T(8,128)(2,1)S(1)}, bf16[16384,64]{0,1:T(8,128)(2,1)}, u32[]{:S(2)}) copy-start(bf16[16384,64]{0,1:T(8,128)(2,1)} %param.13) | copy-start | bytes 6291460
Sparse Core Ops, SparseCore 0:
  79.5 109.1 all-reduce.1
where the time goes:
time: 205 us; the launch traced here: 204 us
  waiting for transfers between devices  116 us (57%)
  matrix products  32 us (16%)
  other arithmetic  14.5 us (7%)
  between operations  14.3 us (7%)
  starting transfers between devices  13.4 us (7%)
  blocking collectives  10.5 us (5%)
  local copies, waits for them, and re-layouts  3.65 us (2%)
    psum x1, waiting for transfers between devices, on_device(): lax.psum(partial_value.astype(jnp.bfloat16), 'tensor').astype(jnp.float32)  109 us
    all_to_all x1, blocking collectives, on_device(): lax.all_to_all(attended, 'tensor', split_axis=1, concat_axis=0, tiled=True)  10.5 us
    dot_general x1, matrix products, on_device(): jnp.dot(head_rows, w_out, preferred_element_type=jnp.float32)  10.1 us
    dot_general x1, matrix products, on_device(): queries = jnp.dot(normed_in, w_query, preferred_element_type=jnp.float32)  9.43 us
    reduce_sum x2, other arithmetic, normalize(): mean_square = jnp.mean(floats * floats, axis=-1, keepdims=True)  8.56 us
    all_to_all x1, waiting for transfers between devices, on_device(): lax.all_to_all(queries, 'tensor', split_axis=0, concat_axis=1, tiled=True)  7.49 us
    all_to_all x1, starting transfers between devices, on_device(): lax.all_to_all(keyval, 'tensor', split_axis=0, concat_axis=1, tiled=True)  7.39 us
    all_to_all x1, starting transfers between devices, on_device(): lax.all_to_all(queries, 'tensor', split_axis=0, concat_axis=1, tiled=True)  6 us
  transfers between devices with their start and end apart: 3, of which 2 were waited for; matrix products, arithmetic and copies ran while one was open for 6% of the time, Pallas kernels for 0%

commit v1 on v0

--- a/solution.py
+++ b/solution.py
@@ -1,8 +1,11 @@
+import functools
 import math
 
 import jax
 import jax.numpy as jnp
 from jax import lax
+from jax.experimental import pallas as pl
+from jax.experimental.pallas import tpu as pltpu
 from jax.sharding import PartitionSpec as P
 
 HD = 128
@@ -76,6 +79,72 @@
     return mixed.astype(jnp.bfloat16).reshape(row_count, -1)
 
 
+def bit_orders(count):
+    bits = list(range(count.bit_length() - 1))
+    return (bits, bits[:1] + bits[2:] + bits[1:2])
+
+
+def place(offset, order):
+    spot = 0
+    for bit in order:
+        spot = spot * 2 + ((offset >> bit) & 1)
+    return spot
+
+
+def project_kernel(count, offsets, heads_ref, w_ref, first_ref, second_ref, w_buffer, arrived):
+    me = lax.axis_index("tensor")
+    width = w_buffer.shape[2]
+    orders = bit_orders(count)
+    half = len(offsets)
+    copies = []
+    for slot, offset in enumerate(offsets):
+        column = pl.multiple_of(jnp.bitwise_xor(me, offset) * width, width)
+        copies.append(
+            pltpu.make_async_copy(
+                w_ref.at[:, pl.ds(column, width)], w_buffer.at[slot], arrived.at[slot]
+            )
+        )
+        copies[-1].start()
+    heads = heads_ref[...]
+    for slot, offset in enumerate(offsets):
+        copies[slot].wait()
+        product = jnp.dot(heads, w_buffer[slot], preferred_element_type=jnp.float32).astype(
+            jnp.bfloat16
+        )
+        first_ref[place(offset, orders[0]) % half] = product[:, : width // 2]
+        second_ref[place(offset, orders[1]) % half] = product[:, width // 2 :]
+
+
+def project(heads, w_out, count, offsets):
+    rows, depth = heads.shape
+    width = w_out.shape[1] // count
+    share = jax.ShapeDtypeStruct((len(offsets), rows, width // 2), jnp.bfloat16)
+    return pl.pallas_call(
+        functools.partial(project_kernel, count, offsets),
+        out_shape=(share, share),
+        in_specs=[pl.BlockSpec(memory_space=pltpu.VMEM), pl.BlockSpec(memory_space=pl.ANY)],
+        out_specs=(pl.BlockSpec(memory_space=pltpu.VMEM),) * 2,
+        scratch_shapes=[
+            pltpu.VMEM((len(offsets), depth, width), jnp.bfloat16),
+            pltpu.SemaphoreType.DMA((len(offsets),)),
+        ],
+        compiler_params=pltpu.CompilerParams(vmem_limit_bytes=30 * 1024 * 1024),
+        cost_estimate=pl.CostEstimate(
+            flops=2 * rows * depth * width * len(offsets),
+            bytes_accessed=2 * (depth + rows) * width * len(offsets),
+            transcendentals=0,
+        ),
+    )(heads, w_out)
+
+
+def swap(values, bit, count):
+    return lax.ppermute(values, "tensor", [(i, i ^ (1 << bit)) for i in range(count)])
+
+
+def add(one, other):
+    return (one.astype(jnp.float32) + other.astype(jnp.float32)).astype(jnp.bfloat16)
+
+
 def on_device(
     hidden_in,
     attn_gain,
@@ -89,26 +158,48 @@
     positions,
 ):
     row_count = hidden_in.shape[0]
+    count = lax.axis_size("tensor")
     my_index = lax.axis_index("tensor")
     normed_in = normalize(hidden_in, attn_gain)
     queries = jnp.dot(normed_in, w_query, preferred_element_type=jnp.float32)
     queries = queries.reshape(row_count, queries.shape[1] // HD, HD)
     queries = rotate(queries, positions).astype(jnp.bfloat16).reshape(row_count, -1)
     keyval = jnp.dot(normed_in, w_keyval, preferred_element_type=jnp.float32).astype(jnp.bfloat16)
-    row_queries, row_keyval = (
-        lax.all_to_all(queries, "tensor", split_axis=0, concat_axis=1, tiled=True),
-        lax.all_to_all(keyval, "tensor", split_axis=0, concat_axis=1, tiled=True),
-    )
-    rows_here = row_queries.shape[0]
+    query_width = queries.shape[1]
+    rows_here = row_count // count
+    both = lax.all_to_all(
+        jnp.concatenate([queries, keyval], axis=1).reshape(count, rows_here, -1),
+        "tensor",
+        split_axis=0,
+        concat_axis=0,
+        tiled=True,
+    )
+    both = jnp.swapaxes(both, 0, 1)
+    row_queries = both[..., :query_width].reshape(rows_here, -1)
+    row_keyval = both[..., query_width:].reshape(rows_here, -1)
     own_positions = lax.dynamic_slice_in_dim(positions, my_index * rows_here, rows_here)
     attended = attend(row_queries, row_keyval, cache_keys, cache_values, lengths, own_positions)
     head_rows = lax.all_to_all(attended, "tensor", split_axis=1, concat_axis=0, tiled=True)
-    partial_value = jnp.dot(head_rows, w_out, preferred_element_type=jnp.float32)
-    summed = lax.psum(partial_value.astype(jnp.bfloat16), "tensor").astype(jnp.float32)
-    full_stream = (hidden_in.astype(jnp.float32) + summed).astype(jnp.bfloat16)
+
+    orders = bit_orders(count)
+    sent = project(head_rows, w_out, count, list(range(1, count, 2)))
+    received = [swap(block, orders[k][0], count) for k, block in enumerate(sent)]
+    kept = project(head_rows, w_out, count, list(range(0, count, 2)))
+    sums = []
+    for k, order in enumerate(orders):
+        keep, arrival = kept[k], received[k]
+        for bit in order[1:]:
+            half = keep.shape[0] // 2
+            leave = add(keep[half:], arrival[half:])
+            stay = add(keep[:half], arrival[:half])
+            keep, arrival = stay, swap(leave, bit, count)
+        sums.append(keep[0].astype(jnp.float32) + arrival[0].astype(jnp.float32))
+    summed = jnp.concatenate(sums, axis=1)
+    share_width = w_out.shape[1] // count
+    mine = lax.dynamic_slice_in_dim(hidden_in, my_index * share_width, share_width, 1)
+    stream = (mine.astype(jnp.float32) + summed).astype(jnp.bfloat16)
+    full_stream = lax.all_gather(stream, "tensor", axis=1, tiled=True)
     normed = normalize(full_stream, ffn_gain)
-    share_width = w_out.shape[1] // lax.axis_size("tensor")
-    stream = lax.dynamic_slice_in_dim(full_stream, my_index * share_width, share_width, 1)
     return (stream, normed)
 
 

time: 205 us -> 181 us (0.88)
  waiting for transfers between devices: 116 us -> 90.8 us
  matrix products: 32 us -> 22 us
  Pallas kernels: 0 us -> 8.26 us
  local copies, waits for them, and re-layouts: 3.65 us -> 6.7 us
  starting transfers between devices: 13.4 us -> 11.1 us
  other arithmetic: 14.5 us -> 16.7 us
    psum x1 -> x0, waiting for transfers between devices: 109 us -> none  [on_device(): lax.psum(partial_value.astype(jnp.bfloat16), 'tensor').astype(jnp.float32)]
    all_gather x0 -> x1, waiting for transfers between devices: none -> 50.7 us  [on_device(): full_stream = lax.all_gather(stream, 'tensor', axis=1, tiled=True)]
    ppermute x0 -> x8, waiting for transfers between devices: none -> 32 us  [swap(): lax.ppermute(values, 'tensor', [(i, i ^ 1 << bit) for i in range(count)])]
    dot_general x1 -> x0, matrix products: 10.1 us -> none  [on_device(): jnp.dot(head_rows, w_out, preferred_element_type=jnp.float32)]
    pallas_call x0 -> x2, Pallas kernels: none -> 8.26 us  [project(): pl.pallas_call(functools.partial(project_kernel, count, offsets), out_sha...]
    all_to_all x2 -> x1, starting transfers between devices: 13.4 us -> 7.39 us  [on_device(): lax.all_to_all(jnp.concatenate([queries, keyval], axis=1).reshape(count,...]
    unnamed x14 -> x16, local copies, waits for them, and re-layouts: 1.58 us -> 6.01 us
    ppermute x0 -> x8, starting transfers between devices: none -> 3.71 us  [swap(): lax.ppermute(values, 'tensor', [(i, i ^ 1 << bit) for i in range(count)])]
  transfers between devices with their start and end apart: 3 -> 10, of which waited for: 2 -> 6; matrix products, arithmetic and copies ran while one was open for 6% -> 1% of each run, Pallas kernels for 0% -> 2%
where the time goes in v1:
time: 181 us
  waiting for transfers between devices  90.8 us (50%)
  matrix products  22 us (12%)
  other arithmetic  16.7 us (9%)
  between operations  14.4 us (8%)
  starting transfers between devices  11.1 us (6%)
  blocking collectives  10.5 us (6%)
  Pallas kernels  8.26 us (5%)
  local copies, waits for them, and re-layouts  6.7 us (4%)
    all_gather x1, waiting for transfers between devices, on_device(): full_stream = lax.all_gather(stream, 'tensor', axis=1, tiled=True)  50.7 us
    ppermute x8, waiting for transfers between devices, swap(): lax.ppermute(values, 'tensor', [(i, i ^ 1 << bit) for i in range(count)])  32 us
    all_to_all x1, blocking collectives, on_device(): lax.all_to_all(attended, 'tensor', split_axis=1, concat_axis=0, tiled=True)  10.5 us
    dot_general x1, matrix products, on_device(): queries = jnp.dot(normed_in, w_query, preferred_element_type=jnp.float32)  9.44 us
    pallas_call x2, Pallas kernels, project(): pl.pallas_call(functools.partial(project_kernel, count, offsets), out_sha...  8.26 us
    all_to_all x1, waiting for transfers between devices, on_device(): lax.all_to_all(jnp.concatenate([queries, keyval], axis=1).reshape(count,...  8.13 us
    all_to_all x1, starting transfers between devices, on_device(): lax.all_to_all(jnp.concatenate([queries, keyval], axis=1).reshape(count,...  7.39 us
    reduce_sum x2, other arithmetic, normalize(): mean_square = jnp.mean(floats * floats, axis=-1, keepdims=True)  6.71 us
  transfers between devices with their start and end apart: 10, of which 6 were waited for; matrix products, arithmetic and copies ran while one was open for 1% of the time, Pallas kernels for 2%

profile of v1, /device:TPU:0, one launch (start us, length us, event | category | flops | bytes accessed | tf_op | source)
XLA Modules:
  0.0 180.5 jit_solution(13495726849189208959)
XLA Ops:
  7.2 0.0 copy-start
  7.2 0.0 copy-start.4
  7.2 0.8 convert_element_type.191
  8.0 3.5 %fusion = f32[128]{0:T(128)S(1)} fusion(bf16[128,16384]{1,0:T(8,128)(2,1)} %param.10), kind=kLoop, calls=%fused_computation.4 | loop fusion | flops 6291328 | bytes 4194816 | tf_op jit(solution)/shard_map/reduce_sum | solution.py:20
  11.5 0.8 convert_element_type.189
  12.3 0.0 copy-done
  12.3 1.7 fusion.24
  14.0 0.1 copy.28
  14.1 0.0 copy-start.6
  14.1 0.0 copy-start.7
  14.1 9.4 %fusion.16 = f32[128,512]{1,0:T(8,128)S(1)} fusion(bf16[16384,512]{1,0:T(8,128)(2,1)} %param.12, bf16[128,16384]{1,0:T(8,128)(2,1)} %param.10, f32[16384]{0:T(1024)S(1)} %convert_element_type.189, f32[128]{0:T(128)S(1)} %add_rsqrt_fusion.1), kind=kOutput, calls=%fused_computation.22 | convolution fusion | flops 2155872256 | bytes 21299712 | tf_op jit(solution)/shard_map/dot_general | solution.py:164
  23.5 0.1 reshape.181
  23.6 0.3 multiply_cosine_fusion
  24.0 0.3 subtract_convert_fusion
  24.3 0.2 pad_maximum_fusion.1
  24.5 0.1 convert_element_type.192
  24.5 0.7 pad_maximum_fusion
  25.2 7.4 %all-to-all-start = ((bf16[16,8,576]{2,1,0:T(8,128)(2,1)}), bf16[16,8,576]{2,1,0:T(8,128)(2,1)S(1)}, u32[]{:S(2)}, u32[]{:S(2)}) async-start(bf16[16,8,576]{2,1,0:T(8,128)(2,1)} %pad_maximum_fusion), calls=%async_computation | async-start | bytes 327680 | tf_op jit(solution)/shard_map/all_to_all | solution.py:170
  32.6 0.0 all-gather.2.cloned.1.call-start
  32.7 0.1 iota_compare_fusion
  32.7 0.1 dynamic-slice_convert_fusion
  32.8 0.1 multiply_cosine_fusion.1
  32.9 8.1 %all-to-all-done = bf16[16,8,576]{2,1,0:T(8,128)(2,1)S(1)} async-done(((bf16[16,8,576]{2,1,0:T(8,128)(2,1)}), bf16[16,8,576]{2,1,0:T(8,128)(2,1)S(1)}, u32[]{:S(2)}, u32[]{:S(2)}) %all-to-all-start) | async-done | bytes 147488 | tf_op jit(solution)/shard_map/all_to_all | solution.py:170
  41.1 0.1 reshape_reshape.3
  41.2 0.1 reshape.183
  41.4 0.1 subtract_convert_fusion.1
  41.4 0.1 maximum_bitcast_fusion
  41.5 0.2 fusion.33
  41.7 5.8 %fusion.12 = (f32[8,4,16]{2,1,0:T(4,128)S(1)}, f32[8,4,16,1024]{3,2,1,0:T(8,128)S(1)}) fusion(pred[8,1024]{1,0:T(8,128)(4,1)S(1)} %iota_compare_fusion, bf16[8,4,16,128]{3,2,1,0:T(8,128)(2,1)S(1)} %reshape_reshape.3, bf16[8,1024,512]{2,1,0:T(8,128)(2,1)} %param.14), kind=kOutput, calls=%fused_computation.19 | convolution fusion | flops 135790080 | bytes 10627072 | tf_op jit(solution)/shard_map/rgqd,rlgd->rgql/dot_general | solution.py:59
  47.5 0.6 fusion.13
  48.1 5.0 %fusion.21 = bf16[8,4,16,128]{3,2,1,0:T(8,128)(2,1)S(1)} fusion(f32[8,4,16,1024]{3,2,1,0:T(8,128)S(1)} %get-tuple-element.31, f32[8,4,16]{2,1,0:T(4,128)S(1)} %get-tuple-element.21, f32[8,4,16]{2,1,0:T(4,128)S(1)} %multiply_maximum_fusion, pred[8,1024]{1,0:T(8,128)(4,1)S(1)} %iota_compare_fusion, f32[8,4,128]{2,1,0:T(4,128)S(1)} %copy.33, ...), kind=kOutput, calls=%fused_computation.24 | convolution fusion | flops 137035776 | bytes 10647552 | tf_op jit(solution)/shard_map/rgql,rlgd->rgqd/dot_general | solution.py:74
  53.1 0.1 all_to_all.18
  53.2 0.1 copy.34
  53.3 10.5 %all_to_all.24 = bf16[8,16,512]{2,0,1:T(8,128)(2,1)S(1)} all-to-all(bf16[8,16,512]{2,0,1:T(8,128)(2,1)S(1)} %copy.34), channel_id=1, replica_groups=mesh['groups'=2,'tensor'=16] {'tensor'}, dimensions={1} | all-to-all | bytes 262144 | tf_op jit(solution)/shard_map/all_to_all | solution.py:182
  63.8 5.8 %copy-done.2 = bf16[512,16384]{1,0:T(8,128)(2,1)S(1)} copy-done((bf16[512,16384]{1,0:T(8,128)(2,1)S(1)}, bf16[512,16384]{1,0:T(8,128)(2,1)}, u32[]{:S(2)}) %copy-start.2) | copy-done | bytes 16777240
  69.6 4.1 %shard_map.114 = (bf16[8,128,512]{2,1,0:T(8,128)(2,1)S(1)}, bf16[8,128,512]{2,1,0:T(8,128)(2,1)S(1)}) custom-call(bf16[128,512]{1,0:T(8,128)(2,1)S(1)} %bitcast.49, bf16[512,16384]{1,0:T(8,128)(2,1)S(1)} %copy-done.2), custom_call_target="tpu_custom_call" | custom-call | flops 1073741824 | bytes 10485760 | tf_op jit(solution)/shard_map/pallas_call | solution.py:122
  73.7 0.1 collective-permute-start.4
  73.8 0.5 collective-permute-start
  74.3 4.1 %shard_map.113 = (bf16[8,128,512]{2,1,0:T(8,128)(2,1)S(1)}, bf16[8,128,512]{2,1,0:T(8,128)(2,1)S(1)}) custom-call(bf16[128,512]{1,0:T(8,128)(2,1)S(1)} %bitcast.50, bf16[512,16384]{1,0:T(8,128)(2,1)S(1)} %copy-done.2), custom_call_target="tpu_custom_call" | custom-call | flops 1073741824 | bytes 10485760 | tf_op jit(solution)/shard_map/pallas_call | solution.py:122
  78.4 0.0 collective-permute-done.4
  78.4 0.3 add_convert_fusion.1
  78.7 0.1 collective-permute-start.5
  78.8 0.0 collective-permute-done
  78.8 0.0 copy-start.5
  78.8 0.3 add_convert_fusion.3
  79.2 0.4 collective-permute-start.1
  79.5 13.2 %collective-permute-done.5 = bf16[4,128,512]{2,1,0:T(8,128)(2,1)S(1)} collective-permute-done((bf16[4,128,512]{2,1,0:T(8,128)(2,1)S(1)}, bf16[4,128,512]{2,1,0:T(8,128)(2,1)S(1)}, u32[]{:S(2)}, u32[]{:S(2)}) %collective-permute-start.5) | collective-permute-done | bytes 524320 | tf_op jit(solution)/shard_map/ppermute | solution.py:141
  92.7 0.1 add_convert_fusion.5
  92.9 0.4 collective-permute-start.6
  93.3 0.0 collective-permute-done.1
  93.3 0.1 add_convert_fusion.7
  93.4 1.6 collective-permute-start.2
  95.0 11.8 %collective-permute-done.6 = bf16[2,128,512]{2,1,0:T(8,128)(2,1)S(1)} collective-permute-done((bf16[2,128,512]{2,1,0:T(8,128)(2,1)S(1)}, bf16[2,128,512]{2,1,0:T(8,128)(2,1)S(1)}, u32[]{:S(2)}, u32[]{:S(2)}) %collective-permute-start.6) | collective-permute-done | bytes 262176 | tf_op jit(solution)/shard_map/ppermute | solution.py:141
  106.9 0.4 collective-permute-start.7
  107.4 0.0 collective-permute-done.2
  107.4 0.2 collective-permute-start.3
  107.6 4.7 %collective-permute-done.7 = bf16[1,128,512]{2,1,0:T(8,128)(2,1)S(1)} collective-permute-done((bf16[1,128,512]{2,1,0:T(8,128)(2,1)S(1)}, bf16[1,128,512]{2,1,0:T(8,128)(2,1)S(1)}, u32[]{:S(2)}, u32[]{:S(2)}) %collective-permute-start.7) | collective-permute-done | bytes 131104 | tf_op jit(solution)/shard_map/ppermute | solution.py:141
  112.4 2.2 %collective-permute-done.3 = bf16[1,128,512]{2,1,0:T(8,128)(2,1)S(1)} collective-permute-done((bf16[1,128,512]{2,1,0:T(8,128)(2,1)S(1)}, bf16[1,128,512]{2,1,0:T(8,128)(2,1)S(1)}, u32[]{:S(2)}, u32[]{:S(2)}) %collective-permute-start.3) | collective-permute-done | bytes 131104 | tf_op jit(solution)/shard_map/ppermute | solution.py:141
  114.7 1.7 fusion.32
  116.4 0.0 all-gather.2.cloned.1.call-update
  116.5 50.7 %all-gather.2.cloned.1.call-done = bf16[128,16384]{1,0:T(8,128)(2,1)} async-done(((bf16[128,1024]{1,0:T(8,128)(2,1)}), bf16[128,16384]{1,0:T(8,128)(2,1)}) %all-gather.2.cloned.1.call-update) | async-done | bytes 4194320 | tf_op jit(solution)/shard_map/all_gather | solution.py:201
  167.1 3.2 %fusion.3 = f32[128]{0:T(128)S(1)} fusion(bf16[128,16384]{1,0:T(8,128)(2,1)} %all-gather.2.cloned.1.call-done), kind=kLoop, calls=%fused_computation.7 | loop fusion | flops 6291328 | bytes 4194816 | tf_op jit(solution)/shard_map/reduce_sum | solution.py:20
  170.4 0.2 copy-done.3
  170.6 3.1 %fusion.5 = bf16[128,16384]{1,0:T(8,128)(2,1)} fusion(bf16[128,16384]{1,0:T(8,128)(2,1)S(1)} %copy-done.3, f32[16384]{0:T(1024)S(1)} %convert_element_type.243, f32[128]{0:T(128)S(1)} %add_rsqrt_fusion), kind=kLoop, calls=%fused_computation.9 | loop fusion | flops 8388608 | bytes 8454656 | tf_op jit(solution)/shard_map/convert_element_type | solution.py:21
  (24 shorter events, 0.3 us)
Async XLA Ops:
  7.2 5.1 %copy-start = (bf16[16384,64]{0,1:T(8,128)(2,1)S(1)}, bf16[16384,64]{0,1:T(8,128)(2,1)}, u32[]{:S(2)}) copy-start(bf16[16384,64]{0,1:T(8,128)(2,1)} %param.13) | copy-start | bytes 6291460
  7.2 5.1 %copy-start.4 = (bf16[128,16384]{1,0:T(8,128)(2,1)S(1)}, bf16[128,16384]{1,0:T(8,128)(2,1)}, u32[]{:S(2)}) copy-start(bf16[128,16384]{1,0:T(8,128)(2,1)} %param.10) | copy-start | bytes 12582916
  14.1 18.6 %copy-start.6 = (s32[8]{0:T(128)S(1)}, s32[8]{0:T(128)}, u32[]{:S(2)}) copy-start(s32[8]{0:T(128)} %param.18) | copy-start | bytes 100
  14.1 18.7 %copy-start.7 = (s32[128]{0:T(128)S(1)}, s32[128]{0:T(128)}, u32[]{:S(2)}) copy-start(s32[128]{0:T(128)} %param.19) | copy-start | bytes 1540
  25.2 15.9 %all-to-all-start = ((bf16[16,8,576]{2,1,0:T(8,128)(2,1)}), bf16[16,8,576]{2,1,0:T(8,128)(2,1)S(1)}, u32[]{:S(2)}, u32[]{:S(2)}) async-start(bf16[16,8,576]{2,1,0:T(8,128)(2,1)} %pad_maximum_fusion), calls=%async_computation | async-start | bytes 327680 | tf_op jit(solution)/shard_map/all_to_all | solution.py:170
  32.6 134.5 %all-gather.2.cloned.1.call-start = ((), (), s32[]{:S(2)}) async-start(), calls=%async_computation.2 | async-start | bytes 4456448 | tf_op jit(solution)/shard_map/all_gather | solution.py:201
  63.8 5.8 %copy-start.2 = (bf16[512,16384]{1,0:T(8,128)(2,1)S(1)}, bf16[512,16384]{1,0:T(8,128)(2,1)}, u32[]{:S(2)}) copy-start(bf16[512,16384]{1,0:T(8,128)(2,1)} %w_ref.3) | copy-start | bytes 50331652
  73.7 4.7 %collective-permute-start.4 = (bf16[8,128,512]{2,1,0:T(8,128)(2,1)S(1)}, bf16[8,128,512]{2,1,0:T(8,128)(2,1)S(1)}, u32[]{:S(2)}, u32[]{:S(2)}) collective-permute-start(bf16[8,128,512]{2,1,0:T(8,128)(2,1)S(1)} %get-tuple-element.9), channel_id=1, source_target_pairs={{0,1},{1,0},{2,3},{3,2},{4,5},{5,4},{6,7},{7,6},{8,9},{9,8},{10,11... | collective-permute-start | bytes 3145736 | tf_op jit(solution)/shard_map/ppermute | solution.py:141
  73.8 5.0 %collective-permute-start = (bf16[8,128,512]{2,1,0:T(8,128)(2,1)S(1)}, bf16[8,128,512]{2,1,0:T(8,128)(2,1)S(1)}, u32[]{:S(2)}, u32[]{:S(2)}) collective-permute-start(bf16[8,128,512]{2,1,0:T(8,128)(2,1)S(1)} %get-tuple-element.7), channel_id=1, source_target_pairs={{0,1},{1,0},{2,3},{3,2},{4,5},{5,4},{6,7},{7,6},{8,9},{9,8},{10,11... | collective-permute-start | bytes 3145736 | tf_op jit(solution)/shard_map/ppermute | solution.py:141
  78.7 14.0 %collective-permute-start.5 = (bf16[4,128,512]{2,1,0:T(8,128)(2,1)S(1)}, bf16[4,128,512]{2,1,0:T(8,128)(2,1)S(1)}, u32[]{:S(2)}, u32[]{:S(2)}) collective-permute-start(bf16[4,128,512]{2,1,0:T(8,128)(2,1)S(1)} %get-tuple-element.13), channel_id=1, source_target_pairs={{0,4},{1,5},{2,6},{3,7},{4,0},{5,1},{6,2},{7,3},{8,12},{9,13},{10,... | collective-permute-start | bytes 1572872 | tf_op jit(solution)/shard_map/ppermute | solution.py:141
  78.8 37.6 %copy-start.5 = (bf16[16384]{0:T(1024)(128)(2,1)S(1)}, bf16[16384]{0:T(1024)(128)(2,1)}, u32[]{:S(2)}) copy-start(bf16[16384]{0:T(1024)(128)(2,1)} %param.17) | copy-start | bytes 98308
  79.2 14.1 %collective-permute-start.1 = (bf16[4,128,512]{2,1,0:T(8,128)(2,1)S(1)}, bf16[4,128,512]{2,1,0:T(8,128)(2,1)S(1)}, u32[]{:S(2)}, u32[]{:S(2)}) collective-permute-start(bf16[4,128,512]{2,1,0:T(8,128)(2,1)S(1)} %get-tuple-element.11), channel_id=1, source_target_pairs={{0,2},{1,3},{2,0},{3,1},{4,6},{5,7},{6,4},{7,5},{8,10},{9,11},{10,... | collective-permute-start | bytes 1572872 | tf_op jit(solution)/shard_map/ppermute | solution.py:141
  92.9 14.0 %collective-permute-start.6 = (bf16[2,128,512]{2,1,0:T(8,128)(2,1)S(1)}, bf16[2,128,512]{2,1,0:T(8,128)(2,1)S(1)}, u32[]{:S(2)}, u32[]{:S(2)}) collective-permute-start(bf16[2,128,512]{2,1,0:T(8,128)(2,1)S(1)} %get-tuple-element.17), channel_id=1, source_target_pairs={{0,8},{1,9},{2,10},{3,11},{4,12},{5,13},{6,14},{7,15},{8,0},{9,1},... | collective-permute-start | bytes 786440 | tf_op jit(solution)/shard_map/ppermute | solution.py:141
  93.4 13.9 %collective-permute-start.2 = (bf16[2,128,512]{2,1,0:T(8,128)(2,1)S(1)}, bf16[2,128,512]{2,1,0:T(8,128)(2,1)S(1)}, u32[]{:S(2)}, u32[]{:S(2)}) collective-permute-start(bf16[2,128,512]{2,1,0:T(8,128)(2,1)S(1)} %get-tuple-element.15), channel_id=1, source_target_pairs={{0,4},{1,5},{2,6},{3,7},{4,0},{5,1},{6,2},{7,3},{8,12},{9,13},{10,... | collective-permute-start | bytes 786440 | tf_op jit(solution)/shard_map/ppermute | solution.py:141
  106.9 5.4 %collective-permute-start.7 = (bf16[1,128,512]{2,1,0:T(8,128)(2,1)S(1)}, bf16[1,128,512]{2,1,0:T(8,128)(2,1)S(1)}, u32[]{:S(2)}, u32[]{:S(2)}) collective-permute-start(bf16[1,128,512]{2,1,0:T(8,128)(2,1)S(1)} %add_convert_fusion.8), channel_id=1, source_target_pairs={{0,2},{1,3},{2,0},{3,1},{4,6},{5,7},{6,4},{7,5},{8,10},{9,11},{10,... | collective-permute-start | bytes 393224 | tf_op jit(solution)/shard_map/ppermute | solution.py:141
  107.4 7.2 %collective-permute-start.3 = (bf16[1,128,512]{2,1,0:T(8,128)(2,1)S(1)}, bf16[1,128,512]{2,1,0:T(8,128)(2,1)S(1)}, u32[]{:S(2)}, u32[]{:S(2)}) collective-permute-start(bf16[1,128,512]{2,1,0:T(8,128)(2,1)S(1)} %add_convert_fusion.10), channel_id=1, source_target_pairs={{0,8},{1,9},{2,10},{3,11},{4,12},{5,13},{6,14},{7,15},{8,0},{9,1},... | collective-permute-start | bytes 393224 | tf_op jit(solution)/shard_map/ppermute | solution.py:141
  167.1 3.4 %copy-start.3 = (bf16[128,16384]{1,0:T(8,128)(2,1)S(1)}, bf16[128,16384]{1,0:T(8,128)(2,1)}, u32[]{:S(2)}) copy-start(bf16[128,16384]{1,0:T(8,128)(2,1)} %all-gather.2.cloned.1.call-done) | copy-start | bytes 12582916
  170.4 3.3 %copy-start.1 = (bf16[16384,64]{0,1:T(8,128)(2,1)S(1)}, bf16[16384,64]{0,1:T(8,128)(2,1)}, u32[]{:S(2)}) copy-start(bf16[16384,64]{0,1:T(8,128)(2,1)} %param.13) | copy-start | bytes 6291460
Sparse Core Ops, SparseCore 0:
  116.5 50.5 all-gather.1

commit v2 on v1

--- a/solution.py
+++ b/solution.py
@@ -79,9 +79,22 @@
     return mixed.astype(jnp.bfloat16).reshape(row_count, -1)
 
 
-def bit_orders(count):
-    bits = list(range(count.bit_length() - 1))
-    return (bits, bits[:1] + bits[2:] + bits[1:2])
+def plans(count):
+    bits = list(range(1, count.bit_length() - 1))
+    turned = bits[::-1]
+    crossed = turned[:-2] + turned[:-3:-1]
+    return [
+        (bits, turned),
+        (bits, crossed),
+        (bits, crossed),
+        (bits[1:] + bits[:1], turned),
+    ]
+
+
+def timetable(count):
+    if count == 16:
+        return [int(c) for c in "03013120032130121302120321013232"]
+    return [s for _ in range(2 * (count.bit_length() - 2) + 2) for s in (0, 3, 1, 2)]
 
 
 def place(offset, order):
@@ -91,11 +104,10 @@
     return spot
 
 
-def project_kernel(count, offsets, heads_ref, w_ref, first_ref, second_ref, w_buffer, arrived):
+def project_kernel(count, offsets, heads_ref, w_ref, *refs):
+    *set_refs, w_buffer, arrived = refs
     me = lax.axis_index("tensor")
     width = w_buffer.shape[2]
-    orders = bit_orders(count)
-    half = len(offsets)
     copies = []
     for slot, offset in enumerate(offsets):
         column = pl.multiple_of(jnp.bitwise_xor(me, offset) * width, width)
@@ -111,30 +123,71 @@
         product = jnp.dot(heads, w_buffer[slot], preferred_element_type=jnp.float32).astype(
             jnp.bfloat16
         )
-        first_ref[place(offset, orders[0]) % half] = product[:, : width // 2]
-        second_ref[place(offset, orders[1]) % half] = product[:, width // 2 :]
+        start = 0
+        for ref, (order, _) in zip(set_refs, plans(count)):
+            ref[place(offset, order)] = product[start : start + ref.shape[1]]
+            start += ref.shape[1]
 
 
 def project(heads, w_out, count, offsets):
     rows, depth = heads.shape
     width = w_out.shape[1] // count
-    share = jax.ShapeDtypeStruct((len(offsets), rows, width // 2), jnp.bfloat16)
+    sets = len(plans(count))
+    share = jax.ShapeDtypeStruct((len(offsets), rows // sets, width), jnp.bfloat16)
     return pl.pallas_call(
         functools.partial(project_kernel, count, offsets),
-        out_shape=(share, share),
+        out_shape=(share,) * sets,
         in_specs=[pl.BlockSpec(memory_space=pltpu.VMEM), pl.BlockSpec(memory_space=pl.ANY)],
-        out_specs=(pl.BlockSpec(memory_space=pltpu.VMEM),) * 2,
+        out_specs=(pl.BlockSpec(memory_space=pltpu.VMEM),) * sets,
         scratch_shapes=[
             pltpu.VMEM((len(offsets), depth, width), jnp.bfloat16),
             pltpu.SemaphoreType.DMA((len(offsets),)),
         ],
-        compiler_params=pltpu.CompilerParams(vmem_limit_bytes=30 * 1024 * 1024),
+        compiler_params=pltpu.CompilerParams(vmem_limit_bytes=50 * 1024 * 1024),
         cost_estimate=pl.CostEstimate(
             flops=2 * rows * depth * width * len(offsets),
             bytes_accessed=2 * (depth + rows) * width * len(offsets),
             transcendentals=0,
         ),
     )(heads, w_out)
+
+
+def finish_kernel(offsets, own_ref, other_ref, gain_ref, *refs):
+    out_ref = refs[-1]
+    me = lax.axis_index("tensor")
+    half, rows, width = own_ref.shape
+    total = jnp.zeros((rows, width), jnp.float32)
+    for ref in (own_ref, other_ref):
+        for k in range(half):
+            block = ref[k].astype(jnp.float32)
+            total = total + block * block
+    mean_square = jnp.sum(total, axis=1, keepdims=True) / (2 * half * width)
+    scale = lax.rsqrt(mean_square + epsilon)
+    for k, offset in enumerate(offsets):
+        block = (own_ref if k < half else other_ref)[k % half].astype(jnp.float32)
+        index = jnp.bitwise_xor(me, offset)
+        column = pl.multiple_of(index * width, width)
+        gain = gain_ref[pl.ds(index, 1), :]
+        out_ref[:, pl.ds(column, width)] = (block * scale * gain).astype(jnp.bfloat16)
+
+
+def finish(own, other, gain, offsets, which, sets, earlier):
+    half, rows, width = own.shape
+    columns = 2 * half * width
+    operands = [own, other, gain] + ([] if earlier is None else [earlier])
+    whole = pl.BlockSpec(memory_space=pltpu.VMEM)
+    return pl.pallas_call(
+        functools.partial(finish_kernel, offsets),
+        grid=(1,),
+        out_shape=jax.ShapeDtypeStruct((rows * sets, columns), jnp.bfloat16),
+        in_specs=[whole] * 3 + [pl.BlockSpec(memory_space=pl.ANY)] * (len(operands) - 3),
+        out_specs=pl.BlockSpec((rows, columns), lambda i: (which, 0)),
+        input_output_aliases={} if earlier is None else {3: 0},
+        compiler_params=pltpu.CompilerParams(vmem_limit_bytes=24 * 1024 * 1024),
+        cost_estimate=pl.CostEstimate(
+            flops=6 * rows * columns, bytes_accessed=4 * rows * columns, transcendentals=0
+        ),
+    )(*operands)
 
 
 def swap(values, bit, count):
@@ -181,26 +234,47 @@
     attended = attend(row_queries, row_keyval, cache_keys, cache_values, lengths, own_positions)
     head_rows = lax.all_to_all(attended, "tensor", split_axis=1, concat_axis=0, tiled=True)
 
-    orders = bit_orders(count)
-    sent = project(head_rows, w_out, count, list(range(1, count, 2)))
-    received = [swap(block, orders[k][0], count) for k, block in enumerate(sent)]
-    kept = project(head_rows, w_out, count, list(range(0, count, 2)))
-    sums = []
-    for k, order in enumerate(orders):
-        keep, arrival = kept[k], received[k]
-        for bit in order[1:]:
-            half = keep.shape[0] // 2
-            leave = add(keep[half:], arrival[half:])
-            stay = add(keep[:half], arrival[:half])
-            keep, arrival = stay, swap(leave, bit, count)
-        sums.append(keep[0].astype(jnp.float32) + arrival[0].astype(jnp.float32))
-    summed = jnp.concatenate(sums, axis=1)
     share_width = w_out.shape[1] // count
     mine = lax.dynamic_slice_in_dim(hidden_in, my_index * share_width, share_width, 1)
-    stream = (mine.astype(jnp.float32) + summed).astype(jnp.bfloat16)
-    full_stream = lax.all_gather(stream, "tensor", axis=1, tiled=True)
-    normed = normalize(full_stream, ffn_gain)
-    return (stream, normed)
+    gain = ffn_gain.astype(jnp.float32).reshape(count, share_width)
+    orders = plans(count)
+    sets = len(orders)
+    set_rows = row_count // sets
+    sent = project(head_rows, w_out, count, list(range(1, count, 2)))
+    arrivals = [swap(block, 0, count) for block in sent]
+    held = list(project(head_rows, w_out, count, list(range(0, count, 2))))
+
+    streams = [None] * sets
+    offsets = [[0] for _ in range(sets)]
+    steps = [0] * sets
+    last = None
+    normed = None
+    for k in timetable(count):
+        scatter, gather = orders[k]
+        step = steps[k]
+        steps[k] += 1
+        if last is not None:
+            held[k], arrivals[k], _ = lax.optimization_barrier((held[k], arrivals[k], last))
+        if step < len(scatter):
+            half = held[k].shape[0] // 2
+            last = add(held[k][half:], arrivals[k][half:])
+            held[k] = add(held[k][:half], arrivals[k][:half])
+            arrivals[k] = swap(last, scatter[step], count)
+            continue
+        if step == len(scatter):
+            own_rows = mine[k * set_rows : (k + 1) * set_rows].astype(jnp.float32)
+            total = held[k][0].astype(jnp.float32) + arrivals[k][0].astype(jnp.float32)
+            streams[k] = (own_rows + total).astype(jnp.bfloat16)
+            last = held[k] = streams[k][None]
+        elif step <= len(scatter) + len(gather):
+            last = held[k] = jnp.concatenate([held[k], arrivals[k]], axis=0)
+        else:
+            last = normed = finish(held[k], arrivals[k], gain, offsets[k], k, sets, normed)
+            continue
+        bit = (gather + [0])[step - len(scatter)]
+        arrivals[k] = swap(held[k], bit, count)
+        offsets[k] = offsets[k] + [offset ^ (1 << bit) for offset in offsets[k]]
+    return (jnp.concatenate(streams, axis=0), normed)
 
 
 def solution(mesh):

time: 181 us -> 137 us (0.76)
  waiting for transfers between devices: 90.8 us -> 43.2 us
  starting transfers between devices: 11.1 us -> 31.6 us
  between operations: 14.4 us -> 1.27 us
  Pallas kernels: 8.26 us -> 14.3 us
  local copies, waits for them, and re-layouts: 6.7 us -> 1.04 us
  other arithmetic: 16.7 us -> 12.3 us
    all_gather x1 -> x0, waiting for transfers between devices: 50.7 us -> none  [on_device(): full_stream = lax.all_gather(stream, 'tensor', axis=1, tiled=True)]
    ppermute x8 -> x32, starting transfers between devices: 3.71 us -> 24.2 us  [swap(): lax.ppermute(values, 'tensor', [(i, i ^ 1 << bit) for i in range(count)])]
    pallas_call x0 -> x4, Pallas kernels: none -> 6.61 us  [finish(): pl.pallas_call(functools.partial(finish_kernel, offsets), grid=(1,), out_...]
    unnamed x16 -> x24, local copies, waits for them, and re-layouts: 6.01 us -> 0.17 us
    reduce_sum x2 -> x1, other arithmetic: 6.71 us -> 3.44 us  [normalize(): mean_square = jnp.mean(floats * floats, axis=-1, keepdims=True)]
    ppermute x8 -> x32, waiting for transfers between devices: 32 us -> 35 us  [swap(): lax.ppermute(values, 'tensor', [(i, i ^ 1 << bit) for i in range(count)])]
    dot_general x1, matrix products: 1.65 us -> 3.84 us  [on_device(): jnp.dot(normed_in, w_keyval, preferred_element_type=jnp.float32)]
    convert_element_type x2 -> x4, other arithmetic: 4.82 us -> 3.47 us  [on_device(): streams[k] = (own_rows + total).astype(jnp.bfloat16)]
  transfers between devices with their start and end apart: 10 -> 33, of which waited for: 6 -> 13; matrix products, arithmetic and copies ran while one was open for 1% -> 4% of each run, Pallas kernels for 2% -> 6%
where the time goes in v2:
time: 137 us
  waiting for transfers between devices  43.2 us (32%)
  starting transfers between devices  31.6 us (23%)
  matrix products  22.8 us (17%)
  Pallas kernels  14.3 us (10%)
  other arithmetic  12.3 us (9%)
  blocking collectives  10.5 us (8%)
    ppermute x32, waiting for transfers between devices, swap(): lax.ppermute(values, 'tensor', [(i, i ^ 1 << bit) for i in range(count)])  35 us
    ppermute x32, starting transfers between devices, swap(): lax.ppermute(values, 'tensor', [(i, i ^ 1 << bit) for i in range(count)])  24.2 us
    all_to_all x1, blocking collectives, on_device(): lax.all_to_all(attended, 'tensor', split_axis=1, concat_axis=0, tiled=True)  10.5 us
    all_to_all x1, waiting for transfers between devices, on_device(): lax.all_to_all(jnp.concatenate([queries, keyval], axis=1).reshape(count,...  8.18 us
    dot_general x1, matrix products, on_device(): queries = jnp.dot(normed_in, w_query, preferred_element_type=jnp.float32)  8.14 us
    pallas_call x2, Pallas kernels, project(): pl.pallas_call(functools.partial(project_kernel, count, offsets), out_sha...  7.66 us
    all_to_all x1, starting transfers between devices, on_device(): lax.all_to_all(jnp.concatenate([queries, keyval], axis=1).reshape(count,...  7.39 us
    pallas_call x4, Pallas kernels, finish(): pl.pallas_call(functools.partial(finish_kernel, offsets), grid=(1,), out_...  6.61 us
  transfers between devices with their start and end apart: 33, of which 13 were waited for; matrix products, arithmetic and copies ran while one was open for 4% of the time, Pallas kernels for 6%

profile of v2, /device:TPU:0, one launch (start us, length us, event | category | flops | bytes accessed | tf_op | source)
XLA Modules:
  0.0 136.9 jit_solution(16997900562320546350)
XLA Ops:
  0.7 0.9 convert_element_type.323
  1.6 3.4 %fusion = f32[128]{0:T(128)S(1)} fusion(bf16[128,16384]{1,0:T(8,128)(2,1)} %param.10), kind=kLoop, calls=%fused_computation.2 | loop fusion | flops 6291328 | bytes 4194816 | tf_op jit(solution)/shard_map/reduce_sum | solution.py:20
  5.1 8.1 %fusion.13 = f32[128,512]{1,0:T(8,128)S(1)} fusion(bf16[16384,512]{1,0:T(8,128)(2,1)} %param.12, bf16[128,16384]{1,0:T(8,128)(2,1)S(1)} %copy-done.2, f32[16384]{0:T(1024)S(1)} %convert_element_type.323, f32[128]{0:T(128)S(1)} %add_rsqrt_fusion), kind=kOutput, calls=%fused_computation.17 | convolution fusion | flops 2155872256 | bytes 21299712 | tf_op jit(solution)/shard_map/dot_general | solution.py:217
  13.4 0.3 multiply_cosine_fusion
  13.7 0.3 subtract_convert_fusion
  14.0 0.2 pad_maximum_fusion.2
  14.2 3.8 %fusion.21 = bf16[128,64]{0,1:T(8,128)(2,1)S(1)} fusion(bf16[16384,64]{0,1:T(8,128)(2,1)S(1)} %copy-done, bf16[128,16384]{1,0:T(8,128)(2,1)} %param.10, f32[16384]{0:T(1024)S(1)} %convert_element_type.323, f32[128]{0:T(128)S(1)} %add_rsqrt_fusion), kind=kOutput, calls=%fused_computation.20 | convolution fusion | flops 276832256 | bytes 6373888 | tf_op jit(solution)/shard_map/dot_general | solution.py:220
  18.1 0.1 copy.31
  18.2 0.7 pad_maximum_fusion.1
  18.9 7.4 %all-to-all-start = ((bf16[16,8,576]{2,1,0:T(8,128)(2,1)}), bf16[16,8,576]{2,1,0:T(8,128)(2,1)S(1)}, u32[]{:S(2)}, u32[]{:S(2)}) async-start(bf16[16,8,576]{2,1,0:T(8,128)(2,1)} %pad_maximum_fusion.1), calls=%async_computation | async-start | bytes 327680 | tf_op jit(solution)/shard_map/all_to_all | solution.py:223
  26.5 0.1 multiply_cosine_fusion.1
  26.6 8.2 %all-to-all-done = bf16[16,8,576]{2,1,0:T(8,128)(2,1)S(1)} async-done(((bf16[16,8,576]{2,1,0:T(8,128)(2,1)}), bf16[16,8,576]{2,1,0:T(8,128)(2,1)S(1)}, u32[]{:S(2)}, u32[]{:S(2)}) %all-to-all-start) | async-done | bytes 147488 | tf_op jit(solution)/shard_map/all_to_all | solution.py:223
  34.8 0.1 reshape.185
  35.2 0.2 fusion.33
  35.4 5.8 %fusion.9 = (f32[8,4,16]{2,1,0:T(4,128)S(1)}, f32[8,4,16,1024]{3,2,1,0:T(8,128)S(1)}) fusion(pred[8,1024]{1,0:T(8,128)(4,1)S(1)} %iota_compare_fusion, bf16[8,4,16,128]{3,2,1,0:T(8,128)(2,1)S(1)} %reshape_reshape.3, bf16[8,1024,512]{2,1,0:T(8,128)(2,1)} %param.14), kind=kOutput, calls=%fused_computation.14 | convolution fusion | flops 135790080 | bytes 10627072 | tf_op jit(solution)/shard_map/rgqd,rlgd->rgql/dot_general | solution.py:59
  41.2 0.6 fusion.10
  41.8 4.9 %fusion.18 = bf16[8,4,16,128]{3,2,1,0:T(8,128)(2,1)S(1)} fusion(f32[8,4,16,1024]{3,2,1,0:T(8,128)S(1)} %get-tuple-element.179, f32[8,4,16]{2,1,0:T(4,128)S(1)} %get-tuple-element.169, f32[8,4,16]{2,1,0:T(4,128)S(1)} %multiply_maximum_fusion, pred[8,1024]{1,0:T(8,128)(4,1)S(1)} %iota_compare_fusion, f32[8,4,128]{2,1,0:T(4,128)S(1)} %copy.36, ...), kind=kOutput, calls=%fused_computation.19 | convolution fusion | flops 137035776 | bytes 10647552 | tf_op jit(solution)/shard_map/rgql,rlgd->rgqd/dot_general | solution.py:74
  46.9 10.5 %all_to_all.24 = bf16[8,16,512]{2,0,1:T(8,128)(2,1)S(1)} all-to-all(bf16[8,16,512]{2,0,1:T(8,128)(2,1)S(1)} %copy.37), channel_id=1, replica_groups=mesh['groups'=2,'tensor'=16] {'tensor'}, dimensions={1} | all-to-all | bytes 262144 | tf_op jit(solution)/shard_map/all_to_all | solution.py:235
  57.4 3.8 %shard_map.114 = (bf16[8,32,1024]{2,1,0:T(8,128)(2,1)S(1)}, bf16[8,32,1024]{2,1,0:T(8,128)(2,1)S(1)}, bf16[8,32,1024]{2,1,0:T(8,128)(2,1)S(1)}, bf16[8,32,1024]{2,1,0:T(8,128)(2,1)S(1)}) custom-call(bf16[128,512]{1,0:T(8,128)(2,1)S(1)} %bitcast.65, bf16[512,16384]{1,0:T(8,128)(2,1)} %w_ref.3), custom_call_target="tpu_custom_call" | custom-call | flops 1073741824 | bytes 10485760 | tf_op jit(solution)/shard_map/pallas_call | solution.py:137
  61.3 0.5 collective-permute-start.2
  61.9 3.8 %shard_map.113 = (bf16[8,32,1024]{2,1,0:T(8,128)(2,1)S(1)}, bf16[8,32,1024]{2,1,0:T(8,128)(2,1)S(1)}, bf16[8,32,1024]{2,1,0:T(8,128)(2,1)S(1)}, bf16[8,32,1024]{2,1,0:T(8,128)(2,1)S(1)}) custom-call(bf16[128,512]{1,0:T(8,128)(2,1)S(1)} %bitcast.66, bf16[512,16384]{1,0:T(8,128)(2,1)} %w_ref.3), custom_call_target="tpu_custom_call" | custom-call | flops 1073741824 | bytes 10485760 | tf_op jit(solution)/shard_map/pallas_call | solution.py:137
  65.7 0.2 add_convert_fusion.7
  66.0 0.5 collective-permute-start.4
  66.5 0.2 add_convert_fusion.5
  66.7 0.2 collective-permute-start.7
  66.9 7.7 %collective-permute-done.1 = bf16[4,32,1024]{2,1,0:T(8,128)(2,1)S(1)} collective-permute-done((bf16[4,32,1024]{2,1,0:T(8,128)(2,1)S(1)}, bf16[4,32,1024]{2,1,0:T(8,128)(2,1)S(1)}, u32[]{:S(2)}, u32[]{:S(2)}) %collective-permute-start.1) | collective-permute-done | bytes 262176 | tf_op jit(solution)/shard_map/ppermute | solution.py:194
  74.7 0.2 add_convert_fusion.4
  74.9 0.3 collective-permute-start.6
  75.4 7.5 %collective-permute-done.6 = bf16[4,32,1024]{2,1,0:T(8,128)(2,1)S(1)} collective-permute-done((bf16[4,32,1024]{2,1,0:T(8,128)(2,1)S(1)}, bf16[4,32,1024]{2,1,0:T(8,128)(2,1)S(1)}, u32[]{:S(2)}, u32[]{:S(2)}) %collective-permute-start.6) | collective-permute-done | bytes 262176 | tf_op jit(solution)/shard_map/ppermute | solution.py:194
  82.9 0.2 add_convert_fusion
  83.2 0.4 collective-permute-start.8
  83.6 2.6 %collective-permute-start.11 = (bf16[2,32,1024]{2,1,0:T(8,128)(2,1)S(1)}, bf16[2,32,1024]{2,1,0:T(8,128)(2,1)S(1)}, u32[]{:S(2)}, u32[]{:S(2)}) collective-permute-start(bf16[2,32,1024]{2,1,0:T(8,128)(2,1)S(1)} %get-tuple-element.156), channel_id=1, source_target_pairs={{0,8},{1,9},{2,10},{3,11},{4,12},{5,13},{6,14},{7,15},{8,0},{9,1},... | collective-permute-start | bytes 393224 | tf_op jit(solution)/shard_map/ppermute | solution.py:194
  86.2 0.5 collective-permute-start.10
  86.7 3.4 %collective-permute-done.8 = bf16[1,32,1024]{2,1,0:T(8,128)(2,1)S(1)} collective-permute-done((bf16[1,32,1024]{2,1,0:T(8,128)(2,1)S(1)}, bf16[1,32,1024]{2,1,0:T(8,128)(2,1)S(1)}, u32[]{:S(2)}, u32[]{:S(2)}) %collective-permute-start.8) | collective-permute-done | bytes 65568 | tf_op jit(solution)/shard_map/ppermute | solution.py:194
  90.0 0.9 fusion.32
  91.0 3.1 %collective-permute-done.11 = bf16[2,32,1024]{2,1,0:T(8,128)(2,1)S(1)} collective-permute-done((bf16[2,32,1024]{2,1,0:T(8,128)(2,1)S(1)}, bf16[2,32,1024]{2,1,0:T(8,128)(2,1)S(1)}, u32[]{:S(2)}, u32[]{:S(2)}) %collective-permute-start.11) | collective-permute-done | bytes 131104 | tf_op jit(solution)/shard_map/ppermute | solution.py:194
  94.1 1.2 collective-permute-start.14
  95.5 2.0 %collective-permute-start.12 = (bf16[1,32,1024]{2,1,0:T(8,128)(2,1)S(1)}, bf16[1,32,1024]{2,1,0:T(8,128)(2,1)S(1)}, u32[]{:S(2)}, u32[]{:S(2)}) collective-permute-start(bf16[1,32,1024]{2,1,0:T(8,128)(2,1)S(1)} %get-tuple-element.163), channel_id=1, source_target_pairs={{0,8},{1,9},{2,10},{3,11},{4,12},{5,13},{6,14},{7,15},{8,0},{9,1},... | collective-permute-start | bytes 196616 | tf_op jit(solution)/shard_map/ppermute | solution.py:194
  97.5 0.9 collective-permute-done.14
  98.4 0.9 fusion.31
  99.3 0.2 collective-permute-start.18
  99.5 2.1 %collective-permute-start.17 = (bf16[2,32,1024]{2,1,0:T(8,128)(2,1)S(1)}, bf16[2,32,1024]{2,1,0:T(8,128)(2,1)S(1)}, u32[]{:S(2)}, u32[]{:S(2)}) collective-permute-start(bf16[2,32,1024]{2,1,0:T(8,128)(2,1)S(1)} %constant_dynamic-update-slice_fusion), channel_id=1, source_target_pairs={{0,4},{1,5},{2,6},{3,7},{4,0},{5,1},{6,2},{7,3},{8,12},{9,13},{10,... | collective-permute-start | bytes 393224 | tf_op jit(solution)/shard_map/ppermute | solution.py:194
  101.5 0.9 collective-permute-done.12
  102.4 0.9 fusion.30
  103.3 1.1 collective-permute-start.19
  104.4 2.0 %collective-permute-start.16 = (bf16[1,32,1024]{2,1,0:T(8,128)(2,1)S(1)}, bf16[1,32,1024]{2,1,0:T(8,128)(2,1)S(1)}, u32[]{:S(2)}, u32[]{:S(2)}) collective-permute-start(bf16[1,32,1024]{2,1,0:T(8,128)(2,1)S(1)} %get-tuple-element.160), channel_id=1, source_target_pairs={{0,8},{1,9},{2,10},{3,11},{4,12},{5,13},{6,14},{7,15},{8,0},{9,1},... | collective-permute-start | bytes 196616 | tf_op jit(solution)/shard_map/ppermute | solution.py:194
  106.4 2.7 %collective-permute-done.19 = bf16[1,32,1024]{2,1,0:T(8,128)(2,1)S(1)} collective-permute-done((bf16[1,32,1024]{2,1,0:T(8,128)(2,1)S(1)}, bf16[1,32,1024]{2,1,0:T(8,128)(2,1)S(1)}, u32[]{:S(2)}, u32[]{:S(2)}) %collective-permute-start.19) | collective-permute-done | bytes 65568 | tf_op jit(solution)/shard_map/ppermute | solution.py:194
  109.1 1.3 collective-permute-start.21
  110.6 0.8 collective-permute-start.24
  111.4 0.9 fusion.29
  112.3 2.2 %collective-permute-start.20 = (bf16[1,32,1024]{2,1,0:T(8,128)(2,1)S(1)}, bf16[1,32,1024]{2,1,0:T(8,128)(2,1)S(1)}, u32[]{:S(2)}, u32[]{:S(2)}) collective-permute-start(bf16[1,32,1024]{2,1,0:T(8,128)(2,1)S(1)} %bitcast.75), channel_id=1, source_target_pairs={{0,8},{1,9},{2,10},{3,11},{4,12},{5,13},{6,14},{7,15},{8,0},{9,1},... | collective-permute-start | bytes 196616 | tf_op jit(solution)/shard_map/ppermute | solution.py:194
  114.6 1.0 collective-permute-start.27
  115.5 2.1 %collective-permute-done.20 = bf16[1,32,1024]{2,1,0:T(8,128)(2,1)S(1)} collective-permute-done((bf16[1,32,1024]{2,1,0:T(8,128)(2,1)S(1)}, bf16[1,32,1024]{2,1,0:T(8,128)(2,1)S(1)}, u32[]{:S(2)}, u32[]{:S(2)}) %collective-permute-start.20) | collective-permute-done | bytes 65568 | tf_op jit(solution)/shard_map/ppermute | solution.py:194
  117.7 1.3 collective-permute-start.22
  119.2 3.5 %collective-permute-done.22 = bf16[2,32,1024]{2,1,0:T(8,128)(2,1)S(1)} collective-permute-done((bf16[2,32,1024]{2,1,0:T(8,128)(2,1)S(1)}, bf16[2,32,1024]{2,1,0:T(8,128)(2,1)S(1)}, u32[]{:S(2)}, u32[]{:S(2)}) %collective-permute-start.22) | collective-permute-done | bytes 131104 | tf_op jit(solution)/shard_map/ppermute | solution.py:194
  122.9 1.3 collective-permute-start.26
  124.2 1.9 %collective-permute-start.25 = (bf16[4,32,1024]{2,1,0:T(8,128)(2,1)S(1)}, bf16[4,32,1024]{2,1,0:T(8,128)(2,1)S(1)}, u32[]{:S(2)}, u32[]{:S(2)}) collective-permute-start(bf16[4,32,1024]{2,1,0:T(8,128)(2,1)S(1)} %constant_dynamic-update-slice_fusion.16), channel_id=1, source_target_pairs={{0,4},{1,5},{2,6},{3,7},{4,0},{5,1},{6,2},{7,3},{8,12},{9,13},{10,... | collective-permute-start | bytes 786440 | tf_op jit(solution)/shard_map/ppermute | solution.py:194
  126.1 1.7 %shard_map.115.refs_0_ = bf16[128,16384]{1,0:T(8,128)(2,1)} custom-call(bf16[8,32,1024]{2,1,0:T(8,128)(2,1)S(1)} %constant_dynamic-update-slice_fusion.12.own_ref, bf16[8,32,1024]{2,1,0:T(8,128)(2,1)S(1)} %collective-permute-done.29.other_ref, f32[16,1024]{1,0:T(8,128)S(1)} %reshape.195.gain_ref), custom_call_target="tpu_custom_call" | custom-call | flops 3145728 | bytes 2097152 | tf_op jit(solution)/shard_map/pallas_call | solution.py:179
  127.8 1.7 %shard_map.116.refs_0_ = bf16[128,16384]{1,0:T(8,128)(2,1)} custom-call(bf16[8,32,1024]{2,1,0:T(8,128)(2,1)S(1)} %constant_dynamic-update-slice_fusion.18.own_ref, bf16[8,32,1024]{2,1,0:T(8,128)(2,1)S(1)} %collective-permute-done.28.other_ref, f32[16,1024]{1,0:T(8,128)S(1)} %reshape.195.gain_ref, ...), custom_call_target="tpu_custom_call", output_to_operand_aliasing={{}: (3, {})} | custom-call | flops 3145728 | bytes 2097152 | tf_op jit(solution)/shard_map/pallas_call | solution.py:179
  129.4 2.2 %collective-permute-done.26 = bf16[4,32,1024]{2,1,0:T(8,128)(2,1)S(1)} collective-permute-done((bf16[4,32,1024]{2,1,0:T(8,128)(2,1)S(1)}, bf16[4,32,1024]{2,1,0:T(8,128)(2,1)S(1)}, u32[]{:S(2)}, u32[]{:S(2)}) %collective-permute-start.26) | collective-permute-done | bytes 262176 | tf_op jit(solution)/shard_map/ppermute | solution.py:194
  131.7 1.0 collective-permute-done.25
  132.8 0.7 pad_maximum_fusion
  133.6 1.7 %shard_map.117.refs_0_ = bf16[128,16384]{1,0:T(8,128)(2,1)} custom-call(bf16[8,32,1024]{2,1,0:T(8,128)(2,1)S(1)} %constant_dynamic-update-slice_fusion.20.own_ref, bf16[8,32,1024]{2,1,0:T(8,128)(2,1)S(1)} %collective-permute-done.31.other_ref, f32[16,1024]{1,0:T(8,128)S(1)} %reshape.195.gain_ref, ...), custom_call_target="tpu_custom_call", output_to_operand_aliasing={{}: (3, {})} | custom-call | flops 3145728 | bytes 2097152 | tf_op jit(solution)/shard_map/pallas_call | solution.py:179
  135.3 1.7 %shard_map.118 = bf16[128,16384]{1,0:T(8,128)(2,1)} custom-call(bf16[8,32,1024]{2,1,0:T(8,128)(2,1)S(1)} %constant_dynamic-update-slice_fusion.22.own_ref, bf16[8,32,1024]{2,1,0:T(8,128)(2,1)S(1)} %collective-permute-done.30.other_ref, f32[16,1024]{1,0:T(8,128)S(1)} %reshape.195.gain_ref, ...), custom_call_target="tpu_custom_call", output_to_operand_aliasing={{}: (3, {})} | custom-call | flops 3145728 | bytes 2097152 | tf_op jit(solution)/shard_map/pallas_call | solution.py:179
  (98 shorter events, 2.5 us)
Async XLA Ops:
  0.6 13.6 %copy-start = (bf16[16384,64]{0,1:T(8,128)(2,1)S(1)}, bf16[16384,64]{0,1:T(8,128)(2,1)}, u32[]{:S(2)}) copy-start(bf16[16384,64]{0,1:T(8,128)(2,1)} %param.13) | copy-start | bytes 6291460
  0.6 4.4 %copy-start.2 = (bf16[128,16384]{1,0:T(8,128)(2,1)S(1)}, bf16[128,16384]{1,0:T(8,128)(2,1)}, u32[]{:S(2)}) copy-start(bf16[128,16384]{1,0:T(8,128)(2,1)} %param.10) | copy-start | bytes 12582916
  5.1 8.3 %copy-start.5 = (s32[128]{0:T(128)S(1)}, s32[128]{0:T(128)}, u32[]{:S(2)}) copy-start(s32[128]{0:T(128)} %param.19) | copy-start | bytes 1540
  14.2 12.1 %copy-start.4 = (s32[8]{0:T(128)S(1)}, s32[8]{0:T(128)}, u32[]{:S(2)}) copy-start(s32[8]{0:T(128)} %param.18) | copy-start | bytes 100
  18.9 15.9 %all-to-all-start = ((bf16[16,8,576]{2,1,0:T(8,128)(2,1)}), bf16[16,8,576]{2,1,0:T(8,128)(2,1)S(1)}, u32[]{:S(2)}, u32[]{:S(2)}) async-start(bf16[16,8,576]{2,1,0:T(8,128)(2,1)} %pad_maximum_fusion.1), calls=%async_computation | async-start | bytes 327680 | tf_op jit(solution)/shard_map/all_to_all | solution.py:223
  61.2 4.5 %collective-permute-start = (bf16[8,32,1024]{2,1,0:T(8,128)(2,1)S(1)}, bf16[8,32,1024]{2,1,0:T(8,128)(2,1)S(1)}, u32[]{:S(2)}, u32[]{:S(2)}) collective-permute-start(bf16[8,32,1024]{2,1,0:T(8,128)(2,1)S(1)} %get-tuple-element.73), channel_id=1, source_target_pairs={{0,1},{1,0},{2,3},{3,2},{4,5},{5,4},{6,7},{7,6},{8,9},{9,8},{10,11... | collective-permute-start | bytes 1572872 | tf_op jit(solution)/shard_map/ppermute | solution.py:194
  61.3 5.2 %collective-permute-start.2 = (bf16[8,32,1024]{2,1,0:T(8,128)(2,1)S(1)}, bf16[8,32,1024]{2,1,0:T(8,128)(2,1)S(1)}, u32[]{:S(2)}, u32[]{:S(2)}) collective-permute-start(bf16[8,32,1024]{2,1,0:T(8,128)(2,1)S(1)} %get-tuple-element.75), channel_id=1, source_target_pairs={{0,1},{1,0},{2,3},{3,2},{4,5},{5,4},{6,7},{7,6},{8,9},{9,8},{10,11... | collective-permute-start | bytes 1572872 | tf_op jit(solution)/shard_map/ppermute | solution.py:194
  61.8 12.9 %collective-permute-start.5 = (bf16[8,32,1024]{2,1,0:T(8,128)(2,1)S(1)}, bf16[8,32,1024]{2,1,0:T(8,128)(2,1)S(1)}, u32[]{:S(2)}, u32[]{:S(2)}) collective-permute-start(bf16[8,32,1024]{2,1,0:T(8,128)(2,1)S(1)} %get-tuple-element.83), channel_id=1, source_target_pairs={{0,1},{1,0},{2,3},{3,2},{4,5},{5,4},{6,7},{7,6},{8,9},{9,8},{10,11... | collective-permute-start | bytes 1572872 | tf_op jit(solution)/shard_map/ppermute | solution.py:194
  65.9 8.7 %collective-permute-start.1 = (bf16[4,32,1024]{2,1,0:T(8,128)(2,1)S(1)}, bf16[4,32,1024]{2,1,0:T(8,128)(2,1)S(1)}, u32[]{:S(2)}, u32[]{:S(2)}) collective-permute-start(bf16[4,32,1024]{2,1,0:T(8,128)(2,1)S(1)} %get-tuple-element.147), channel_id=1, source_target_pairs={{0,2},{1,3},{2,0},{3,1},{4,6},{5,7},{6,4},{7,5},{8,10},{9,11},{10,... | collective-permute-start | bytes 786440 | tf_op jit(solution)/shard_map/ppermute | solution.py:194
  66.0 16.9 %collective-permute-start.4 = (bf16[8,32,1024]{2,1,0:T(8,128)(2,1)S(1)}, bf16[8,32,1024]{2,1,0:T(8,128)(2,1)S(1)}, u32[]{:S(2)}, u32[]{:S(2)}) collective-permute-start(bf16[8,32,1024]{2,1,0:T(8,128)(2,1)S(1)} %get-tuple-element.81), channel_id=1, source_target_pairs={{0,1},{1,0},{2,3},{3,2},{4,5},{5,4},{6,7},{7,6},{8,9},{9,8},{10,11... | collective-permute-start | bytes 1572872 | tf_op jit(solution)/shard_map/ppermute | solution.py:194
  66.7 8.6 %collective-permute-start.7 = (bf16[4,32,1024]{2,1,0:T(8,128)(2,1)S(1)}, bf16[4,32,1024]{2,1,0:T(8,128)(2,1)S(1)}, u32[]{:S(2)}, u32[]{:S(2)}) collective-permute-start(bf16[4,32,1024]{2,1,0:T(8,128)(2,1)S(1)} %get-tuple-element.148), channel_id=1, source_target_pairs={{0,4},{1,5},{2,6},{3,7},{4,0},{5,1},{6,2},{7,3},{8,12},{9,13},{10,... | collective-permute-start | bytes 786440 | tf_op jit(solution)/shard_map/ppermute | solution.py:194
  74.9 7.9 %collective-permute-start.6 = (bf16[4,32,1024]{2,1,0:T(8,128)(2,1)S(1)}, bf16[4,32,1024]{2,1,0:T(8,128)(2,1)S(1)}, u32[]{:S(2)}, u32[]{:S(2)}) collective-permute-start(bf16[4,32,1024]{2,1,0:T(8,128)(2,1)S(1)} %get-tuple-element.145), channel_id=1, source_target_pairs={{0,2},{1,3},{2,0},{3,1},{4,6},{5,7},{6,4},{7,5},{8,10},{9,11},{10,... | collective-permute-start | bytes 786440 | tf_op jit(solution)/shard_map/ppermute | solution.py:194
  75.3 7.9 %collective-permute-start.3 = (bf16[2,32,1024]{2,1,0:T(8,128)(2,1)S(1)}, bf16[2,32,1024]{2,1,0:T(8,128)(2,1)S(1)}, u32[]{:S(2)}, u32[]{:S(2)}) collective-permute-start(bf16[2,32,1024]{2,1,0:T(8,128)(2,1)S(1)} %get-tuple-element.155), channel_id=1, source_target_pairs={{0,4},{1,5},{2,6},{3,7},{4,0},{5,1},{6,2},{7,3},{8,12},{9,13},{10,... | collective-permute-start | bytes 393224 | tf_op jit(solution)/shard_map/ppermute | solution.py:194
  83.2 42.9 %copy-start.3 = (bf16[16384]{0:T(1024)(128)(2,1)S(1)}, bf16[16384]{0:T(1024)(128)(2,1)}, u32[]{:S(2)}) copy-start(bf16[16384]{0:T(1024)(128)(2,1)} %param.17) | copy-start | bytes 98308
  83.2 6.8 %collective-permute-start.8 = (bf16[1,32,1024]{2,1,0:T(8,128)(2,1)S(1)}, bf16[1,32,1024]{2,1,0:T(8,128)(2,1)S(1)}, u32[]{:S(2)}, u32[]{:S(2)}) collective-permute-start(bf16[1,32,1024]{2,1,0:T(8,128)(2,1)S(1)} %get-tuple-element.166), channel_id=1, source_target_pairs={{0,8},{1,9},{2,10},{3,11},{4,12},{5,13},{6,14},{7,15},{8,0},{9,1},... | collective-permute-start | bytes 196616 | tf_op jit(solution)/shard_map/ppermute | solution.py:194
  83.6 10.5 %collective-permute-start.11 = (bf16[2,32,1024]{2,1,0:T(8,128)(2,1)S(1)}, bf16[2,32,1024]{2,1,0:T(8,128)(2,1)S(1)}, u32[]{:S(2)}, u32[]{:S(2)}) collective-permute-start(bf16[2,32,1024]{2,1,0:T(8,128)(2,1)S(1)} %get-tuple-element.156), channel_id=1, source_target_pairs={{0,8},{1,9},{2,10},{3,11},{4,12},{5,13},{6,14},{7,15},{8,0},{9,1},... | collective-permute-start | bytes 393224 | tf_op jit(solution)/shard_map/ppermute | solution.py:194
  86.2 9.1 %collective-permute-start.10 = (bf16[4,32,1024]{2,1,0:T(8,128)(2,1)S(1)}, bf16[4,32,1024]{2,1,0:T(8,128)(2,1)S(1)}, u32[]{:S(2)}, u32[]{:S(2)}) collective-permute-start(bf16[4,32,1024]{2,1,0:T(8,128)(2,1)S(1)} %get-tuple-element.143), channel_id=1, source_target_pairs={{0,2},{1,3},{2,0},{3,1},{4,6},{5,7},{6,4},{7,5},{8,10},{9,11},{10,... | collective-permute-start | bytes 786440 | tf_op jit(solution)/shard_map/ppermute | solution.py:194
  86.7 8.8 %collective-permute-start.9 = (bf16[2,32,1024]{2,1,0:T(8,128)(2,1)S(1)}, bf16[2,32,1024]{2,1,0:T(8,128)(2,1)S(1)}, u32[]{:S(2)}, u32[]{:S(2)}) collective-permute-start(bf16[2,32,1024]{2,1,0:T(8,128)(2,1)S(1)} %get-tuple-element.153), channel_id=1, source_target_pairs={{0,4},{1,5},{2,6},{3,7},{4,0},{5,1},{6,2},{7,3},{8,12},{9,13},{10,... | collective-permute-start | bytes 393224 | tf_op jit(solution)/shard_map/ppermute | solution.py:194
  90.9 8.6 %collective-permute-start.13 = (bf16[1,32,1024]{2,1,0:T(8,128)(2,1)S(1)}, bf16[1,32,1024]{2,1,0:T(8,128)(2,1)S(1)}, u32[]{:S(2)}, u32[]{:S(2)}) collective-permute-start(bf16[1,32,1024]{2,1,0:T(8,128)(2,1)S(1)} %bitcast.69), channel_id=1, source_target_pairs={{0,8},{1,9},{2,10},{3,11},{4,12},{5,13},{6,14},{7,15},{8,0},{9,1},... | collective-permute-start | bytes 196616 | tf_op jit(solution)/shard_map/ppermute | solution.py:194
  94.1 4.3 %collective-permute-start.14 = (bf16[1,32,1024]{2,1,0:T(8,128)(2,1)S(1)}, bf16[1,32,1024]{2,1,0:T(8,128)(2,1)S(1)}, u32[]{:S(2)}, u32[]{:S(2)}) collective-permute-start(bf16[1,32,1024]{2,1,0:T(8,128)(2,1)S(1)} %get-tuple-element.164), channel_id=1, source_target_pairs={{0,2},{1,3},{2,0},{3,1},{4,6},{5,7},{6,4},{7,5},{8,10},{9,11},{10,... | collective-permute-start | bytes 196616 | tf_op jit(solution)/shard_map/ppermute | solution.py:194
  95.4 9.0 %collective-permute-start.15 = (bf16[2,32,1024]{2,1,0:T(8,128)(2,1)S(1)}, bf16[2,32,1024]{2,1,0:T(8,128)(2,1)S(1)}, u32[]{:S(2)}, u32[]{:S(2)}) collective-permute-start(bf16[2,32,1024]{2,1,0:T(8,128)(2,1)S(1)} %get-tuple-element.151), channel_id=1, source_target_pairs={{0,4},{1,5},{2,6},{3,7},{4,0},{5,1},{6,2},{7,3},{8,12},{9,13},{10,... | collective-permute-start | bytes 393224 | tf_op jit(solution)/shard_map/ppermute | solution.py:194
  95.5 6.9 %collective-permute-start.12 = (bf16[1,32,1024]{2,1,0:T(8,128)(2,1)S(1)}, bf16[1,32,1024]{2,1,0:T(8,128)(2,1)S(1)}, u32[]{:S(2)}, u32[]{:S(2)}) collective-permute-start(bf16[1,32,1024]{2,1,0:T(8,128)(2,1)S(1)} %get-tuple-element.163), channel_id=1, source_target_pairs={{0,8},{1,9},{2,10},{3,11},{4,12},{5,13},{6,14},{7,15},{8,0},{9,1},... | collective-permute-start | bytes 196616 | tf_op jit(solution)/shard_map/ppermute | solution.py:194
  99.3 11.2 %collective-permute-start.18 = (bf16[1,32,1024]{2,1,0:T(8,128)(2,1)S(1)}, bf16[1,32,1024]{2,1,0:T(8,128)(2,1)S(1)}, u32[]{:S(2)}, u32[]{:S(2)}) collective-permute-start(bf16[1,32,1024]{2,1,0:T(8,128)(2,1)S(1)} %bitcast.71), channel_id=1, source_target_pairs={{0,8},{1,9},{2,10},{3,11},{4,12},{5,13},{6,14},{7,15},{8,0},{9,1},... | collective-permute-start | bytes 196616 | tf_op jit(solution)/shard_map/ppermute | solution.py:194
  99.5 11.1 %collective-permute-start.17 = (bf16[2,32,1024]{2,1,0:T(8,128)(2,1)S(1)}, bf16[2,32,1024]{2,1,0:T(8,128)(2,1)S(1)}, u32[]{:S(2)}, u32[]{:S(2)}) collective-permute-start(bf16[2,32,1024]{2,1,0:T(8,128)(2,1)S(1)} %constant_dynamic-update-slice_fusion), channel_id=1, source_target_pairs={{0,4},{1,5},{2,6},{3,7},{4,0},{5,1},{6,2},{7,3},{8,12},{9,13},{10,... | collective-permute-start | bytes 393224 | tf_op jit(solution)/shard_map/ppermute | solution.py:194
  103.3 5.8 %collective-permute-start.19 = (bf16[1,32,1024]{2,1,0:T(8,128)(2,1)S(1)}, bf16[1,32,1024]{2,1,0:T(8,128)(2,1)S(1)}, u32[]{:S(2)}, u32[]{:S(2)}) collective-permute-start(bf16[1,32,1024]{2,1,0:T(8,128)(2,1)S(1)} %bitcast.73), channel_id=1, source_target_pairs={{0,8},{1,9},{2,10},{3,11},{4,12},{5,13},{6,14},{7,15},{8,0},{9,1},... | collective-permute-start | bytes 196616 | tf_op jit(solution)/shard_map/ppermute | solution.py:194
  104.4 7.0 %collective-permute-start.16 = (bf16[1,32,1024]{2,1,0:T(8,128)(2,1)S(1)}, bf16[1,32,1024]{2,1,0:T(8,128)(2,1)S(1)}, u32[]{:S(2)}, u32[]{:S(2)}) collective-permute-start(bf16[1,32,1024]{2,1,0:T(8,128)(2,1)S(1)} %get-tuple-element.160), channel_id=1, source_target_pairs={{0,8},{1,9},{2,10},{3,11},{4,12},{5,13},{6,14},{7,15},{8,0},{9,1},... | collective-permute-start | bytes 196616 | tf_op jit(solution)/shard_map/ppermute | solution.py:194
  109.1 5.4 %collective-permute-start.21 = (bf16[2,32,1024]{2,1,0:T(8,128)(2,1)S(1)}, bf16[2,32,1024]{2,1,0:T(8,128)(2,1)S(1)}, u32[]{:S(2)}, u32[]{:S(2)}) collective-permute-start(bf16[2,32,1024]{2,1,0:T(8,128)(2,1)S(1)} %constant_dynamic-update-slice_fusion.2), channel_id=1, source_target_pairs={{0,2},{1,3},{2,0},{3,1},{4,6},{5,7},{6,4},{7,5},{8,10},{9,11},{10,... | collective-permute-start | bytes 393224 | tf_op jit(solution)/shard_map/ppermute | solution.py:194
  110.5 8.6 %collective-permute-start.23 = (bf16[2,32,1024]{2,1,0:T(8,128)(2,1)S(1)}, bf16[2,32,1024]{2,1,0:T(8,128)(2,1)S(1)}, u32[]{:S(2)}, u32[]{:S(2)}) collective-permute-start(bf16[2,32,1024]{2,1,0:T(8,128)(2,1)S(1)} %constant_dynamic-update-slice_fusion.4), channel_id=1, source_target_pairs={{0,4},{1,5},{2,6},{3,7},{4,0},{5,1},{6,2},{7,3},{8,12},{9,13},{10,... | collective-permute-start | bytes 393224 | tf_op jit(solution)/shard_map/ppermute | solution.py:194
  110.6 8.4 %collective-permute-start.24 = (bf16[4,32,1024]{2,1,0:T(8,128)(2,1)S(1)}, bf16[4,32,1024]{2,1,0:T(8,128)(2,1)S(1)}, u32[]{:S(2)}, u32[]{:S(2)}) collective-permute-start(bf16[4,32,1024]{2,1,0:T(8,128)(2,1)S(1)} %constant_dynamic-update-slice_fusion.6), channel_id=1, source_target_pairs={{0,2},{1,3},{2,0},{3,1},{4,6},{5,7},{6,4},{7,5},{8,10},{9,11},{10,... | collective-permute-start | bytes 786440 | tf_op jit(solution)/shard_map/ppermute | solution.py:194
  112.3 5.3 %collective-permute-start.20 = (bf16[1,32,1024]{2,1,0:T(8,128)(2,1)S(1)}, bf16[1,32,1024]{2,1,0:T(8,128)(2,1)S(1)}, u32[]{:S(2)}, u32[]{:S(2)}) collective-permute-start(bf16[1,32,1024]{2,1,0:T(8,128)(2,1)S(1)} %bitcast.75), channel_id=1, source_target_pairs={{0,8},{1,9},{2,10},{3,11},{4,12},{5,13},{6,14},{7,15},{8,0},{9,1},... | collective-permute-start | bytes 196616 | tf_op jit(solution)/shard_map/ppermute | solution.py:194
  114.6 8.2 %collective-permute-start.27 = (bf16[4,32,1024]{2,1,0:T(8,128)(2,1)S(1)}, bf16[4,32,1024]{2,1,0:T(8,128)(2,1)S(1)}, u32[]{:S(2)}, u32[]{:S(2)}) collective-permute-start(bf16[4,32,1024]{2,1,0:T(8,128)(2,1)S(1)} %constant_dynamic-update-slice_fusion.8), channel_id=1, source_target_pairs={{0,4},{1,5},{2,6},{3,7},{4,0},{5,1},{6,2},{7,3},{8,12},{9,13},{10,... | collective-permute-start | bytes 786440 | tf_op jit(solution)/shard_map/ppermute | solution.py:194
  117.7 5.0 %collective-permute-start.22 = (bf16[2,32,1024]{2,1,0:T(8,128)(2,1)S(1)}, bf16[2,32,1024]{2,1,0:T(8,128)(2,1)S(1)}, u32[]{:S(2)}, u32[]{:S(2)}) collective-permute-start(bf16[2,32,1024]{2,1,0:T(8,128)(2,1)S(1)} %constant_dynamic-update-slice_fusion.10), channel_id=1, source_target_pairs={{0,2},{1,3},{2,0},{3,1},{4,6},{5,7},{6,4},{7,5},{8,10},{9,11},{10,... | collective-permute-start | bytes 393224 | tf_op jit(solution)/shard_map/ppermute | solution.py:194
  119.0 7.1 %collective-permute-start.29 = (bf16[8,32,1024]{2,1,0:T(8,128)(2,1)S(1)}, bf16[8,32,1024]{2,1,0:T(8,128)(2,1)S(1)}, u32[]{:S(2)}, u32[]{:S(2)}) collective-permute-start(bf16[8,32,1024]{2,1,0:T(8,128)(2,1)S(1)} %constant_dynamic-update-slice_fusion.12.own_ref), channel_id=1, source_target_pairs={{0,1},{1,0},{2,3},{3,2},{4,5},{5,4},{6,7},{7,6},{8,9},{9,8},{10,11... | collective-permute-start | bytes 1572872 | tf_op jit(solution)/shard_map/ppermute | solution.py:194
  122.8 5.0 %collective-permute-start.28 = (bf16[8,32,1024]{2,1,0:T(8,128)(2,1)S(1)}, bf16[8,32,1024]{2,1,0:T(8,128)(2,1)S(1)}, u32[]{:S(2)}, u32[]{:S(2)}) collective-permute-start(bf16[8,32,1024]{2,1,0:T(8,128)(2,1)S(1)} %constant_dynamic-update-slice_fusion.18.own_ref), channel_id=1, source_target_pairs={{0,1},{1,0},{2,3},{3,2},{4,5},{5,4},{6,7},{7,6},{8,9},{9,8},{10,11... | collective-permute-start | bytes 1572872 | tf_op jit(solution)/shard_map/ppermute | solution.py:194
  122.9 8.7 %collective-permute-start.26 = (bf16[4,32,1024]{2,1,0:T(8,128)(2,1)S(1)}, bf16[4,32,1024]{2,1,0:T(8,128)(2,1)S(1)}, u32[]{:S(2)}, u32[]{:S(2)}) collective-permute-start(bf16[4,32,1024]{2,1,0:T(8,128)(2,1)S(1)} %constant_dynamic-update-slice_fusion.14), channel_id=1, source_target_pairs={{0,2},{1,3},{2,0},{3,1},{4,6},{5,7},{6,4},{7,5},{8,10},{9,11},{10,... | collective-permute-start | bytes 786440 | tf_op jit(solution)/shard_map/ppermute | solution.py:194
  124.2 8.5 %collective-permute-start.25 = (bf16[4,32,1024]{2,1,0:T(8,128)(2,1)S(1)}, bf16[4,32,1024]{2,1,0:T(8,128)(2,1)S(1)}, u32[]{:S(2)}, u32[]{:S(2)}) collective-permute-start(bf16[4,32,1024]{2,1,0:T(8,128)(2,1)S(1)} %constant_dynamic-update-slice_fusion.16), channel_id=1, source_target_pairs={{0,4},{1,5},{2,6},{3,7},{4,0},{5,1},{6,2},{7,3},{8,12},{9,13},{10,... | collective-permute-start | bytes 786440 | tf_op jit(solution)/shard_map/ppermute | solution.py:194
  131.7 2.0 %collective-permute-start.31 = (bf16[8,32,1024]{2,1,0:T(8,128)(2,1)S(1)}, bf16[8,32,1024]{2,1,0:T(8,128)(2,1)S(1)}, u32[]{:S(2)}, u32[]{:S(2)}) collective-permute-start(bf16[8,32,1024]{2,1,0:T(8,128)(2,1)S(1)} %constant_dynamic-update-slice_fusion.20.own_ref), channel_id=1, source_target_pairs={{0,1},{1,0},{2,3},{3,2},{4,5},{5,4},{6,7},{7,6},{8,9},{9,8},{10,11... | collective-permute-start | bytes 1572872 | tf_op jit(solution)/shard_map/ppermute | solution.py:194
  132.8 2.5 %collective-permute-start.30 = (bf16[8,32,1024]{2,1,0:T(8,128)(2,1)S(1)}, bf16[8,32,1024]{2,1,0:T(8,128)(2,1)S(1)}, u32[]{:S(2)}, u32[]{:S(2)}) collective-permute-start(bf16[8,32,1024]{2,1,0:T(8,128)(2,1)S(1)} %constant_dynamic-update-slice_fusion.22.own_ref), channel_id=1, source_target_pairs={{0,1},{1,0},{2,3},{3,2},{4,5},{5,4},{6,7},{7,6},{8,9},{9,8},{10,11... | collective-permute-start | bytes 1572872 | tf_op jit(solution)/shard_map/ppermute | solution.py:194
  133.6 3.3 %copy-start.1 = (bf16[16384,64]{0,1:T(8,128)(2,1)S(1)}, bf16[16384,64]{0,1:T(8,128)(2,1)}, u32[]{:S(2)}) copy-start(bf16[16384,64]{0,1:T(8,128)(2,1)} %param.13) | copy-start | bytes 6291460

commit v3 on v2

--- a/solution.py
+++ b/solution.py
@@ -15,68 +15,251 @@
 rope_theta = 500000.0
 
 
-def normalize(values, gain):
-    floats = values.astype(jnp.float32)
-    mean_square = jnp.mean(floats * floats, axis=-1, keepdims=True)
-    return (floats * lax.rsqrt(mean_square + epsilon) * gain.astype(jnp.float32)).astype(
-        jnp.bfloat16
-    )
-
-
-def rotate(values, positions):
-    half_width = values.shape[-1] // 2
-    frequency = jnp.exp(
-        jnp.arange(half_width, dtype=jnp.float32) * (-math.log(rope_theta) / half_width)
-    )
+def turns(positions):
+    half = HD // 2
+    entry = jnp.arange(HD, dtype=jnp.int32)
+    frequency = jnp.exp((entry % half).astype(jnp.float32) * (-math.log(rope_theta) / half))
     angles = positions.astype(jnp.float32)[:, None] * frequency[None, :]
-    cosine = jnp.cos(angles)[:, None, :]
-    sine_part = jnp.sin(angles)[:, None, :]
-    first_half = values[..., :half_width]
-    second_half = values[..., half_width:]
-    return jnp.concatenate(
-        [
-            first_half * cosine - second_half * sine_part,
-            second_half * cosine + first_half * sine_part,
+    sign = jnp.where(entry < half, -1.0, 1.0)
+    return jnp.cos(angles), jnp.sin(angles) * sign
+
+
+def rotate(head, cosine, sine):
+    return head * cosine + pltpu.roll(head, HD // 2, 1) * sine
+
+
+def input_kernel(count, hidden_ref, gain_ref, w_ref, kv_ref, cosine_ref, sine_ref, *refs):
+    *out_refs, hidden, w_buffer, kv_buffer, products, kv_products, result, h_sem, w_sem, kv_sem = refs
+    me = lax.axis_index("tensor")
+    rows, columns = hidden.shape
+    chunks = h_sem.shape[0]
+    depth = columns // chunks
+    width = products.shape[1]
+    kv_width = kv_products.shape[1]
+    here = rows // count
+
+    def spans(k):
+        return pl.ds(pl.multiple_of(k * depth, depth), depth)
+
+    def hidden_copy(k):
+        return pltpu.make_async_copy(
+            hidden_ref.at[:, spans(k)], hidden.at[:, spans(k)], h_sem.at[k]
+        )
+
+    def w_copy(k):
+        return pltpu.make_async_copy(
+            w_ref.at[spans(k), :], w_buffer.at[spans(k), :], w_sem.at[k]
+        )
+
+    for k in range(chunks):
+        hidden_copy(k).start()
+    early = chunks // 4
+    for k in range(early):
+        w_copy(k).start()
+    kv_copy = pltpu.make_async_copy(kv_ref, kv_buffer, kv_sem)
+    kv_copy.start()
+
+    def square(k, total):
+        hidden_copy(k).wait()
+        for lane in range(0, depth, 128):
+            part = hidden[:, pl.ds(pl.multiple_of(k * depth + lane, 128), 128)].astype(jnp.float32)
+            total = total + part * part
+        return total
+
+    total = lax.fori_loop(0, chunks, square, jnp.zeros((rows, 128), jnp.float32))
+    for k in range(early, chunks):
+        w_copy(k).start()
+    scale = lax.rsqrt(jnp.sum(total, axis=1, keepdims=True) / columns + epsilon)
+    products[...] = jnp.zeros_like(products)
+    kv_products[...] = jnp.zeros_like(kv_products)
+    kv_copy.wait()
+
+    def multiply(k, carry):
+        floats = hidden[:, spans(k)].astype(jnp.float32)
+        gain = gain_ref[:, spans(k)].astype(jnp.float32)
+        normed = (floats * scale * gain).astype(jnp.bfloat16)
+        w_copy(k).wait()
+        products[...] += jnp.dot(
+            normed, w_buffer[spans(k), :], preferred_element_type=jnp.float32
+        )
+        kv_products[...] += lax.dot_general(
+            normed,
+            kv_buffer[:, spans(k)],
+            (((1,), (1,)), ((), ())),
+            preferred_element_type=jnp.float32,
+        )
+        return carry
+
+    lax.fori_loop(0, chunks, multiply, 0)
+    for start in range(0, width, HD):
+        result[:, start : start + HD] = rotate(
+            products[:, start : start + HD], cosine_ref[...], sine_ref[...]
+        )
+    result[:, width:] = jnp.zeros((rows, HD), jnp.float32)
+    result[:, width : width + kv_width] = kv_products[...]
+    shift = lax.rem(me, HD // kv_width) * kv_width
+    result[:, width:] = pltpu.roll(result[:, width:], shift, 1)
+    for k, ref in enumerate(out_refs):
+        block = pl.ds(pl.multiple_of(jnp.bitwise_xor(me, k) * here, here), here)
+        ref[...] = result[block, :].astype(jnp.bfloat16)
+
+
+def project_in(hidden_in, gain, w_query, w_keyval, cosine, sine, count):
+    rows, columns = hidden_in.shape
+    width, kv_width = w_query.shape[1], w_keyval.shape[1]
+    chunks = 16
+    vmem = pl.BlockSpec(memory_space=pltpu.VMEM)
+    whole = pl.BlockSpec(memory_space=pl.ANY)
+    share = jax.ShapeDtypeStruct((rows // count, width + HD), jnp.bfloat16)
+    return pl.pallas_call(
+        functools.partial(input_kernel, count),
+        out_shape=(share,) * count,
+        in_specs=[whole, vmem, whole, whole, vmem, vmem],
+        out_specs=(vmem,) * count,
+        scratch_shapes=[
+            pltpu.VMEM((rows, columns), jnp.bfloat16),
+            pltpu.VMEM((columns, width), jnp.bfloat16),
+            pltpu.VMEM((kv_width, columns), jnp.bfloat16),
+            pltpu.VMEM((rows, width), jnp.float32),
+            pltpu.VMEM((rows, kv_width), jnp.float32),
+            pltpu.VMEM((rows, width + HD), jnp.float32),
+            pltpu.SemaphoreType.DMA((chunks,)),
+            pltpu.SemaphoreType.DMA((chunks,)),
+            pltpu.SemaphoreType.DMA,
         ],
-        axis=-1,
-    )
-
-
-def attend(queries, keyval, cache_keys, cache_values, lengths, positions):
-    row_count = queries.shape[0]
-    key_width = keyval.shape[1] // 2
+        compiler_params=pltpu.CompilerParams(vmem_limit_bytes=50 * 1024 * 1024),
+        cost_estimate=pl.CostEstimate(
+            flops=2 * rows * columns * (width + kv_width),
+            bytes_accessed=2 * columns * (rows + width + kv_width),
+            transcendentals=0,
+        ),
+    )(hidden_in, gain, w_query, w_keyval.T, cosine, sine)
+
+
+def attend_kernel(count, lengths_ref, cosine_ref, sine_ref, keys_ref, values_ref, *refs):
+    in_refs, out_refs = refs[:count], refs[count : 2 * count]
+    queries, attended, keys, values, k_sem, v_sem = refs[2 * count :]
+    me = lax.axis_index("tensor")
+    here, span, key_width = keys.shape
     kv_groups = key_width // HD
-    span = cache_keys.shape[1]
-    grouped = queries.reshape(row_count, kv_groups, -1, HD)
-    new_keys = rotate(
-        keyval[:, :key_width].astype(jnp.float32).reshape(row_count, kv_groups, HD), positions
-    ).astype(jnp.bfloat16)
-    new_values = keyval[:, key_width:].reshape(row_count, kv_groups, HD)
-    old_keys = cache_keys.reshape(row_count, span, kv_groups, HD)
-    old_values = cache_values.reshape(row_count, span, kv_groups, HD)
+    parts = attended.shape[0]
+    copies = []
+    for row in range(here):
+        copies.append(
+            (
+                pltpu.make_async_copy(keys_ref.at[row], keys.at[row], k_sem.at[row]),
+                pltpu.make_async_copy(values_ref.at[row], values.at[row], v_sem.at[row]),
+            )
+        )
+        for copy in copies[-1]:
+            copy.start()
+
+    for k, ref in enumerate(in_refs):
+        block = pl.ds(pl.multiple_of(jnp.bitwise_xor(me, k) * here, here), here)
+        for part in range(parts + 1):
+            queries[part, block, :] = ref[:, part * HD : (part + 1) * HD].astype(jnp.float32)
+    mine = pl.ds(pl.multiple_of(me * here, here), here)
+    cosine, sine = cosine_ref[mine, :], sine_ref[mine, :]
+    shares = count // (2 * kv_groups)
+    tiles = []
+    for tile in range(2 * kv_groups):
+        joined = jnp.zeros((here, HD), jnp.float32)
+        for device in range(tile * shares, (tile + 1) * shares):
+            joined = joined + queries[parts, device * here : (device + 1) * here, :]
+        tiles.append(joined)
+    new_keys = [rotate(tile, cosine, sine) for tile in tiles[:kv_groups]]
+    new_keys = jnp.concatenate(new_keys, axis=1).astype(jnp.bfloat16).astype(jnp.float32)
+    new_values = jnp.concatenate(tiles[kv_groups:], axis=1)
+
+    shape = (parts * count, key_width)
+    group_devices = count // kv_groups
+    device = lax.rem(lax.broadcasted_iota(jnp.int32, shape, 0), count)
+    column = lax.broadcasted_iota(jnp.int32, shape, 1)
+    own_group = lax.div(device, group_devices) == lax.div(column, HD)
+    token = lax.broadcasted_iota(jnp.int32, (parts * count, span), 1)
     score_scale = HD ** (-0.5)
-    scores = (
-        jnp.einsum("rgqd,rlgd->rgql", grouped, old_keys, preferred_element_type=jnp.float32)
-        * score_scale
-    )
-    valid_mask = jnp.arange(span)[None, :] < lengths[:, None]
-    scores = jnp.where(valid_mask[:, None, None, :], scores, -1e30)
-    own_score = (
-        jnp.einsum("rgqd,rgd->rgq", grouped, new_keys, preferred_element_type=jnp.float32)
-        * score_scale
-    )
-    largest = jnp.maximum(jnp.max(scores, axis=-1), own_score)
-    expsum = jnp.exp(scores - largest[..., None])
-    own_exp = jnp.exp(own_score - largest)
-    totals = jnp.sum(expsum, axis=-1) + own_exp
-    weights = (expsum / totals[..., None]).astype(jnp.bfloat16)
-    own_weight = (own_exp / totals).astype(jnp.bfloat16)
-    mixed = jnp.einsum("rgql,rlgd->rgqd", weights, old_values, preferred_element_type=jnp.float32)
-    mixed = (
-        mixed
-        + own_weight.astype(jnp.float32)[..., None] * new_values.astype(jnp.float32)[:, :, None, :]
-    )
-    return mixed.astype(jnp.bfloat16).reshape(row_count, -1)
+    for row in range(here):
+        heads = jnp.concatenate(
+            [
+                queries[part, pl.ds(row, count, stride=here), :]
+                for part in range(parts)
+            ],
+            axis=0,
+        )
+        heads = jnp.where(own_group, jnp.concatenate([heads] * kv_groups, axis=1), 0.0)
+        own_score = (
+            jnp.sum(heads * new_keys[row : row + 1], axis=1, keepdims=True) * score_scale
+        )
+        copies[row][0].wait()
+        scores = (
+            lax.dot_general(
+                heads.astype(jnp.bfloat16),
+                keys[row],
+                (((1,), (1,)), ((), ())),
+                preferred_element_type=jnp.float32,
+            )
+            * score_scale
+        )
+        scores = jnp.where(token < lengths_ref[row], scores, -1e30)
+        largest = jnp.maximum(jnp.max(scores, axis=1, keepdims=True), own_score)
+        raised = jnp.exp(scores - largest)
+        own_raised = jnp.exp(own_score - largest)
+        share = 1.0 / (jnp.sum(raised, axis=1, keepdims=True) + own_raised)
+        weights = (raised * share).astype(jnp.bfloat16)
+        own_weight = (own_raised * share).astype(jnp.bfloat16).astype(jnp.float32)
+        copies[row][1].wait()
+        mixed = jnp.dot(weights, values[row], preferred_element_type=jnp.float32)
+        mixed = mixed + own_weight * new_values[row : row + 1]
+        mixed = jnp.where(own_group, mixed, 0.0)
+        chosen = mixed[:, :HD]
+        for group in range(1, kv_groups):
+            chosen = chosen + mixed[:, group * HD : (group + 1) * HD]
+        for part in range(parts):
+            attended[part, pl.ds(row, count, stride=here), :] = chosen[
+                part * count : (part + 1) * count
+            ]
+    for k, ref in enumerate(out_refs):
+        block = pl.ds(pl.multiple_of(jnp.bitwise_xor(me, k) * here, here), here)
+        for part in range(parts):
+            ref[:, part * HD : (part + 1) * HD] = attended[part, block, :].astype(jnp.bfloat16)
+
+
+def attend(blocks, lengths, cosine, sine, cache_keys, cache_values):
+    count = len(blocks)
+    here, span, key_width = cache_keys.shape
+    width = blocks[0].shape[1] - HD
+    vmem = pl.BlockSpec(memory_space=pltpu.VMEM)
+    whole = pl.BlockSpec(memory_space=pl.ANY)
+    share = jax.ShapeDtypeStruct((here, width), jnp.bfloat16)
+    return pl.pallas_call(
+        functools.partial(attend_kernel, count),
+        out_shape=(share,) * count,
+        in_specs=[pl.BlockSpec(memory_space=pltpu.SMEM), vmem, vmem, whole, whole]
+        + [vmem] * count,
+        out_specs=(vmem,) * count,
+        scratch_shapes=[
+            pltpu.VMEM((width // HD + 1, here * count, HD), jnp.float32),
+            pltpu.VMEM((width // HD, here * count, HD), jnp.float32),
+            pltpu.VMEM((here, span, key_width), jnp.bfloat16),
+            pltpu.VMEM((here, span, key_width), jnp.bfloat16),
+            pltpu.SemaphoreType.DMA((here,)),
+            pltpu.SemaphoreType.DMA((here,)),
+        ],
+        compiler_params=pltpu.CompilerParams(vmem_limit_bytes=50 * 1024 * 1024),
+        cost_estimate=pl.CostEstimate(
+            flops=4 * here * count * width * span,
+            bytes_accessed=4 * here * span * key_width,
+            transcendentals=here * count * width // HD * span,
+        ),
+    )(lengths, cosine, sine, cache_keys, cache_values, *blocks)
+
+
+def exchange(blocks):
+    count = len(blocks)
+    return [blocks[0]] + [
+        lax.ppermute(blocks[k], "tensor", [(i, i ^ k) for i in range(count)])
+        for k in range(1, count)
+    ]
 
 
 def plans(count):
@@ -104,8 +287,9 @@
     return spot
 
 
-def project_kernel(count, offsets, heads_ref, w_ref, *refs):
-    *set_refs, w_buffer, arrived = refs
+def project_kernel(count, offsets, w_ref, *refs):
+    in_refs = refs[:count]
+    *set_refs, heads_buffer, w_buffer, arrived = refs[count:]
     me = lax.axis_index("tensor")
     width = w_buffer.shape[2]
     copies = []
@@ -117,7 +301,11 @@
             )
         )
         copies[-1].start()
-    heads = heads_ref[...]
+    here = in_refs[0].shape[0]
+    for k, ref in enumerate(in_refs):
+        block = pl.ds(pl.multiple_of(jnp.bitwise_xor(me, k) * here, here), here)
+        heads_buffer[block, :] = ref[...].astype(jnp.float32)
+    heads = heads_buffer[...].astype(jnp.bfloat16)
     for slot, offset in enumerate(offsets):
         copies[slot].wait()
         product = jnp.dot(heads, w_buffer[slot], preferred_element_type=jnp.float32).astype(
@@ -129,17 +317,20 @@
             start += ref.shape[1]
 
 
-def project(heads, w_out, count, offsets):
-    rows, depth = heads.shape
+def project(blocks, w_out, offsets):
+    count = len(blocks)
+    rows, depth = blocks[0].shape[0] * count, blocks[0].shape[1]
     width = w_out.shape[1] // count
     sets = len(plans(count))
     share = jax.ShapeDtypeStruct((len(offsets), rows // sets, width), jnp.bfloat16)
     return pl.pallas_call(
         functools.partial(project_kernel, count, offsets),
         out_shape=(share,) * sets,
-        in_specs=[pl.BlockSpec(memory_space=pltpu.VMEM), pl.BlockSpec(memory_space=pl.ANY)],
+        in_specs=[pl.BlockSpec(memory_space=pl.ANY)]
+        + [pl.BlockSpec(memory_space=pltpu.VMEM)] * count,
         out_specs=(pl.BlockSpec(memory_space=pltpu.VMEM),) * sets,
         scratch_shapes=[
+            pltpu.VMEM((rows, depth), jnp.float32),
             pltpu.VMEM((len(offsets), depth, width), jnp.bfloat16),
             pltpu.SemaphoreType.DMA((len(offsets),)),
         ],
@@ -149,7 +340,7 @@
             bytes_accessed=2 * (depth + rows) * width * len(offsets),
             transcendentals=0,
         ),
-    )(heads, w_out)
+    )(w_out, *blocks)
 
 
 def finish_kernel(offsets, own_ref, other_ref, gain_ref, *refs):
@@ -213,36 +404,22 @@
     row_count = hidden_in.shape[0]
     count = lax.axis_size("tensor")
     my_index = lax.axis_index("tensor")
-    normed_in = normalize(hidden_in, attn_gain)
-    queries = jnp.dot(normed_in, w_query, preferred_element_type=jnp.float32)
-    queries = queries.reshape(row_count, queries.shape[1] // HD, HD)
-    queries = rotate(queries, positions).astype(jnp.bfloat16).reshape(row_count, -1)
-    keyval = jnp.dot(normed_in, w_keyval, preferred_element_type=jnp.float32).astype(jnp.bfloat16)
-    query_width = queries.shape[1]
-    rows_here = row_count // count
-    both = lax.all_to_all(
-        jnp.concatenate([queries, keyval], axis=1).reshape(count, rows_here, -1),
-        "tensor",
-        split_axis=0,
-        concat_axis=0,
-        tiled=True,
+    cosine, sine = turns(positions)
+    blocks = project_in(
+        hidden_in, attn_gain.reshape(1, -1), w_query, w_keyval, cosine, sine, count
     )
-    both = jnp.swapaxes(both, 0, 1)
-    row_queries = both[..., :query_width].reshape(rows_here, -1)
-    row_keyval = both[..., query_width:].reshape(rows_here, -1)
-    own_positions = lax.dynamic_slice_in_dim(positions, my_index * rows_here, rows_here)
-    attended = attend(row_queries, row_keyval, cache_keys, cache_values, lengths, own_positions)
-    head_rows = lax.all_to_all(attended, "tensor", split_axis=1, concat_axis=0, tiled=True)
-
+    head_blocks = exchange(
+        attend(exchange(blocks), lengths, cosine, sine, cache_keys, cache_values)
+    )
     share_width = w_out.shape[1] // count
     mine = lax.dynamic_slice_in_dim(hidden_in, my_index * share_width, share_width, 1)
     gain = ffn_gain.astype(jnp.float32).reshape(count, share_width)
     orders = plans(count)
     sets = len(orders)
     set_rows = row_count // sets
-    sent = project(head_rows, w_out, count, list(range(1, count, 2)))
+    sent = project(head_blocks, w_out, list(range(1, count, 2)))
     arrivals = [swap(block, 0, count) for block in sent]
-    held = list(project(head_rows, w_out, count, list(range(0, count, 2))))
+    held = list(project(head_blocks, w_out, list(range(0, count, 2))))
 
     streams = [None] * sets
     offsets = [[0] for _ in range(sets)]

time: 137 us -> 158 us (1.15)
  starting transfers between devices: 31.6 us -> 71.3 us
  matrix products: 22.8 us -> 0 us
  Pallas kernels: 14.3 us -> 35.2 us
  blocking collectives: 10.5 us -> 0 us
  other arithmetic: 12.3 us -> 6.3 us
  waiting for transfers between devices: 43.2 us -> 41.5 us
  local copies, waits for them, and re-layouts: 1.04 us -> 2.69 us
    ppermute x0 -> x30, starting transfers between devices: none -> 43.7 us  [exchange(): lax.ppermute(blocks[k], 'tensor', [(i, i ^ k) for i in range(count)])]
    dot_general x5 -> x0, matrix products: 22.8 us -> none  [the longest x1 8.14 us: on_device(): queries = jnp.dot(normed_in, w_query, preferred_element_type=jnp.float32)]
    pallas_call x0 -> x2, Pallas kernels: none -> 20.9 us  [the longest x1 11.4 us: project_in(): pl.pallas_call(functools.partial(input_kernel, count), out_shape=(share,)...]
    all_to_all x1 -> x0, blocking collectives: 10.5 us -> none  [on_device(): lax.all_to_all(attended, 'tensor', split_axis=1, concat_axis=0, tiled=True)]
    all_to_all x1 -> x0, waiting for transfers between devices: 8.18 us -> none  [on_device(): lax.all_to_all(jnp.concatenate([queries, keyval], axis=1).reshape(count,...]
    all_to_all x1 -> x0, starting transfers between devices: 7.39 us -> none  [on_device(): lax.all_to_all(jnp.concatenate([queries, keyval], axis=1).reshape(count,...]
    ppermute x0 -> x30, waiting for transfers between devices: none -> 6.66 us  [exchange(): lax.ppermute(blocks[k], 'tensor', [(i, i ^ k) for i in range(count)])]
    reduce_sum x2 -> x0, other arithmetic: 4.04 us -> none  [the longest x1 3.44 us: normalize(): mean_square = jnp.mean(floats * floats, axis=-1, keepdims=True)]
  transfers between devices with their start and end apart: 33 -> 62, of which waited for: 13 -> 19; matrix products, arithmetic and copies ran while one was open for 4% -> 4% of each run, Pallas kernels for 6% -> 6%
where the time goes in v3:
time: 158 us
  starting transfers between devices  71.3 us (45%)
  waiting for transfers between devices  41.5 us (26%)
  Pallas kernels  35.2 us (22%)
  other arithmetic  6.3 us (4%)
  local copies, waits for them, and re-layouts  2.69 us (2%)
    ppermute x30, starting transfers between devices, exchange(): lax.ppermute(blocks[k], 'tensor', [(i, i ^ k) for i in range(count)])  43.7 us
    ppermute x32, waiting for transfers between devices, swap(): lax.ppermute(values, 'tensor', [(i, i ^ 1 << bit) for i in range(count)])  34.8 us
    ppermute x32, starting transfers between devices, swap(): lax.ppermute(values, 'tensor', [(i, i ^ 1 << bit) for i in range(count)])  27.6 us
    pallas_call x1, Pallas kernels, project_in(): pl.pallas_call(functools.partial(input_kernel, count), out_shape=(share,)...  11.4 us
    pallas_call x1, Pallas kernels, attend(): pl.pallas_call(functools.partial(attend_kernel, count), out_shape=(share,...  9.54 us
    pallas_call x2, Pallas kernels, project(): pl.pallas_call(functools.partial(project_kernel, count, offsets), out_sha...  7.67 us
    ppermute x30, waiting for transfers between devices, exchange(): lax.ppermute(blocks[k], 'tensor', [(i, i ^ k) for i in range(count)])  6.66 us
    pallas_call x4, Pallas kernels, finish(): pl.pallas_call(functools.partial(finish_kernel, offsets), grid=(1,), out_...  6.61 us
  transfers between devices with their start and end apart: 62, of which 19 were waited for; matrix products, arithmetic and copies ran while one was open for 4% of the time, Pallas kernels for 6%

profile of v3, /device:TPU:0, one launch (start us, length us, event | category | flops | bytes accessed | tf_op | source)
XLA Modules:
  0.0 158.0 jit_solution(3628854424436465420)
XLA Ops:
  1.3 0.8 reshape.42.gain_ref
  2.4 1.6 %copy-done = bf16[16384,64]{0,1:T(8,128)(2,1)S(1)} copy-done((bf16[16384,64]{0,1:T(8,128)(2,1)S(1)}, bf16[16384,64]{0,1:T(8,128)(2,1)}, u32[]{:S(2)}) %copy-start) | copy-done | bytes 2097176
  4.0 11.4 %shard_map.113 = (bf16[8,640]{1,0:T(8,128)(2,1)S(1)}, bf16[8,640]{1,0:T(8,128)(2,1)S(1)}, bf16[8,640]{1,0:T(8,128)(2,1)S(1)}, bf16[8,640]{1,0:T(8,128)(2,1)S(1)}...) custom-call(bf16[128,16384]{1,0:T(8,128)(2,1)} %hidden_ref.1, ...), custom_call_target="tpu_custom_call" | custom-call | flops 2415919104 | bytes 23068672 | tf_op jit(solution)/shard_map/pallas_call | solution.py:114
  15.9 2.6 %collective-permute-start.1 = (bf16[8,640]{1,0:T(8,128)(2,1)S(1)}, bf16[8,640]{1,0:T(8,128)(2,1)S(1)}, u32[]{:S(2)}, u32[]{:S(2)}) collective-permute-start(bf16[8,640]{1,0:T(8,128)(2,1)S(1)} %get-tuple-element.106), channel_id=1, source_target_pairs={{0,2},{1,3},{2,0},{3,1},{4,6},{5,7},{6,4},{7,5},{8,10},{9,11},{10,... | collective-permute-start | bytes 30728 | tf_op jit(solution)/shard_map/ppermute | solution.py:260
  18.5 2.3 %collective-permute-start.10 = (bf16[8,640]{1,0:T(8,128)(2,1)S(1)}, bf16[8,640]{1,0:T(8,128)(2,1)S(1)}, u32[]{:S(2)}, u32[]{:S(2)}) collective-permute-start(bf16[8,640]{1,0:T(8,128)(2,1)S(1)} %get-tuple-element.115), channel_id=1, source_target_pairs={{0,11},{1,10},{2,9},{3,8},{4,15},{5,14},{6,13},{7,12},{8,3},{9,2},... | collective-permute-start | bytes 30728 | tf_op jit(solution)/shard_map/ppermute | solution.py:260
  20.8 1.3 collective-permute-start.11
  22.2 2.1 %collective-permute-start.12 = (bf16[8,640]{1,0:T(8,128)(2,1)S(1)}, bf16[8,640]{1,0:T(8,128)(2,1)S(1)}, u32[]{:S(2)}, u32[]{:S(2)}) collective-permute-start(bf16[8,640]{1,0:T(8,128)(2,1)S(1)} %get-tuple-element.117), channel_id=1, source_target_pairs={{0,13},{1,12},{2,15},{3,14},{4,9},{5,8},{6,11},{7,10},{8,5},{9,4},... | collective-permute-start | bytes 30728 | tf_op jit(solution)/shard_map/ppermute | solution.py:260
  24.3 2.3 %collective-permute-start.13 = (bf16[8,640]{1,0:T(8,128)(2,1)S(1)}, bf16[8,640]{1,0:T(8,128)(2,1)S(1)}, u32[]{:S(2)}, u32[]{:S(2)}) collective-permute-start(bf16[8,640]{1,0:T(8,128)(2,1)S(1)} %get-tuple-element.118), channel_id=1, source_target_pairs={{0,14},{1,15},{2,12},{3,13},{4,10},{5,11},{6,8},{7,9},{8,6},{9,7},... | collective-permute-start | bytes 30728 | tf_op jit(solution)/shard_map/ppermute | solution.py:260
  26.6 2.2 %collective-permute-start.14 = (bf16[8,640]{1,0:T(8,128)(2,1)S(1)}, bf16[8,640]{1,0:T(8,128)(2,1)S(1)}, u32[]{:S(2)}, u32[]{:S(2)}) collective-permute-start(bf16[8,640]{1,0:T(8,128)(2,1)S(1)} %get-tuple-element.119), channel_id=1, source_target_pairs={{0,15},{1,14},{2,13},{3,12},{4,11},{5,10},{6,9},{7,8},{8,7},{9,6},... | collective-permute-start | bytes 30728 | tf_op jit(solution)/shard_map/ppermute | solution.py:260
  28.8 1.5 collective-permute-start.2
  30.3 1.5 collective-permute-start.4
  32.4 2.3 %collective-permute-start.6 = (bf16[8,640]{1,0:T(8,128)(2,1)S(1)}, bf16[8,640]{1,0:T(8,128)(2,1)S(1)}, u32[]{:S(2)}, u32[]{:S(2)}) collective-permute-start(bf16[8,640]{1,0:T(8,128)(2,1)S(1)} %get-tuple-element.111), channel_id=1, source_target_pairs={{0,7},{1,6},{2,5},{3,4},{4,3},{5,2},{6,1},{7,0},{8,15},{9,14},{10,... | collective-permute-start | bytes 30728 | tf_op jit(solution)/shard_map/ppermute | solution.py:260
  35.2 1.9 %collective-permute-start.8 = (bf16[8,640]{1,0:T(8,128)(2,1)S(1)}, bf16[8,640]{1,0:T(8,128)(2,1)S(1)}, u32[]{:S(2)}, u32[]{:S(2)}) collective-permute-start(bf16[8,640]{1,0:T(8,128)(2,1)S(1)} %get-tuple-element.113), channel_id=1, source_target_pairs={{0,9},{1,8},{2,11},{3,10},{4,13},{5,12},{6,15},{7,14},{8,1},{9,0},... | collective-permute-start | bytes 30728 | tf_op jit(solution)/shard_map/ppermute | solution.py:260
  37.1 1.6 %collective-permute-start.9 = (bf16[8,640]{1,0:T(8,128)(2,1)S(1)}, bf16[8,640]{1,0:T(8,128)(2,1)S(1)}, u32[]{:S(2)}, u32[]{:S(2)}) collective-permute-start(bf16[8,640]{1,0:T(8,128)(2,1)S(1)} %get-tuple-element.114), channel_id=1, source_target_pairs={{0,10},{1,11},{2,8},{3,9},{4,14},{5,15},{6,12},{7,13},{8,2},{9,3},... | collective-permute-start | bytes 30728 | tf_op jit(solution)/shard_map/ppermute | solution.py:260
  39.3 3.3 %collective-permute-done.9.refs_10_ = bf16[8,640]{1,0:T(8,128)(2,1)S(1)} collective-permute-done((bf16[8,640]{1,0:T(8,128)(2,1)S(1)}, bf16[8,640]{1,0:T(8,128)(2,1)S(1)}, u32[]{:S(2)}, u32[]{:S(2)}) %collective-permute-start.9) | collective-permute-done | bytes 10272 | tf_op jit(solution)/shard_map/ppermute | solution.py:260
  42.6 9.5 %shard_map.114 = (bf16[8,512]{1,0:T(8,128)(2,1)S(1)}, bf16[8,512]{1,0:T(8,128)(2,1)S(1)}, bf16[8,512]{1,0:T(8,128)(2,1)S(1)}, bf16[8,512]{1,0:T(8,128)(2,1)S(1)}...) custom-call(s32[8]{0:T(128)S(1)} %copy-done.1, ...), custom_call_target="tpu_custom_call" | custom-call | flops 268435456 | bytes 16777216 | tf_op jit(solution)/shard_map/pallas_call | solution.py:234
  52.9 1.2 collective-permute-start.17
  54.7 1.0 collective-permute-start.19
  56.4 2.1 %collective-permute-start.21 = (bf16[8,512]{1,0:T(8,128)(2,1)S(1)}, bf16[8,512]{1,0:T(8,128)(2,1)S(1)}, u32[]{:S(2)}, u32[]{:S(2)}) collective-permute-start(bf16[8,512]{1,0:T(8,128)(2,1)S(1)} %get-tuple-element.127), channel_id=1, source_target_pairs={{0,7},{1,6},{2,5},{3,4},{4,3},{5,2},{6,1},{7,0},{8,15},{9,14},{10,... | collective-permute-start | bytes 24584 | tf_op jit(solution)/shard_map/ppermute | solution.py:260
  59.2 1.9 %collective-permute-start.23 = (bf16[8,512]{1,0:T(8,128)(2,1)S(1)}, bf16[8,512]{1,0:T(8,128)(2,1)S(1)}, u32[]{:S(2)}, u32[]{:S(2)}) collective-permute-start(bf16[8,512]{1,0:T(8,128)(2,1)S(1)} %get-tuple-element.129), channel_id=1, source_target_pairs={{0,9},{1,8},{2,11},{3,10},{4,13},{5,12},{6,15},{7,14},{8,1},{9,0},... | collective-permute-start | bytes 24584 | tf_op jit(solution)/shard_map/ppermute | solution.py:260
  61.1 1.6 %collective-permute-start.24 = (bf16[8,512]{1,0:T(8,128)(2,1)S(1)}, bf16[8,512]{1,0:T(8,128)(2,1)S(1)}, u32[]{:S(2)}, u32[]{:S(2)}) collective-permute-start(bf16[8,512]{1,0:T(8,128)(2,1)S(1)} %get-tuple-element.130), channel_id=1, source_target_pairs={{0,10},{1,11},{2,8},{3,9},{4,14},{5,15},{6,12},{7,13},{8,2},{9,3},... | collective-permute-start | bytes 24584 | tf_op jit(solution)/shard_map/ppermute | solution.py:260
  62.7 2.0 %collective-permute-start.25 = (bf16[8,512]{1,0:T(8,128)(2,1)S(1)}, bf16[8,512]{1,0:T(8,128)(2,1)S(1)}, u32[]{:S(2)}, u32[]{:S(2)}) collective-permute-start(bf16[8,512]{1,0:T(8,128)(2,1)S(1)} %get-tuple-element.131), channel_id=1, source_target_pairs={{0,11},{1,10},{2,9},{3,8},{4,15},{5,14},{6,13},{7,12},{8,3},{9,2},... | collective-permute-start | bytes 24584 | tf_op jit(solution)/shard_map/ppermute | solution.py:260
  64.7 1.3 collective-permute-start.26
  66.0 2.2 %collective-permute-start.27 = (bf16[8,512]{1,0:T(8,128)(2,1)S(1)}, bf16[8,512]{1,0:T(8,128)(2,1)S(1)}, u32[]{:S(2)}, u32[]{:S(2)}) collective-permute-start(bf16[8,512]{1,0:T(8,128)(2,1)S(1)} %get-tuple-element.133), channel_id=1, source_target_pairs={{0,13},{1,12},{2,15},{3,14},{4,9},{5,8},{6,11},{7,10},{8,5},{9,4},... | collective-permute-start | bytes 24584 | tf_op jit(solution)/shard_map/ppermute | solution.py:260
  68.2 1.4 collective-permute-start.28
  69.6 3.1 %collective-permute-start.29 = (bf16[8,512]{1,0:T(8,128)(2,1)S(1)}, bf16[8,512]{1,0:T(8,128)(2,1)S(1)}, u32[]{:S(2)}, u32[]{:S(2)}) collective-permute-start(bf16[8,512]{1,0:T(8,128)(2,1)S(1)} %get-tuple-element.135), channel_id=1, source_target_pairs={{0,15},{1,14},{2,13},{3,12},{4,11},{5,10},{6,9},{7,8},{8,7},{9,6},... | collective-permute-start | bytes 24584 | tf_op jit(solution)/shard_map/ppermute | solution.py:260
  72.7 1.8 %collective-permute-done.28.refs_14_ = bf16[8,512]{1,0:T(8,128)(2,1)S(1)} collective-permute-done((bf16[8,512]{1,0:T(8,128)(2,1)S(1)}, bf16[8,512]{1,0:T(8,128)(2,1)S(1)}, u32[]{:S(2)}, u32[]{:S(2)}) %collective-permute-start.28) | collective-permute-done | bytes 8224 | tf_op jit(solution)/shard_map/ppermute | solution.py:260
  74.5 0.8 collective-permute-done.29.refs_15_
  75.4 3.8 %shard_map.116 = (bf16[8,32,1024]{2,1,0:T(8,128)(2,1)S(1)}, bf16[8,32,1024]{2,1,0:T(8,128)(2,1)S(1)}, bf16[8,32,1024]{2,1,0:T(8,128)(2,1)S(1)}, bf16[8,32,1024]{2,1,0:T(8,128)(2,1)S(1)}) custom-call(bf16[512,16384]{1,0:T(8,128)(2,1)} %w_ref.5, bf16[8,512]{1,0:T(8,128)(2,1)S(1)} %get-tuple-element.120.refs_0_, ...), custom_call_target="tpu_custom_call" | custom-call | flops 1073741824 | bytes 10485760 | tf_op jit(solution)/shard_map/pallas_call | solution.py:326
  79.9 3.8 %shard_map.115 = (bf16[8,32,1024]{2,1,0:T(8,128)(2,1)S(1)}, bf16[8,32,1024]{2,1,0:T(8,128)(2,1)S(1)}, bf16[8,32,1024]{2,1,0:T(8,128)(2,1)S(1)}, bf16[8,32,1024]{2,1,0:T(8,128)(2,1)S(1)}) custom-call(bf16[512,16384]{1,0:T(8,128)(2,1)} %w_ref.5, bf16[8,512]{1,0:T(8,128)(2,1)S(1)} %get-tuple-element.120.refs_0_, ...), custom_call_target="tpu_custom_call" | custom-call | flops 1073741824 | bytes 10485760 | tf_op jit(solution)/shard_map/pallas_call | solution.py:326
  83.9 1.5 collective-permute-start.31
  85.8 6.8 %collective-permute-done.31 = bf16[4,32,1024]{2,1,0:T(8,128)(2,1)S(1)} collective-permute-done((bf16[4,32,1024]{2,1,0:T(8,128)(2,1)S(1)}, bf16[4,32,1024]{2,1,0:T(8,128)(2,1)S(1)}, u32[]{:S(2)}, u32[]{:S(2)}) %collective-permute-start.31) | collective-permute-done | bytes 262176 | tf_op jit(solution)/shard_map/ppermute | solution.py:385
  92.9 1.4 collective-permute-start.36
  94.5 6.3 %collective-permute-done.36 = bf16[4,32,1024]{2,1,0:T(8,128)(2,1)S(1)} collective-permute-done((bf16[4,32,1024]{2,1,0:T(8,128)(2,1)S(1)}, bf16[4,32,1024]{2,1,0:T(8,128)(2,1)S(1)}, u32[]{:S(2)}, u32[]{:S(2)}) %collective-permute-start.36) | collective-permute-done | bytes 262176 | tf_op jit(solution)/shard_map/ppermute | solution.py:385
  101.2 2.9 %collective-permute-start.41 = (bf16[2,32,1024]{2,1,0:T(8,128)(2,1)S(1)}, bf16[2,32,1024]{2,1,0:T(8,128)(2,1)S(1)}, u32[]{:S(2)}, u32[]{:S(2)}) collective-permute-start(bf16[2,32,1024]{2,1,0:T(8,128)(2,1)S(1)} %get-tuple-element.220), channel_id=1, source_target_pairs={{0,8},{1,9},{2,10},{3,11},{4,12},{5,13},{6,14},{7,15},{8,0},{9,1},... | collective-permute-start | bytes 393224 | tf_op jit(solution)/shard_map/ppermute | solution.py:385
  104.2 1.3 collective-permute-start.40
  105.7 5.2 %collective-permute-done.38 = bf16[1,32,1024]{2,1,0:T(8,128)(2,1)S(1)} collective-permute-done((bf16[1,32,1024]{2,1,0:T(8,128)(2,1)S(1)}, bf16[1,32,1024]{2,1,0:T(8,128)(2,1)S(1)}, u32[]{:S(2)}, u32[]{:S(2)}) %collective-permute-start.38) | collective-permute-done | bytes 65568 | tf_op jit(solution)/shard_map/ppermute | solution.py:385
  110.9 0.9 fusion.3
  111.9 1.1 collective-permute-done.41
  113.0 1.6 collective-permute-start.44
  114.6 0.8 collective-permute-start.45
  115.4 1.8 %collective-permute-start.42 = (bf16[1,32,1024]{2,1,0:T(8,128)(2,1)S(1)}, bf16[1,32,1024]{2,1,0:T(8,128)(2,1)S(1)}, u32[]{:S(2)}, u32[]{:S(2)}) collective-permute-start(bf16[1,32,1024]{2,1,0:T(8,128)(2,1)S(1)} %get-tuple-element.225), channel_id=1, source_target_pairs={{0,8},{1,9},{2,10},{3,11},{4,12},{5,13},{6,14},{7,15},{8,0},{9,1},... | collective-permute-start | bytes 196616 | tf_op jit(solution)/shard_map/ppermute | solution.py:385
  117.3 0.9 fusion.2
  118.2 1.9 %collective-permute-start.48 = (bf16[1,32,1024]{2,1,0:T(8,128)(2,1)S(1)}, bf16[1,32,1024]{2,1,0:T(8,128)(2,1)S(1)}, u32[]{:S(2)}, u32[]{:S(2)}) collective-permute-start(bf16[1,32,1024]{2,1,0:T(8,128)(2,1)S(1)} %bitcast.24), channel_id=1, source_target_pairs={{0,8},{1,9},{2,10},{3,11},{4,12},{5,13},{6,14},{7,15},{8,0},{9,1},... | collective-permute-start | bytes 196616 | tf_op jit(solution)/shard_map/ppermute | solution.py:385
  120.1 0.8 collective-permute-start.47
  121.2 0.9 fusion.1
  122.1 2.4 %collective-permute-start.49 = (bf16[1,32,1024]{2,1,0:T(8,128)(2,1)S(1)}, bf16[1,32,1024]{2,1,0:T(8,128)(2,1)S(1)}, u32[]{:S(2)}, u32[]{:S(2)}) collective-permute-start(bf16[1,32,1024]{2,1,0:T(8,128)(2,1)S(1)} %bitcast.26), channel_id=1, source_target_pairs={{0,8},{1,9},{2,10},{3,11},{4,12},{5,13},{6,14},{7,15},{8,0},{9,1},... | collective-permute-start | bytes 196616 | tf_op jit(solution)/shard_map/ppermute | solution.py:385
  124.5 0.8 collective-permute-start.46
  125.4 2.1 %collective-permute-done.49 = bf16[1,32,1024]{2,1,0:T(8,128)(2,1)S(1)} collective-permute-done((bf16[1,32,1024]{2,1,0:T(8,128)(2,1)S(1)}, bf16[1,32,1024]{2,1,0:T(8,128)(2,1)S(1)}, u32[]{:S(2)}, u32[]{:S(2)}) %collective-permute-start.49) | collective-permute-done | bytes 65568 | tf_op jit(solution)/shard_map/ppermute | solution.py:385
  127.4 1.5 collective-permute-start.51
  128.9 2.3 %collective-permute-start.53 = (bf16[2,32,1024]{2,1,0:T(8,128)(2,1)S(1)}, bf16[2,32,1024]{2,1,0:T(8,128)(2,1)S(1)}, u32[]{:S(2)}, u32[]{:S(2)}) collective-permute-start(bf16[2,32,1024]{2,1,0:T(8,128)(2,1)S(1)} %constant_dynamic-update-slice_fusion.4), channel_id=1, source_target_pairs={{0,4},{1,5},{2,6},{3,7},{4,0},{5,1},{6,2},{7,3},{8,12},{9,13},{10,... | collective-permute-start | bytes 393224 | tf_op jit(solution)/shard_map/ppermute | solution.py:385
  131.3 0.8 collective-permute-start.54
  132.1 0.9 fusion
  133.9 1.3 collective-permute-start.57
  135.1 3.6 %collective-permute-done.50 = bf16[1,32,1024]{2,1,0:T(8,128)(2,1)S(1)} collective-permute-done((bf16[1,32,1024]{2,1,0:T(8,128)(2,1)S(1)}, bf16[1,32,1024]{2,1,0:T(8,128)(2,1)S(1)}, u32[]{:S(2)}, u32[]{:S(2)}) %collective-permute-start.50) | collective-permute-done | bytes 65568 | tf_op jit(solution)/shard_map/ppermute | solution.py:385
  138.8 1.3 collective-permute-start.52
  140.2 3.6 %collective-permute-done.52 = bf16[2,32,1024]{2,1,0:T(8,128)(2,1)S(1)} collective-permute-done((bf16[2,32,1024]{2,1,0:T(8,128)(2,1)S(1)}, bf16[2,32,1024]{2,1,0:T(8,128)(2,1)S(1)}, u32[]{:S(2)}, u32[]{:S(2)}) %collective-permute-start.52) | collective-permute-done | bytes 131104 | tf_op jit(solution)/shard_map/ppermute | solution.py:385
  144.0 1.3 collective-permute-start.56
  145.5 1.7 %shard_map.117.refs_0_ = bf16[128,16384]{1,0:T(8,128)(2,1)} custom-call(bf16[8,32,1024]{2,1,0:T(8,128)(2,1)S(1)} %constant_dynamic-update-slice_fusion.12.own_ref, bf16[8,32,1024]{2,1,0:T(8,128)(2,1)S(1)} %collective-permute-done.59.other_ref, f32[16,1024]{1,0:T(8,128)S(1)} %reshape.46.gain_ref), custom_call_target="tpu_custom_call" | custom-call | flops 3145728 | bytes 2097152 | tf_op jit(solution)/shard_map/pallas_call | solution.py:370
  147.1 1.7 %shard_map.118.refs_0_ = bf16[128,16384]{1,0:T(8,128)(2,1)} custom-call(bf16[8,32,1024]{2,1,0:T(8,128)(2,1)S(1)} %constant_dynamic-update-slice_fusion.18.own_ref, bf16[8,32,1024]{2,1,0:T(8,128)(2,1)S(1)} %collective-permute-done.58.other_ref, f32[16,1024]{1,0:T(8,128)S(1)} %reshape.46.gain_ref, ...), custom_call_target="tpu_custom_call", output_to_operand_aliasing={{}: (3, {})} | custom-call | flops 3145728 | bytes 2097152 | tf_op jit(solution)/shard_map/pallas_call | solution.py:370
  148.8 3.9 %collective-permute-done.56 = bf16[4,32,1024]{2,1,0:T(8,128)(2,1)S(1)} collective-permute-done((bf16[4,32,1024]{2,1,0:T(8,128)(2,1)S(1)}, bf16[4,32,1024]{2,1,0:T(8,128)(2,1)S(1)}, u32[]{:S(2)}, u32[]{:S(2)}) %collective-permute-start.56) | collective-permute-done | bytes 262176 | tf_op jit(solution)/shard_map/ppermute | solution.py:385
  152.8 0.8 collective-permute-done.55
  154.7 1.7 %shard_map.119.refs_0_ = bf16[128,16384]{1,0:T(8,128)(2,1)} custom-call(bf16[8,32,1024]{2,1,0:T(8,128)(2,1)S(1)} %constant_dynamic-update-slice_fusion.20.own_ref, bf16[8,32,1024]{2,1,0:T(8,128)(2,1)S(1)} %collective-permute-done.61.other_ref, f32[16,1024]{1,0:T(8,128)S(1)} %reshape.46.gain_ref, ...), custom_call_target="tpu_custom_call", output_to_operand_aliasing={{}: (3, {})} | custom-call | flops 3145728 | bytes 2097152 | tf_op jit(solution)/shard_map/pallas_call | solution.py:370
  156.4 1.7 %shard_map.120 = bf16[128,16384]{1,0:T(8,128)(2,1)} custom-call(bf16[8,32,1024]{2,1,0:T(8,128)(2,1)S(1)} %constant_dynamic-update-slice_fusion.22.own_ref, bf16[8,32,1024]{2,1,0:T(8,128)(2,1)S(1)} %collective-permute-done.60.other_ref, f32[16,1024]{1,0:T(8,128)S(1)} %reshape.46.gain_ref, ...), custom_call_target="tpu_custom_call", output_to_operand_aliasing={{}: (3, {})} | custom-call | flops 3145728 | bytes 2097152 | tf_op jit(solution)/shard_map/pallas_call | solution.py:370
  (120 shorter events, 11.3 us)
Async XLA Ops:
  4.0 38.6 %copy-start.1 = (s32[8]{0:T(128)S(1)}, s32[8]{0:T(128)}, u32[]{:S(2)}) copy-start(s32[8]{0:T(128)} %lengths_ref.1) | copy-start | bytes 100
  15.4 8.9 %collective-permute-start = (bf16[8,640]{1,0:T(8,128)(2,1)S(1)}, bf16[8,640]{1,0:T(8,128)(2,1)S(1)}, u32[]{:S(2)}, u32[]{:S(2)}) collective-permute-start(bf16[8,640]{1,0:T(8,128)(2,1)S(1)} %get-tuple-element.105), channel_id=1, source_target_pairs={{0,1},{1,0},{2,3},{3,2},{4,5},{5,4},{6,7},{7,6},{8,9},{9,8},{10,11... | collective-permute-start | bytes 30728 | tf_op jit(solution)/shard_map/ppermute | solution.py:260
  15.9 10.7 %collective-permute-start.1 = (bf16[8,640]{1,0:T(8,128)(2,1)S(1)}, bf16[8,640]{1,0:T(8,128)(2,1)S(1)}, u32[]{:S(2)}, u32[]{:S(2)}) collective-permute-start(bf16[8,640]{1,0:T(8,128)(2,1)S(1)} %get-tuple-element.106), channel_id=1, source_target_pairs={{0,2},{1,3},{2,0},{3,1},{4,6},{5,7},{6,4},{7,5},{8,10},{9,11},{10,... | collective-permute-start | bytes 30728 | tf_op jit(solution)/shard_map/ppermute | solution.py:260
  18.5 10.3 %collective-permute-start.10 = (bf16[8,640]{1,0:T(8,128)(2,1)S(1)}, bf16[8,640]{1,0:T(8,128)(2,1)S(1)}, u32[]{:S(2)}, u32[]{:S(2)}) collective-permute-start(bf16[8,640]{1,0:T(8,128)(2,1)S(1)} %get-tuple-element.115), channel_id=1, source_target_pairs={{0,11},{1,10},{2,9},{3,8},{4,15},{5,14},{6,13},{7,12},{8,3},{9,2},... | collective-permute-start | bytes 30728 | tf_op jit(solution)/shard_map/ppermute | solution.py:260
  20.8 9.5 %collective-permute-start.11 = (bf16[8,640]{1,0:T(8,128)(2,1)S(1)}, bf16[8,640]{1,0:T(8,128)(2,1)S(1)}, u32[]{:S(2)}, u32[]{:S(2)}) collective-permute-start(bf16[8,640]{1,0:T(8,128)(2,1)S(1)} %get-tuple-element.116), channel_id=1, source_target_pairs={{0,12},{1,13},{2,14},{3,15},{4,8},{5,9},{6,10},{7,11},{8,4},{9,5},... | collective-permute-start | bytes 30728 | tf_op jit(solution)/shard_map/ppermute | solution.py:260
  22.2 8.1 %collective-permute-start.12 = (bf16[8,640]{1,0:T(8,128)(2,1)S(1)}, bf16[8,640]{1,0:T(8,128)(2,1)S(1)}, u32[]{:S(2)}, u32[]{:S(2)}) collective-permute-start(bf16[8,640]{1,0:T(8,128)(2,1)S(1)} %get-tuple-element.117), channel_id=1, source_target_pairs={{0,13},{1,12},{2,15},{3,14},{4,9},{5,8},{6,11},{7,10},{8,5},{9,4},... | collective-permute-start | bytes 30728 | tf_op jit(solution)/shard_map/ppermute | solution.py:260
  24.3 7.5 %collective-permute-start.13 = (bf16[8,640]{1,0:T(8,128)(2,1)S(1)}, bf16[8,640]{1,0:T(8,128)(2,1)S(1)}, u32[]{:S(2)}, u32[]{:S(2)}) collective-permute-start(bf16[8,640]{1,0:T(8,128)(2,1)S(1)} %get-tuple-element.118), channel_id=1, source_target_pairs={{0,14},{1,15},{2,12},{3,13},{4,10},{5,11},{6,8},{7,9},{8,6},{9,7},... | collective-permute-start | bytes 30728 | tf_op jit(solution)/shard_map/ppermute | solution.py:260
  26.6 5.8 %collective-permute-start.14 = (bf16[8,640]{1,0:T(8,128)(2,1)S(1)}, bf16[8,640]{1,0:T(8,128)(2,1)S(1)}, u32[]{:S(2)}, u32[]{:S(2)}) collective-permute-start(bf16[8,640]{1,0:T(8,128)(2,1)S(1)} %get-tuple-element.119), channel_id=1, source_target_pairs={{0,15},{1,14},{2,13},{3,12},{4,11},{5,10},{6,9},{7,8},{8,7},{9,6},... | collective-permute-start | bytes 30728 | tf_op jit(solution)/shard_map/ppermute | solution.py:260
  28.8 5.9 %collective-permute-start.2 = (bf16[8,640]{1,0:T(8,128)(2,1)S(1)}, bf16[8,640]{1,0:T(8,128)(2,1)S(1)}, u32[]{:S(2)}, u32[]{:S(2)}) collective-permute-start(bf16[8,640]{1,0:T(8,128)(2,1)S(1)} %get-tuple-element.107), channel_id=1, source_target_pairs={{0,3},{1,2},{2,1},{3,0},{4,7},{5,6},{6,5},{7,4},{8,11},{9,10},{10,... | collective-permute-start | bytes 30728 | tf_op jit(solution)/shard_map/ppermute | solution.py:260
  30.3 4.9 %collective-permute-start.3 = (bf16[8,640]{1,0:T(8,128)(2,1)S(1)}, bf16[8,640]{1,0:T(8,128)(2,1)S(1)}, u32[]{:S(2)}, u32[]{:S(2)}) collective-permute-start(bf16[8,640]{1,0:T(8,128)(2,1)S(1)} %get-tuple-element.108), channel_id=1, source_target_pairs={{0,4},{1,5},{2,6},{3,7},{4,0},{5,1},{6,2},{7,3},{8,12},{9,13},{10,... | collective-permute-start | bytes 30728 | tf_op jit(solution)/shard_map/ppermute | solution.py:260
  30.3 6.8 %collective-permute-start.4 = (bf16[8,640]{1,0:T(8,128)(2,1)S(1)}, bf16[8,640]{1,0:T(8,128)(2,1)S(1)}, u32[]{:S(2)}, u32[]{:S(2)}) collective-permute-start(bf16[8,640]{1,0:T(8,128)(2,1)S(1)} %get-tuple-element.109), channel_id=1, source_target_pairs={{0,5},{1,4},{2,7},{3,6},{4,1},{5,0},{6,3},{7,2},{8,13},{9,12},{10,... | collective-permute-start | bytes 30728 | tf_op jit(solution)/shard_map/ppermute | solution.py:260
  31.8 6.9 %collective-permute-start.5 = (bf16[8,640]{1,0:T(8,128)(2,1)S(1)}, bf16[8,640]{1,0:T(8,128)(2,1)S(1)}, u32[]{:S(2)}, u32[]{:S(2)}) collective-permute-start(bf16[8,640]{1,0:T(8,128)(2,1)S(1)} %get-tuple-element.110), channel_id=1, source_target_pairs={{0,6},{1,7},{2,4},{3,5},{4,2},{5,3},{6,0},{7,1},{8,14},{9,15},{10,... | collective-permute-start | bytes 30728 | tf_op jit(solution)/shard_map/ppermute | solution.py:260
  32.4 6.3 %collective-permute-start.6 = (bf16[8,640]{1,0:T(8,128)(2,1)S(1)}, bf16[8,640]{1,0:T(8,128)(2,1)S(1)}, u32[]{:S(2)}, u32[]{:S(2)}) collective-permute-start(bf16[8,640]{1,0:T(8,128)(2,1)S(1)} %get-tuple-element.111), channel_id=1, source_target_pairs={{0,7},{1,6},{2,5},{3,4},{4,3},{5,2},{6,1},{7,0},{8,15},{9,14},{10,... | collective-permute-start | bytes 30728 | tf_op jit(solution)/shard_map/ppermute | solution.py:260
  34.7 4.6 %collective-permute-start.7 = (bf16[8,640]{1,0:T(8,128)(2,1)S(1)}, bf16[8,640]{1,0:T(8,128)(2,1)S(1)}, u32[]{:S(2)}, u32[]{:S(2)}) collective-permute-start(bf16[8,640]{1,0:T(8,128)(2,1)S(1)} %get-tuple-element.112), channel_id=1, source_target_pairs={{0,8},{1,9},{2,10},{3,11},{4,12},{5,13},{6,14},{7,15},{8,0},{9,1},... | collective-permute-start | bytes 30728 | tf_op jit(solution)/shard_map/ppermute | solution.py:260
  35.2 4.1 %collective-permute-start.8 = (bf16[8,640]{1,0:T(8,128)(2,1)S(1)}, bf16[8,640]{1,0:T(8,128)(2,1)S(1)}, u32[]{:S(2)}, u32[]{:S(2)}) collective-permute-start(bf16[8,640]{1,0:T(8,128)(2,1)S(1)} %get-tuple-element.113), channel_id=1, source_target_pairs={{0,9},{1,8},{2,11},{3,10},{4,13},{5,12},{6,15},{7,14},{8,1},{9,0},... | collective-permute-start | bytes 30728 | tf_op jit(solution)/shard_map/ppermute | solution.py:260
  37.1 5.5 %collective-permute-start.9 = (bf16[8,640]{1,0:T(8,128)(2,1)S(1)}, bf16[8,640]{1,0:T(8,128)(2,1)S(1)}, u32[]{:S(2)}, u32[]{:S(2)}) collective-permute-start(bf16[8,640]{1,0:T(8,128)(2,1)S(1)} %get-tuple-element.114), channel_id=1, source_target_pairs={{0,10},{1,11},{2,8},{3,9},{4,14},{5,15},{6,12},{7,13},{8,2},{9,3},... | collective-permute-start | bytes 30728 | tf_op jit(solution)/shard_map/ppermute | solution.py:260
  52.1 3.6 %collective-permute-start.15 = (bf16[8,512]{1,0:T(8,128)(2,1)S(1)}, bf16[8,512]{1,0:T(8,128)(2,1)S(1)}, u32[]{:S(2)}, u32[]{:S(2)}) collective-permute-start(bf16[8,512]{1,0:T(8,128)(2,1)S(1)} %get-tuple-element.121), channel_id=1, source_target_pairs={{0,1},{1,0},{2,3},{3,2},{4,5},{5,4},{6,7},{7,6},{8,9},{9,8},{10,11... | collective-permute-start | bytes 24584 | tf_op jit(solution)/shard_map/ppermute | solution.py:260
  52.2 4.2 %collective-permute-start.16 = (bf16[8,512]{1,0:T(8,128)(2,1)S(1)}, bf16[8,512]{1,0:T(8,128)(2,1)S(1)}, u32[]{:S(2)}, u32[]{:S(2)}) collective-permute-start(bf16[8,512]{1,0:T(8,128)(2,1)S(1)} %get-tuple-element.122), channel_id=1, source_target_pairs={{0,2},{1,3},{2,0},{3,1},{4,6},{5,7},{6,4},{7,5},{8,10},{9,11},{10,... | collective-permute-start | bytes 24584 | tf_op jit(solution)/shard_map/ppermute | solution.py:260
  52.9 5.6 %collective-permute-start.17 = (bf16[8,512]{1,0:T(8,128)(2,1)S(1)}, bf16[8,512]{1,0:T(8,128)(2,1)S(1)}, u32[]{:S(2)}, u32[]{:S(2)}) collective-permute-start(bf16[8,512]{1,0:T(8,128)(2,1)S(1)} %get-tuple-element.123), channel_id=1, source_target_pairs={{0,3},{1,2},{2,1},{3,0},{4,7},{5,6},{6,5},{7,4},{8,11},{9,10},{10,... | collective-permute-start | bytes 24584 | tf_op jit(solution)/shard_map/ppermute | solution.py:260
  54.1 5.1 %collective-permute-start.18 = (bf16[8,512]{1,0:T(8,128)(2,1)S(1)}, bf16[8,512]{1,0:T(8,128)(2,1)S(1)}, u32[]{:S(2)}, u32[]{:S(2)}) collective-permute-start(bf16[8,512]{1,0:T(8,128)(2,1)S(1)} %get-tuple-element.124), channel_id=1, source_target_pairs={{0,4},{1,5},{2,6},{3,7},{4,0},{5,1},{6,2},{7,3},{8,12},{9,13},{10,... | collective-permute-start | bytes 24584 | tf_op jit(solution)/shard_map/ppermute | solution.py:260
  54.7 6.3 %collective-permute-start.19 = (bf16[8,512]{1,0:T(8,128)(2,1)S(1)}, bf16[8,512]{1,0:T(8,128)(2,1)S(1)}, u32[]{:S(2)}, u32[]{:S(2)}) collective-permute-start(bf16[8,512]{1,0:T(8,128)(2,1)S(1)} %get-tuple-element.125), channel_id=1, source_target_pairs={{0,5},{1,4},{2,7},{3,6},{4,1},{5,0},{6,3},{7,2},{8,13},{9,12},{10,... | collective-permute-start | bytes 24584 | tf_op jit(solution)/shard_map/ppermute | solution.py:260
  55.8 6.9 %collective-permute-start.20 = (bf16[8,512]{1,0:T(8,128)(2,1)S(1)}, bf16[8,512]{1,0:T(8,128)(2,1)S(1)}, u32[]{:S(2)}, u32[]{:S(2)}) collective-permute-start(bf16[8,512]{1,0:T(8,128)(2,1)S(1)} %get-tuple-element.126), channel_id=1, source_target_pairs={{0,6},{1,7},{2,4},{3,5},{4,2},{5,3},{6,0},{7,1},{8,14},{9,15},{10,... | collective-permute-start | bytes 24584 | tf_op jit(solution)/shard_map/ppermute | solution.py:260
  56.4 8.3 %collective-permute-start.21 = (bf16[8,512]{1,0:T(8,128)(2,1)S(1)}, bf16[8,512]{1,0:T(8,128)(2,1)S(1)}, u32[]{:S(2)}, u32[]{:S(2)}) collective-permute-start(bf16[8,512]{1,0:T(8,128)(2,1)S(1)} %get-tuple-element.127), channel_id=1, source_target_pairs={{0,7},{1,6},{2,5},{3,4},{4,3},{5,2},{6,1},{7,0},{8,15},{9,14},{10,... | collective-permute-start | bytes 24584 | tf_op jit(solution)/shard_map/ppermute | solution.py:260
  58.5 7.5 %collective-permute-start.22 = (bf16[8,512]{1,0:T(8,128)(2,1)S(1)}, bf16[8,512]{1,0:T(8,128)(2,1)S(1)}, u32[]{:S(2)}, u32[]{:S(2)}) collective-permute-start(bf16[8,512]{1,0:T(8,128)(2,1)S(1)} %get-tuple-element.128), channel_id=1, source_target_pairs={{0,8},{1,9},{2,10},{3,11},{4,12},{5,13},{6,14},{7,15},{8,0},{9,1},... | collective-permute-start | bytes 24584 | tf_op jit(solution)/shard_map/ppermute | solution.py:260
  59.2 9.0 %collective-permute-start.23 = (bf16[8,512]{1,0:T(8,128)(2,1)S(1)}, bf16[8,512]{1,0:T(8,128)(2,1)S(1)}, u32[]{:S(2)}, u32[]{:S(2)}) collective-permute-start(bf16[8,512]{1,0:T(8,128)(2,1)S(1)} %get-tuple-element.129), channel_id=1, source_target_pairs={{0,9},{1,8},{2,11},{3,10},{4,13},{5,12},{6,15},{7,14},{8,1},{9,0},... | collective-permute-start | bytes 24584 | tf_op jit(solution)/shard_map/ppermute | solution.py:260
  61.1 8.5 %collective-permute-start.24 = (bf16[8,512]{1,0:T(8,128)(2,1)S(1)}, bf16[8,512]{1,0:T(8,128)(2,1)S(1)}, u32[]{:S(2)}, u32[]{:S(2)}) collective-permute-start(bf16[8,512]{1,0:T(8,128)(2,1)S(1)} %get-tuple-element.130), channel_id=1, source_target_pairs={{0,10},{1,11},{2,8},{3,9},{4,14},{5,15},{6,12},{7,13},{8,2},{9,3},... | collective-permute-start | bytes 24584 | tf_op jit(solution)/shard_map/ppermute | solution.py:260
  62.7 10.0 %collective-permute-start.25 = (bf16[8,512]{1,0:T(8,128)(2,1)S(1)}, bf16[8,512]{1,0:T(8,128)(2,1)S(1)}, u32[]{:S(2)}, u32[]{:S(2)}) collective-permute-start(bf16[8,512]{1,0:T(8,128)(2,1)S(1)} %get-tuple-element.131), channel_id=1, source_target_pairs={{0,11},{1,10},{2,9},{3,8},{4,15},{5,14},{6,13},{7,12},{8,3},{9,2},... | collective-permute-start | bytes 24584 | tf_op jit(solution)/shard_map/ppermute | solution.py:260
  64.7 8.0 %collective-permute-start.26 = (bf16[8,512]{1,0:T(8,128)(2,1)S(1)}, bf16[8,512]{1,0:T(8,128)(2,1)S(1)}, u32[]{:S(2)}, u32[]{:S(2)}) collective-permute-start(bf16[8,512]{1,0:T(8,128)(2,1)S(1)} %get-tuple-element.132), channel_id=1, source_target_pairs={{0,12},{1,13},{2,14},{3,15},{4,8},{5,9},{6,10},{7,11},{8,4},{9,5},... | collective-permute-start | bytes 24584 | tf_op jit(solution)/shard_map/ppermute | solution.py:260
  66.0 6.7 %collective-permute-start.27 = (bf16[8,512]{1,0:T(8,128)(2,1)S(1)}, bf16[8,512]{1,0:T(8,128)(2,1)S(1)}, u32[]{:S(2)}, u32[]{:S(2)}) collective-permute-start(bf16[8,512]{1,0:T(8,128)(2,1)S(1)} %get-tuple-element.133), channel_id=1, source_target_pairs={{0,13},{1,12},{2,15},{3,14},{4,9},{5,8},{6,11},{7,10},{8,5},{9,4},... | collective-permute-start | bytes 24584 | tf_op jit(solution)/shard_map/ppermute | solution.py:260
  68.2 6.3 %collective-permute-start.28 = (bf16[8,512]{1,0:T(8,128)(2,1)S(1)}, bf16[8,512]{1,0:T(8,128)(2,1)S(1)}, u32[]{:S(2)}, u32[]{:S(2)}) collective-permute-start(bf16[8,512]{1,0:T(8,128)(2,1)S(1)} %get-tuple-element.134), channel_id=1, source_target_pairs={{0,14},{1,15},{2,12},{3,13},{4,10},{5,11},{6,8},{7,9},{8,6},{9,7},... | collective-permute-start | bytes 24584 | tf_op jit(solution)/shard_map/ppermute | solution.py:260
  69.6 5.8 %collective-permute-start.29 = (bf16[8,512]{1,0:T(8,128)(2,1)S(1)}, bf16[8,512]{1,0:T(8,128)(2,1)S(1)}, u32[]{:S(2)}, u32[]{:S(2)}) collective-permute-start(bf16[8,512]{1,0:T(8,128)(2,1)S(1)} %get-tuple-element.135), channel_id=1, source_target_pairs={{0,15},{1,14},{2,13},{3,12},{4,11},{5,10},{6,9},{7,8},{8,7},{9,6},... | collective-permute-start | bytes 24584 | tf_op jit(solution)/shard_map/ppermute | solution.py:260
  79.2 4.5 %collective-permute-start.30 = (bf16[8,32,1024]{2,1,0:T(8,128)(2,1)S(1)}, bf16[8,32,1024]{2,1,0:T(8,128)(2,1)S(1)}, u32[]{:S(2)}, u32[]{:S(2)}) collective-permute-start(bf16[8,32,1024]{2,1,0:T(8,128)(2,1)S(1)} %get-tuple-element.137), channel_id=1, source_target_pairs={{0,1},{1,0},{2,3},{3,2},{4,5},{5,4},{6,7},{7,6},{8,9},{9,8},{10,11... | collective-permute-start | bytes 1572872 | tf_op jit(solution)/shard_map/ppermute | solution.py:385
  79.4 6.1 %collective-permute-start.32 = (bf16[8,32,1024]{2,1,0:T(8,128)(2,1)S(1)}, bf16[8,32,1024]{2,1,0:T(8,128)(2,1)S(1)}, u32[]{:S(2)}, u32[]{:S(2)}) collective-permute-start(bf16[8,32,1024]{2,1,0:T(8,128)(2,1)S(1)} %get-tuple-element.139), channel_id=1, source_target_pairs={{0,1},{1,0},{2,3},{3,2},{4,5},{5,4},{6,7},{7,6},{8,9},{9,8},{10,11... | collective-permute-start | bytes 1572872 | tf_op jit(solution)/shard_map/ppermute | solution.py:385
  79.8 12.9 %collective-permute-start.35 = (bf16[8,32,1024]{2,1,0:T(8,128)(2,1)S(1)}, bf16[8,32,1024]{2,1,0:T(8,128)(2,1)S(1)}, u32[]{:S(2)}, u32[]{:S(2)}) collective-permute-start(bf16[8,32,1024]{2,1,0:T(8,128)(2,1)S(1)} %get-tuple-element.147), channel_id=1, source_target_pairs={{0,1},{1,0},{2,3},{3,2},{4,5},{5,4},{6,7},{7,6},{8,9},{9,8},{10,11... | collective-permute-start | bytes 1572872 | tf_op jit(solution)/shard_map/ppermute | solution.py:385
  83.9 8.7 %collective-permute-start.31 = (bf16[4,32,1024]{2,1,0:T(8,128)(2,1)S(1)}, bf16[4,32,1024]{2,1,0:T(8,128)(2,1)S(1)}, u32[]{:S(2)}, u32[]{:S(2)}) collective-permute-start(bf16[4,32,1024]{2,1,0:T(8,128)(2,1)S(1)} %get-tuple-element.211), channel_id=1, source_target_pairs={{0,2},{1,3},{2,0},{3,1},{4,6},{5,7},{6,4},{7,5},{8,10},{9,11},{10,... | collective-permute-start | bytes 786440 | tf_op jit(solution)/shard_map/ppermute | solution.py:385
  85.5 15.4 %collective-permute-start.34 = (bf16[8,32,1024]{2,1,0:T(8,128)(2,1)S(1)}, bf16[8,32,1024]{2,1,0:T(8,128)(2,1)S(1)}, u32[]{:S(2)}, u32[]{:S(2)}) collective-permute-start(bf16[8,32,1024]{2,1,0:T(8,128)(2,1)S(1)} %get-tuple-element.145), channel_id=1, source_target_pairs={{0,1},{1,0},{2,3},{3,2},{4,5},{5,4},{6,7},{7,6},{8,9},{9,8},{10,11... | collective-permute-start | bytes 1572872 | tf_op jit(solution)/shard_map/ppermute | solution.py:385
  85.7 8.7 %collective-permute-start.37 = (bf16[4,32,1024]{2,1,0:T(8,128)(2,1)S(1)}, bf16[4,32,1024]{2,1,0:T(8,128)(2,1)S(1)}, u32[]{:S(2)}, u32[]{:S(2)}) collective-permute-start(bf16[4,32,1024]{2,1,0:T(8,128)(2,1)S(1)} %get-tuple-element.212), channel_id=1, source_target_pairs={{0,4},{1,5},{2,6},{3,7},{4,0},{5,1},{6,2},{7,3},{8,12},{9,13},{10,... | collective-permute-start | bytes 786440 | tf_op jit(solution)/shard_map/ppermute | solution.py:385
  92.9 7.9 %collective-permute-start.36 = (bf16[4,32,1024]{2,1,0:T(8,128)(2,1)S(1)}, bf16[4,32,1024]{2,1,0:T(8,128)(2,1)S(1)}, u32[]{:S(2)}, u32[]{:S(2)}) collective-permute-start(bf16[4,32,1024]{2,1,0:T(8,128)(2,1)S(1)} %get-tuple-element.209), channel_id=1, source_target_pairs={{0,2},{1,3},{2,0},{3,1},{4,6},{5,7},{6,4},{7,5},{8,10},{9,11},{10,... | collective-permute-start | bytes 786440 | tf_op jit(solution)/shard_map/ppermute | solution.py:385
  94.3 6.8 %collective-permute-start.33 = (bf16[2,32,1024]{2,1,0:T(8,128)(2,1)S(1)}, bf16[2,32,1024]{2,1,0:T(8,128)(2,1)S(1)}, u32[]{:S(2)}, u32[]{:S(2)}) collective-permute-start(bf16[2,32,1024]{2,1,0:T(8,128)(2,1)S(1)} %get-tuple-element.219), channel_id=1, source_target_pairs={{0,4},{1,5},{2,6},{3,7},{4,0},{5,1},{6,2},{7,3},{8,12},{9,13},{10,... | collective-permute-start | bytes 393224 | tf_op jit(solution)/shard_map/ppermute | solution.py:385
  101.2 44.3 %copy-start.2 = (bf16[16384]{0:T(1024)(128)(2,1)S(1)}, bf16[16384]{0:T(1024)(128)(2,1)}, u32[]{:S(2)}) copy-start(bf16[16384]{0:T(1024)(128)(2,1)} %param.17) | copy-start | bytes 98308
  101.2 9.8 %collective-permute-start.38 = (bf16[1,32,1024]{2,1,0:T(8,128)(2,1)S(1)}, bf16[1,32,1024]{2,1,0:T(8,128)(2,1)S(1)}, u32[]{:S(2)}, u32[]{:S(2)}) collective-permute-start(bf16[1,32,1024]{2,1,0:T(8,128)(2,1)S(1)} %get-tuple-element.228), channel_id=1, source_target_pairs={{0,8},{1,9},{2,10},{3,11},{4,12},{5,13},{6,14},{7,15},{8,0},{9,1},... | collective-permute-start | bytes 196616 | tf_op jit(solution)/shard_map/ppermute | solution.py:385
  101.2 11.7 %collective-permute-start.41 = (bf16[2,32,1024]{2,1,0:T(8,128)(2,1)S(1)}, bf16[2,32,1024]{2,1,0:T(8,128)(2,1)S(1)}, u32[]{:S(2)}, u32[]{:S(2)}) collective-permute-start(bf16[2,32,1024]{2,1,0:T(8,128)(2,1)S(1)} %get-tuple-element.220), channel_id=1, source_target_pairs={{0,8},{1,9},{2,10},{3,11},{4,12},{5,13},{6,14},{7,15},{8,0},{9,1},... | collective-permute-start | bytes 393224 | tf_op jit(solution)/shard_map/ppermute | solution.py:385
  104.2 10.4 %collective-permute-start.40 = (bf16[4,32,1024]{2,1,0:T(8,128)(2,1)S(1)}, bf16[4,32,1024]{2,1,0:T(8,128)(2,1)S(1)}, u32[]{:S(2)}, u32[]{:S(2)}) collective-permute-start(bf16[4,32,1024]{2,1,0:T(8,128)(2,1)S(1)} %get-tuple-element.207), channel_id=1, source_target_pairs={{0,2},{1,3},{2,0},{3,1},{4,6},{5,7},{6,4},{7,5},{8,10},{9,11},{10,... | collective-permute-start | bytes 786440 | tf_op jit(solution)/shard_map/ppermute | solution.py:385
  105.4 10.0 %collective-permute-start.39 = (bf16[2,32,1024]{2,1,0:T(8,128)(2,1)S(1)}, bf16[2,32,1024]{2,1,0:T(8,128)(2,1)S(1)}, u32[]{:S(2)}, u32[]{:S(2)}) collective-permute-start(bf16[2,32,1024]{2,1,0:T(8,128)(2,1)S(1)} %get-tuple-element.217), channel_id=1, source_target_pairs={{0,4},{1,5},{2,6},{3,7},{4,0},{5,1},{6,2},{7,3},{8,12},{9,13},{10,... | collective-permute-start | bytes 393224 | tf_op jit(solution)/shard_map/ppermute | solution.py:385
  111.8 8.3 %collective-permute-start.43 = (bf16[1,32,1024]{2,1,0:T(8,128)(2,1)S(1)}, bf16[1,32,1024]{2,1,0:T(8,128)(2,1)S(1)}, u32[]{:S(2)}, u32[]{:S(2)}) collective-permute-start(bf16[1,32,1024]{2,1,0:T(8,128)(2,1)S(1)} %bitcast.22), channel_id=1, source_target_pairs={{0,8},{1,9},{2,10},{3,11},{4,12},{5,13},{6,14},{7,15},{8,0},{9,1},... | collective-permute-start | bytes 196616 | tf_op jit(solution)/shard_map/ppermute | solution.py:385
  113.0 4.3 %collective-permute-start.44 = (bf16[1,32,1024]{2,1,0:T(8,128)(2,1)S(1)}, bf16[1,32,1024]{2,1,0:T(8,128)(2,1)S(1)}, u32[]{:S(2)}, u32[]{:S(2)}) collective-permute-start(bf16[1,32,1024]{2,1,0:T(8,128)(2,1)S(1)} %get-tuple-element.226), channel_id=1, source_target_pairs={{0,2},{1,3},{2,0},{3,1},{4,6},{5,7},{6,4},{7,5},{8,10},{9,11},{10,... | collective-permute-start | bytes 196616 | tf_op jit(solution)/shard_map/ppermute | solution.py:385
  114.6 9.9 %collective-permute-start.45 = (bf16[2,32,1024]{2,1,0:T(8,128)(2,1)S(1)}, bf16[2,32,1024]{2,1,0:T(8,128)(2,1)S(1)}, u32[]{:S(2)}, u32[]{:S(2)}) collective-permute-start(bf16[2,32,1024]{2,1,0:T(8,128)(2,1)S(1)} %get-tuple-element.215), channel_id=1, source_target_pairs={{0,4},{1,5},{2,6},{3,7},{4,0},{5,1},{6,2},{7,3},{8,12},{9,13},{10,... | collective-permute-start | bytes 393224 | tf_op jit(solution)/shard_map/ppermute | solution.py:385
  115.4 5.8 %collective-permute-start.42 = (bf16[1,32,1024]{2,1,0:T(8,128)(2,1)S(1)}, bf16[1,32,1024]{2,1,0:T(8,128)(2,1)S(1)}, u32[]{:S(2)}, u32[]{:S(2)}) collective-permute-start(bf16[1,32,1024]{2,1,0:T(8,128)(2,1)S(1)} %get-tuple-element.225), channel_id=1, source_target_pairs={{0,8},{1,9},{2,10},{3,11},{4,12},{5,13},{6,14},{7,15},{8,0},{9,1},... | collective-permute-start | bytes 196616 | tf_op jit(solution)/shard_map/ppermute | solution.py:385
  118.2 10.8 %collective-permute-start.48 = (bf16[1,32,1024]{2,1,0:T(8,128)(2,1)S(1)}, bf16[1,32,1024]{2,1,0:T(8,128)(2,1)S(1)}, u32[]{:S(2)}, u32[]{:S(2)}) collective-permute-start(bf16[1,32,1024]{2,1,0:T(8,128)(2,1)S(1)} %bitcast.24), channel_id=1, source_target_pairs={{0,8},{1,9},{2,10},{3,11},{4,12},{5,13},{6,14},{7,15},{8,0},{9,1},... | collective-permute-start | bytes 196616 | tf_op jit(solution)/shard_map/ppermute | solution.py:385
  120.1 11.1 %collective-permute-start.47 = (bf16[2,32,1024]{2,1,0:T(8,128)(2,1)S(1)}, bf16[2,32,1024]{2,1,0:T(8,128)(2,1)S(1)}, u32[]{:S(2)}, u32[]{:S(2)}) collective-permute-start(bf16[2,32,1024]{2,1,0:T(8,128)(2,1)S(1)} %constant_dynamic-update-slice_fusion), channel_id=1, source_target_pairs={{0,4},{1,5},{2,6},{3,7},{4,0},{5,1},{6,2},{7,3},{8,12},{9,13},{10,... | collective-permute-start | bytes 393224 | tf_op jit(solution)/shard_map/ppermute | solution.py:385
  122.1 5.3 %collective-permute-start.49 = (bf16[1,32,1024]{2,1,0:T(8,128)(2,1)S(1)}, bf16[1,32,1024]{2,1,0:T(8,128)(2,1)S(1)}, u32[]{:S(2)}, u32[]{:S(2)}) collective-permute-start(bf16[1,32,1024]{2,1,0:T(8,128)(2,1)S(1)} %bitcast.26), channel_id=1, source_target_pairs={{0,8},{1,9},{2,10},{3,11},{4,12},{5,13},{6,14},{7,15},{8,0},{9,1},... | collective-permute-start | bytes 196616 | tf_op jit(solution)/shard_map/ppermute | solution.py:385
  124.5 7.6 %collective-permute-start.46 = (bf16[1,32,1024]{2,1,0:T(8,128)(2,1)S(1)}, bf16[1,32,1024]{2,1,0:T(8,128)(2,1)S(1)}, u32[]{:S(2)}, u32[]{:S(2)}) collective-permute-start(bf16[1,32,1024]{2,1,0:T(8,128)(2,1)S(1)} %get-tuple-element.222), channel_id=1, source_target_pairs={{0,8},{1,9},{2,10},{3,11},{4,12},{5,13},{6,14},{7,15},{8,0},{9,1},... | collective-permute-start | bytes 196616 | tf_op jit(solution)/shard_map/ppermute | solution.py:385
  127.4 6.4 %collective-permute-start.51 = (bf16[2,32,1024]{2,1,0:T(8,128)(2,1)S(1)}, bf16[2,32,1024]{2,1,0:T(8,128)(2,1)S(1)}, u32[]{:S(2)}, u32[]{:S(2)}) collective-permute-start(bf16[2,32,1024]{2,1,0:T(8,128)(2,1)S(1)} %constant_dynamic-update-slice_fusion.2), channel_id=1, source_target_pairs={{0,2},{1,3},{2,0},{3,1},{4,6},{5,7},{6,4},{7,5},{8,10},{9,11},{10,... | collective-permute-start | bytes 393224 | tf_op jit(solution)/shard_map/ppermute | solution.py:385
  128.9 11.3 %collective-permute-start.53 = (bf16[2,32,1024]{2,1,0:T(8,128)(2,1)S(1)}, bf16[2,32,1024]{2,1,0:T(8,128)(2,1)S(1)}, u32[]{:S(2)}, u32[]{:S(2)}) collective-permute-start(bf16[2,32,1024]{2,1,0:T(8,128)(2,1)S(1)} %constant_dynamic-update-slice_fusion.4), channel_id=1, source_target_pairs={{0,4},{1,5},{2,6},{3,7},{4,0},{5,1},{6,2},{7,3},{8,12},{9,13},{10,... | collective-permute-start | bytes 393224 | tf_op jit(solution)/shard_map/ppermute | solution.py:385
  131.3 8.8 %collective-permute-start.54 = (bf16[4,32,1024]{2,1,0:T(8,128)(2,1)S(1)}, bf16[4,32,1024]{2,1,0:T(8,128)(2,1)S(1)}, u32[]{:S(2)}, u32[]{:S(2)}) collective-permute-start(bf16[4,32,1024]{2,1,0:T(8,128)(2,1)S(1)} %constant_dynamic-update-slice_fusion.6), channel_id=1, source_target_pairs={{0,2},{1,3},{2,0},{3,1},{4,6},{5,7},{6,4},{7,5},{8,10},{9,11},{10,... | collective-permute-start | bytes 786440 | tf_op jit(solution)/shard_map/ppermute | solution.py:385
  133.0 5.8 %collective-permute-start.50 = (bf16[1,32,1024]{2,1,0:T(8,128)(2,1)S(1)}, bf16[1,32,1024]{2,1,0:T(8,128)(2,1)S(1)}, u32[]{:S(2)}, u32[]{:S(2)}) collective-permute-start(bf16[1,32,1024]{2,1,0:T(8,128)(2,1)S(1)} %bitcast.28), channel_id=1, source_target_pairs={{0,8},{1,9},{2,10},{3,11},{4,12},{5,13},{6,14},{7,15},{8,0},{9,1},... | collective-permute-start | bytes 196616 | tf_op jit(solution)/shard_map/ppermute | solution.py:385
  133.9 10.0 %collective-permute-start.57 = (bf16[4,32,1024]{2,1,0:T(8,128)(2,1)S(1)}, bf16[4,32,1024]{2,1,0:T(8,128)(2,1)S(1)}, u32[]{:S(2)}, u32[]{:S(2)}) collective-permute-start(bf16[4,32,1024]{2,1,0:T(8,128)(2,1)S(1)} %constant_dynamic-update-slice_fusion.8), channel_id=1, source_target_pairs={{0,4},{1,5},{2,6},{3,7},{4,0},{5,1},{6,2},{7,3},{8,12},{9,13},{10,... | collective-permute-start | bytes 786440 | tf_op jit(solution)/shard_map/ppermute | solution.py:385
  138.8 5.0 %collective-permute-start.52 = (bf16[2,32,1024]{2,1,0:T(8,128)(2,1)S(1)}, bf16[2,32,1024]{2,1,0:T(8,128)(2,1)S(1)}, u32[]{:S(2)}, u32[]{:S(2)}) collective-permute-start(bf16[2,32,1024]{2,1,0:T(8,128)(2,1)S(1)} %constant_dynamic-update-slice_fusion.10), channel_id=1, source_target_pairs={{0,2},{1,3},{2,0},{3,1},{4,6},{5,7},{6,4},{7,5},{8,10},{9,11},{10,... | collective-permute-start | bytes 393224 | tf_op jit(solution)/shard_map/ppermute | solution.py:385
  140.1 5.3 %collective-permute-start.59 = (bf16[8,32,1024]{2,1,0:T(8,128)(2,1)S(1)}, bf16[8,32,1024]{2,1,0:T(8,128)(2,1)S(1)}, u32[]{:S(2)}, u32[]{:S(2)}) collective-permute-start(bf16[8,32,1024]{2,1,0:T(8,128)(2,1)S(1)} %constant_dynamic-update-slice_fusion.12.own_ref), channel_id=1, source_target_pairs={{0,1},{1,0},{2,3},{3,2},{4,5},{5,4},{6,7},{7,6},{8,9},{9,8},{10,11... | collective-permute-start | bytes 1572872 | tf_op jit(solution)/shard_map/ppermute | solution.py:385
  143.9 3.2 %collective-permute-start.58 = (bf16[8,32,1024]{2,1,0:T(8,128)(2,1)S(1)}, bf16[8,32,1024]{2,1,0:T(8,128)(2,1)S(1)}, u32[]{:S(2)}, u32[]{:S(2)}) collective-permute-start(bf16[8,32,1024]{2,1,0:T(8,128)(2,1)S(1)} %constant_dynamic-update-slice_fusion.18.own_ref), channel_id=1, source_target_pairs={{0,1},{1,0},{2,3},{3,2},{4,5},{5,4},{6,7},{7,6},{8,9},{9,8},{10,11... | collective-permute-start | bytes 1572872 | tf_op jit(solution)/shard_map/ppermute | solution.py:385
  144.0 8.7 %collective-permute-start.56 = (bf16[4,32,1024]{2,1,0:T(8,128)(2,1)S(1)}, bf16[4,32,1024]{2,1,0:T(8,128)(2,1)S(1)}, u32[]{:S(2)}, u32[]{:S(2)}) collective-permute-start(bf16[4,32,1024]{2,1,0:T(8,128)(2,1)S(1)} %constant_dynamic-update-slice_fusion.14), channel_id=1, source_target_pairs={{0,2},{1,3},{2,0},{3,1},{4,6},{5,7},{6,4},{7,5},{8,10},{9,11},{10,... | collective-permute-start | bytes 786440 | tf_op jit(solution)/shard_map/ppermute | solution.py:385
  145.3 8.4 %collective-permute-start.55 = (bf16[4,32,1024]{2,1,0:T(8,128)(2,1)S(1)}, bf16[4,32,1024]{2,1,0:T(8,128)(2,1)S(1)}, u32[]{:S(2)}, u32[]{:S(2)}) collective-permute-start(bf16[4,32,1024]{2,1,0:T(8,128)(2,1)S(1)} %constant_dynamic-update-slice_fusion.16), channel_id=1, source_target_pairs={{0,4},{1,5},{2,6},{3,7},{4,0},{5,1},{6,2},{7,3},{8,12},{9,13},{10,... | collective-permute-start | bytes 786440 | tf_op jit(solution)/shard_map/ppermute | solution.py:385
  152.8 2.0 %collective-permute-start.61 = (bf16[8,32,1024]{2,1,0:T(8,128)(2,1)S(1)}, bf16[8,32,1024]{2,1,0:T(8,128)(2,1)S(1)}, u32[]{:S(2)}, u32[]{:S(2)}) collective-permute-start(bf16[8,32,1024]{2,1,0:T(8,128)(2,1)S(1)} %constant_dynamic-update-slice_fusion.20.own_ref), channel_id=1, source_target_pairs={{0,1},{1,0},{2,3},{3,2},{4,5},{5,4},{6,7},{7,6},{8,9},{9,8},{10,11... | collective-permute-start | bytes 1572872 | tf_op jit(solution)/shard_map/ppermute | solution.py:385
  153.7 2.7 %collective-permute-start.60 = (bf16[8,32,1024]{2,1,0:T(8,128)(2,1)S(1)}, bf16[8,32,1024]{2,1,0:T(8,128)(2,1)S(1)}, u32[]{:S(2)}, u32[]{:S(2)}) collective-permute-start(bf16[8,32,1024]{2,1,0:T(8,128)(2,1)S(1)} %constant_dynamic-update-slice_fusion.22.own_ref), channel_id=1, source_target_pairs={{0,1},{1,0},{2,3},{3,2},{4,5},{5,4},{6,7},{7,6},{8,9},{9,8},{10,11... | collective-permute-start | bytes 1572872 | tf_op jit(solution)/shard_map/ppermute | solution.py:385
  (1 other events, 1.6 us)

commit v4 on v3

v4 whole, which is shorter than its diff:
```python
import functools
import math

import jax
import jax.numpy as jnp
from jax import lax
from jax.experimental import pallas as pl
from jax.experimental.pallas import tpu as pltpu
from jax.sharding import PartitionSpec as P

HD = 128


TABLE = "20210320213032013021313012023131"

epsilon = 1e-05
rope_theta = 500000.0


def turns(positions):
    half = HD // 2
    entry = jnp.arange(HD, dtype=jnp.int32)
    frequency = jnp.exp((entry % half).astype(jnp.float32) * (-math.log(rope_theta) / half))
    angles = positions.astype(jnp.float32)[:, None] * frequency[None, :]
    sign = jnp.where(entry < half, -1.0, 1.0)
    return jnp.cos(angles), jnp.sin(angles) * sign


def rotate(head, cosine, sine):
    return head * cosine + pltpu.roll(head, HD // 2, 1) * sine


def input_kernel(count, hidden_ref, gain_ref, w_ref, kv_ref, cosine_ref, sine_ref, *refs):
    out_ref, hidden, w_buffer, kv_buffer, normed, products, kv_products, *sems = refs
    h_sem, w_sem, kv_sem = sems
    me = lax.axis_index("tensor")
    rows, columns = hidden.shape
    depth = normed.shape[2]
    chunks = columns // depth
    width = products.shape[1]
    kv_width = kv_products.shape[1]
    here = rows // count

    def span(k):
        return pl.ds(k * depth, depth)

    def hidden_copy(k):
        return pltpu.make_async_copy(
            hidden_ref.at[:, span(k)], hidden.at[:, span(k)], h_sem.at[k]
        )

    def w_copy(k):
        return pltpu.make_async_copy(w_ref.at[span(k), :], w_buffer.at[span(k), :], w_sem.at[k])

    for k in range(chunks):
        hidden_copy(k).start()
    early = chunks // 4
    for k in range(early):
        w_copy(k).start()
    kv_copy = pltpu.make_async_copy(kv_ref, kv_buffer, kv_sem)
    kv_copy.start()
    products[...] = jnp.zeros_like(products)
    kv_products[...] = jnp.zeros_like(kv_products)
    total = jnp.zeros((rows, 128), jnp.float32)
    for k in range(chunks):
        hidden_copy(k).wait()
        for lane in range(k * depth, (k + 1) * depth, 128):
            part = hidden[:, lane : lane + 128].astype(jnp.float32)
            total = total + part * part
    for k in range(early, chunks):
        w_copy(k).start()
    scale = lax.rsqrt(jnp.sum(total, axis=1, keepdims=True) / columns + epsilon)

    def norm(k):
        floats = hidden[:, span(k)].astype(jnp.float32)
        gain = gain_ref[:, span(k)].astype(jnp.float32)
        normed[k % 2] = (floats * scale * gain).astype(jnp.bfloat16)

    norm(0)
    kv_copy.wait()
    for k in range(chunks):
        w_copy(k).wait()
        products[...] += jnp.dot(
            normed[k % 2], w_buffer[span(k), :], preferred_element_type=jnp.float32
        )
        kv_products[...] += lax.dot_general(
            normed[k % 2],
            kv_buffer[:, span(k)],
            (((1,), (1,)), ((), ())),
            preferred_element_type=jnp.float32,
        )
        if k + 1 < chunks:
            norm(k + 1)

    shift = lax.rem(me, HD // kv_width) * kv_width
    blank = jnp.zeros((rows, HD - kv_width), jnp.float32)
    moved = pltpu.roll(jnp.concatenate([kv_products[...], blank], axis=1), shift, 1)
    results = [
        rotate(products[:, start : start + HD], cosine_ref[...], sine_ref[...])
        for start in range(0, width, HD)
    ] + [moved]
    for part, result in enumerate(results):
        for k in range(count):
            out_ref[k, :, part * HD : (part + 1) * HD] = result[
                k * here : (k + 1) * here
            ].astype(jnp.bfloat16)


def project_in(hidden_in, gain, w_query, w_keyval, cosine, sine, count):
    rows, columns = hidden_in.shape
    width, kv_width = w_query.shape[1], w_keyval.shape[1]
    depth = columns // 8
    chunks = columns // depth
    vmem = pl.BlockSpec(memory_space=pltpu.VMEM)
    whole = pl.BlockSpec(memory_space=pltpu.HBM)
    return pl.pallas_call(
        functools.partial(input_kernel, count),
        out_shape=jax.ShapeDtypeStruct((count, rows // count, width + HD), jnp.bfloat16),
        in_specs=[whole, vmem, whole, whole, vmem, vmem],
        out_specs=vmem,
        scratch_shapes=[
            pltpu.VMEM((rows, columns), jnp.bfloat16),
            pltpu.VMEM((columns, width), jnp.bfloat16),
            pltpu.VMEM((kv_width, columns), jnp.bfloat16),
            pltpu.VMEM((2, rows, depth), jnp.bfloat16),
            pltpu.VMEM((rows, width), jnp.float32),
            pltpu.VMEM((rows, kv_width), jnp.float32),
            pltpu.SemaphoreType.DMA((chunks,)),
            pltpu.SemaphoreType.DMA((chunks,)),
            pltpu.SemaphoreType.DMA,
        ],
        compiler_params=pltpu.CompilerParams(vmem_limit_bytes=40 * 1024 * 1024),
        cost_estimate=pl.CostEstimate(
            flops=2 * rows * columns * (width + kv_width),
            bytes_accessed=2 * columns * (rows + width + kv_width),
            transcendentals=0,
        ),
    )(hidden_in, gain, w_query, w_keyval.T, cosine, sine)


def attend_kernel(count, lengths_ref, cosine_ref, sine_ref, keys_ref, values_ref, *refs):
    in_ref, out_ref, queries, attended, scores, weights, keys, values, k_sem, v_sem = refs
    me = lax.axis_index("tensor")
    here, span, key_width = keys.shape
    kv_groups = key_width // HD
    parts = attended.shape[0]

    def key_copy(row):
        return pltpu.make_async_copy(keys_ref.at[row], keys.at[row], k_sem.at[row])

    def value_copy(row):
        return pltpu.make_async_copy(values_ref.at[row], values.at[row], v_sem.at[row])

    for row in range(here + 2):
        if row < here:
            key_copy(row).start()
        if row >= 2:
            value_copy(row - 2).start()

    for device in range(count):
        for part in range(parts + 1):
            queries[part, device * here : (device + 1) * here, :] = in_ref[
                device, :, part * HD : (part + 1) * HD
            ].astype(jnp.float32)
    mine = pl.ds(pl.multiple_of(me * here, here), here)
    cosine, sine = cosine_ref[mine, :], sine_ref[mine, :]
    shares = count // (2 * kv_groups)
    tiles = []
    for tile in range(2 * kv_groups):
        joined = jnp.zeros((here, HD), jnp.float32)
        for device in range(tile * shares, (tile + 1) * shares):
            joined = joined + queries[parts, device * here : (device + 1) * here, :]
        tiles.append(joined)
    new_keys = [rotate(tile, cosine, sine) for tile in tiles[:kv_groups]]
    new_keys = jnp.concatenate(new_keys, axis=1).astype(jnp.bfloat16).astype(jnp.float32)
    new_values = jnp.concatenate(tiles[kv_groups:], axis=1)

    shape = (parts * count, key_width)
    group_devices = count // kv_groups
    device = lax.rem(lax.broadcasted_iota(jnp.int32, shape, 0), count)
    column = lax.broadcasted_iota(jnp.int32, shape, 1)
    own_group = lax.div(device, group_devices) == lax.div(column, HD)
    token = lax.broadcasted_iota(jnp.int32, (1, span), 1)
    score_scale = HD ** (-0.5)
    own_scores, own_weights = {}, {}

    def score(row):
        heads = jnp.concatenate(
            [queries[part, pl.ds(row, count, stride=here), :] for part in range(parts)], axis=0
        )
        heads = jnp.where(own_group, jnp.concatenate([heads] * kv_groups, axis=1), 0.0)
        own_scores[row] = (
            jnp.sum(heads * new_keys[row : row + 1], axis=1, keepdims=True) * score_scale
        )
        scores[row % 2] = lax.dot_general(
            heads.astype(jnp.bfloat16),
            keys[row],
            (((1,), (1,)), ((), ())),
            preferred_element_type=jnp.float32,
        )

    def weigh(row):
        valid = token < lengths_ref[row]
        scaled = jnp.where(valid, scores[row % 2] * score_scale, -1e30)
        largest = jnp.maximum(jnp.max(scaled, axis=1, keepdims=True), own_scores[row])
        raised = jnp.exp(scaled - largest)
        own_raised = jnp.exp(own_scores[row] - largest)
        share = 1.0 / (jnp.sum(raised, axis=1, keepdims=True) + own_raised)
        weights[row % 2] = (raised * share).astype(jnp.bfloat16)
        own_weights[row] = (own_raised * share).astype(jnp.bfloat16).astype(jnp.float32)

    def mix(row):
        mixed = jnp.dot(weights[row % 2], values[row], preferred_element_type=jnp.float32)
        mixed = mixed + own_weights[row] * new_values[row : row + 1]
        mixed = jnp.where(own_group, mixed, 0.0)
        chosen = mixed[:, :HD]
        for group in range(1, kv_groups):
            chosen = chosen + mixed[:, group * HD : (group + 1) * HD]
        for part in range(parts):
            attended[part, pl.ds(row, count, stride=here), :] = chosen[
                part * count : (part + 1) * count
            ]

    for step in range(here + 2):
        if step < here:
            key_copy(step).wait()
        if step >= 2:
            value_copy(step - 2).wait()
        if step >= 2:
            mix(step - 2)
        if 1 <= step <= here:
            weigh(step - 1)
        if step < here:
            score(step)
    for k in range(count):
        for part in range(parts):
            out_ref[k, :, part * HD : (part + 1) * HD] = attended[
                part, k * here : (k + 1) * here, :
            ].astype(jnp.bfloat16)


def attend(blocks, lengths, cosine, sine, cache_keys, cache_values):
    count = blocks.shape[0]
    here, span, key_width = cache_keys.shape
    width = blocks.shape[2] - HD
    heads = count * width // HD
    vmem = pl.BlockSpec(memory_space=pltpu.VMEM)
    whole = pl.BlockSpec(memory_space=pltpu.HBM)
    return pl.pallas_call(
        functools.partial(attend_kernel, count),
        out_shape=jax.ShapeDtypeStruct((count, here, width), jnp.bfloat16),
        in_specs=[pl.BlockSpec(memory_space=pltpu.SMEM), vmem, vmem, whole, whole, vmem],
        out_specs=vmem,
        scratch_shapes=[
            pltpu.VMEM((width // HD + 1, here * count, HD), jnp.float32),
            pltpu.VMEM((width // HD, here * count, HD), jnp.float32),
            pltpu.VMEM((2, heads, span), jnp.float32),
            pltpu.VMEM((2, heads, span), jnp.bfloat16),
            pltpu.VMEM((here, span, key_width), jnp.bfloat16),
            pltpu.VMEM((here, span, key_width), jnp.bfloat16),
            pltpu.SemaphoreType.DMA((here,)),
            pltpu.SemaphoreType.DMA((here,)),
        ],
        compiler_params=pltpu.CompilerParams(vmem_limit_bytes=40 * 1024 * 1024),
        cost_estimate=pl.CostEstimate(
            flops=4 * here * count * width * span,
            bytes_accessed=4 * here * span * key_width,
            transcendentals=here * heads * span,
        ),
    )(lengths, cosine, sine, cache_keys, cache_values, blocks)


def exchange(blocks):
    return lax.all_to_all(blocks, "tensor", split_axis=0, concat_axis=0, tiled=True)


def plans(count):
    bits = list(range(1, count.bit_length() - 1))
    turned = bits[::-1]
    late = bits[1:2] + bits[:1] + bits[2:]
    return [(late, late[::-1]), (bits, turned), (bits, turned), (late, late[::-1])]


def timetable(count):
    if count == 16:
        return [int(c) for c in TABLE]
    return [s for _ in range(2 * (count.bit_length() - 2) + 2) for s in (0, 3, 1, 2)]


def place(offset, order):
    spot = 0
    for bit in order:
        spot = spot * 2 + ((offset >> bit) & 1)
    return spot


def project_kernel(count, offsets, w_ref, *refs):
    in_ref, *set_refs, heads_buffer, w_buffer, arrived = refs
    me = lax.axis_index("tensor")
    width = w_buffer.shape[2]
    copies = []
    for slot, offset in enumerate(offsets):
        column = pl.multiple_of(jnp.bitwise_xor(me, offset) * width, width)
        copies.append(
            pltpu.make_async_copy(
                w_ref.at[:, pl.ds(column, width)], w_buffer.at[slot], arrived.at[slot]
            )
        )
        copies[-1].start()
    here = in_ref.shape[1]
    for k in range(count):
        heads_buffer[k * here : (k + 1) * here, :] = in_ref[k].astype(jnp.float32)
    heads = heads_buffer[...].astype(jnp.bfloat16)
    for slot, offset in enumerate(offsets):
        copies[slot].wait()
        product = jnp.dot(heads, w_buffer[slot], preferred_element_type=jnp.float32).astype(
            jnp.bfloat16
        )
        start = 0
        for ref, (order, _) in zip(set_refs, plans(count)):
            ref[place(offset, order)] = product[start : start + ref.shape[1]]
            start += ref.shape[1]


def project(blocks, w_out, offsets):
    count, here, depth = blocks.shape
    rows = count * here
    width = w_out.shape[1] // count
    sets = len(plans(count))
    share = jax.ShapeDtypeStruct((len(offsets), rows // sets, width), jnp.bfloat16)
    return pl.pallas_call(
        functools.partial(project_kernel, count, offsets),
        out_shape=(share,) * sets,
        in_specs=[pl.BlockSpec(memory_space=pltpu.HBM), pl.BlockSpec(memory_space=pltpu.VMEM)],
        out_specs=(pl.BlockSpec(memory_space=pltpu.VMEM),) * sets,
        scratch_shapes=[
            pltpu.VMEM((rows, depth), jnp.float32),
            pltpu.VMEM((len(offsets), depth, width), jnp.bfloat16),
            pltpu.SemaphoreType.DMA((len(offsets),)),
        ],
        compiler_params=pltpu.CompilerParams(vmem_limit_bytes=30 * 1024 * 1024),
        cost_estimate=pl.CostEstimate(
            flops=2 * rows * depth * width * len(offsets),
            bytes_accessed=2 * (depth + rows) * width * len(offsets),
            transcendentals=0,
        ),
    )(w_out, blocks)


def finish_kernel(offsets, own_ref, other_ref, gain_ref, *refs):
    out_ref = refs[-1]
    me = lax.axis_index("tensor")
    half, rows, width = own_ref.shape
    total = jnp.zeros((rows, width), jnp.float32)
    for ref in (own_ref, other_ref):
        for k in range(half):
            block = ref[k].astype(jnp.float32)
            total = total + block * block
    mean_square = jnp.sum(total, axis=1, keepdims=True) / (2 * half * width)
    scale = lax.rsqrt(mean_square + epsilon)
    for k, offset in enumerate(offsets):
        block = (own_ref if k < half else other_ref)[k % half].astype(jnp.float32)
        index = jnp.bitwise_xor(me, offset)
        column = pl.multiple_of(index * width, width)
        gain = gain_ref[pl.ds(index, 1), :]
        out_ref[:, pl.ds(column, width)] = (block * scale * gain).astype(jnp.bfloat16)


def finish(own, other, gain, offsets, which, sets, earlier):
    half, rows, width = own.shape
    columns = 2 * half * width
    operands = [own, other, gain] + ([] if earlier is None else [earlier])
    whole = pl.BlockSpec(memory_space=pltpu.VMEM)
    return pl.pallas_call(
        functools.partial(finish_kernel, offsets),
        grid=(1,),
        out_shape=jax.ShapeDtypeStruct((rows * sets, columns), jnp.bfloat16),
        in_specs=[whole] * 3 + [pl.BlockSpec(memory_space=pl.ANY)] * (len(operands) - 3),
        out_specs=pl.BlockSpec((rows, columns), lambda i: (which, 0)),
        input_output_aliases={} if earlier is None else {3: 0},
        compiler_params=pltpu.CompilerParams(vmem_limit_bytes=24 * 1024 * 1024),
        cost_estimate=pl.CostEstimate(
            flops=6 * rows * columns, bytes_accessed=4 * rows * columns, transcendentals=0
        ),
    )(*operands)


def swap(values, bit, count):
    return lax.ppermute(values, "tensor", [(i, i ^ (1 << bit)) for i in range(count)])


def add(one, other):
    return (one.astype(jnp.float32) + other.astype(jnp.float32)).astype(jnp.bfloat16)


def on_device(
    hidden_in,
    attn_gain,
    w_query,
    w_keyval,
    cache_keys,
    cache_values,
    w_out,
    ffn_gain,
    lengths,
    positions,
):
    row_count = hidden_in.shape[0]
    count = lax.axis_size("tensor")
    my_index = lax.axis_index("tensor")
    cosine, sine = turns(positions)
    blocks = project_in(
        hidden_in, attn_gain.reshape(1, -1), w_query, w_keyval, cosine, sine, count
    )
    head_blocks = exchange(
        attend(exchange(blocks), lengths, cosine, sine, cache_keys, cache_values)
    )
    share_width = w_out.shape[1] // count
    mine = lax.dynamic_slice_in_dim(hidden_in, my_index * share_width, share_width, 1)
    gain = ffn_gain.astype(jnp.float32).reshape(count, share_width)
    orders = plans(count)
    sets = len(orders)
    set_rows = row_count // sets
    sent = project(head_blocks, w_out, list(range(1, count, 2)))
    arrivals = [swap(block, 0, count) for block in sent]
    kept = project(head_blocks, w_out, list(range(0, count, 2)))

    def halves(keep, arrival):
        half = keep.shape[0] // 2
        return add(keep[:half], arrival[:half]), add(keep[half:], arrival[half:])

    held, leaving = zip(*[halves(kept[k], arrivals[k]) for k in range(sets)])
    held = list(held)
    streams = [None] * sets
    offsets = [[0] for _ in range(sets)]
    steps = [0] * sets
    last = normed = None
    for k in timetable(count):
        scatter, gather = orders[k]
        step = steps[k]
        steps[k] += 1
        if step == 0:
            if last is None:
                last = leaving[k]
            else:
                last, _ = lax.optimization_barrier((leaving[k], last))
            arrivals[k] = swap(last, scatter[0], count)
            continue
        held[k], arrivals[k], _ = lax.optimization_barrier((held[k], arrivals[k], last))
        if step < len(scatter):
            held[k], last = halves(held[k], arrivals[k])
            arrivals[k] = swap(last, scatter[step], count)
            continue
        if step == len(scatter):
            own_rows = mine[k * set_rows : (k + 1) * set_rows].astype(jnp.float32)
            total = held[k][0].astype(jnp.float32) + arrivals[k][0].astype(jnp.float32)
            streams[k] = (own_rows + total).astype(jnp.bfloat16)
            last = held[k] = streams[k][None]
        elif step <= len(scatter) + len(gather):
            last = held[k] = jnp.concatenate([held[k], arrivals[k]], axis=0)
        else:
            last = normed = finish(held[k], arrivals[k], gain, offsets[k], k, sets, normed)
            continue
        bit = (gather + [0])[step - len(scatter)]
        arrivals[k] = swap(held[k], bit, count)
        offsets[k] = offsets[k] + [offset ^ (1 << bit) for offset in offsets[k]]
    return (jnp.concatenate(streams, axis=0), normed)


def solution(mesh):
    placed = (
        P("groups", None),
        P(),
        P(None, "tensor"),
        P(None, "tensor"),
        P(("groups", "tensor"), None, None),
        P(("groups", "tensor"), None, None),
        P("tensor", None),
        P(),
        P(("groups", "tensor")),
        P("groups"),
    )
    return jax.shard_map(
        on_device,
        mesh=mesh,
        in_specs=placed,
        out_specs=(P("groups", "tensor"), P("groups", None)),
        check_vma=False,
    )
```

time: 158 us -> 135 us (0.85)
  starting transfers between devices: 71.3 us -> 25.8 us
  blocking collectives: 0 us -> 26.2 us
  local copies, waits for them, and re-layouts: 2.69 us -> 16.6 us
  waiting for transfers between devices: 41.5 us -> 29.2 us
  Pallas kernels: 35.2 us -> 29.7 us
    ppermute x30 -> x0, starting transfers between devices: 43.7 us -> none  [exchange(): lax.ppermute(blocks[k], 'tensor', [(i, i ^ k) for i in range(count)])]
    all_to_all x0 -> x2, blocking collectives: none -> 26.2 us  [exchange(): lax.all_to_all(blocks, 'tensor', split_axis=0, concat_axis=0, tiled=True)]
    unnamed x18 -> x28, local copies, waits for them, and re-layouts: 1.73 us -> 15.5 us
    ppermute x30 -> x0, waiting for transfers between devices: 6.66 us -> none  [exchange(): lax.ppermute(blocks[k], 'tensor', [(i, i ^ k) for i in range(count)])]
    pallas_call x2, Pallas kernels: 20.9 us -> 14.8 us  [the longest x1 8.23 us: project_in(): pl.pallas_call(functools.partial(input_kernel, count), out_shape=jax.Shap...]
    ppermute x32, waiting for transfers between devices: 34.8 us -> 29.2 us  [swap(): lax.ppermute(values, 'tensor', [(i, i ^ 1 << bit) for i in range(count)])]
    ppermute x32, starting transfers between devices: 27.6 us -> 25.8 us  [swap(): lax.ppermute(values, 'tensor', [(i, i ^ 1 << bit) for i in range(count)])]
  transfers between devices with their start and end apart: 62 -> 32, of which waited for: 19 -> 12; matrix products, arithmetic and copies ran while one was open for 4% -> 4% of each run, Pallas kernels for 6% -> 7%
where the time goes in v4:
time: 135 us
  Pallas kernels  29.7 us (22%)
  waiting for transfers between devices  29.2 us (22%)
  blocking collectives  26.2 us (19%)
  starting transfers between devices  25.8 us (19%)
  local copies, waits for them, and re-layouts  16.6 us (12%)
  other arithmetic  6.33 us (5%)
    ppermute x32, waiting for transfers between devices, swap(): lax.ppermute(values, 'tensor', [(i, i ^ 1 << bit) for i in range(count)])  29.2 us
    all_to_all x2, blocking collectives, exchange(): lax.all_to_all(blocks, 'tensor', split_axis=0, concat_axis=0, tiled=True)  26.2 us
    ppermute x32, starting transfers between devices, swap(): lax.ppermute(values, 'tensor', [(i, i ^ 1 << bit) for i in range(count)])  25.8 us
    unnamed x28, local copies, waits for them, and re-layouts  15.5 us
    pallas_call x2, Pallas kernels, project(): pl.pallas_call(functools.partial(project_kernel, count, offsets), out_sha...  8.25 us
    pallas_call x1, Pallas kernels, project_in(): pl.pallas_call(functools.partial(input_kernel, count), out_shape=jax.Shap...  8.23 us
    pallas_call x1, Pallas kernels, attend(): pl.pallas_call(functools.partial(attend_kernel, count), out_shape=jax.Sha...  6.62 us
    pallas_call x4, Pallas kernels, finish(): pl.pallas_call(functools.partial(finish_kernel, offsets), grid=(1,), out_...  6.61 us
  transfers between devices with their start and end apart: 32, of which 12 were waited for; matrix products, arithmetic and copies ran while one was open for 4% of the time, Pallas kernels for 7%

profile of v4, /device:TPU:0, one launch (start us, length us, event | category | flops | bytes accessed | tf_op | source)
XLA Modules:
  0.0 134.8 jit_solution(14228441253981336447)
XLA Ops:
  0.6 0.7 convert_element_type.284
  1.3 0.9 reshape.42.gain_ref
  2.3 0.3 fusion.4
  2.6 2.2 %copy-done.2 = bf16[128,16384]{1,0:T(8,128)(2,1)S(1)} copy-done((bf16[128,16384]{1,0:T(8,128)(2,1)S(1)}, bf16[128,16384]{1,0:T(8,128)(2,1)}, u32[]{:S(2)}) %copy-start.2) | copy-done | bytes 4194328
  4.8 1.6 %copy-done.3 = bf16[16384,64]{0,1:T(8,128)(2,1)S(1)} copy-done((bf16[16384,64]{0,1:T(8,128)(2,1)S(1)}, bf16[16384,64]{0,1:T(8,128)(2,1)}, u32[]{:S(2)}) %copy-start.3) | copy-done | bytes 2097176
  6.4 8.2 %shard_map.113 = bf16[16,8,640]{2,1,0:T(8,128)(2,1)S(1)} custom-call(bf16[128,16384]{1,0:T(8,128)(2,1)S(1)} %copy-done.2, bf16[1,16384]{1,0:T(2,128)(2,1)S(1)} %reshape.42.gain_ref, bf16[16384,512]{1,0:T(8,128)(2,1)} %w_ref.3, bf16[64,16384]{1,0:T(8,128)(2,1)S(1)} %bitcast.23, f32[128,128]{1,0:T(8,128)S(1)} %get-tuple-element.161.cosine_ref, ...), custom_call_target="tpu_custom_call" | custom-call | flops 2415919104 | bytes 23068672 | tf_op jit(solution)/shard_map/pallas_call | solution.py:116
  14.6 15.7 %all_to_all.10.refs_0_ = bf16[16,8,640]{2,1,0:T(8,128)(2,1)S(1)} all-to-all(bf16[16,8,640]{2,1,0:T(8,128)(2,1)S(1)} %shard_map.113), channel_id=1, replica_groups=mesh['groups'=2,'tensor'=16] {'tensor'}, dimensions={0} | all-to-all | bytes 327680 | tf_op jit(solution)/shard_map/all_to_all | solution.py:274
  30.3 6.6 %shard_map.114 = bf16[16,8,512]{2,1,0:T(8,128)(2,1)S(1)} custom-call(s32[8]{0:T(128)S(1)} %copy-done.4, f32[128,128]{1,0:T(8,128)S(1)} %get-tuple-element.161.cosine_ref, f32[128,128]{1,0:T(8,128)S(1)} %get-tuple-element.160.sine_ref, bf16[8,1024,512]{2,1,0:T(8,128)(2,1)S(1)} %bitcast.22, bf16[8,1024,512]{2,1,0:T(8,128)(2,1)} %values_ref.1, ...), custom_call_target="tpu_custom_call" | custom-call | flops 268435456 | bytes 16777216 | tf_op jit(solution)/shard_map/pallas_call | solution.py:249
  36.9 10.5 %all_to_all.11.refs_0_ = bf16[16,8,512]{2,1,0:T(8,128)(2,1)S(1)} all-to-all(bf16[16,8,512]{2,1,0:T(8,128)(2,1)S(1)} %shard_map.114), channel_id=1, replica_groups=mesh['groups'=2,'tensor'=16] {'tensor'}, dimensions={0} | all-to-all | bytes 262144 | tf_op jit(solution)/shard_map/all_to_all | solution.py:274
  47.4 5.8 %copy-done = bf16[512,16384]{1,0:T(8,128)(2,1)S(1)} copy-done((bf16[512,16384]{1,0:T(8,128)(2,1)S(1)}, bf16[512,16384]{1,0:T(8,128)(2,1)}, u32[]{:S(2)}) %copy-start) | copy-done | bytes 16777240
  53.2 4.1 %shard_map.116 = (bf16[8,32,1024]{2,1,0:T(8,128)(2,1)S(1)}, bf16[8,32,1024]{2,1,0:T(8,128)(2,1)S(1)}, bf16[8,32,1024]{2,1,0:T(8,128)(2,1)S(1)}, bf16[8,32,1024]{2,1,0:T(8,128)(2,1)S(1)}) custom-call(bf16[512,16384]{1,0:T(8,128)(2,1)S(1)} %copy-done, bf16[16,8,512]{2,1,0:T(8,128)(2,1)S(1)} %all_to_all.11.refs_0_), custom_call_target="tpu_custom_call" | custom-call | flops 1073741824 | bytes 10485760 | tf_op jit(solution)/shard_map/pallas_call | solution.py:331
  57.3 0.1 collective-permute-start.1
  57.4 0.5 collective-permute-start
  57.9 0.1 collective-permute-start.3
  58.0 0.4 collective-permute-start.7
  58.4 5.8 %copy-done.1 = bf16[512,16384]{1,0:T(8,128)(2,1)S(1)} copy-done((bf16[512,16384]{1,0:T(8,128)(2,1)S(1)}, bf16[512,16384]{1,0:T(8,128)(2,1)}, u32[]{:S(2)}) %copy-start.1) | copy-done | bytes 16777240
  64.2 4.1 %shard_map.115 = (bf16[8,32,1024]{2,1,0:T(8,128)(2,1)S(1)}, bf16[8,32,1024]{2,1,0:T(8,128)(2,1)S(1)}, bf16[8,32,1024]{2,1,0:T(8,128)(2,1)S(1)}, bf16[8,32,1024]{2,1,0:T(8,128)(2,1)S(1)}) custom-call(bf16[512,16384]{1,0:T(8,128)(2,1)S(1)} %copy-done.1, bf16[16,8,512]{2,1,0:T(8,128)(2,1)S(1)} %all_to_all.11.refs_0_), custom_call_target="tpu_custom_call" | custom-call | flops 1073741824 | bytes 10485760 | tf_op jit(solution)/shard_map/pallas_call | solution.py:331
  68.3 0.2 add_convert_fusion.3
  68.5 0.1 collective-permute-start.4
  68.6 0.2 add_convert_fusion.6
  68.8 0.4 collective-permute-start.2
  69.2 0.2 add_convert_fusion
  69.4 0.2 add_convert_fusion.2
  69.6 7.3 %collective-permute-done.4 = bf16[4,32,1024]{2,1,0:T(8,128)(2,1)S(1)} collective-permute-done((bf16[4,32,1024]{2,1,0:T(8,128)(2,1)S(1)}, bf16[4,32,1024]{2,1,0:T(8,128)(2,1)S(1)}, u32[]{:S(2)}, u32[]{:S(2)}) %collective-permute-start.4) | collective-permute-done | bytes 262176 | tf_op jit(solution)/shard_map/ppermute | solution.py:389
  77.0 0.7 collective-permute-start.10
  77.8 1.5 %collective-permute-start.5 = (bf16[2,32,1024]{2,1,0:T(8,128)(2,1)S(1)}, bf16[2,32,1024]{2,1,0:T(8,128)(2,1)S(1)}, u32[]{:S(2)}, u32[]{:S(2)}) collective-permute-start(bf16[2,32,1024]{2,1,0:T(8,128)(2,1)S(1)} %get-tuple-element.149), channel_id=1, source_target_pairs={{0,2},{1,3},{2,0},{3,1},{4,6},{5,7},{6,4},{7,5},{8,10},{9,11},{10,... | collective-permute-start | bytes 393224 | tf_op jit(solution)/shard_map/ppermute | solution.py:389
  79.3 1.9 %collective-permute-start.9 = (bf16[4,32,1024]{2,1,0:T(8,128)(2,1)S(1)}, bf16[4,32,1024]{2,1,0:T(8,128)(2,1)S(1)}, u32[]{:S(2)}, u32[]{:S(2)}) collective-permute-start(bf16[4,32,1024]{2,1,0:T(8,128)(2,1)S(1)} %get-tuple-element.83), channel_id=1, source_target_pairs={{0,4},{1,5},{2,6},{3,7},{4,0},{5,1},{6,2},{7,3},{8,12},{9,13},{10,... | collective-permute-start | bytes 786440 | tf_op jit(solution)/shard_map/ppermute | solution.py:389
  81.2 2.2 %collective-permute-done.6 = bf16[2,32,1024]{2,1,0:T(8,128)(2,1)S(1)} collective-permute-done((bf16[2,32,1024]{2,1,0:T(8,128)(2,1)S(1)}, bf16[2,32,1024]{2,1,0:T(8,128)(2,1)S(1)}, u32[]{:S(2)}, u32[]{:S(2)}) %collective-permute-start.6) | collective-permute-done | bytes 131104 | tf_op jit(solution)/shard_map/ppermute | solution.py:389
  83.5 3.9 %collective-permute-done.5 = bf16[2,32,1024]{2,1,0:T(8,128)(2,1)S(1)} collective-permute-done((bf16[2,32,1024]{2,1,0:T(8,128)(2,1)S(1)}, bf16[2,32,1024]{2,1,0:T(8,128)(2,1)S(1)}, u32[]{:S(2)}, u32[]{:S(2)}) %collective-permute-start.5) | collective-permute-done | bytes 131104 | tf_op jit(solution)/shard_map/ppermute | solution.py:389
  87.4 1.2 collective-permute-start.8
  88.6 0.8 collective-permute-done.11
  89.4 0.9 fusion.3
  90.2 1.1 collective-permute-start.14
  91.4 1.7 %collective-permute-start.12 = (bf16[2,32,1024]{2,1,0:T(8,128)(2,1)S(1)}, bf16[2,32,1024]{2,1,0:T(8,128)(2,1)S(1)}, u32[]{:S(2)}, u32[]{:S(2)}) collective-permute-start(bf16[2,32,1024]{2,1,0:T(8,128)(2,1)S(1)} %get-tuple-element.145), channel_id=1, source_target_pairs={{0,4},{1,5},{2,6},{3,7},{4,0},{5,1},{6,2},{7,3},{8,12},{9,13},{10,... | collective-permute-start | bytes 393224 | tf_op jit(solution)/shard_map/ppermute | solution.py:389
  93.2 0.7 collective-permute-start.15
  93.9 0.9 fusion.2
  94.8 0.7 collective-permute-start.13
  95.4 2.8 %collective-permute-done.15 = bf16[2,32,1024]{2,1,0:T(8,128)(2,1)S(1)} collective-permute-done((bf16[2,32,1024]{2,1,0:T(8,128)(2,1)S(1)}, bf16[2,32,1024]{2,1,0:T(8,128)(2,1)S(1)}, u32[]{:S(2)}, u32[]{:S(2)}) %collective-permute-start.15) | collective-permute-done | bytes 131104 | tf_op jit(solution)/shard_map/ppermute | solution.py:389
  98.3 0.5 collective-permute-start.19
  98.8 1.9 %collective-permute-start.17 = (bf16[2,32,1024]{2,1,0:T(8,128)(2,1)S(1)}, bf16[2,32,1024]{2,1,0:T(8,128)(2,1)S(1)}, u32[]{:S(2)}, u32[]{:S(2)}) collective-permute-start(bf16[2,32,1024]{2,1,0:T(8,128)(2,1)S(1)} %constant_dynamic-update-slice_fusion), channel_id=1, source_target_pairs={{0,4},{1,5},{2,6},{3,7},{4,0},{5,1},{6,2},{7,3},{8,12},{9,13},{10,... | collective-permute-start | bytes 393224 | tf_op jit(solution)/shard_map/ppermute | solution.py:389
  100.7 1.4 %collective-permute-start.18 = (bf16[2,32,1024]{2,1,0:T(8,128)(2,1)S(1)}, bf16[2,32,1024]{2,1,0:T(8,128)(2,1)S(1)}, u32[]{:S(2)}, u32[]{:S(2)}) collective-permute-start(bf16[2,32,1024]{2,1,0:T(8,128)(2,1)S(1)} %constant_dynamic-update-slice_fusion.2), channel_id=1, source_target_pairs={{0,2},{1,3},{2,0},{3,1},{4,6},{5,7},{6,4},{7,5},{8,10},{9,11},{10,... | collective-permute-start | bytes 393224 | tf_op jit(solution)/shard_map/ppermute | solution.py:389
  102.1 0.6 collective-permute-start.16
  102.7 1.8 %collective-permute-done.19 = bf16[1,32,1024]{2,1,0:T(8,128)(2,1)S(1)} collective-permute-done((bf16[1,32,1024]{2,1,0:T(8,128)(2,1)S(1)}, bf16[1,32,1024]{2,1,0:T(8,128)(2,1)S(1)}, u32[]{:S(2)}, u32[]{:S(2)}) %collective-permute-start.19) | collective-permute-done | bytes 65568 | tf_op jit(solution)/shard_map/ppermute | solution.py:389
  104.5 0.9 fusion.1
  105.4 0.7 collective-permute-start.21
  106.1 0.9 collective-permute-done.18
  107.0 1.6 %collective-permute-start.23 = (bf16[4,32,1024]{2,1,0:T(8,128)(2,1)S(1)}, bf16[4,32,1024]{2,1,0:T(8,128)(2,1)S(1)}, u32[]{:S(2)}, u32[]{:S(2)}) collective-permute-start(bf16[4,32,1024]{2,1,0:T(8,128)(2,1)S(1)} %constant_dynamic-update-slice_fusion.4), channel_id=1, source_target_pairs={{0,4},{1,5},{2,6},{3,7},{4,0},{5,1},{6,2},{7,3},{8,12},{9,13},{10,... | collective-permute-start | bytes 786440 | tf_op jit(solution)/shard_map/ppermute | solution.py:389
  108.6 0.1 collective-permute-start.27
  108.7 0.9 fusion
  109.6 1.6 %collective-permute-start.20 = (bf16[1,32,1024]{2,1,0:T(8,128)(2,1)S(1)}, bf16[1,32,1024]{2,1,0:T(8,128)(2,1)S(1)}, u32[]{:S(2)}, u32[]{:S(2)}) collective-permute-start(bf16[1,32,1024]{2,1,0:T(8,128)(2,1)S(1)} %bitcast.30), channel_id=1, source_target_pairs={{0,8},{1,9},{2,10},{3,11},{4,12},{5,13},{6,14},{7,15},{8,0},{9,1},... | collective-permute-start | bytes 196616 | tf_op jit(solution)/shard_map/ppermute | solution.py:389
  111.2 0.7 collective-permute-done.21
  112.0 0.9 collective-permute-start.24
  112.8 2.1 %collective-permute-done.20 = bf16[1,32,1024]{2,1,0:T(8,128)(2,1)S(1)} collective-permute-done((bf16[1,32,1024]{2,1,0:T(8,128)(2,1)S(1)}, bf16[1,32,1024]{2,1,0:T(8,128)(2,1)S(1)}, u32[]{:S(2)}, u32[]{:S(2)}) %collective-permute-start.20) | collective-permute-done | bytes 65568 | tf_op jit(solution)/shard_map/ppermute | solution.py:389
  115.0 2.1 %collective-permute-start.22 = (bf16[2,32,1024]{2,1,0:T(8,128)(2,1)S(1)}, bf16[2,32,1024]{2,1,0:T(8,128)(2,1)S(1)}, u32[]{:S(2)}, u32[]{:S(2)}) collective-permute-start(bf16[2,32,1024]{2,1,0:T(8,128)(2,1)S(1)} %constant_dynamic-update-slice_fusion.10), channel_id=1, source_target_pairs={{0,4},{1,5},{2,6},{3,7},{4,0},{5,1},{6,2},{7,3},{8,12},{9,13},{10,... | collective-permute-start | bytes 393224 | tf_op jit(solution)/shard_map/ppermute | solution.py:389
  117.2 2.8 %collective-permute-done.22 = bf16[2,32,1024]{2,1,0:T(8,128)(2,1)S(1)} collective-permute-done((bf16[2,32,1024]{2,1,0:T(8,128)(2,1)S(1)}, bf16[2,32,1024]{2,1,0:T(8,128)(2,1)S(1)}, u32[]{:S(2)}, u32[]{:S(2)}) %collective-permute-start.22) | collective-permute-done | bytes 131104 | tf_op jit(solution)/shard_map/ppermute | solution.py:389
  120.2 2.1 %collective-permute-start.26 = (bf16[4,32,1024]{2,1,0:T(8,128)(2,1)S(1)}, bf16[4,32,1024]{2,1,0:T(8,128)(2,1)S(1)}, u32[]{:S(2)}, u32[]{:S(2)}) collective-permute-start(bf16[4,32,1024]{2,1,0:T(8,128)(2,1)S(1)} %constant_dynamic-update-slice_fusion.12), channel_id=1, source_target_pairs={{0,4},{1,5},{2,6},{3,7},{4,0},{5,1},{6,2},{7,3},{8,12},{9,13},{10,... | collective-permute-start | bytes 786440 | tf_op jit(solution)/shard_map/ppermute | solution.py:389
  122.3 1.1 collective-permute-start.25
  123.4 1.7 %shard_map.117.refs_0_ = bf16[128,16384]{1,0:T(8,128)(2,1)} custom-call(bf16[8,32,1024]{2,1,0:T(8,128)(2,1)S(1)} %constant_dynamic-update-slice_fusion.14.own_ref, bf16[8,32,1024]{2,1,0:T(8,128)(2,1)S(1)} %collective-permute-done.29.other_ref, f32[16,1024]{1,0:T(8,128)S(1)} %reshape.46.gain_ref), custom_call_target="tpu_custom_call" | custom-call | flops 3145728 | bytes 2097152 | tf_op jit(solution)/shard_map/pallas_call | solution.py:374
  125.0 1.7 %shard_map.118.refs_0_ = bf16[128,16384]{1,0:T(8,128)(2,1)} custom-call(bf16[8,32,1024]{2,1,0:T(8,128)(2,1)S(1)} %constant_dynamic-update-slice_fusion.18.own_ref, bf16[8,32,1024]{2,1,0:T(8,128)(2,1)S(1)} %collective-permute-done.28.other_ref, f32[16,1024]{1,0:T(8,128)S(1)} %reshape.46.gain_ref, ...), custom_call_target="tpu_custom_call", output_to_operand_aliasing={{}: (3, {})} | custom-call | flops 3145728 | bytes 2097152 | tf_op jit(solution)/shard_map/pallas_call | solution.py:374
  126.7 2.5 %collective-permute-done.26 = bf16[4,32,1024]{2,1,0:T(8,128)(2,1)S(1)} collective-permute-done((bf16[4,32,1024]{2,1,0:T(8,128)(2,1)S(1)}, bf16[4,32,1024]{2,1,0:T(8,128)(2,1)S(1)}, u32[]{:S(2)}, u32[]{:S(2)}) %collective-permute-start.26) | collective-permute-done | bytes 262176 | tf_op jit(solution)/shard_map/ppermute | solution.py:389
  129.3 1.3 %collective-permute-done.25 = bf16[4,32,1024]{2,1,0:T(8,128)(2,1)S(1)} collective-permute-done((bf16[4,32,1024]{2,1,0:T(8,128)(2,1)S(1)}, bf16[4,32,1024]{2,1,0:T(8,128)(2,1)S(1)}, u32[]{:S(2)}, u32[]{:S(2)}) %collective-permute-start.25) | collective-permute-done | bytes 262176 | tf_op jit(solution)/shard_map/ppermute | solution.py:389
  130.8 0.7 pad_maximum_fusion
  131.5 1.7 %shard_map.119.refs_0_ = bf16[128,16384]{1,0:T(8,128)(2,1)} custom-call(bf16[8,32,1024]{2,1,0:T(8,128)(2,1)S(1)} %constant_dynamic-update-slice_fusion.20.own_ref, bf16[8,32,1024]{2,1,0:T(8,128)(2,1)S(1)} %collective-permute-done.31.other_ref, f32[16,1024]{1,0:T(8,128)S(1)} %reshape.46.gain_ref, ...), custom_call_target="tpu_custom_call", output_to_operand_aliasing={{}: (3, {})} | custom-call | flops 3145728 | bytes 2097152 | tf_op jit(solution)/shard_map/pallas_call | solution.py:374
  133.2 1.7 %shard_map.120 = bf16[128,16384]{1,0:T(8,128)(2,1)} custom-call(bf16[8,32,1024]{2,1,0:T(8,128)(2,1)S(1)} %constant_dynamic-update-slice_fusion.22.own_ref, bf16[8,32,1024]{2,1,0:T(8,128)(2,1)S(1)} %collective-permute-done.30.other_ref, f32[16,1024]{1,0:T(8,128)S(1)} %reshape.46.gain_ref, ...), custom_call_target="tpu_custom_call", output_to_operand_aliasing={{}: (3, {})} | custom-call | flops 3145728 | bytes 2097152 | tf_op jit(solution)/shard_map/pallas_call | solution.py:374
  (73 shorter events, 1.2 us)
Async XLA Ops:
  1.3 29.0 %slice-start = ((s8[8388608]{0:T(1024)(128)(4,1)}), s8[4194304]{0:T(1024)(128)(4,1)S(1)}, s32[]{:S(2)}) async-start(s8[8388608]{0:T(1024)(128)(4,1)} %bitcast.21), calls=%async_computation.2 | async-start | bytes 8388608
  2.6 2.2 %copy-start.2 = (bf16[128,16384]{1,0:T(8,128)(2,1)S(1)}, bf16[128,16384]{1,0:T(8,128)(2,1)}, u32[]{:S(2)}) copy-start(bf16[128,16384]{1,0:T(8,128)(2,1)} %hidden_ref.1) | copy-start | bytes 12582916
  4.8 1.6 %copy-start.3 = (bf16[16384,64]{0,1:T(8,128)(2,1)S(1)}, bf16[16384,64]{0,1:T(8,128)(2,1)}, u32[]{:S(2)}) copy-start(bf16[16384,64]{0,1:T(8,128)(2,1)} %param.13) | copy-start | bytes 6291460
  6.4 23.9 %slice-start.1 = ((s8[8388608]{0:T(1024)(128)(4,1)}), s8[4194304]{0:T(1024)(128)(4,1)S(1)}, s32[]{:S(2)}) async-start(s8[8388608]{0:T(1024)(128)(4,1)} %bitcast.21), calls=%async_computation.3 | async-start | bytes 8388608
  6.4 23.9 %copy-start.4 = (s32[8]{0:T(128)S(1)}, s32[8]{0:T(128)}, u32[]{:S(2)}) copy-start(s32[8]{0:T(128)} %lengths_ref.1) | copy-start | bytes 100
  47.4 5.8 %copy-start = (bf16[512,16384]{1,0:T(8,128)(2,1)S(1)}, bf16[512,16384]{1,0:T(8,128)(2,1)}, u32[]{:S(2)}) copy-start(bf16[512,16384]{1,0:T(8,128)(2,1)} %w_ref.5) | copy-start | bytes 50331652
  57.3 11.0 %collective-permute-start.1 = (bf16[8,32,1024]{2,1,0:T(8,128)(2,1)S(1)}, bf16[8,32,1024]{2,1,0:T(8,128)(2,1)S(1)}, u32[]{:S(2)}, u32[]{:S(2)}) collective-permute-start(bf16[8,32,1024]{2,1,0:T(8,128)(2,1)S(1)} %get-tuple-element.72), channel_id=1, source_target_pairs={{0,1},{1,0},{2,3},{3,2},{4,5},{5,4},{6,7},{7,6},{8,9},{9,8},{10,11... | collective-permute-start | bytes 1572872 | tf_op jit(solution)/shard_map/ppermute | solution.py:389
  57.4 11.2 %collective-permute-start = (bf16[8,32,1024]{2,1,0:T(8,128)(2,1)S(1)}, bf16[8,32,1024]{2,1,0:T(8,128)(2,1)S(1)}, u32[]{:S(2)}, u32[]{:S(2)}) collective-permute-start(bf16[8,32,1024]{2,1,0:T(8,128)(2,1)S(1)} %get-tuple-element.70), channel_id=1, source_target_pairs={{0,1},{1,0},{2,3},{3,2},{4,5},{5,4},{6,7},{7,6},{8,9},{9,8},{10,11... | collective-permute-start | bytes 1572872 | tf_op jit(solution)/shard_map/ppermute | solution.py:389
  57.9 11.3 %collective-permute-start.3 = (bf16[8,32,1024]{2,1,0:T(8,128)(2,1)S(1)}, bf16[8,32,1024]{2,1,0:T(8,128)(2,1)S(1)}, u32[]{:S(2)}, u32[]{:S(2)}) collective-permute-start(bf16[8,32,1024]{2,1,0:T(8,128)(2,1)S(1)} %get-tuple-element.75), channel_id=1, source_target_pairs={{0,1},{1,0},{2,3},{3,2},{4,5},{5,4},{6,7},{7,6},{8,9},{9,8},{10,11... | collective-permute-start | bytes 1572872 | tf_op jit(solution)/shard_map/ppermute | solution.py:389
  58.0 11.4 %collective-permute-start.7 = (bf16[8,32,1024]{2,1,0:T(8,128)(2,1)S(1)}, bf16[8,32,1024]{2,1,0:T(8,128)(2,1)S(1)}, u32[]{:S(2)}, u32[]{:S(2)}) collective-permute-start(bf16[8,32,1024]{2,1,0:T(8,128)(2,1)S(1)} %get-tuple-element.82), channel_id=1, source_target_pairs={{0,1},{1,0},{2,3},{3,2},{4,5},{5,4},{6,7},{7,6},{8,9},{9,8},{10,11... | collective-permute-start | bytes 1572872 | tf_op jit(solution)/shard_map/ppermute | solution.py:389
  58.4 5.8 %copy-start.1 = (bf16[512,16384]{1,0:T(8,128)(2,1)S(1)}, bf16[512,16384]{1,0:T(8,128)(2,1)}, u32[]{:S(2)}) copy-start(bf16[512,16384]{1,0:T(8,128)(2,1)} %w_ref.5) | copy-start | bytes 50331652
  68.5 8.4 %collective-permute-start.4 = (bf16[4,32,1024]{2,1,0:T(8,128)(2,1)S(1)}, bf16[4,32,1024]{2,1,0:T(8,128)(2,1)S(1)}, u32[]{:S(2)}, u32[]{:S(2)}) collective-permute-start(bf16[4,32,1024]{2,1,0:T(8,128)(2,1)S(1)} %get-tuple-element.139), channel_id=1, source_target_pairs={{0,2},{1,3},{2,0},{3,1},{4,6},{5,7},{6,4},{7,5},{8,10},{9,11},{10,... | collective-permute-start | bytes 786440 | tf_op jit(solution)/shard_map/ppermute | solution.py:389
  68.8 8.9 %collective-permute-start.2 = (bf16[4,32,1024]{2,1,0:T(8,128)(2,1)S(1)}, bf16[4,32,1024]{2,1,0:T(8,128)(2,1)S(1)}, u32[]{:S(2)}, u32[]{:S(2)}) collective-permute-start(bf16[4,32,1024]{2,1,0:T(8,128)(2,1)S(1)} %get-tuple-element.73), channel_id=1, source_target_pairs={{0,4},{1,5},{2,6},{3,7},{4,0},{5,1},{6,2},{7,3},{8,12},{9,13},{10,... | collective-permute-start | bytes 786440 | tf_op jit(solution)/shard_map/ppermute | solution.py:389
  77.0 6.4 %collective-permute-start.6 = (bf16[2,32,1024]{2,1,0:T(8,128)(2,1)S(1)}, bf16[2,32,1024]{2,1,0:T(8,128)(2,1)S(1)}, u32[]{:S(2)}, u32[]{:S(2)}) collective-permute-start(bf16[2,32,1024]{2,1,0:T(8,128)(2,1)S(1)} %get-tuple-element.151), channel_id=1, source_target_pairs={{0,4},{1,5},{2,6},{3,7},{4,0},{5,1},{6,2},{7,3},{8,12},{9,13},{10,... | collective-permute-start | bytes 393224 | tf_op jit(solution)/shard_map/ppermute | solution.py:389
  77.0 14.3 %collective-permute-start.10 = (bf16[4,32,1024]{2,1,0:T(8,128)(2,1)S(1)}, bf16[4,32,1024]{2,1,0:T(8,128)(2,1)S(1)}, u32[]{:S(2)}, u32[]{:S(2)}) collective-permute-start(bf16[4,32,1024]{2,1,0:T(8,128)(2,1)S(1)} %get-tuple-element.78), channel_id=1, source_target_pairs={{0,2},{1,3},{2,0},{3,1},{4,6},{5,7},{6,4},{7,5},{8,10},{9,11},{10,... | collective-permute-start | bytes 786440 | tf_op jit(solution)/shard_map/ppermute | solution.py:389
  77.8 9.6 %collective-permute-start.5 = (bf16[2,32,1024]{2,1,0:T(8,128)(2,1)S(1)}, bf16[2,32,1024]{2,1,0:T(8,128)(2,1)S(1)}, u32[]{:S(2)}, u32[]{:S(2)}) collective-permute-start(bf16[2,32,1024]{2,1,0:T(8,128)(2,1)S(1)} %get-tuple-element.149), channel_id=1, source_target_pairs={{0,2},{1,3},{2,0},{3,1},{4,6},{5,7},{6,4},{7,5},{8,10},{9,11},{10,... | collective-permute-start | bytes 393224 | tf_op jit(solution)/shard_map/ppermute | solution.py:389
  79.3 13.9 %collective-permute-start.9 = (bf16[4,32,1024]{2,1,0:T(8,128)(2,1)S(1)}, bf16[4,32,1024]{2,1,0:T(8,128)(2,1)S(1)}, u32[]{:S(2)}, u32[]{:S(2)}) collective-permute-start(bf16[4,32,1024]{2,1,0:T(8,128)(2,1)S(1)} %get-tuple-element.83), channel_id=1, source_target_pairs={{0,4},{1,5},{2,6},{3,7},{4,0},{5,1},{6,2},{7,3},{8,12},{9,13},{10,... | collective-permute-start | bytes 786440 | tf_op jit(solution)/shard_map/ppermute | solution.py:389
  83.4 5.9 %collective-permute-start.11 = (bf16[1,32,1024]{2,1,0:T(8,128)(2,1)S(1)}, bf16[1,32,1024]{2,1,0:T(8,128)(2,1)S(1)}, u32[]{:S(2)}, u32[]{:S(2)}) collective-permute-start(bf16[1,32,1024]{2,1,0:T(8,128)(2,1)S(1)} %get-tuple-element.158), channel_id=1, source_target_pairs={{0,8},{1,9},{2,10},{3,11},{4,12},{5,13},{6,14},{7,15},{8,0},{9,1},... | collective-permute-start | bytes 196616 | tf_op jit(solution)/shard_map/ppermute | solution.py:389
  87.4 6.5 %collective-permute-start.8 = (bf16[1,32,1024]{2,1,0:T(8,128)(2,1)S(1)}, bf16[1,32,1024]{2,1,0:T(8,128)(2,1)S(1)}, u32[]{:S(2)}, u32[]{:S(2)}) collective-permute-start(bf16[1,32,1024]{2,1,0:T(8,128)(2,1)S(1)} %get-tuple-element.157), channel_id=1, source_target_pairs={{0,8},{1,9},{2,10},{3,11},{4,12},{5,13},{6,14},{7,15},{8,0},{9,1},... | collective-permute-start | bytes 196616 | tf_op jit(solution)/shard_map/ppermute | solution.py:389
  90.2 8.5 %collective-permute-start.14 = (bf16[1,32,1024]{2,1,0:T(8,128)(2,1)S(1)}, bf16[1,32,1024]{2,1,0:T(8,128)(2,1)S(1)}, u32[]{:S(2)}, u32[]{:S(2)}) collective-permute-start(bf16[1,32,1024]{2,1,0:T(8,128)(2,1)S(1)} %bitcast.24), channel_id=1, source_target_pairs={{0,8},{1,9},{2,10},{3,11},{4,12},{5,13},{6,14},{7,15},{8,0},{9,1},... | collective-permute-start | bytes 196616 | tf_op jit(solution)/shard_map/ppermute | solution.py:389
  91.3 32.0 %copy-start.5 = (bf16[16384]{0:T(1024)(128)(2,1)S(1)}, bf16[16384]{0:T(1024)(128)(2,1)}, u32[]{:S(2)}) copy-start(bf16[16384]{0:T(1024)(128)(2,1)} %param.17) | copy-start | bytes 98308
  91.4 10.7 %collective-permute-start.12 = (bf16[2,32,1024]{2,1,0:T(8,128)(2,1)S(1)}, bf16[2,32,1024]{2,1,0:T(8,128)(2,1)S(1)}, u32[]{:S(2)}, u32[]{:S(2)}) collective-permute-start(bf16[2,32,1024]{2,1,0:T(8,128)(2,1)S(1)} %get-tuple-element.145), channel_id=1, source_target_pairs={{0,4},{1,5},{2,6},{3,7},{4,0},{5,1},{6,2},{7,3},{8,12},{9,13},{10,... | collective-permute-start | bytes 393224 | tf_op jit(solution)/shard_map/ppermute | solution.py:389
  93.2 5.0 %collective-permute-start.15 = (bf16[2,32,1024]{2,1,0:T(8,128)(2,1)S(1)}, bf16[2,32,1024]{2,1,0:T(8,128)(2,1)S(1)}, u32[]{:S(2)}, u32[]{:S(2)}) collective-permute-start(bf16[2,32,1024]{2,1,0:T(8,128)(2,1)S(1)} %get-tuple-element.146), channel_id=1, source_target_pairs={{0,2},{1,3},{2,0},{3,1},{4,6},{5,7},{6,4},{7,5},{8,10},{9,11},{10,... | collective-permute-start | bytes 393224 | tf_op jit(solution)/shard_map/ppermute | solution.py:389
  94.8 5.9 %collective-permute-start.13 = (bf16[1,32,1024]{2,1,0:T(8,128)(2,1)S(1)}, bf16[1,32,1024]{2,1,0:T(8,128)(2,1)S(1)}, u32[]{:S(2)}, u32[]{:S(2)}) collective-permute-start(bf16[1,32,1024]{2,1,0:T(8,128)(2,1)S(1)} %bitcast.26), channel_id=1, source_target_pairs={{0,8},{1,9},{2,10},{3,11},{4,12},{5,13},{6,14},{7,15},{8,0},{9,1},... | collective-permute-start | bytes 196616 | tf_op jit(solution)/shard_map/ppermute | solution.py:389
  98.3 6.3 %collective-permute-start.19 = (bf16[1,32,1024]{2,1,0:T(8,128)(2,1)S(1)}, bf16[1,32,1024]{2,1,0:T(8,128)(2,1)S(1)}, u32[]{:S(2)}, u32[]{:S(2)}) collective-permute-start(bf16[1,32,1024]{2,1,0:T(8,128)(2,1)S(1)} %get-tuple-element.154), channel_id=1, source_target_pairs={{0,8},{1,9},{2,10},{3,11},{4,12},{5,13},{6,14},{7,15},{8,0},{9,1},... | collective-permute-start | bytes 196616 | tf_op jit(solution)/shard_map/ppermute | solution.py:389
  98.8 9.8 %collective-permute-start.17 = (bf16[2,32,1024]{2,1,0:T(8,128)(2,1)S(1)}, bf16[2,32,1024]{2,1,0:T(8,128)(2,1)S(1)}, u32[]{:S(2)}, u32[]{:S(2)}) collective-permute-start(bf16[2,32,1024]{2,1,0:T(8,128)(2,1)S(1)} %constant_dynamic-update-slice_fusion), channel_id=1, source_target_pairs={{0,4},{1,5},{2,6},{3,7},{4,0},{5,1},{6,2},{7,3},{8,12},{9,13},{10,... | collective-permute-start | bytes 393224 | tf_op jit(solution)/shard_map/ppermute | solution.py:389
  100.7 6.2 %collective-permute-start.18 = (bf16[2,32,1024]{2,1,0:T(8,128)(2,1)S(1)}, bf16[2,32,1024]{2,1,0:T(8,128)(2,1)S(1)}, u32[]{:S(2)}, u32[]{:S(2)}) collective-permute-start(bf16[2,32,1024]{2,1,0:T(8,128)(2,1)S(1)} %constant_dynamic-update-slice_fusion.2), channel_id=1, source_target_pairs={{0,2},{1,3},{2,0},{3,1},{4,6},{5,7},{6,4},{7,5},{8,10},{9,11},{10,... | collective-permute-start | bytes 393224 | tf_op jit(solution)/shard_map/ppermute | solution.py:389
  102.1 6.6 %collective-permute-start.16 = (bf16[1,32,1024]{2,1,0:T(8,128)(2,1)S(1)}, bf16[1,32,1024]{2,1,0:T(8,128)(2,1)S(1)}, u32[]{:S(2)}, u32[]{:S(2)}) collective-permute-start(bf16[1,32,1024]{2,1,0:T(8,128)(2,1)S(1)} %get-tuple-element.153), channel_id=1, source_target_pairs={{0,8},{1,9},{2,10},{3,11},{4,12},{5,13},{6,14},{7,15},{8,0},{9,1},... | collective-permute-start | bytes 196616 | tf_op jit(solution)/shard_map/ppermute | solution.py:389
  105.4 6.5 %collective-permute-start.21 = (bf16[1,32,1024]{2,1,0:T(8,128)(2,1)S(1)}, bf16[1,32,1024]{2,1,0:T(8,128)(2,1)S(1)}, u32[]{:S(2)}, u32[]{:S(2)}) collective-permute-start(bf16[1,32,1024]{2,1,0:T(8,128)(2,1)S(1)} %bitcast.28), channel_id=1, source_target_pairs={{0,8},{1,9},{2,10},{3,11},{4,12},{5,13},{6,14},{7,15},{8,0},{9,1},... | collective-permute-start | bytes 196616 | tf_op jit(solution)/shard_map/ppermute | solution.py:389
  107.0 10.1 %collective-permute-start.23 = (bf16[4,32,1024]{2,1,0:T(8,128)(2,1)S(1)}, bf16[4,32,1024]{2,1,0:T(8,128)(2,1)S(1)}, u32[]{:S(2)}, u32[]{:S(2)}) collective-permute-start(bf16[4,32,1024]{2,1,0:T(8,128)(2,1)S(1)} %constant_dynamic-update-slice_fusion.4), channel_id=1, source_target_pairs={{0,4},{1,5},{2,6},{3,7},{4,0},{5,1},{6,2},{7,3},{8,12},{9,13},{10,... | collective-permute-start | bytes 786440 | tf_op jit(solution)/shard_map/ppermute | solution.py:389
  108.6 11.4 %collective-permute-start.27 = (bf16[4,32,1024]{2,1,0:T(8,128)(2,1)S(1)}, bf16[4,32,1024]{2,1,0:T(8,128)(2,1)S(1)}, u32[]{:S(2)}, u32[]{:S(2)}) collective-permute-start(bf16[4,32,1024]{2,1,0:T(8,128)(2,1)S(1)} %constant_dynamic-update-slice_fusion.6), channel_id=1, source_target_pairs={{0,2},{1,3},{2,0},{3,1},{4,6},{5,7},{6,4},{7,5},{8,10},{9,11},{10,... | collective-permute-start | bytes 786440 | tf_op jit(solution)/shard_map/ppermute | solution.py:389
  109.6 5.3 %collective-permute-start.20 = (bf16[1,32,1024]{2,1,0:T(8,128)(2,1)S(1)}, bf16[1,32,1024]{2,1,0:T(8,128)(2,1)S(1)}, u32[]{:S(2)}, u32[]{:S(2)}) collective-permute-start(bf16[1,32,1024]{2,1,0:T(8,128)(2,1)S(1)} %bitcast.30), channel_id=1, source_target_pairs={{0,8},{1,9},{2,10},{3,11},{4,12},{5,13},{6,14},{7,15},{8,0},{9,1},... | collective-permute-start | bytes 196616 | tf_op jit(solution)/shard_map/ppermute | solution.py:389
  112.0 5.1 %collective-permute-start.24 = (bf16[2,32,1024]{2,1,0:T(8,128)(2,1)S(1)}, bf16[2,32,1024]{2,1,0:T(8,128)(2,1)S(1)}, u32[]{:S(2)}, u32[]{:S(2)}) collective-permute-start(bf16[2,32,1024]{2,1,0:T(8,128)(2,1)S(1)} %constant_dynamic-update-slice_fusion.8), channel_id=1, source_target_pairs={{0,2},{1,3},{2,0},{3,1},{4,6},{5,7},{6,4},{7,5},{8,10},{9,11},{10,... | collective-permute-start | bytes 393224 | tf_op jit(solution)/shard_map/ppermute | solution.py:389
  115.0 5.1 %collective-permute-start.22 = (bf16[2,32,1024]{2,1,0:T(8,128)(2,1)S(1)}, bf16[2,32,1024]{2,1,0:T(8,128)(2,1)S(1)}, u32[]{:S(2)}, u32[]{:S(2)}) collective-permute-start(bf16[2,32,1024]{2,1,0:T(8,128)(2,1)S(1)} %constant_dynamic-update-slice_fusion.10), channel_id=1, source_target_pairs={{0,4},{1,5},{2,6},{3,7},{4,0},{5,1},{6,2},{7,3},{8,12},{9,13},{10,... | collective-permute-start | bytes 393224 | tf_op jit(solution)/shard_map/ppermute | solution.py:389
  117.2 6.2 %collective-permute-start.29 = (bf16[8,32,1024]{2,1,0:T(8,128)(2,1)S(1)}, bf16[8,32,1024]{2,1,0:T(8,128)(2,1)S(1)}, u32[]{:S(2)}, u32[]{:S(2)}) collective-permute-start(bf16[8,32,1024]{2,1,0:T(8,128)(2,1)S(1)} %constant_dynamic-update-slice_fusion.14.own_ref), channel_id=1, source_target_pairs={{0,1},{1,0},{2,3},{3,2},{4,5},{5,4},{6,7},{7,6},{8,9},{9,8},{10,11... | collective-permute-start | bytes 1572872 | tf_op jit(solution)/shard_map/ppermute | solution.py:389
  120.1 4.9 %collective-permute-start.28 = (bf16[8,32,1024]{2,1,0:T(8,128)(2,1)S(1)}, bf16[8,32,1024]{2,1,0:T(8,128)(2,1)S(1)}, u32[]{:S(2)}, u32[]{:S(2)}) collective-permute-start(bf16[8,32,1024]{2,1,0:T(8,128)(2,1)S(1)} %constant_dynamic-update-slice_fusion.18.own_ref), channel_id=1, source_target_pairs={{0,1},{1,0},{2,3},{3,2},{4,5},{5,4},{6,7},{7,6},{8,9},{9,8},{10,11... | collective-permute-start | bytes 1572872 | tf_op jit(solution)/shard_map/ppermute | solution.py:389
  120.2 9.0 %collective-permute-start.26 = (bf16[4,32,1024]{2,1,0:T(8,128)(2,1)S(1)}, bf16[4,32,1024]{2,1,0:T(8,128)(2,1)S(1)}, u32[]{:S(2)}, u32[]{:S(2)}) collective-permute-start(bf16[4,32,1024]{2,1,0:T(8,128)(2,1)S(1)} %constant_dynamic-update-slice_fusion.12), channel_id=1, source_target_pairs={{0,4},{1,5},{2,6},{3,7},{4,0},{5,1},{6,2},{7,3},{8,12},{9,13},{10,... | collective-permute-start | bytes 786440 | tf_op jit(solution)/shard_map/ppermute | solution.py:389
  122.3 8.4 %collective-permute-start.25 = (bf16[4,32,1024]{2,1,0:T(8,128)(2,1)S(1)}, bf16[4,32,1024]{2,1,0:T(8,128)(2,1)S(1)}, u32[]{:S(2)}, u32[]{:S(2)}) collective-permute-start(bf16[4,32,1024]{2,1,0:T(8,128)(2,1)S(1)} %constant_dynamic-update-slice_fusion.16), channel_id=1, source_target_pairs={{0,2},{1,3},{2,0},{3,1},{4,6},{5,7},{6,4},{7,5},{8,10},{9,11},{10,... | collective-permute-start | bytes 786440 | tf_op jit(solution)/shard_map/ppermute | solution.py:389
  129.2 2.3 %collective-permute-start.31 = (bf16[8,32,1024]{2,1,0:T(8,128)(2,1)S(1)}, bf16[8,32,1024]{2,1,0:T(8,128)(2,1)S(1)}, u32[]{:S(2)}, u32[]{:S(2)}) collective-permute-start(bf16[8,32,1024]{2,1,0:T(8,128)(2,1)S(1)} %constant_dynamic-update-slice_fusion.20.own_ref), channel_id=1, source_target_pairs={{0,1},{1,0},{2,3},{3,2},{4,5},{5,4},{6,7},{7,6},{8,9},{9,8},{10,11... | collective-permute-start | bytes 1572872 | tf_op jit(solution)/shard_map/ppermute | solution.py:389
  130.7 2.5 %collective-permute-start.30 = (bf16[8,32,1024]{2,1,0:T(8,128)(2,1)S(1)}, bf16[8,32,1024]{2,1,0:T(8,128)(2,1)S(1)}, u32[]{:S(2)}, u32[]{:S(2)}) collective-permute-start(bf16[8,32,1024]{2,1,0:T(8,128)(2,1)S(1)} %constant_dynamic-update-slice_fusion.22.own_ref), channel_id=1, source_target_pairs={{0,1},{1,0},{2,3},{3,2},{4,5},{5,4},{6,7},{7,6},{8,9},{9,8},{10,11... | collective-permute-start | bytes 1572872 | tf_op jit(solution)/shard_map/ppermute | solution.py:389

commit v5 on v4

--- a/solution.py
+++ b/solution.py
@@ -112,7 +112,7 @@
     depth = columns // 8
     chunks = columns // depth
     vmem = pl.BlockSpec(memory_space=pltpu.VMEM)
-    whole = pl.BlockSpec(memory_space=pltpu.HBM)
+    whole = pl.BlockSpec(memory_space=pl.ANY)
     return pl.pallas_call(
         functools.partial(input_kernel, count),
         out_shape=jax.ShapeDtypeStruct((count, rows // count, width + HD), jnp.bfloat16),
@@ -129,7 +129,7 @@
             pltpu.SemaphoreType.DMA((chunks,)),
             pltpu.SemaphoreType.DMA,
         ],
-        compiler_params=pltpu.CompilerParams(vmem_limit_bytes=40 * 1024 * 1024),
+        compiler_params=pltpu.CompilerParams(vmem_limit_bytes=60 * 1024 * 1024),
         cost_estimate=pl.CostEstimate(
             flops=2 * rows * columns * (width + kv_width),
             bytes_accessed=2 * columns * (rows + width + kv_width),
@@ -245,7 +245,7 @@
     width = blocks.shape[2] - HD
     heads = count * width // HD
     vmem = pl.BlockSpec(memory_space=pltpu.VMEM)
-    whole = pl.BlockSpec(memory_space=pltpu.HBM)
+    whole = pl.BlockSpec(memory_space=pl.ANY)
     return pl.pallas_call(
         functools.partial(attend_kernel, count),
         out_shape=jax.ShapeDtypeStruct((count, here, width), jnp.bfloat16),
@@ -261,7 +261,7 @@
             pltpu.SemaphoreType.DMA((here,)),
             pltpu.SemaphoreType.DMA((here,)),
         ],
-        compiler_params=pltpu.CompilerParams(vmem_limit_bytes=40 * 1024 * 1024),
+        compiler_params=pltpu.CompilerParams(vmem_limit_bytes=56 * 1024 * 1024),
         cost_estimate=pl.CostEstimate(
             flops=4 * here * count * width * span,
             bytes_accessed=4 * here * span * key_width,
@@ -271,7 +271,14 @@
 
 
 def exchange(blocks):
-    return lax.all_to_all(blocks, "tensor", split_axis=0, concat_axis=0, tiled=True)
+    count, inner = blocks.shape[0], 4
+    outer = count // inner
+    near = [[o * inner + i for i in range(inner)] for o in range(outer)]
+    far = [[o * inner + i for o in range(outer)] for i in range(inner)]
+    square = blocks.reshape(outer, inner, *blocks.shape[1:])
+    square = lax.all_to_all(square, "tensor", 1, 1, axis_index_groups=near, tiled=True)
+    square = lax.all_to_all(square, "tensor", 0, 0, axis_index_groups=far, tiled=True)
+    return square.reshape(blocks.shape)
 
 
 def plans(count):
@@ -331,14 +338,14 @@
     return pl.pallas_call(
         functools.partial(project_kernel, count, offsets),
         out_shape=(share,) * sets,
-        in_specs=[pl.BlockSpec(memory_space=pltpu.HBM), pl.BlockSpec(memory_space=pltpu.VMEM)],
+        in_specs=[pl.BlockSpec(memory_space=pl.ANY), pl.BlockSpec(memory_space=pltpu.VMEM)],
         out_specs=(pl.BlockSpec(memory_space=pltpu.VMEM),) * sets,
         scratch_shapes=[
             pltpu.VMEM((rows, depth), jnp.float32),
             pltpu.VMEM((len(offsets), depth, width), jnp.bfloat16),
             pltpu.SemaphoreType.DMA((len(offsets),)),
         ],
-        compiler_params=pltpu.CompilerParams(vmem_limit_bytes=30 * 1024 * 1024),
+        compiler_params=pltpu.CompilerParams(vmem_limit_bytes=49 * 1024 * 1024),
         cost_estimate=pl.CostEstimate(
             flops=2 * rows * depth * width * len(offsets),
             bytes_accessed=2 * (depth + rows) * width * len(offsets),

time: 135 us -> 139 us (1.030)
  local copies, waits for them, and re-layouts: 16.6 us -> 3.59 us
  blocking collectives: 26.2 us -> 36.3 us
  Pallas kernels: 29.7 us -> 34.8 us
    unnamed x28 -> x14, local copies, waits for them, and re-layouts: 15.5 us -> 0.14 us
    all_to_all x2 -> x4, blocking collectives: 26.2 us -> 36.3 us  [the longest x2 20.3 us: exchange(): lax.all_to_all(square, 'tensor', 0, 0, axis_index_groups=far, tiled=True)]
    pallas_call x1, Pallas kernels: 8.23 us -> 11.8 us  [project_in(): pl.pallas_call(functools.partial(input_kernel, count), out_shape=jax.Shap...]
    pallas_call x1, Pallas kernels: 6.62 us -> 8.67 us  [attend(): pl.pallas_call(functools.partial(attend_kernel, count), out_shape=jax.Sha...]
    reshape x0 -> x2, local copies, waits for them, and re-layouts: none -> 1.85 us  [exchange(): square = blocks.reshape(outer, inner, *blocks.shape[1:])]
  transfers between devices with their start and end apart: 32 -> 32, of which waited for: 12 -> 12; matrix products, arithmetic and copies ran while one was open for 4% -> 4% of each run, Pallas kernels for 7% -> 6%
where the time goes in v5:
time: 139 us
  blocking collectives  36.3 us (26%)
  Pallas kernels  34.8 us (25%)
  waiting for transfers between devices  29.3 us (21%)
  starting transfers between devices  26.6 us (19%)
  other arithmetic  6.99 us (5%)
  local copies, waits for them, and re-layouts  3.59 us (3%)
    ppermute x32, waiting for transfers between devices, swap(): lax.ppermute(values, 'tensor', [(i, i ^ 1 << bit) for i in range(count)])  29.3 us
    ppermute x32, starting transfers between devices, swap(): lax.ppermute(values, 'tensor', [(i, i ^ 1 << bit) for i in range(count)])  26.6 us
    all_to_all x2, blocking collectives, exchange(): lax.all_to_all(square, 'tensor', 0, 0, axis_index_groups=far, tiled=True)  20.3 us
    all_to_all x2, blocking collectives, exchange(): lax.all_to_all(square, 'tensor', 1, 1, axis_index_groups=near, tiled=True)  16 us
    pallas_call x1, Pallas kernels, project_in(): pl.pallas_call(functools.partial(input_kernel, count), out_shape=jax.Shap...  11.8 us
    pallas_call x1, Pallas kernels, attend(): pl.pallas_call(functools.partial(attend_kernel, count), out_shape=jax.Sha...  8.67 us
    pallas_call x2, Pallas kernels, project(): pl.pallas_call(functools.partial(project_kernel, count, offsets), out_sha...  7.66 us
    pallas_call x4, Pallas kernels, finish(): pl.pallas_call(functools.partial(finish_kernel, offsets), grid=(1,), out_...  6.61 us
  transfers between devices with their start and end apart: 32, of which 12 were waited for; matrix products, arithmetic and copies ran while one was open for 4% of the time, Pallas kernels for 6%

profile of v5, /device:TPU:0, one launch (start us, length us, event | category | flops | bytes accessed | tf_op | source)
XLA Modules:
  0.0 138.5 jit_solution(17762528648700167506)
XLA Ops:
  0.6 0.7 convert_element_type.284
  1.3 1.4 %reshape.54.gain_ref = bf16[1,16384]{1,0:T(2,128)(2,1)} reshape(bf16[16384]{0:T(1024)(128)(2,1)} %param.11) | data formatting | bytes 65536 | tf_op jit(solution)/shard_map/reshape | solution.py:420
  2.7 1.0 fusion.4
  3.7 11.8 %shard_map.113 = bf16[16,8,640]{2,1,0:T(8,128)(2,1)} custom-call(bf16[128,16384]{1,0:T(8,128)(2,1)} %hidden_ref.1, bf16[1,16384]{1,0:T(2,128)(2,1)} %reshape.54.gain_ref, bf16[16384,512]{1,0:T(8,128)(2,1)} %w_ref.3, bf16[64,16384]{1,0:T(8,128)(2,1)} %bitcast.27, f32[128,128]{1,0:T(8,128)} %get-tuple-element.161.cosine_ref, ...), custom_call_target="tpu_custom_call" | custom-call | flops 2415919104 | bytes 23068672 | tf_op jit(solution)/shard_map/pallas_call | solution.py:116
  15.5 0.9 copy.19
  16.5 9.0 %all_to_all.20 = bf16[4,4,8,640]{3,2,0,1:T(8,128)(2,1)S(1)} all-to-all(bf16[4,4,8,640]{3,2,0,1:T(8,128)(2,1)S(1)} %copy.19), channel_id=1, replica_groups={{0,1,2,3},{4,5,6,7},{8,9,10,11},{12,13,14,15},{16,17,18,19},{20,21,22,2..., dimensions={1} | all-to-all | bytes 327680 | tf_op jit(solution)/shard_map/all_to_all | solution.py:279
  25.5 11.8 %all_to_all.21 = bf16[4,4,8,640]{3,2,1,0:T(8,128)(2,1)} all-to-all(bf16[4,4,8,640]{3,2,1,0:T(8,128)(2,1)S(1)} %copy.20), channel_id=1, replica_groups={{0,4,8,12},{1,5,9,13},{2,6,10,14},{3,7,11,15},{16,20,24,28},{17,21,25,2..., dimensions={0} | all-to-all | bytes 327680 | tf_op jit(solution)/shard_map/all_to_all | solution.py:280
  37.3 8.7 %shard_map.114 = bf16[16,8,512]{2,1,0:T(8,128)(2,1)} custom-call(s32[8]{0:T(128)} %lengths_ref.1, f32[128,128]{1,0:T(8,128)} %get-tuple-element.161.cosine_ref, f32[128,128]{1,0:T(8,128)} %get-tuple-element.160.sine_ref, bf16[8,1024,512]{2,1,0:T(8,128)(2,1)} %keys_ref.1, bf16[8,1024,512]{2,1,0:T(8,128)(2,1)} %values_ref.1, bf16[16,8,640]{2,1,0:T(8,128)(2,1)} %bitcast.28), custom_call_target="tpu_custom_call" | custom-call | flops 268435456 | bytes 16777216 | tf_op jit(solution)/shard_map/pallas_call | solution.py:249
  45.9 0.9 copy.21
  46.9 7.0 %all_to_all.22 = bf16[4,4,8,512]{3,2,0,1:T(8,128)(2,1)S(1)} all-to-all(bf16[4,4,8,512]{3,2,0,1:T(8,128)(2,1)S(1)} %copy.21), channel_id=1, replica_groups={{0,1,2,3},{4,5,6,7},{8,9,10,11},{12,13,14,15},{16,17,18,19},{20,21,22,2..., dimensions={1} | all-to-all | bytes 262144 | tf_op jit(solution)/shard_map/all_to_all | solution.py:279
  53.9 8.5 %all_to_all.23 = bf16[4,4,8,512]{3,2,1,0:T(8,128)(2,1)S(1)} all-to-all(bf16[4,4,8,512]{3,2,1,0:T(8,128)(2,1)S(1)} %copy.22), channel_id=1, replica_groups={{0,4,8,12},{1,5,9,13},{2,6,10,14},{3,7,11,15},{16,20,24,28},{17,21,25,2..., dimensions={0} | all-to-all | bytes 262144 | tf_op jit(solution)/shard_map/all_to_all | solution.py:280
  62.4 3.8 %shard_map.116 = (bf16[8,32,1024]{2,1,0:T(8,128)(2,1)S(1)}, bf16[8,32,1024]{2,1,0:T(8,128)(2,1)S(1)}, bf16[8,32,1024]{2,1,0:T(8,128)(2,1)S(1)}, bf16[8,32,1024]{2,1,0:T(8,128)(2,1)S(1)}) custom-call(bf16[512,16384]{1,0:T(8,128)(2,1)} %w_ref.5, bf16[16,8,512]{2,1,0:T(8,128)(2,1)S(1)} %bitcast.25), custom_call_target="tpu_custom_call" | custom-call | flops 1073741824 | bytes 10485760 | tf_op jit(solution)/shard_map/pallas_call | solution.py:338
  66.3 0.5 collective-permute-start
  66.8 0.1 collective-permute-start.3
  66.9 3.8 %shard_map.115 = (bf16[8,32,1024]{2,1,0:T(8,128)(2,1)S(1)}, bf16[8,32,1024]{2,1,0:T(8,128)(2,1)S(1)}, bf16[8,32,1024]{2,1,0:T(8,128)(2,1)S(1)}, bf16[8,32,1024]{2,1,0:T(8,128)(2,1)S(1)}) custom-call(bf16[512,16384]{1,0:T(8,128)(2,1)} %w_ref.5, bf16[16,8,512]{2,1,0:T(8,128)(2,1)S(1)} %bitcast.26), custom_call_target="tpu_custom_call" | custom-call | flops 1073741824 | bytes 10485760 | tf_op jit(solution)/shard_map/pallas_call | solution.py:338
  70.8 0.5 collective-permute-start.7
  71.3 0.2 add_convert_fusion.3
  71.4 0.5 collective-permute-start.4
  72.0 0.2 add_convert_fusion.6
  72.2 1.1 collective-permute-start.2
  73.3 0.2 add_convert_fusion
  73.5 0.2 add_convert_fusion.2
  73.7 6.2 %collective-permute-done.4 = bf16[4,32,1024]{2,1,0:T(8,128)(2,1)S(1)} collective-permute-done((bf16[4,32,1024]{2,1,0:T(8,128)(2,1)S(1)}, bf16[4,32,1024]{2,1,0:T(8,128)(2,1)S(1)}, u32[]{:S(2)}, u32[]{:S(2)}) %collective-permute-start.4) | collective-permute-done | bytes 262176 | tf_op jit(solution)/shard_map/ppermute | solution.py:396
  79.9 1.2 collective-permute-start.6
  81.0 0.4 collective-permute-start.10
  81.5 1.7 %collective-permute-start.5 = (bf16[2,32,1024]{2,1,0:T(8,128)(2,1)S(1)}, bf16[2,32,1024]{2,1,0:T(8,128)(2,1)S(1)}, u32[]{:S(2)}, u32[]{:S(2)}) collective-permute-start(bf16[2,32,1024]{2,1,0:T(8,128)(2,1)S(1)} %get-tuple-element.149), channel_id=1, source_target_pairs={{0,2},{1,3},{2,0},{3,1},{4,6},{5,7},{6,4},{7,5},{8,10},{9,11},{10,... | collective-permute-start | bytes 393224 | tf_op jit(solution)/shard_map/ppermute | solution.py:396
  83.2 0.9 collective-permute-start.9
  84.1 1.5 %collective-permute-done.6 = bf16[2,32,1024]{2,1,0:T(8,128)(2,1)S(1)} collective-permute-done((bf16[2,32,1024]{2,1,0:T(8,128)(2,1)S(1)}, bf16[2,32,1024]{2,1,0:T(8,128)(2,1)S(1)}, u32[]{:S(2)}, u32[]{:S(2)}) %collective-permute-start.6) | collective-permute-done | bytes 131104 | tf_op jit(solution)/shard_map/ppermute | solution.py:396
  85.7 0.7 collective-permute-start.11
  86.4 4.6 %collective-permute-done.5 = bf16[2,32,1024]{2,1,0:T(8,128)(2,1)S(1)} collective-permute-done((bf16[2,32,1024]{2,1,0:T(8,128)(2,1)S(1)}, bf16[2,32,1024]{2,1,0:T(8,128)(2,1)S(1)}, u32[]{:S(2)}, u32[]{:S(2)}) %collective-permute-start.5) | collective-permute-done | bytes 131104 | tf_op jit(solution)/shard_map/ppermute | solution.py:396
  91.1 0.9 collective-permute-start.8
  92.0 0.9 fusion.3
  92.8 2.5 %collective-permute-start.14 = (bf16[1,32,1024]{2,1,0:T(8,128)(2,1)S(1)}, bf16[1,32,1024]{2,1,0:T(8,128)(2,1)S(1)}, u32[]{:S(2)}, u32[]{:S(2)}) collective-permute-start(bf16[1,32,1024]{2,1,0:T(8,128)(2,1)S(1)} %bitcast.30), channel_id=1, source_target_pairs={{0,8},{1,9},{2,10},{3,11},{4,12},{5,13},{6,14},{7,15},{8,0},{9,1},... | collective-permute-start | bytes 196616 | tf_op jit(solution)/shard_map/ppermute | solution.py:396
  95.4 0.6 collective-permute-start.12
  96.1 0.5 collective-permute-start.15
  96.7 0.9 fusion.2
  97.6 1.3 collective-permute-start.13
  98.8 2.3 %collective-permute-done.15 = bf16[2,32,1024]{2,1,0:T(8,128)(2,1)S(1)} collective-permute-done((bf16[2,32,1024]{2,1,0:T(8,128)(2,1)S(1)}, bf16[2,32,1024]{2,1,0:T(8,128)(2,1)S(1)}, u32[]{:S(2)}, u32[]{:S(2)}) %collective-permute-start.15) | collective-permute-done | bytes 131104 | tf_op jit(solution)/shard_map/ppermute | solution.py:396
  101.2 0.8 collective-permute-start.19
  102.0 1.2 collective-permute-start.17
  103.3 0.5 collective-permute-done.13
  103.8 0.6 collective-permute-start.18
  104.5 1.5 %collective-permute-start.16 = (bf16[1,32,1024]{2,1,0:T(8,128)(2,1)S(1)}, bf16[1,32,1024]{2,1,0:T(8,128)(2,1)S(1)}, u32[]{:S(2)}, u32[]{:S(2)}) collective-permute-start(bf16[1,32,1024]{2,1,0:T(8,128)(2,1)S(1)} %get-tuple-element.153), channel_id=1, source_target_pairs={{0,8},{1,9},{2,10},{3,11},{4,12},{5,13},{6,14},{7,15},{8,0},{9,1},... | collective-permute-start | bytes 196616 | tf_op jit(solution)/shard_map/ppermute | solution.py:396
  106.0 2.0 %collective-permute-done.19 = bf16[1,32,1024]{2,1,0:T(8,128)(2,1)S(1)} collective-permute-done((bf16[1,32,1024]{2,1,0:T(8,128)(2,1)S(1)}, bf16[1,32,1024]{2,1,0:T(8,128)(2,1)S(1)}, u32[]{:S(2)}, u32[]{:S(2)}) %collective-permute-start.19) | collective-permute-done | bytes 65568 | tf_op jit(solution)/shard_map/ppermute | solution.py:396
  108.0 0.9 fusion.1
  108.9 1.1 collective-permute-done.18
  110.0 1.6 %collective-permute-start.23 = (bf16[4,32,1024]{2,1,0:T(8,128)(2,1)S(1)}, bf16[4,32,1024]{2,1,0:T(8,128)(2,1)S(1)}, u32[]{:S(2)}, u32[]{:S(2)}) collective-permute-start(bf16[4,32,1024]{2,1,0:T(8,128)(2,1)S(1)} %constant_dynamic-update-slice_fusion.4), channel_id=1, source_target_pairs={{0,4},{1,5},{2,6},{3,7},{4,0},{5,1},{6,2},{7,3},{8,12},{9,13},{10,... | collective-permute-start | bytes 786440 | tf_op jit(solution)/shard_map/ppermute | solution.py:396
  111.6 1.2 collective-permute-start.27
  112.8 0.9 fusion
  113.6 0.9 collective-permute-start.20
  114.5 0.7 collective-permute-done.21
  115.2 1.0 collective-permute-start.24
  116.3 2.7 %collective-permute-done.20 = bf16[1,32,1024]{2,1,0:T(8,128)(2,1)S(1)} collective-permute-done((bf16[1,32,1024]{2,1,0:T(8,128)(2,1)S(1)}, bf16[1,32,1024]{2,1,0:T(8,128)(2,1)S(1)}, u32[]{:S(2)}, u32[]{:S(2)}) %collective-permute-start.20) | collective-permute-done | bytes 65568 | tf_op jit(solution)/shard_map/ppermute | solution.py:396
  119.0 1.8 %collective-permute-start.22 = (bf16[2,32,1024]{2,1,0:T(8,128)(2,1)S(1)}, bf16[2,32,1024]{2,1,0:T(8,128)(2,1)S(1)}, u32[]{:S(2)}, u32[]{:S(2)}) collective-permute-start(bf16[2,32,1024]{2,1,0:T(8,128)(2,1)S(1)} %constant_dynamic-update-slice_fusion.10), channel_id=1, source_target_pairs={{0,4},{1,5},{2,6},{3,7},{4,0},{5,1},{6,2},{7,3},{8,12},{9,13},{10,... | collective-permute-start | bytes 393224 | tf_op jit(solution)/shard_map/ppermute | solution.py:396
  121.0 3.1 %collective-permute-done.22 = bf16[2,32,1024]{2,1,0:T(8,128)(2,1)S(1)} collective-permute-done((bf16[2,32,1024]{2,1,0:T(8,128)(2,1)S(1)}, bf16[2,32,1024]{2,1,0:T(8,128)(2,1)S(1)}, u32[]{:S(2)}, u32[]{:S(2)}) %collective-permute-start.22) | collective-permute-done | bytes 131104 | tf_op jit(solution)/shard_map/ppermute | solution.py:396
  124.2 1.8 %collective-permute-start.26 = (bf16[4,32,1024]{2,1,0:T(8,128)(2,1)S(1)}, bf16[4,32,1024]{2,1,0:T(8,128)(2,1)S(1)}, u32[]{:S(2)}, u32[]{:S(2)}) collective-permute-start(bf16[4,32,1024]{2,1,0:T(8,128)(2,1)S(1)} %constant_dynamic-update-slice_fusion.12), channel_id=1, source_target_pairs={{0,4},{1,5},{2,6},{3,7},{4,0},{5,1},{6,2},{7,3},{8,12},{9,13},{10,... | collective-permute-start | bytes 786440 | tf_op jit(solution)/shard_map/ppermute | solution.py:396
  126.0 0.3 collective-permute-start.25
  126.4 1.7 %shard_map.117.refs_0_ = bf16[128,16384]{1,0:T(8,128)(2,1)} custom-call(bf16[8,32,1024]{2,1,0:T(8,128)(2,1)S(1)} %constant_dynamic-update-slice_fusion.14.own_ref, bf16[8,32,1024]{2,1,0:T(8,128)(2,1)S(1)} %collective-permute-done.29.other_ref, f32[16,1024]{1,0:T(8,128)S(1)} %reshape.62.gain_ref), custom_call_target="tpu_custom_call" | custom-call | flops 3145728 | bytes 2097152 | tf_op jit(solution)/shard_map/pallas_call | solution.py:381
  128.0 1.7 %shard_map.118.refs_0_ = bf16[128,16384]{1,0:T(8,128)(2,1)} custom-call(bf16[8,32,1024]{2,1,0:T(8,128)(2,1)S(1)} %constant_dynamic-update-slice_fusion.18.own_ref, bf16[8,32,1024]{2,1,0:T(8,128)(2,1)S(1)} %collective-permute-done.28.other_ref, f32[16,1024]{1,0:T(8,128)S(1)} %reshape.62.gain_ref, ...), custom_call_target="tpu_custom_call", output_to_operand_aliasing={{}: (3, {})} | custom-call | flops 3145728 | bytes 2097152 | tf_op jit(solution)/shard_map/pallas_call | solution.py:381
  129.7 3.2 %collective-permute-done.26 = bf16[4,32,1024]{2,1,0:T(8,128)(2,1)S(1)} collective-permute-done((bf16[4,32,1024]{2,1,0:T(8,128)(2,1)S(1)}, bf16[4,32,1024]{2,1,0:T(8,128)(2,1)S(1)}, u32[]{:S(2)}, u32[]{:S(2)}) %collective-permute-start.26) | collective-permute-done | bytes 262176 | tf_op jit(solution)/shard_map/ppermute | solution.py:396
  133.0 1.3 collective-permute-done.25
  134.5 0.7 pad_maximum_fusion
  135.2 1.7 %shard_map.119.refs_0_ = bf16[128,16384]{1,0:T(8,128)(2,1)} custom-call(bf16[8,32,1024]{2,1,0:T(8,128)(2,1)S(1)} %constant_dynamic-update-slice_fusion.20.own_ref, bf16[8,32,1024]{2,1,0:T(8,128)(2,1)S(1)} %collective-permute-done.31.other_ref, f32[16,1024]{1,0:T(8,128)S(1)} %reshape.62.gain_ref, ...), custom_call_target="tpu_custom_call", output_to_operand_aliasing={{}: (3, {})} | custom-call | flops 3145728 | bytes 2097152 | tf_op jit(solution)/shard_map/pallas_call | solution.py:381
  136.9 1.7 %shard_map.120 = bf16[128,16384]{1,0:T(8,128)(2,1)} custom-call(bf16[8,32,1024]{2,1,0:T(8,128)(2,1)S(1)} %constant_dynamic-update-slice_fusion.22.own_ref, bf16[8,32,1024]{2,1,0:T(8,128)(2,1)S(1)} %collective-permute-done.30.other_ref, f32[16,1024]{1,0:T(8,128)S(1)} %reshape.62.gain_ref, ...), custom_call_target="tpu_custom_call", output_to_operand_aliasing={{}: (3, {})} | custom-call | flops 3145728 | bytes 2097152 | tf_op jit(solution)/shard_map/pallas_call | solution.py:381
  (64 shorter events, 1.2 us)
Async XLA Ops:
  66.3 5.0 %collective-permute-start.1 = (bf16[8,32,1024]{2,1,0:T(8,128)(2,1)S(1)}, bf16[8,32,1024]{2,1,0:T(8,128)(2,1)S(1)}, u32[]{:S(2)}, u32[]{:S(2)}) collective-permute-start(bf16[8,32,1024]{2,1,0:T(8,128)(2,1)S(1)} %get-tuple-element.72), channel_id=1, source_target_pairs={{0,1},{1,0},{2,3},{3,2},{4,5},{5,4},{6,7},{7,6},{8,9},{9,8},{10,11... | collective-permute-start | bytes 1572872 | tf_op jit(solution)/shard_map/ppermute | solution.py:396
  66.3 5.7 %collective-permute-start = (bf16[8,32,1024]{2,1,0:T(8,128)(2,1)S(1)}, bf16[8,32,1024]{2,1,0:T(8,128)(2,1)S(1)}, u32[]{:S(2)}, u32[]{:S(2)}) collective-permute-start(bf16[8,32,1024]{2,1,0:T(8,128)(2,1)S(1)} %get-tuple-element.70), channel_id=1, source_target_pairs={{0,1},{1,0},{2,3},{3,2},{4,5},{5,4},{6,7},{7,6},{8,9},{9,8},{10,11... | collective-permute-start | bytes 1572872 | tf_op jit(solution)/shard_map/ppermute | solution.py:396
  66.8 6.4 %collective-permute-start.3 = (bf16[8,32,1024]{2,1,0:T(8,128)(2,1)S(1)}, bf16[8,32,1024]{2,1,0:T(8,128)(2,1)S(1)}, u32[]{:S(2)}, u32[]{:S(2)}) collective-permute-start(bf16[8,32,1024]{2,1,0:T(8,128)(2,1)S(1)} %get-tuple-element.75), channel_id=1, source_target_pairs={{0,1},{1,0},{2,3},{3,2},{4,5},{5,4},{6,7},{7,6},{8,9},{9,8},{10,11... | collective-permute-start | bytes 1572872 | tf_op jit(solution)/shard_map/ppermute | solution.py:396
  70.8 2.7 %collective-permute-start.7 = (bf16[8,32,1024]{2,1,0:T(8,128)(2,1)S(1)}, bf16[8,32,1024]{2,1,0:T(8,128)(2,1)S(1)}, u32[]{:S(2)}, u32[]{:S(2)}) collective-permute-start(bf16[8,32,1024]{2,1,0:T(8,128)(2,1)S(1)} %get-tuple-element.82), channel_id=1, source_target_pairs={{0,1},{1,0},{2,3},{3,2},{4,5},{5,4},{6,7},{7,6},{8,9},{9,8},{10,11... | collective-permute-start | bytes 1572872 | tf_op jit(solution)/shard_map/ppermute | solution.py:396
  71.4 8.4 %collective-permute-start.4 = (bf16[4,32,1024]{2,1,0:T(8,128)(2,1)S(1)}, bf16[4,32,1024]{2,1,0:T(8,128)(2,1)S(1)}, u32[]{:S(2)}, u32[]{:S(2)}) collective-permute-start(bf16[4,32,1024]{2,1,0:T(8,128)(2,1)S(1)} %get-tuple-element.139), channel_id=1, source_target_pairs={{0,2},{1,3},{2,0},{3,1},{4,6},{5,7},{6,4},{7,5},{8,10},{9,11},{10,... | collective-permute-start | bytes 786440 | tf_op jit(solution)/shard_map/ppermute | solution.py:396
  72.2 9.2 %collective-permute-start.2 = (bf16[4,32,1024]{2,1,0:T(8,128)(2,1)S(1)}, bf16[4,32,1024]{2,1,0:T(8,128)(2,1)S(1)}, u32[]{:S(2)}, u32[]{:S(2)}) collective-permute-start(bf16[4,32,1024]{2,1,0:T(8,128)(2,1)S(1)} %get-tuple-element.73), channel_id=1, source_target_pairs={{0,4},{1,5},{2,6},{3,7},{4,0},{5,1},{6,2},{7,3},{8,12},{9,13},{10,... | collective-permute-start | bytes 786440 | tf_op jit(solution)/shard_map/ppermute | solution.py:396
  79.9 5.8 %collective-permute-start.6 = (bf16[2,32,1024]{2,1,0:T(8,128)(2,1)S(1)}, bf16[2,32,1024]{2,1,0:T(8,128)(2,1)S(1)}, u32[]{:S(2)}, u32[]{:S(2)}) collective-permute-start(bf16[2,32,1024]{2,1,0:T(8,128)(2,1)S(1)} %get-tuple-element.151), channel_id=1, source_target_pairs={{0,4},{1,5},{2,6},{3,7},{4,0},{5,1},{6,2},{7,3},{8,12},{9,13},{10,... | collective-permute-start | bytes 393224 | tf_op jit(solution)/shard_map/ppermute | solution.py:396
  81.0 14.3 %collective-permute-start.10 = (bf16[4,32,1024]{2,1,0:T(8,128)(2,1)S(1)}, bf16[4,32,1024]{2,1,0:T(8,128)(2,1)S(1)}, u32[]{:S(2)}, u32[]{:S(2)}) collective-permute-start(bf16[4,32,1024]{2,1,0:T(8,128)(2,1)S(1)} %get-tuple-element.78), channel_id=1, source_target_pairs={{0,2},{1,3},{2,0},{3,1},{4,6},{5,7},{6,4},{7,5},{8,10},{9,11},{10,... | collective-permute-start | bytes 786440 | tf_op jit(solution)/shard_map/ppermute | solution.py:396
  81.5 9.5 %collective-permute-start.5 = (bf16[2,32,1024]{2,1,0:T(8,128)(2,1)S(1)}, bf16[2,32,1024]{2,1,0:T(8,128)(2,1)S(1)}, u32[]{:S(2)}, u32[]{:S(2)}) collective-permute-start(bf16[2,32,1024]{2,1,0:T(8,128)(2,1)S(1)} %get-tuple-element.149), channel_id=1, source_target_pairs={{0,2},{1,3},{2,0},{3,1},{4,6},{5,7},{6,4},{7,5},{8,10},{9,11},{10,... | collective-permute-start | bytes 393224 | tf_op jit(solution)/shard_map/ppermute | solution.py:396
  83.2 12.9 %collective-permute-start.9 = (bf16[4,32,1024]{2,1,0:T(8,128)(2,1)S(1)}, bf16[4,32,1024]{2,1,0:T(8,128)(2,1)S(1)}, u32[]{:S(2)}, u32[]{:S(2)}) collective-permute-start(bf16[4,32,1024]{2,1,0:T(8,128)(2,1)S(1)} %get-tuple-element.83), channel_id=1, source_target_pairs={{0,4},{1,5},{2,6},{3,7},{4,0},{5,1},{6,2},{7,3},{8,12},{9,13},{10,... | collective-permute-start | bytes 786440 | tf_op jit(solution)/shard_map/ppermute | solution.py:396
  85.7 6.3 %collective-permute-start.11 = (bf16[1,32,1024]{2,1,0:T(8,128)(2,1)S(1)}, bf16[1,32,1024]{2,1,0:T(8,128)(2,1)S(1)}, u32[]{:S(2)}, u32[]{:S(2)}) collective-permute-start(bf16[1,32,1024]{2,1,0:T(8,128)(2,1)S(1)} %get-tuple-element.158), channel_id=1, source_target_pairs={{0,8},{1,9},{2,10},{3,11},{4,12},{5,13},{6,14},{7,15},{8,0},{9,1},... | collective-permute-start | bytes 196616 | tf_op jit(solution)/shard_map/ppermute | solution.py:396
  91.1 5.6 %collective-permute-start.8 = (bf16[1,32,1024]{2,1,0:T(8,128)(2,1)S(1)}, bf16[1,32,1024]{2,1,0:T(8,128)(2,1)S(1)}, u32[]{:S(2)}, u32[]{:S(2)}) collective-permute-start(bf16[1,32,1024]{2,1,0:T(8,128)(2,1)S(1)} %get-tuple-element.157), channel_id=1, source_target_pairs={{0,8},{1,9},{2,10},{3,11},{4,12},{5,13},{6,14},{7,15},{8,0},{9,1},... | collective-permute-start | bytes 196616 | tf_op jit(solution)/shard_map/ppermute | solution.py:396
  92.8 9.2 %collective-permute-start.14 = (bf16[1,32,1024]{2,1,0:T(8,128)(2,1)S(1)}, bf16[1,32,1024]{2,1,0:T(8,128)(2,1)S(1)}, u32[]{:S(2)}, u32[]{:S(2)}) collective-permute-start(bf16[1,32,1024]{2,1,0:T(8,128)(2,1)S(1)} %bitcast.30), channel_id=1, source_target_pairs={{0,8},{1,9},{2,10},{3,11},{4,12},{5,13},{6,14},{7,15},{8,0},{9,1},... | collective-permute-start | bytes 196616 | tf_op jit(solution)/shard_map/ppermute | solution.py:396
  95.4 31.0 %copy-start = (bf16[16384]{0:T(1024)(128)(2,1)S(1)}, bf16[16384]{0:T(1024)(128)(2,1)}, u32[]{:S(2)}) copy-start(bf16[16384]{0:T(1024)(128)(2,1)} %param.17) | copy-start | bytes 98308
  95.4 9.0 %collective-permute-start.12 = (bf16[2,32,1024]{2,1,0:T(8,128)(2,1)S(1)}, bf16[2,32,1024]{2,1,0:T(8,128)(2,1)S(1)}, u32[]{:S(2)}, u32[]{:S(2)}) collective-permute-start(bf16[2,32,1024]{2,1,0:T(8,128)(2,1)S(1)} %get-tuple-element.145), channel_id=1, source_target_pairs={{0,4},{1,5},{2,6},{3,7},{4,0},{5,1},{6,2},{7,3},{8,12},{9,13},{10,... | collective-permute-start | bytes 393224 | tf_op jit(solution)/shard_map/ppermute | solution.py:396
  96.1 5.0 %collective-permute-start.15 = (bf16[2,32,1024]{2,1,0:T(8,128)(2,1)S(1)}, bf16[2,32,1024]{2,1,0:T(8,128)(2,1)S(1)}, u32[]{:S(2)}, u32[]{:S(2)}) collective-permute-start(bf16[2,32,1024]{2,1,0:T(8,128)(2,1)S(1)} %get-tuple-element.146), channel_id=1, source_target_pairs={{0,2},{1,3},{2,0},{3,1},{4,6},{5,7},{6,4},{7,5},{8,10},{9,11},{10,... | collective-permute-start | bytes 393224 | tf_op jit(solution)/shard_map/ppermute | solution.py:396
  97.6 6.3 %collective-permute-start.13 = (bf16[1,32,1024]{2,1,0:T(8,128)(2,1)S(1)}, bf16[1,32,1024]{2,1,0:T(8,128)(2,1)S(1)}, u32[]{:S(2)}, u32[]{:S(2)}) collective-permute-start(bf16[1,32,1024]{2,1,0:T(8,128)(2,1)S(1)} %bitcast.32), channel_id=1, source_target_pairs={{0,8},{1,9},{2,10},{3,11},{4,12},{5,13},{6,14},{7,15},{8,0},{9,1},... | collective-permute-start | bytes 196616 | tf_op jit(solution)/shard_map/ppermute | solution.py:396
  101.2 6.8 %collective-permute-start.19 = (bf16[1,32,1024]{2,1,0:T(8,128)(2,1)S(1)}, bf16[1,32,1024]{2,1,0:T(8,128)(2,1)S(1)}, u32[]{:S(2)}, u32[]{:S(2)}) collective-permute-start(bf16[1,32,1024]{2,1,0:T(8,128)(2,1)S(1)} %get-tuple-element.154), channel_id=1, source_target_pairs={{0,8},{1,9},{2,10},{3,11},{4,12},{5,13},{6,14},{7,15},{8,0},{9,1},... | collective-permute-start | bytes 196616 | tf_op jit(solution)/shard_map/ppermute | solution.py:396
  102.0 9.5 %collective-permute-start.17 = (bf16[2,32,1024]{2,1,0:T(8,128)(2,1)S(1)}, bf16[2,32,1024]{2,1,0:T(8,128)(2,1)S(1)}, u32[]{:S(2)}, u32[]{:S(2)}) collective-permute-start(bf16[2,32,1024]{2,1,0:T(8,128)(2,1)S(1)} %constant_dynamic-update-slice_fusion), channel_id=1, source_target_pairs={{0,4},{1,5},{2,6},{3,7},{4,0},{5,1},{6,2},{7,3},{8,12},{9,13},{10,... | collective-permute-start | bytes 393224 | tf_op jit(solution)/shard_map/ppermute | solution.py:396
  103.8 6.1 %collective-permute-start.18 = (bf16[2,32,1024]{2,1,0:T(8,128)(2,1)S(1)}, bf16[2,32,1024]{2,1,0:T(8,128)(2,1)S(1)}, u32[]{:S(2)}, u32[]{:S(2)}) collective-permute-start(bf16[2,32,1024]{2,1,0:T(8,128)(2,1)S(1)} %constant_dynamic-update-slice_fusion.2), channel_id=1, source_target_pairs={{0,2},{1,3},{2,0},{3,1},{4,6},{5,7},{6,4},{7,5},{8,10},{9,11},{10,... | collective-permute-start | bytes 393224 | tf_op jit(solution)/shard_map/ppermute | solution.py:396
  104.5 8.3 %collective-permute-start.16 = (bf16[1,32,1024]{2,1,0:T(8,128)(2,1)S(1)}, bf16[1,32,1024]{2,1,0:T(8,128)(2,1)S(1)}, u32[]{:S(2)}, u32[]{:S(2)}) collective-permute-start(bf16[1,32,1024]{2,1,0:T(8,128)(2,1)S(1)} %get-tuple-element.153), channel_id=1, source_target_pairs={{0,8},{1,9},{2,10},{3,11},{4,12},{5,13},{6,14},{7,15},{8,0},{9,1},... | collective-permute-start | bytes 196616 | tf_op jit(solution)/shard_map/ppermute | solution.py:396
  108.8 6.4 %collective-permute-start.21 = (bf16[1,32,1024]{2,1,0:T(8,128)(2,1)S(1)}, bf16[1,32,1024]{2,1,0:T(8,128)(2,1)S(1)}, u32[]{:S(2)}, u32[]{:S(2)}) collective-permute-start(bf16[1,32,1024]{2,1,0:T(8,128)(2,1)S(1)} %bitcast.34), channel_id=1, source_target_pairs={{0,8},{1,9},{2,10},{3,11},{4,12},{5,13},{6,14},{7,15},{8,0},{9,1},... | collective-permute-start | bytes 196616 | tf_op jit(solution)/shard_map/ppermute | solution.py:396
  110.0 10.8 %collective-permute-start.23 = (bf16[4,32,1024]{2,1,0:T(8,128)(2,1)S(1)}, bf16[4,32,1024]{2,1,0:T(8,128)(2,1)S(1)}, u32[]{:S(2)}, u32[]{:S(2)}) collective-permute-start(bf16[4,32,1024]{2,1,0:T(8,128)(2,1)S(1)} %constant_dynamic-update-slice_fusion.4), channel_id=1, source_target_pairs={{0,4},{1,5},{2,6},{3,7},{4,0},{5,1},{6,2},{7,3},{8,12},{9,13},{10,... | collective-permute-start | bytes 786440 | tf_op jit(solution)/shard_map/ppermute | solution.py:396
  111.6 12.4 %collective-permute-start.27 = (bf16[4,32,1024]{2,1,0:T(8,128)(2,1)S(1)}, bf16[4,32,1024]{2,1,0:T(8,128)(2,1)S(1)}, u32[]{:S(2)}, u32[]{:S(2)}) collective-permute-start(bf16[4,32,1024]{2,1,0:T(8,128)(2,1)S(1)} %constant_dynamic-update-slice_fusion.6), channel_id=1, source_target_pairs={{0,2},{1,3},{2,0},{3,1},{4,6},{5,7},{6,4},{7,5},{8,10},{9,11},{10,... | collective-permute-start | bytes 786440 | tf_op jit(solution)/shard_map/ppermute | solution.py:396
  113.6 5.3 %collective-permute-start.20 = (bf16[1,32,1024]{2,1,0:T(8,128)(2,1)S(1)}, bf16[1,32,1024]{2,1,0:T(8,128)(2,1)S(1)}, u32[]{:S(2)}, u32[]{:S(2)}) collective-permute-start(bf16[1,32,1024]{2,1,0:T(8,128)(2,1)S(1)} %bitcast.36), channel_id=1, source_target_pairs={{0,8},{1,9},{2,10},{3,11},{4,12},{5,13},{6,14},{7,15},{8,0},{9,1},... | collective-permute-start | bytes 196616 | tf_op jit(solution)/shard_map/ppermute | solution.py:396
  115.2 5.5 %collective-permute-start.24 = (bf16[2,32,1024]{2,1,0:T(8,128)(2,1)S(1)}, bf16[2,32,1024]{2,1,0:T(8,128)(2,1)S(1)}, u32[]{:S(2)}, u32[]{:S(2)}) collective-permute-start(bf16[2,32,1024]{2,1,0:T(8,128)(2,1)S(1)} %constant_dynamic-update-slice_fusion.8), channel_id=1, source_target_pairs={{0,2},{1,3},{2,0},{3,1},{4,6},{5,7},{6,4},{7,5},{8,10},{9,11},{10,... | collective-permute-start | bytes 393224 | tf_op jit(solution)/shard_map/ppermute | solution.py:396
  119.0 5.0 %collective-permute-start.22 = (bf16[2,32,1024]{2,1,0:T(8,128)(2,1)S(1)}, bf16[2,32,1024]{2,1,0:T(8,128)(2,1)S(1)}, u32[]{:S(2)}, u32[]{:S(2)}) collective-permute-start(bf16[2,32,1024]{2,1,0:T(8,128)(2,1)S(1)} %constant_dynamic-update-slice_fusion.10), channel_id=1, source_target_pairs={{0,4},{1,5},{2,6},{3,7},{4,0},{5,1},{6,2},{7,3},{8,12},{9,13},{10,... | collective-permute-start | bytes 393224 | tf_op jit(solution)/shard_map/ppermute | solution.py:396
  120.9 5.5 %collective-permute-start.29 = (bf16[8,32,1024]{2,1,0:T(8,128)(2,1)S(1)}, bf16[8,32,1024]{2,1,0:T(8,128)(2,1)S(1)}, u32[]{:S(2)}, u32[]{:S(2)}) collective-permute-start(bf16[8,32,1024]{2,1,0:T(8,128)(2,1)S(1)} %constant_dynamic-update-slice_fusion.14.own_ref), channel_id=1, source_target_pairs={{0,1},{1,0},{2,3},{3,2},{4,5},{5,4},{6,7},{7,6},{8,9},{9,8},{10,11... | collective-permute-start | bytes 1572872 | tf_op jit(solution)/shard_map/ppermute | solution.py:396
  124.1 3.9 %collective-permute-start.28 = (bf16[8,32,1024]{2,1,0:T(8,128)(2,1)S(1)}, bf16[8,32,1024]{2,1,0:T(8,128)(2,1)S(1)}, u32[]{:S(2)}, u32[]{:S(2)}) collective-permute-start(bf16[8,32,1024]{2,1,0:T(8,128)(2,1)S(1)} %constant_dynamic-update-slice_fusion.18.own_ref), channel_id=1, source_target_pairs={{0,1},{1,0},{2,3},{3,2},{4,5},{5,4},{6,7},{7,6},{8,9},{9,8},{10,11... | collective-permute-start | bytes 1572872 | tf_op jit(solution)/shard_map/ppermute | solution.py:396
  124.2 8.7 %collective-permute-start.26 = (bf16[4,32,1024]{2,1,0:T(8,128)(2,1)S(1)}, bf16[4,32,1024]{2,1,0:T(8,128)(2,1)S(1)}, u32[]{:S(2)}, u32[]{:S(2)}) collective-permute-start(bf16[4,32,1024]{2,1,0:T(8,128)(2,1)S(1)} %constant_dynamic-update-slice_fusion.12), channel_id=1, source_target_pairs={{0,4},{1,5},{2,6},{3,7},{4,0},{5,1},{6,2},{7,3},{8,12},{9,13},{10,... | collective-permute-start | bytes 786440 | tf_op jit(solution)/shard_map/ppermute | solution.py:396
  126.0 8.4 %collective-permute-start.25 = (bf16[4,32,1024]{2,1,0:T(8,128)(2,1)S(1)}, bf16[4,32,1024]{2,1,0:T(8,128)(2,1)S(1)}, u32[]{:S(2)}, u32[]{:S(2)}) collective-permute-start(bf16[4,32,1024]{2,1,0:T(8,128)(2,1)S(1)} %constant_dynamic-update-slice_fusion.16), channel_id=1, source_target_pairs={{0,2},{1,3},{2,0},{3,1},{4,6},{5,7},{6,4},{7,5},{8,10},{9,11},{10,... | collective-permute-start | bytes 786440 | tf_op jit(solution)/shard_map/ppermute | solution.py:396
  133.0 2.2 %collective-permute-start.31 = (bf16[8,32,1024]{2,1,0:T(8,128)(2,1)S(1)}, bf16[8,32,1024]{2,1,0:T(8,128)(2,1)S(1)}, u32[]{:S(2)}, u32[]{:S(2)}) collective-permute-start(bf16[8,32,1024]{2,1,0:T(8,128)(2,1)S(1)} %constant_dynamic-update-slice_fusion.20.own_ref), channel_id=1, source_target_pairs={{0,1},{1,0},{2,3},{3,2},{4,5},{5,4},{6,7},{7,6},{8,9},{9,8},{10,11... | collective-permute-start | bytes 1572872 | tf_op jit(solution)/shard_map/ppermute | solution.py:396
  134.4 2.5 %collective-permute-start.30 = (bf16[8,32,1024]{2,1,0:T(8,128)(2,1)S(1)}, bf16[8,32,1024]{2,1,0:T(8,128)(2,1)S(1)}, u32[]{:S(2)}, u32[]{:S(2)}) collective-permute-start(bf16[8,32,1024]{2,1,0:T(8,128)(2,1)S(1)} %constant_dynamic-update-slice_fusion.22.own_ref), channel_id=1, source_target_pairs={{0,1},{1,0},{2,3},{3,2},{4,5},{5,4},{6,7},{7,6},{8,9},{9,8},{10,11... | collective-permute-start | bytes 1572872 | tf_op jit(solution)/shard_map/ppermute | solution.py:396

commit v6 on v4

--- a/solution.py
+++ b/solution.py
@@ -31,8 +31,8 @@
 
 
 def input_kernel(count, hidden_ref, gain_ref, w_ref, kv_ref, cosine_ref, sine_ref, *refs):
-    out_ref, hidden, w_buffer, kv_buffer, normed, products, kv_products, *sems = refs
-    h_sem, w_sem, kv_sem = sems
+    out_ref, mine_ref, hidden, w_buffer, kv_buffer, normed, products, kv_products, *sems = refs
+    h_sem, w_sem, kv_sem, mine_sem = sems
     me = lax.axis_index("tensor")
     rows, columns = hidden.shape
     depth = normed.shape[2]
@@ -54,26 +54,26 @@
 
     for k in range(chunks):
         hidden_copy(k).start()
-    early = chunks // 4
-    for k in range(early):
-        w_copy(k).start()
     kv_copy = pltpu.make_async_copy(kv_ref, kv_buffer, kv_sem)
-    kv_copy.start()
+    own = pl.ds(pl.multiple_of(me * (columns // count), columns // count), columns // count)
+    mine_copy = pltpu.make_async_copy(hidden_ref.at[:, own], mine_ref, mine_sem)
     products[...] = jnp.zeros_like(products)
     kv_products[...] = jnp.zeros_like(kv_products)
     total = jnp.zeros((rows, 128), jnp.float32)
     for k in range(chunks):
         hidden_copy(k).wait()
+        w_copy(k).start()
+        if k == 0:
+            kv_copy.start()
         for lane in range(k * depth, (k + 1) * depth, 128):
             part = hidden[:, lane : lane + 128].astype(jnp.float32)
             total = total + part * part
-    for k in range(early, chunks):
-        w_copy(k).start()
+    mine_copy.start()
     scale = lax.rsqrt(jnp.sum(total, axis=1, keepdims=True) / columns + epsilon)
 
     def norm(k):
         floats = hidden[:, span(k)].astype(jnp.float32)
-        gain = gain_ref[:, span(k)].astype(jnp.float32)
+        gain = gain_ref[span(k)].astype(jnp.float32).reshape(1, depth)
         normed[k % 2] = (floats * scale * gain).astype(jnp.bfloat16)
 
     norm(0)
@@ -104,6 +104,7 @@
             out_ref[k, :, part * HD : (part + 1) * HD] = result[
                 k * here : (k + 1) * here
             ].astype(jnp.bfloat16)
+    mine_copy.wait()
 
 
 def project_in(hidden_in, gain, w_query, w_keyval, cosine, sine, count):
@@ -112,12 +113,15 @@
     depth = columns // 8
     chunks = columns // depth
     vmem = pl.BlockSpec(memory_space=pltpu.VMEM)
-    whole = pl.BlockSpec(memory_space=pltpu.HBM)
+    whole = pl.BlockSpec(memory_space=pl.ANY)
     return pl.pallas_call(
         functools.partial(input_kernel, count),
-        out_shape=jax.ShapeDtypeStruct((count, rows // count, width + HD), jnp.bfloat16),
+        out_shape=(
+            jax.ShapeDtypeStruct((count, rows // count, width + HD), jnp.bfloat16),
+            jax.ShapeDtypeStruct((rows, columns // count), jnp.bfloat16),
+        ),
         in_specs=[whole, vmem, whole, whole, vmem, vmem],
-        out_specs=vmem,
+        out_specs=(vmem, vmem),
         scratch_shapes=[
             pltpu.VMEM((rows, columns), jnp.bfloat16),
             pltpu.VMEM((columns, width), jnp.bfloat16),
@@ -128,8 +132,9 @@
             pltpu.SemaphoreType.DMA((chunks,)),
             pltpu.SemaphoreType.DMA((chunks,)),
             pltpu.SemaphoreType.DMA,
+            pltpu.SemaphoreType.DMA,
         ],
-        compiler_params=pltpu.CompilerParams(vmem_limit_bytes=40 * 1024 * 1024),
+        compiler_params=pltpu.CompilerParams(vmem_limit_bytes=52 * 1024 * 1024),
         cost_estimate=pl.CostEstimate(
             flops=2 * rows * columns * (width + kv_width),
             bytes_accessed=2 * columns * (rows + width + kv_width),
@@ -245,7 +250,7 @@
     width = blocks.shape[2] - HD
     heads = count * width // HD
     vmem = pl.BlockSpec(memory_space=pltpu.VMEM)
-    whole = pl.BlockSpec(memory_space=pltpu.HBM)
+    whole = pl.BlockSpec(memory_space=pl.ANY)
     return pl.pallas_call(
         functools.partial(attend_kernel, count),
         out_shape=jax.ShapeDtypeStruct((count, here, width), jnp.bfloat16),
@@ -331,14 +336,14 @@
     return pl.pallas_call(
         functools.partial(project_kernel, count, offsets),
         out_shape=(share,) * sets,
-        in_specs=[pl.BlockSpec(memory_space=pltpu.HBM), pl.BlockSpec(memory_space=pltpu.VMEM)],
+        in_specs=[pl.BlockSpec(memory_space=pl.ANY), pl.BlockSpec(memory_space=pltpu.VMEM)],
         out_specs=(pl.BlockSpec(memory_space=pltpu.VMEM),) * sets,
         scratch_shapes=[
             pltpu.VMEM((rows, depth), jnp.float32),
             pltpu.VMEM((len(offsets), depth, width), jnp.bfloat16),
             pltpu.SemaphoreType.DMA((len(offsets),)),
         ],
-        compiler_params=pltpu.CompilerParams(vmem_limit_bytes=30 * 1024 * 1024),
+        compiler_params=pltpu.CompilerParams(vmem_limit_bytes=48 * 1024 * 1024),
         cost_estimate=pl.CostEstimate(
             flops=2 * rows * depth * width * len(offsets),
             bytes_accessed=2 * (depth + rows) * width * len(offsets),
@@ -407,16 +412,14 @@
 ):
     row_count = hidden_in.shape[0]
     count = lax.axis_size("tensor")
-    my_index = lax.axis_index("tensor")
     cosine, sine = turns(positions)
-    blocks = project_in(
-        hidden_in, attn_gain.reshape(1, -1), w_query, w_keyval, cosine, sine, count
+    blocks, mine = project_in(
+        hidden_in, attn_gain, w_query, w_keyval, cosine, sine, count
     )
     head_blocks = exchange(
         attend(exchange(blocks), lengths, cosine, sine, cache_keys, cache_values)
     )
     share_width = w_out.shape[1] // count
-    mine = lax.dynamic_slice_in_dim(hidden_in, my_index * share_width, share_width, 1)
     gain = ffn_gain.astype(jnp.float32).reshape(count, share_width)
     orders = plans(count)
     sets = len(orders)

time: 135 us -> 121 us (0.90)
  local copies, waits for them, and re-layouts: 16.6 us -> 1.22 us
  other arithmetic: 6.33 us -> 2.97 us
  waiting for transfers between devices: 29.2 us -> 32.2 us
  Pallas kernels: 29.7 us -> 31.7 us
    unnamed x28 -> x22, local copies, waits for them, and re-layouts: 15.5 us -> 1.05 us
    convert_element_type x4, other arithmetic: 3.47 us -> 0.11 us  [on_device(): streams[k] = (own_rows + total).astype(jnp.bfloat16)]
    ppermute x32, waiting for transfers between devices: 29.2 us -> 32.2 us  [swap(): lax.ppermute(values, 'tensor', [(i, i ^ 1 << bit) for i in range(count)])]
    pallas_call x1, Pallas kernels: 8.23 us -> 10.8 us  [project_in(): pl.pallas_call(functools.partial(input_kernel, count), out_shape=(jax.Sha...]
  transfers between devices with their start and end apart: 32 -> 32, of which waited for: 12 -> 12; matrix products, arithmetic and copies ran while one was open for 4% -> 2% of each run, Pallas kernels for 7% -> 7%
where the time goes in v6:
time: 121 us
  waiting for transfers between devices  32.2 us (27%)
  Pallas kernels  31.7 us (26%)
  blocking collectives  26.2 us (22%)
  starting transfers between devices  25.3 us (21%)
  other arithmetic  2.97 us (2%)
  local copies, waits for them, and re-layouts  1.22 us (1%)
    ppermute x32, waiting for transfers between devices, swap(): lax.ppermute(values, 'tensor', [(i, i ^ 1 << bit) for i in range(count)])  32.2 us
    all_to_all x2, blocking collectives, exchange(): lax.all_to_all(blocks, 'tensor', split_axis=0, concat_axis=0, tiled=True)  26.2 us
    ppermute x32, starting transfers between devices, swap(): lax.ppermute(values, 'tensor', [(i, i ^ 1 << bit) for i in range(count)])  25.3 us
    pallas_call x1, Pallas kernels, project_in(): pl.pallas_call(functools.partial(input_kernel, count), out_shape=(jax.Sha...  10.8 us
    pallas_call x2, Pallas kernels, project(): pl.pallas_call(functools.partial(project_kernel, count, offsets), out_sha...  7.67 us
    pallas_call x1, Pallas kernels, attend(): pl.pallas_call(functools.partial(attend_kernel, count), out_shape=jax.Sha...  6.62 us
    pallas_call x4, Pallas kernels, finish(): pl.pallas_call(functools.partial(finish_kernel, offsets), grid=(1,), out_...  6.61 us
  transfers between devices with their start and end apart: 32, of which 12 were waited for; matrix products, arithmetic and copies ran while one was open for 2% of the time, Pallas kernels for 7%

profile of v6, /device:TPU:0, one launch (start us, length us, event | category | flops | bytes accessed | tf_op | source)
XLA Modules:
  0.0 120.5 jit_solution(15495581780646774305)
XLA Ops:
  0.6 0.7 convert_element_type.283
  1.3 0.3 fusion.4
  1.6 0.9 copy-done
  2.5 10.8 %shard_map.113 = (bf16[16,8,640]{2,1,0:T(8,128)(2,1)S(1)}, bf16[128,1024]{1,0:T(8,128)(2,1)S(1)}) custom-call(bf16[128,16384]{1,0:T(8,128)(2,1)} %hidden_ref.1, bf16[16384]{0:T(1024)(128)(2,1)S(1)} %copy-done, bf16[16384,512]{1,0:T(8,128)(2,1)} %w_ref.3, bf16[64,16384]{1,0:T(8,128)(2,1)} %bitcast.23, f32[128,128]{1,0:T(8,128)S(1)} %get-tuple-element.165.cosine_ref, ...), custom_call_target="tpu_custom_call" | custom-call | flops 2415919104 | bytes 23068672 | tf_op jit(solution)/shard_map/pallas_call | solution.py:117
  13.3 15.6 %all_to_all.10.refs_0_ = bf16[16,8,640]{2,1,0:T(8,128)(2,1)S(1)} all-to-all(bf16[16,8,640]{2,1,0:T(8,128)(2,1)S(1)} %get-tuple-element.72), channel_id=1, replica_groups=mesh['groups'=2,'tensor'=16] {'tensor'}, dimensions={0} | all-to-all | bytes 327680 | tf_op jit(solution)/shard_map/all_to_all | solution.py:279
  29.0 6.6 %shard_map.114 = bf16[16,8,512]{2,1,0:T(8,128)(2,1)S(1)} custom-call(s32[8]{0:T(128)S(1)} %copy-done.1, f32[128,128]{1,0:T(8,128)S(1)} %get-tuple-element.165.cosine_ref, f32[128,128]{1,0:T(8,128)S(1)} %get-tuple-element.164.sine_ref, bf16[8,1024,512]{2,1,0:T(8,128)(2,1)S(1)} %bitcast.22, bf16[8,1024,512]{2,1,0:T(8,128)(2,1)} %values_ref.1, ...), custom_call_target="tpu_custom_call" | custom-call | flops 268435456 | bytes 16777216 | tf_op jit(solution)/shard_map/pallas_call | solution.py:254
  35.6 10.5 %all_to_all.11.refs_0_ = bf16[16,8,512]{2,1,0:T(8,128)(2,1)S(1)} all-to-all(bf16[16,8,512]{2,1,0:T(8,128)(2,1)S(1)} %shard_map.114), channel_id=1, replica_groups=mesh['groups'=2,'tensor'=16] {'tensor'}, dimensions={0} | all-to-all | bytes 262144 | tf_op jit(solution)/shard_map/all_to_all | solution.py:279
  46.1 3.8 %shard_map.116 = (bf16[8,32,1024]{2,1,0:T(8,128)(2,1)S(1)}, bf16[8,32,1024]{2,1,0:T(8,128)(2,1)S(1)}, bf16[8,32,1024]{2,1,0:T(8,128)(2,1)S(1)}, bf16[8,32,1024]{2,1,0:T(8,128)(2,1)S(1)}) custom-call(bf16[512,16384]{1,0:T(8,128)(2,1)} %w_ref.5, bf16[16,8,512]{2,1,0:T(8,128)(2,1)S(1)} %all_to_all.11.refs_0_), custom_call_target="tpu_custom_call" | custom-call | flops 1073741824 | bytes 10485760 | tf_op jit(solution)/shard_map/pallas_call | solution.py:336
  50.0 0.1 collective-permute-start.1
  50.1 0.5 collective-permute-start
  50.6 0.1 collective-permute-start.3
  50.6 0.4 collective-permute-start.7
  51.1 3.8 %shard_map.115 = (bf16[8,32,1024]{2,1,0:T(8,128)(2,1)S(1)}, bf16[8,32,1024]{2,1,0:T(8,128)(2,1)S(1)}, bf16[8,32,1024]{2,1,0:T(8,128)(2,1)S(1)}, bf16[8,32,1024]{2,1,0:T(8,128)(2,1)S(1)}) custom-call(bf16[512,16384]{1,0:T(8,128)(2,1)} %w_ref.5, bf16[16,8,512]{2,1,0:T(8,128)(2,1)S(1)} %all_to_all.11.refs_0_), custom_call_target="tpu_custom_call" | custom-call | flops 1073741824 | bytes 10485760 | tf_op jit(solution)/shard_map/pallas_call | solution.py:336
  54.9 0.2 add_convert_fusion.3
  55.1 0.1 collective-permute-start.4
  55.2 0.2 add_convert_fusion.6
  55.4 0.4 collective-permute-start.2
  55.8 0.2 add_convert_fusion
  56.0 0.2 add_convert_fusion.2
  56.2 7.3 %collective-permute-done.4 = bf16[4,32,1024]{2,1,0:T(8,128)(2,1)S(1)} collective-permute-done((bf16[4,32,1024]{2,1,0:T(8,128)(2,1)S(1)}, bf16[4,32,1024]{2,1,0:T(8,128)(2,1)S(1)}, u32[]{:S(2)}, u32[]{:S(2)}) %collective-permute-start.4) | collective-permute-done | bytes 262176 | tf_op jit(solution)/shard_map/ppermute | solution.py:394
  63.5 0.1 add_convert_fusion.12
  63.5 0.1 collective-permute-start.6
  63.6 0.7 collective-permute-start.10
  64.4 1.5 %collective-permute-start.5 = (bf16[2,32,1024]{2,1,0:T(8,128)(2,1)S(1)}, bf16[2,32,1024]{2,1,0:T(8,128)(2,1)S(1)}, u32[]{:S(2)}, u32[]{:S(2)}) collective-permute-start(bf16[2,32,1024]{2,1,0:T(8,128)(2,1)S(1)} %get-tuple-element.153), channel_id=1, source_target_pairs={{0,2},{1,3},{2,0},{3,1},{4,6},{5,7},{6,4},{7,5},{8,10},{9,11},{10,... | collective-permute-start | bytes 393224 | tf_op jit(solution)/shard_map/ppermute | solution.py:394
  65.8 1.9 %collective-permute-start.9 = (bf16[4,32,1024]{2,1,0:T(8,128)(2,1)S(1)}, bf16[4,32,1024]{2,1,0:T(8,128)(2,1)S(1)}, u32[]{:S(2)}, u32[]{:S(2)}) collective-permute-start(bf16[4,32,1024]{2,1,0:T(8,128)(2,1)S(1)} %get-tuple-element.87), channel_id=1, source_target_pairs={{0,4},{1,5},{2,6},{3,7},{4,0},{5,1},{6,2},{7,3},{8,12},{9,13},{10,... | collective-permute-start | bytes 786440 | tf_op jit(solution)/shard_map/ppermute | solution.py:394
  67.8 2.2 %collective-permute-done.6 = bf16[2,32,1024]{2,1,0:T(8,128)(2,1)S(1)} collective-permute-done((bf16[2,32,1024]{2,1,0:T(8,128)(2,1)S(1)}, bf16[2,32,1024]{2,1,0:T(8,128)(2,1)S(1)}, u32[]{:S(2)}, u32[]{:S(2)}) %collective-permute-start.6) | collective-permute-done | bytes 131104 | tf_op jit(solution)/shard_map/ppermute | solution.py:394
  70.0 0.1 collective-permute-start.11
  70.1 3.9 %collective-permute-done.5 = bf16[2,32,1024]{2,1,0:T(8,128)(2,1)S(1)} collective-permute-done((bf16[2,32,1024]{2,1,0:T(8,128)(2,1)S(1)}, bf16[2,32,1024]{2,1,0:T(8,128)(2,1)S(1)}, u32[]{:S(2)}, u32[]{:S(2)}) %collective-permute-start.5) | collective-permute-done | bytes 131104 | tf_op jit(solution)/shard_map/ppermute | solution.py:394
  74.0 1.2 collective-permute-start.8
  75.2 0.8 collective-permute-done.11
  76.0 1.1 collective-permute-start.14
  77.1 0.1 add_convert_fusion.9
  77.2 1.7 %collective-permute-start.12 = (bf16[2,32,1024]{2,1,0:T(8,128)(2,1)S(1)}, bf16[2,32,1024]{2,1,0:T(8,128)(2,1)S(1)}, u32[]{:S(2)}, u32[]{:S(2)}) collective-permute-start(bf16[2,32,1024]{2,1,0:T(8,128)(2,1)S(1)} %get-tuple-element.149), channel_id=1, source_target_pairs={{0,4},{1,5},{2,6},{3,7},{4,0},{5,1},{6,2},{7,3},{8,12},{9,13},{10,... | collective-permute-start | bytes 393224 | tf_op jit(solution)/shard_map/ppermute | solution.py:394
  78.9 0.7 collective-permute-start.15
  79.6 1.3 %collective-permute-start.13 = (bf16[1,32,1024]{2,1,0:T(8,128)(2,1)S(1)}, bf16[1,32,1024]{2,1,0:T(8,128)(2,1)S(1)}, u32[]{:S(2)}, u32[]{:S(2)}) collective-permute-start(bf16[1,32,1024]{2,1,0:T(8,128)(2,1)S(1)} %bitcast.26), channel_id=1, source_target_pairs={{0,8},{1,9},{2,10},{3,11},{4,12},{5,13},{6,14},{7,15},{8,0},{9,1},... | collective-permute-start | bytes 196616 | tf_op jit(solution)/shard_map/ppermute | solution.py:394
  80.9 3.1 %collective-permute-done.15 = bf16[2,32,1024]{2,1,0:T(8,128)(2,1)S(1)} collective-permute-done((bf16[2,32,1024]{2,1,0:T(8,128)(2,1)S(1)}, bf16[2,32,1024]{2,1,0:T(8,128)(2,1)S(1)}, u32[]{:S(2)}, u32[]{:S(2)}) %collective-permute-start.15) | collective-permute-done | bytes 131104 | tf_op jit(solution)/shard_map/ppermute | solution.py:394
  84.0 0.5 collective-permute-start.19
  84.5 1.9 %collective-permute-start.17 = (bf16[2,32,1024]{2,1,0:T(8,128)(2,1)S(1)}, bf16[2,32,1024]{2,1,0:T(8,128)(2,1)S(1)}, u32[]{:S(2)}, u32[]{:S(2)}) collective-permute-start(bf16[2,32,1024]{2,1,0:T(8,128)(2,1)S(1)} %constant_dynamic-update-slice_fusion), channel_id=1, source_target_pairs={{0,4},{1,5},{2,6},{3,7},{4,0},{5,1},{6,2},{7,3},{8,12},{9,13},{10,... | collective-permute-start | bytes 393224 | tf_op jit(solution)/shard_map/ppermute | solution.py:394
  86.5 1.3 %collective-permute-start.18 = (bf16[2,32,1024]{2,1,0:T(8,128)(2,1)S(1)}, bf16[2,32,1024]{2,1,0:T(8,128)(2,1)S(1)}, u32[]{:S(2)}, u32[]{:S(2)}) collective-permute-start(bf16[2,32,1024]{2,1,0:T(8,128)(2,1)S(1)} %constant_dynamic-update-slice_fusion.2), channel_id=1, source_target_pairs={{0,2},{1,3},{2,0},{3,1},{4,6},{5,7},{6,4},{7,5},{8,10},{9,11},{10,... | collective-permute-start | bytes 393224 | tf_op jit(solution)/shard_map/ppermute | solution.py:394
  87.8 0.6 collective-permute-start.16
  88.4 2.8 %collective-permute-done.19 = bf16[1,32,1024]{2,1,0:T(8,128)(2,1)S(1)} collective-permute-done((bf16[1,32,1024]{2,1,0:T(8,128)(2,1)S(1)}, bf16[1,32,1024]{2,1,0:T(8,128)(2,1)S(1)}, u32[]{:S(2)}, u32[]{:S(2)}) %collective-permute-start.19) | collective-permute-done | bytes 65568 | tf_op jit(solution)/shard_map/ppermute | solution.py:394
  91.2 0.1 collective-permute-start.21
  91.3 1.6 %collective-permute-done.18 = bf16[2,32,1024]{2,1,0:T(8,128)(2,1)S(1)} collective-permute-done((bf16[2,32,1024]{2,1,0:T(8,128)(2,1)S(1)}, bf16[2,32,1024]{2,1,0:T(8,128)(2,1)S(1)}, u32[]{:S(2)}, u32[]{:S(2)}) %collective-permute-start.18) | collective-permute-done | bytes 131104 | tf_op jit(solution)/shard_map/ppermute | solution.py:394
  92.9 0.7 collective-permute-start.23
  93.6 0.6 collective-permute-start.27
  94.3 1.3 %collective-permute-start.20 = (bf16[1,32,1024]{2,1,0:T(8,128)(2,1)S(1)}, bf16[1,32,1024]{2,1,0:T(8,128)(2,1)S(1)}, u32[]{:S(2)}, u32[]{:S(2)}) collective-permute-start(bf16[1,32,1024]{2,1,0:T(8,128)(2,1)S(1)} %bitcast.30), channel_id=1, source_target_pairs={{0,8},{1,9},{2,10},{3,11},{4,12},{5,13},{6,14},{7,15},{8,0},{9,1},... | collective-permute-start | bytes 196616 | tf_op jit(solution)/shard_map/ppermute | solution.py:394
  95.6 1.6 %collective-permute-done.21 = bf16[1,32,1024]{2,1,0:T(8,128)(2,1)S(1)} collective-permute-done((bf16[1,32,1024]{2,1,0:T(8,128)(2,1)S(1)}, bf16[1,32,1024]{2,1,0:T(8,128)(2,1)S(1)}, u32[]{:S(2)}, u32[]{:S(2)}) %collective-permute-start.21) | collective-permute-done | bytes 65568 | tf_op jit(solution)/shard_map/ppermute | solution.py:394
  97.2 0.7 collective-permute-start.24
  97.9 1.7 %collective-permute-done.20 = bf16[1,32,1024]{2,1,0:T(8,128)(2,1)S(1)} collective-permute-done((bf16[1,32,1024]{2,1,0:T(8,128)(2,1)S(1)}, bf16[1,32,1024]{2,1,0:T(8,128)(2,1)S(1)}, u32[]{:S(2)}, u32[]{:S(2)}) %collective-permute-start.20) | collective-permute-done | bytes 65568 | tf_op jit(solution)/shard_map/ppermute | solution.py:394
  99.7 3.1 %collective-permute-start.22 = (bf16[2,32,1024]{2,1,0:T(8,128)(2,1)S(1)}, bf16[2,32,1024]{2,1,0:T(8,128)(2,1)S(1)}, u32[]{:S(2)}, u32[]{:S(2)}) collective-permute-start(bf16[2,32,1024]{2,1,0:T(8,128)(2,1)S(1)} %constant_dynamic-update-slice_fusion.10), channel_id=1, source_target_pairs={{0,4},{1,5},{2,6},{3,7},{4,0},{5,1},{6,2},{7,3},{8,12},{9,13},{10,... | collective-permute-start | bytes 393224 | tf_op jit(solution)/shard_map/ppermute | solution.py:394
  102.9 0.1 collective-permute-start.29
  103.0 2.8 %collective-permute-done.22 = bf16[2,32,1024]{2,1,0:T(8,128)(2,1)S(1)} collective-permute-done((bf16[2,32,1024]{2,1,0:T(8,128)(2,1)S(1)}, bf16[2,32,1024]{2,1,0:T(8,128)(2,1)S(1)}, u32[]{:S(2)}, u32[]{:S(2)}) %collective-permute-start.22) | collective-permute-done | bytes 131104 | tf_op jit(solution)/shard_map/ppermute | solution.py:394
  105.8 0.1 collective-permute-start.28
  105.9 2.1 %collective-permute-start.26 = (bf16[4,32,1024]{2,1,0:T(8,128)(2,1)S(1)}, bf16[4,32,1024]{2,1,0:T(8,128)(2,1)S(1)}, u32[]{:S(2)}, u32[]{:S(2)}) collective-permute-start(bf16[4,32,1024]{2,1,0:T(8,128)(2,1)S(1)} %constant_dynamic-update-slice_fusion.12), channel_id=1, source_target_pairs={{0,4},{1,5},{2,6},{3,7},{4,0},{5,1},{6,2},{7,3},{8,12},{9,13},{10,... | collective-permute-start | bytes 786440 | tf_op jit(solution)/shard_map/ppermute | solution.py:394
  108.0 0.4 collective-permute-start.25
  108.4 1.7 %shard_map.117.refs_0_ = bf16[128,16384]{1,0:T(8,128)(2,1)} custom-call(bf16[8,32,1024]{2,1,0:T(8,128)(2,1)S(1)} %constant_dynamic-update-slice_fusion.14.own_ref, bf16[8,32,1024]{2,1,0:T(8,128)(2,1)S(1)} %collective-permute-done.29.other_ref, f32[16,1024]{1,0:T(8,128)S(1)} %reshape.42.gain_ref), custom_call_target="tpu_custom_call" | custom-call | flops 3145728 | bytes 2097152 | tf_op jit(solution)/shard_map/pallas_call | solution.py:379
  110.1 1.7 %shard_map.118.refs_0_ = bf16[128,16384]{1,0:T(8,128)(2,1)} custom-call(bf16[8,32,1024]{2,1,0:T(8,128)(2,1)S(1)} %constant_dynamic-update-slice_fusion.18.own_ref, bf16[8,32,1024]{2,1,0:T(8,128)(2,1)S(1)} %collective-permute-done.28.other_ref, f32[16,1024]{1,0:T(8,128)S(1)} %reshape.42.gain_ref, ...), custom_call_target="tpu_custom_call", output_to_operand_aliasing={{}: (3, {})} | custom-call | flops 3145728 | bytes 2097152 | tf_op jit(solution)/shard_map/pallas_call | solution.py:379
  111.7 3.1 %collective-permute-done.26 = bf16[4,32,1024]{2,1,0:T(8,128)(2,1)S(1)} collective-permute-done((bf16[4,32,1024]{2,1,0:T(8,128)(2,1)S(1)}, bf16[4,32,1024]{2,1,0:T(8,128)(2,1)S(1)}, u32[]{:S(2)}, u32[]{:S(2)}) %collective-permute-start.26) | collective-permute-done | bytes 262176 | tf_op jit(solution)/shard_map/ppermute | solution.py:394
  114.9 0.1 collective-permute-start.31
  115.0 1.3 %collective-permute-done.25 = bf16[4,32,1024]{2,1,0:T(8,128)(2,1)S(1)} collective-permute-done((bf16[4,32,1024]{2,1,0:T(8,128)(2,1)S(1)}, bf16[4,32,1024]{2,1,0:T(8,128)(2,1)S(1)}, u32[]{:S(2)}, u32[]{:S(2)}) %collective-permute-start.25) | collective-permute-done | bytes 262176 | tf_op jit(solution)/shard_map/ppermute | solution.py:394
  116.4 0.1 collective-permute-start.30
  116.5 0.7 pad_maximum_fusion
  117.2 1.7 %shard_map.119.refs_0_ = bf16[128,16384]{1,0:T(8,128)(2,1)} custom-call(bf16[8,32,1024]{2,1,0:T(8,128)(2,1)S(1)} %constant_dynamic-update-slice_fusion.20.own_ref, bf16[8,32,1024]{2,1,0:T(8,128)(2,1)S(1)} %collective-permute-done.31.other_ref, f32[16,1024]{1,0:T(8,128)S(1)} %reshape.42.gain_ref, ...), custom_call_target="tpu_custom_call", output_to_operand_aliasing={{}: (3, {})} | custom-call | flops 3145728 | bytes 2097152 | tf_op jit(solution)/shard_map/pallas_call | solution.py:379
  118.9 1.7 %shard_map.120 = bf16[128,16384]{1,0:T(8,128)(2,1)} custom-call(bf16[8,32,1024]{2,1,0:T(8,128)(2,1)S(1)} %constant_dynamic-update-slice_fusion.22.own_ref, bf16[8,32,1024]{2,1,0:T(8,128)(2,1)S(1)} %collective-permute-done.30.other_ref, f32[16,1024]{1,0:T(8,128)S(1)} %reshape.42.gain_ref, ...), custom_call_target="tpu_custom_call", output_to_operand_aliasing={{}: (3, {})} | custom-call | flops 3145728 | bytes 2097152 | tf_op jit(solution)/shard_map/pallas_call | solution.py:379
  (66 shorter events, 0.8 us)
Async XLA Ops:
  1.6 27.4 %slice-start = ((s8[8388608]{0:T(1024)(128)(4,1)}), s8[4194304]{0:T(1024)(128)(4,1)S(1)}, s32[]{:S(2)}) async-start(s8[8388608]{0:T(1024)(128)(4,1)} %bitcast.21), calls=%async_computation.2 | async-start | bytes 8388608
  1.6 0.9 copy-start
  2.5 26.4 %slice-start.1 = ((s8[8388608]{0:T(1024)(128)(4,1)}), s8[4194304]{0:T(1024)(128)(4,1)S(1)}, s32[]{:S(2)}) async-start(s8[8388608]{0:T(1024)(128)(4,1)} %bitcast.21), calls=%async_computation.3 | async-start | bytes 8388608
  2.5 26.4 %copy-start.1 = (s32[8]{0:T(128)S(1)}, s32[8]{0:T(128)}, u32[]{:S(2)}) copy-start(s32[8]{0:T(128)} %lengths_ref.1) | copy-start | bytes 100
  50.0 4.9 %collective-permute-start.1 = (bf16[8,32,1024]{2,1,0:T(8,128)(2,1)S(1)}, bf16[8,32,1024]{2,1,0:T(8,128)(2,1)S(1)}, u32[]{:S(2)}, u32[]{:S(2)}) collective-permute-start(bf16[8,32,1024]{2,1,0:T(8,128)(2,1)S(1)} %get-tuple-element.76), channel_id=1, source_target_pairs={{0,1},{1,0},{2,3},{3,2},{4,5},{5,4},{6,7},{7,6},{8,9},{9,8},{10,11... | collective-permute-start | bytes 1572872 | tf_op jit(solution)/shard_map/ppermute | solution.py:394
  50.1 5.1 %collective-permute-start = (bf16[8,32,1024]{2,1,0:T(8,128)(2,1)S(1)}, bf16[8,32,1024]{2,1,0:T(8,128)(2,1)S(1)}, u32[]{:S(2)}, u32[]{:S(2)}) collective-permute-start(bf16[8,32,1024]{2,1,0:T(8,128)(2,1)S(1)} %get-tuple-element.74), channel_id=1, source_target_pairs={{0,1},{1,0},{2,3},{3,2},{4,5},{5,4},{6,7},{7,6},{8,9},{9,8},{10,11... | collective-permute-start | bytes 1572872 | tf_op jit(solution)/shard_map/ppermute | solution.py:394
  50.6 5.2 %collective-permute-start.3 = (bf16[8,32,1024]{2,1,0:T(8,128)(2,1)S(1)}, bf16[8,32,1024]{2,1,0:T(8,128)(2,1)S(1)}, u32[]{:S(2)}, u32[]{:S(2)}) collective-permute-start(bf16[8,32,1024]{2,1,0:T(8,128)(2,1)S(1)} %get-tuple-element.79), channel_id=1, source_target_pairs={{0,1},{1,0},{2,3},{3,2},{4,5},{5,4},{6,7},{7,6},{8,9},{9,8},{10,11... | collective-permute-start | bytes 1572872 | tf_op jit(solution)/shard_map/ppermute | solution.py:394
  50.6 5.3 %collective-permute-start.7 = (bf16[8,32,1024]{2,1,0:T(8,128)(2,1)S(1)}, bf16[8,32,1024]{2,1,0:T(8,128)(2,1)S(1)}, u32[]{:S(2)}, u32[]{:S(2)}) collective-permute-start(bf16[8,32,1024]{2,1,0:T(8,128)(2,1)S(1)} %get-tuple-element.86), channel_id=1, source_target_pairs={{0,1},{1,0},{2,3},{3,2},{4,5},{5,4},{6,7},{7,6},{8,9},{9,8},{10,11... | collective-permute-start | bytes 1572872 | tf_op jit(solution)/shard_map/ppermute | solution.py:394
  55.1 8.4 %collective-permute-start.4 = (bf16[4,32,1024]{2,1,0:T(8,128)(2,1)S(1)}, bf16[4,32,1024]{2,1,0:T(8,128)(2,1)S(1)}, u32[]{:S(2)}, u32[]{:S(2)}) collective-permute-start(bf16[4,32,1024]{2,1,0:T(8,128)(2,1)S(1)} %get-tuple-element.143), channel_id=1, source_target_pairs={{0,2},{1,3},{2,0},{3,1},{4,6},{5,7},{6,4},{7,5},{8,10},{9,11},{10,... | collective-permute-start | bytes 786440 | tf_op jit(solution)/shard_map/ppermute | solution.py:394
  55.4 8.9 %collective-permute-start.2 = (bf16[4,32,1024]{2,1,0:T(8,128)(2,1)S(1)}, bf16[4,32,1024]{2,1,0:T(8,128)(2,1)S(1)}, u32[]{:S(2)}, u32[]{:S(2)}) collective-permute-start(bf16[4,32,1024]{2,1,0:T(8,128)(2,1)S(1)} %get-tuple-element.77), channel_id=1, source_target_pairs={{0,4},{1,5},{2,6},{3,7},{4,0},{5,1},{6,2},{7,3},{8,12},{9,13},{10,... | collective-permute-start | bytes 786440 | tf_op jit(solution)/shard_map/ppermute | solution.py:394
  63.5 6.4 %collective-permute-start.6 = (bf16[2,32,1024]{2,1,0:T(8,128)(2,1)S(1)}, bf16[2,32,1024]{2,1,0:T(8,128)(2,1)S(1)}, u32[]{:S(2)}, u32[]{:S(2)}) collective-permute-start(bf16[2,32,1024]{2,1,0:T(8,128)(2,1)S(1)} %get-tuple-element.155), channel_id=1, source_target_pairs={{0,4},{1,5},{2,6},{3,7},{4,0},{5,1},{6,2},{7,3},{8,12},{9,13},{10,... | collective-permute-start | bytes 393224 | tf_op jit(solution)/shard_map/ppermute | solution.py:394
  63.6 13.5 %collective-permute-start.10 = (bf16[4,32,1024]{2,1,0:T(8,128)(2,1)S(1)}, bf16[4,32,1024]{2,1,0:T(8,128)(2,1)S(1)}, u32[]{:S(2)}, u32[]{:S(2)}) collective-permute-start(bf16[4,32,1024]{2,1,0:T(8,128)(2,1)S(1)} %get-tuple-element.82), channel_id=1, source_target_pairs={{0,2},{1,3},{2,0},{3,1},{4,6},{5,7},{6,4},{7,5},{8,10},{9,11},{10,... | collective-permute-start | bytes 786440 | tf_op jit(solution)/shard_map/ppermute | solution.py:394
  64.4 9.6 %collective-permute-start.5 = (bf16[2,32,1024]{2,1,0:T(8,128)(2,1)S(1)}, bf16[2,32,1024]{2,1,0:T(8,128)(2,1)S(1)}, u32[]{:S(2)}, u32[]{:S(2)}) collective-permute-start(bf16[2,32,1024]{2,1,0:T(8,128)(2,1)S(1)} %get-tuple-element.153), channel_id=1, source_target_pairs={{0,2},{1,3},{2,0},{3,1},{4,6},{5,7},{6,4},{7,5},{8,10},{9,11},{10,... | collective-permute-start | bytes 393224 | tf_op jit(solution)/shard_map/ppermute | solution.py:394
  65.8 13.0 %collective-permute-start.9 = (bf16[4,32,1024]{2,1,0:T(8,128)(2,1)S(1)}, bf16[4,32,1024]{2,1,0:T(8,128)(2,1)S(1)}, u32[]{:S(2)}, u32[]{:S(2)}) collective-permute-start(bf16[4,32,1024]{2,1,0:T(8,128)(2,1)S(1)} %get-tuple-element.87), channel_id=1, source_target_pairs={{0,4},{1,5},{2,6},{3,7},{4,0},{5,1},{6,2},{7,3},{8,12},{9,13},{10,... | collective-permute-start | bytes 786440 | tf_op jit(solution)/shard_map/ppermute | solution.py:394
  70.0 5.9 %collective-permute-start.11 = (bf16[1,32,1024]{2,1,0:T(8,128)(2,1)S(1)}, bf16[1,32,1024]{2,1,0:T(8,128)(2,1)S(1)}, u32[]{:S(2)}, u32[]{:S(2)}) collective-permute-start(bf16[1,32,1024]{2,1,0:T(8,128)(2,1)S(1)} %get-tuple-element.162), channel_id=1, source_target_pairs={{0,8},{1,9},{2,10},{3,11},{4,12},{5,13},{6,14},{7,15},{8,0},{9,1},... | collective-permute-start | bytes 196616 | tf_op jit(solution)/shard_map/ppermute | solution.py:394
  74.0 5.6 %collective-permute-start.8 = (bf16[1,32,1024]{2,1,0:T(8,128)(2,1)S(1)}, bf16[1,32,1024]{2,1,0:T(8,128)(2,1)S(1)}, u32[]{:S(2)}, u32[]{:S(2)}) collective-permute-start(bf16[1,32,1024]{2,1,0:T(8,128)(2,1)S(1)} %get-tuple-element.161), channel_id=1, source_target_pairs={{0,8},{1,9},{2,10},{3,11},{4,12},{5,13},{6,14},{7,15},{8,0},{9,1},... | collective-permute-start | bytes 196616 | tf_op jit(solution)/shard_map/ppermute | solution.py:394
  76.0 8.5 %collective-permute-start.14 = (bf16[1,32,1024]{2,1,0:T(8,128)(2,1)S(1)}, bf16[1,32,1024]{2,1,0:T(8,128)(2,1)S(1)}, u32[]{:S(2)}, u32[]{:S(2)}) collective-permute-start(bf16[1,32,1024]{2,1,0:T(8,128)(2,1)S(1)} %bitcast.24), channel_id=1, source_target_pairs={{0,8},{1,9},{2,10},{3,11},{4,12},{5,13},{6,14},{7,15},{8,0},{9,1},... | collective-permute-start | bytes 196616 | tf_op jit(solution)/shard_map/ppermute | solution.py:394
  77.1 31.3 %copy-start.2 = (bf16[16384]{0:T(1024)(128)(2,1)S(1)}, bf16[16384]{0:T(1024)(128)(2,1)}, u32[]{:S(2)}) copy-start(bf16[16384]{0:T(1024)(128)(2,1)} %param.17) | copy-start | bytes 98308
  77.2 10.5 %collective-permute-start.12 = (bf16[2,32,1024]{2,1,0:T(8,128)(2,1)S(1)}, bf16[2,32,1024]{2,1,0:T(8,128)(2,1)S(1)}, u32[]{:S(2)}, u32[]{:S(2)}) collective-permute-start(bf16[2,32,1024]{2,1,0:T(8,128)(2,1)S(1)} %get-tuple-element.149), channel_id=1, source_target_pairs={{0,4},{1,5},{2,6},{3,7},{4,0},{5,1},{6,2},{7,3},{8,12},{9,13},{10,... | collective-permute-start | bytes 393224 | tf_op jit(solution)/shard_map/ppermute | solution.py:394
  78.9 5.0 %collective-permute-start.15 = (bf16[2,32,1024]{2,1,0:T(8,128)(2,1)S(1)}, bf16[2,32,1024]{2,1,0:T(8,128)(2,1)S(1)}, u32[]{:S(2)}, u32[]{:S(2)}) collective-permute-start(bf16[2,32,1024]{2,1,0:T(8,128)(2,1)S(1)} %get-tuple-element.150), channel_id=1, source_target_pairs={{0,2},{1,3},{2,0},{3,1},{4,6},{5,7},{6,4},{7,5},{8,10},{9,11},{10,... | collective-permute-start | bytes 393224 | tf_op jit(solution)/shard_map/ppermute | solution.py:394
  79.6 6.8 %collective-permute-start.13 = (bf16[1,32,1024]{2,1,0:T(8,128)(2,1)S(1)}, bf16[1,32,1024]{2,1,0:T(8,128)(2,1)S(1)}, u32[]{:S(2)}, u32[]{:S(2)}) collective-permute-start(bf16[1,32,1024]{2,1,0:T(8,128)(2,1)S(1)} %bitcast.26), channel_id=1, source_target_pairs={{0,8},{1,9},{2,10},{3,11},{4,12},{5,13},{6,14},{7,15},{8,0},{9,1},... | collective-permute-start | bytes 196616 | tf_op jit(solution)/shard_map/ppermute | solution.py:394
  84.0 7.2 %collective-permute-start.19 = (bf16[1,32,1024]{2,1,0:T(8,128)(2,1)S(1)}, bf16[1,32,1024]{2,1,0:T(8,128)(2,1)S(1)}, u32[]{:S(2)}, u32[]{:S(2)}) collective-permute-start(bf16[1,32,1024]{2,1,0:T(8,128)(2,1)S(1)} %get-tuple-element.158), channel_id=1, source_target_pairs={{0,8},{1,9},{2,10},{3,11},{4,12},{5,13},{6,14},{7,15},{8,0},{9,1},... | collective-permute-start | bytes 196616 | tf_op jit(solution)/shard_map/ppermute | solution.py:394
  84.5 9.1 %collective-permute-start.17 = (bf16[2,32,1024]{2,1,0:T(8,128)(2,1)S(1)}, bf16[2,32,1024]{2,1,0:T(8,128)(2,1)S(1)}, u32[]{:S(2)}, u32[]{:S(2)}) collective-permute-start(bf16[2,32,1024]{2,1,0:T(8,128)(2,1)S(1)} %constant_dynamic-update-slice_fusion), channel_id=1, source_target_pairs={{0,4},{1,5},{2,6},{3,7},{4,0},{5,1},{6,2},{7,3},{8,12},{9,13},{10,... | collective-permute-start | bytes 393224 | tf_op jit(solution)/shard_map/ppermute | solution.py:394
  86.5 6.4 %collective-permute-start.18 = (bf16[2,32,1024]{2,1,0:T(8,128)(2,1)S(1)}, bf16[2,32,1024]{2,1,0:T(8,128)(2,1)S(1)}, u32[]{:S(2)}, u32[]{:S(2)}) collective-permute-start(bf16[2,32,1024]{2,1,0:T(8,128)(2,1)S(1)} %constant_dynamic-update-slice_fusion.2), channel_id=1, source_target_pairs={{0,2},{1,3},{2,0},{3,1},{4,6},{5,7},{6,4},{7,5},{8,10},{9,11},{10,... | collective-permute-start | bytes 393224 | tf_op jit(solution)/shard_map/ppermute | solution.py:394
  87.8 6.5 %collective-permute-start.16 = (bf16[1,32,1024]{2,1,0:T(8,128)(2,1)S(1)}, bf16[1,32,1024]{2,1,0:T(8,128)(2,1)S(1)}, u32[]{:S(2)}, u32[]{:S(2)}) collective-permute-start(bf16[1,32,1024]{2,1,0:T(8,128)(2,1)S(1)} %get-tuple-element.157), channel_id=1, source_target_pairs={{0,8},{1,9},{2,10},{3,11},{4,12},{5,13},{6,14},{7,15},{8,0},{9,1},... | collective-permute-start | bytes 196616 | tf_op jit(solution)/shard_map/ppermute | solution.py:394
  91.2 6.0 %collective-permute-start.21 = (bf16[1,32,1024]{2,1,0:T(8,128)(2,1)S(1)}, bf16[1,32,1024]{2,1,0:T(8,128)(2,1)S(1)}, u32[]{:S(2)}, u32[]{:S(2)}) collective-permute-start(bf16[1,32,1024]{2,1,0:T(8,128)(2,1)S(1)} %bitcast.28), channel_id=1, source_target_pairs={{0,8},{1,9},{2,10},{3,11},{4,12},{5,13},{6,14},{7,15},{8,0},{9,1},... | collective-permute-start | bytes 196616 | tf_op jit(solution)/shard_map/ppermute | solution.py:394
  92.9 9.9 %collective-permute-start.23 = (bf16[4,32,1024]{2,1,0:T(8,128)(2,1)S(1)}, bf16[4,32,1024]{2,1,0:T(8,128)(2,1)S(1)}, u32[]{:S(2)}, u32[]{:S(2)}) collective-permute-start(bf16[4,32,1024]{2,1,0:T(8,128)(2,1)S(1)} %constant_dynamic-update-slice_fusion.4), channel_id=1, source_target_pairs={{0,4},{1,5},{2,6},{3,7},{4,0},{5,1},{6,2},{7,3},{8,12},{9,13},{10,... | collective-permute-start | bytes 786440 | tf_op jit(solution)/shard_map/ppermute | solution.py:394
  93.6 12.1 %collective-permute-start.27 = (bf16[4,32,1024]{2,1,0:T(8,128)(2,1)S(1)}, bf16[4,32,1024]{2,1,0:T(8,128)(2,1)S(1)}, u32[]{:S(2)}, u32[]{:S(2)}) collective-permute-start(bf16[4,32,1024]{2,1,0:T(8,128)(2,1)S(1)} %constant_dynamic-update-slice_fusion.6), channel_id=1, source_target_pairs={{0,2},{1,3},{2,0},{3,1},{4,6},{5,7},{6,4},{7,5},{8,10},{9,11},{10,... | collective-permute-start | bytes 786440 | tf_op jit(solution)/shard_map/ppermute | solution.py:394
  94.3 5.3 %collective-permute-start.20 = (bf16[1,32,1024]{2,1,0:T(8,128)(2,1)S(1)}, bf16[1,32,1024]{2,1,0:T(8,128)(2,1)S(1)}, u32[]{:S(2)}, u32[]{:S(2)}) collective-permute-start(bf16[1,32,1024]{2,1,0:T(8,128)(2,1)S(1)} %bitcast.30), channel_id=1, source_target_pairs={{0,8},{1,9},{2,10},{3,11},{4,12},{5,13},{6,14},{7,15},{8,0},{9,1},... | collective-permute-start | bytes 196616 | tf_op jit(solution)/shard_map/ppermute | solution.py:394
  97.2 5.6 %collective-permute-start.24 = (bf16[2,32,1024]{2,1,0:T(8,128)(2,1)S(1)}, bf16[2,32,1024]{2,1,0:T(8,128)(2,1)S(1)}, u32[]{:S(2)}, u32[]{:S(2)}) collective-permute-start(bf16[2,32,1024]{2,1,0:T(8,128)(2,1)S(1)} %constant_dynamic-update-slice_fusion.8), channel_id=1, source_target_pairs={{0,2},{1,3},{2,0},{3,1},{4,6},{5,7},{6,4},{7,5},{8,10},{9,11},{10,... | collective-permute-start | bytes 393224 | tf_op jit(solution)/shard_map/ppermute | solution.py:394
  99.7 6.1 %collective-permute-start.22 = (bf16[2,32,1024]{2,1,0:T(8,128)(2,1)S(1)}, bf16[2,32,1024]{2,1,0:T(8,128)(2,1)S(1)}, u32[]{:S(2)}, u32[]{:S(2)}) collective-permute-start(bf16[2,32,1024]{2,1,0:T(8,128)(2,1)S(1)} %constant_dynamic-update-slice_fusion.10), channel_id=1, source_target_pairs={{0,4},{1,5},{2,6},{3,7},{4,0},{5,1},{6,2},{7,3},{8,12},{9,13},{10,... | collective-permute-start | bytes 393224 | tf_op jit(solution)/shard_map/ppermute | solution.py:394
  102.9 5.5 %collective-permute-start.29 = (bf16[8,32,1024]{2,1,0:T(8,128)(2,1)S(1)}, bf16[8,32,1024]{2,1,0:T(8,128)(2,1)S(1)}, u32[]{:S(2)}, u32[]{:S(2)}) collective-permute-start(bf16[8,32,1024]{2,1,0:T(8,128)(2,1)S(1)} %constant_dynamic-update-slice_fusion.14.own_ref), channel_id=1, source_target_pairs={{0,1},{1,0},{2,3},{3,2},{4,5},{5,4},{6,7},{7,6},{8,9},{9,8},{10,11... | collective-permute-start | bytes 1572872 | tf_op jit(solution)/shard_map/ppermute | solution.py:394
  105.8 4.3 %collective-permute-start.28 = (bf16[8,32,1024]{2,1,0:T(8,128)(2,1)S(1)}, bf16[8,32,1024]{2,1,0:T(8,128)(2,1)S(1)}, u32[]{:S(2)}, u32[]{:S(2)}) collective-permute-start(bf16[8,32,1024]{2,1,0:T(8,128)(2,1)S(1)} %constant_dynamic-update-slice_fusion.18.own_ref), channel_id=1, source_target_pairs={{0,1},{1,0},{2,3},{3,2},{4,5},{5,4},{6,7},{7,6},{8,9},{9,8},{10,11... | collective-permute-start | bytes 1572872 | tf_op jit(solution)/shard_map/ppermute | solution.py:394
  105.9 9.0 %collective-permute-start.26 = (bf16[4,32,1024]{2,1,0:T(8,128)(2,1)S(1)}, bf16[4,32,1024]{2,1,0:T(8,128)(2,1)S(1)}, u32[]{:S(2)}, u32[]{:S(2)}) collective-permute-start(bf16[4,32,1024]{2,1,0:T(8,128)(2,1)S(1)} %constant_dynamic-update-slice_fusion.12), channel_id=1, source_target_pairs={{0,4},{1,5},{2,6},{3,7},{4,0},{5,1},{6,2},{7,3},{8,12},{9,13},{10,... | collective-permute-start | bytes 786440 | tf_op jit(solution)/shard_map/ppermute | solution.py:394
  108.0 8.4 %collective-permute-start.25 = (bf16[4,32,1024]{2,1,0:T(8,128)(2,1)S(1)}, bf16[4,32,1024]{2,1,0:T(8,128)(2,1)S(1)}, u32[]{:S(2)}, u32[]{:S(2)}) collective-permute-start(bf16[4,32,1024]{2,1,0:T(8,128)(2,1)S(1)} %constant_dynamic-update-slice_fusion.16), channel_id=1, source_target_pairs={{0,2},{1,3},{2,0},{3,1},{4,6},{5,7},{6,4},{7,5},{8,10},{9,11},{10,... | collective-permute-start | bytes 786440 | tf_op jit(solution)/shard_map/ppermute | solution.py:394
  114.9 2.3 %collective-permute-start.31 = (bf16[8,32,1024]{2,1,0:T(8,128)(2,1)S(1)}, bf16[8,32,1024]{2,1,0:T(8,128)(2,1)S(1)}, u32[]{:S(2)}, u32[]{:S(2)}) collective-permute-start(bf16[8,32,1024]{2,1,0:T(8,128)(2,1)S(1)} %constant_dynamic-update-slice_fusion.20.own_ref), channel_id=1, source_target_pairs={{0,1},{1,0},{2,3},{3,2},{4,5},{5,4},{6,7},{7,6},{8,9},{9,8},{10,11... | collective-permute-start | bytes 1572872 | tf_op jit(solution)/shard_map/ppermute | solution.py:394
  116.4 2.5 %collective-permute-start.30 = (bf16[8,32,1024]{2,1,0:T(8,128)(2,1)S(1)}, bf16[8,32,1024]{2,1,0:T(8,128)(2,1)S(1)}, u32[]{:S(2)}, u32[]{:S(2)}) collective-permute-start(bf16[8,32,1024]{2,1,0:T(8,128)(2,1)S(1)} %constant_dynamic-update-slice_fusion.22.own_ref), channel_id=1, source_target_pairs={{0,1},{1,0},{2,3},{3,2},{4,5},{5,4},{6,7},{7,6},{8,9},{9,8},{10,11... | collective-permute-start | bytes 1572872 | tf_op jit(solution)/shard_map/ppermute | solution.py:394

commit v7 on v6

--- a/solution.py
+++ b/solution.py
@@ -11,7 +11,7 @@
 HD = 128
 
 
-TABLE = "20210320213032013021313012023131"
+TABLE = "101203101230310230123230211323"
 
 epsilon = 1e-05
 rope_theta = 500000.0
@@ -31,8 +31,8 @@
 
 
 def input_kernel(count, hidden_ref, gain_ref, w_ref, kv_ref, cosine_ref, sine_ref, *refs):
-    out_ref, mine_ref, hidden, w_buffer, kv_buffer, normed, products, kv_products, *sems = refs
-    h_sem, w_sem, kv_sem, mine_sem = sems
+    out_ref, mine_ref, hidden, gain_buffer, w_buffer, kv_buffer, normed, products, kv_products, *sems = refs
+    h_sem, w_sem, kv_sem, mine_sem, gain_sem = sems
     me = lax.axis_index("tensor")
     rows, columns = hidden.shape
     depth = normed.shape[2]
@@ -54,6 +54,8 @@
 
     for k in range(chunks):
         hidden_copy(k).start()
+    gain_copy = pltpu.make_async_copy(gain_ref, gain_buffer, gain_sem)
+    gain_copy.start()
     kv_copy = pltpu.make_async_copy(kv_ref, kv_buffer, kv_sem)
     own = pl.ds(pl.multiple_of(me * (columns // count), columns // count), columns // count)
     mine_copy = pltpu.make_async_copy(hidden_ref.at[:, own], mine_ref, mine_sem)
@@ -73,9 +75,10 @@
 
     def norm(k):
         floats = hidden[:, span(k)].astype(jnp.float32)
-        gain = gain_ref[span(k)].astype(jnp.float32).reshape(1, depth)
+        gain = gain_buffer[span(k)].astype(jnp.float32).reshape(1, depth)
         normed[k % 2] = (floats * scale * gain).astype(jnp.bfloat16)
 
+    gain_copy.wait()
     norm(0)
     kv_copy.wait()
     for k in range(chunks):
@@ -120,10 +123,11 @@
             jax.ShapeDtypeStruct((count, rows // count, width + HD), jnp.bfloat16),
             jax.ShapeDtypeStruct((rows, columns // count), jnp.bfloat16),
         ),
-        in_specs=[whole, vmem, whole, whole, vmem, vmem],
+        in_specs=[whole, whole, whole, whole, vmem, vmem],
         out_specs=(vmem, vmem),
         scratch_shapes=[
             pltpu.VMEM((rows, columns), jnp.bfloat16),
+            pltpu.VMEM((columns,), jnp.bfloat16),
             pltpu.VMEM((columns, width), jnp.bfloat16),
             pltpu.VMEM((kv_width, columns), jnp.bfloat16),
             pltpu.VMEM((2, rows, depth), jnp.bfloat16),
@@ -131,6 +135,7 @@
             pltpu.VMEM((rows, kv_width), jnp.float32),
             pltpu.SemaphoreType.DMA((chunks,)),
             pltpu.SemaphoreType.DMA((chunks,)),
+            pltpu.SemaphoreType.DMA,
             pltpu.SemaphoreType.DMA,
             pltpu.SemaphoreType.DMA,
         ],
@@ -289,7 +294,8 @@
 def timetable(count):
     if count == 16:
         return [int(c) for c in TABLE]
-    return [s for _ in range(2 * (count.bit_length() - 2) + 2) for s in (0, 3, 1, 2)]
+    steps = 2 * (count.bit_length() - 2) + 1
+    return [s for _ in range(steps) for s in (1, 0, 2, 3)] + [1, 3]
 
 
 def place(offset, order):
@@ -299,10 +305,12 @@
     return spot
 
 
-def project_kernel(count, offsets, w_ref, *refs):
-    in_ref, *set_refs, heads_buffer, w_buffer, arrived = refs
+def project_kernel(count, side, in_ref, w_ref, *refs):
+    *set_refs, heads_buffer, w_buffer, arrived = refs
     me = lax.axis_index("tensor")
     width = w_buffer.shape[2]
+    offsets = [k for k in range(count) if (k >> 1) % 2 == side]
+    offsets = [k for k in offsets if k % 2] + [k for k in offsets if k % 2 == 0]
     copies = []
     for slot, offset in enumerate(offsets):
         column = pl.multiple_of(jnp.bitwise_xor(me, offset) * width, width)
@@ -322,67 +330,76 @@
             jnp.bfloat16
         )
         start = 0
-        for ref, (order, _) in zip(set_refs, plans(count)):
-            ref[place(offset, order)] = product[start : start + ref.shape[1]]
+        for which, (order, _) in enumerate(plans(count)):
+            ref = set_refs[2 * which + (1 - offset % 2)]
+            spot = place(offset, [bit for bit in order if bit != 1])
+            ref[spot] = product[start : start + ref.shape[1]]
             start += ref.shape[1]
 
 
-def project(blocks, w_out, offsets):
+def project(blocks, w_out, side):
     count, here, depth = blocks.shape
     rows = count * here
     width = w_out.shape[1] // count
     sets = len(plans(count))
-    share = jax.ShapeDtypeStruct((len(offsets), rows // sets, width), jnp.bfloat16)
-    return pl.pallas_call(
-        functools.partial(project_kernel, count, offsets),
-        out_shape=(share,) * sets,
-        in_specs=[pl.BlockSpec(memory_space=pl.ANY), pl.BlockSpec(memory_space=pltpu.VMEM)],
-        out_specs=(pl.BlockSpec(memory_space=pltpu.VMEM),) * sets,
+    share = jax.ShapeDtypeStruct((count // 4, rows // sets, width), jnp.bfloat16)
+    outs = pl.pallas_call(
+        functools.partial(project_kernel, count, side),
+        out_shape=(share,) * (2 * sets),
+        in_specs=[pl.BlockSpec(memory_space=pltpu.VMEM), pl.BlockSpec(memory_space=pl.ANY)],
+        out_specs=(pl.BlockSpec(memory_space=pltpu.VMEM),) * (2 * sets),
         scratch_shapes=[
             pltpu.VMEM((rows, depth), jnp.float32),
-            pltpu.VMEM((len(offsets), depth, width), jnp.bfloat16),
-            pltpu.SemaphoreType.DMA((len(offsets),)),
+            pltpu.VMEM((count // 2, depth, width), jnp.bfloat16),
+            pltpu.SemaphoreType.DMA((count // 2,)),
         ],
         compiler_params=pltpu.CompilerParams(vmem_limit_bytes=48 * 1024 * 1024),
         cost_estimate=pl.CostEstimate(
-            flops=2 * rows * depth * width * len(offsets),
-            bytes_accessed=2 * (depth + rows) * width * len(offsets),
+            flops=rows * depth * width * count,
+            bytes_accessed=(depth + rows) * width * count,
             transcendentals=0,
         ),
-    )(w_out, blocks)
-
-
-def finish_kernel(offsets, own_ref, other_ref, gain_ref, *refs):
+    )(blocks, w_out)
+    return outs[0::2], outs[1::2]
+
+
+def finish_kernel(offsets, gain_ref, *refs):
     out_ref = refs[-1]
     me = lax.axis_index("tensor")
-    half, rows, width = own_ref.shape
-    total = jnp.zeros((rows, width), jnp.float32)
-    for ref in (own_ref, other_ref):
-        for k in range(half):
-            block = ref[k].astype(jnp.float32)
-            total = total + block * block
-    mean_square = jnp.sum(total, axis=1, keepdims=True) / (2 * half * width)
-    scale = lax.rsqrt(mean_square + epsilon)
-    for k, offset in enumerate(offsets):
-        block = (own_ref if k < half else other_ref)[k % half].astype(jnp.float32)
-        index = jnp.bitwise_xor(me, offset)
-        column = pl.multiple_of(index * width, width)
-        gain = gain_ref[pl.ds(index, 1), :]
-        out_ref[:, pl.ds(column, width)] = (block * scale * gain).astype(jnp.bfloat16)
-
-
-def finish(own, other, gain, offsets, which, sets, earlier):
-    half, rows, width = own.shape
-    columns = 2 * half * width
-    operands = [own, other, gain] + ([] if earlier is None else [earlier])
-    whole = pl.BlockSpec(memory_space=pltpu.VMEM)
+    half, rows, width = refs[0].shape
+    for k, order in enumerate(offsets):
+        parts = refs[2 * k : 2 * k + 2]
+        total = jnp.zeros((rows, width), jnp.float32)
+        for ref in parts:
+            for spot in range(half):
+                block = ref[spot].astype(jnp.float32)
+                total = total + block * block
+        mean_square = jnp.sum(total, axis=1, keepdims=True) / (2 * half * width)
+        scale = lax.rsqrt(mean_square + epsilon)
+        for spot, offset in enumerate(order):
+            block = parts[spot // half][spot % half].astype(jnp.float32)
+            index = jnp.bitwise_xor(me, offset)
+            column = pl.multiple_of(index * width, width)
+            gain = gain_ref[pl.ds(index, 1), :]
+            out_ref[k * rows : (k + 1) * rows, pl.ds(column, width)] = (
+                block * scale * gain
+            ).astype(jnp.bfloat16)
+
+
+def finish(parts, gain, offsets, which, groups, earlier):
+    half, rows, width = parts[0].shape
+    columns, rows = 2 * half * width, rows * len(offsets)
+    operands = [gain, *parts] + ([] if earlier is None else [earlier])
+    specs = [pl.BlockSpec(memory_space=pltpu.VMEM)] * (1 + len(parts))
+    if earlier is not None:
+        specs.append(pl.BlockSpec(memory_space=pl.ANY))
     return pl.pallas_call(
         functools.partial(finish_kernel, offsets),
         grid=(1,),
-        out_shape=jax.ShapeDtypeStruct((rows * sets, columns), jnp.bfloat16),
-        in_specs=[whole] * 3 + [pl.BlockSpec(memory_space=pl.ANY)] * (len(operands) - 3),
+        out_shape=jax.ShapeDtypeStruct((rows * groups, columns), jnp.bfloat16),
+        in_specs=specs,
         out_specs=pl.BlockSpec((rows, columns), lambda i: (which, 0)),
-        input_output_aliases={} if earlier is None else {3: 0},
+        input_output_aliases={} if earlier is None else {len(operands) - 1: 0},
         compiler_params=pltpu.CompilerParams(vmem_limit_bytes=24 * 1024 * 1024),
         cost_estimate=pl.CostEstimate(
             flops=6 * rows * columns, bytes_accessed=4 * rows * columns, transcendentals=0
@@ -396,6 +413,11 @@
 
 def add(one, other):
     return (one.astype(jnp.float32) + other.astype(jnp.float32)).astype(jnp.bfloat16)
+
+
+def halves(keep, arrival):
+    half = keep.shape[0] // 2
+    return add(keep[:half], arrival[:half]), add(keep[half:], arrival[half:])
 
 
 def on_device(
@@ -413,9 +435,7 @@
     row_count = hidden_in.shape[0]
     count = lax.axis_size("tensor")
     cosine, sine = turns(positions)
-    blocks, mine = project_in(
-        hidden_in, attn_gain, w_query, w_keyval, cosine, sine, count
-    )
+    blocks, mine = project_in(hidden_in, attn_gain, w_query, w_keyval, cosine, sine, count)
     head_blocks = exchange(
         attend(exchange(blocks), lengths, cosine, sine, cache_keys, cache_values)
     )
@@ -424,20 +444,30 @@
     orders = plans(count)
     sets = len(orders)
     set_rows = row_count // sets
-    sent = project(head_blocks, w_out, list(range(1, count, 2)))
-    arrivals = [swap(block, 0, count) for block in sent]
-    kept = project(head_blocks, w_out, list(range(0, count, 2)))
-
-    def halves(keep, arrival):
-        half = keep.shape[0] // 2
-        return add(keep[:half], arrival[:half]), add(keep[half:], arrival[half:])
-
-    held, leaving = zip(*[halves(kept[k], arrivals[k]) for k in range(sets)])
-    held = list(held)
+
+    def core_sums(heads, side):
+        sent, kept = project(heads, w_out, side)
+        arrivals = [swap(block, 0, count) for block in sent]
+        return [add(keep, arrival) for keep, arrival in zip(kept, arrivals)]
+
+    far = core_sums(head_blocks, 1)
+    first = timetable(count)[0]
+    gate, far[first] = lax.optimization_barrier((head_blocks, far[first]))
+    near = core_sums(gate, 0)
+    held, leaving = [], []
+    for k in range(sets):
+        if orders[k][0][0] == 1:
+            held.append(near[k])
+            leaving.append(far[k])
+        else:
+            half = far[k].shape[0] // 2
+            held.append(jnp.concatenate([near[k][:half], far[k][:half]], axis=0))
+            leaving.append(jnp.concatenate([near[k][half:], far[k][half:]], axis=0))
     streams = [None] * sets
     offsets = [[0] for _ in range(sets)]
     steps = [0] * sets
     last = normed = None
+    arrivals = [None] * sets
     for k in timetable(count):
         scatter, gather = orders[k]
         step = steps[k]
@@ -462,7 +492,10 @@
         elif step <= len(scatter) + len(gather):
             last = held[k] = jnp.concatenate([held[k], arrivals[k]], axis=0)
         else:
-            last = normed = finish(held[k], arrivals[k], gain, offsets[k], k, sets, normed)
+            pair = [k - 1, k]
+            parts = [block for m in pair for block in (held[m], arrivals[m])]
+            lists = [offsets[m] for m in pair]
+            last = normed = finish(parts, gain, lists, k // 2, sets // 2, normed)
             continue
         bit = (gather + [0])[step - len(scatter)]
         arrivals[k] = swap(held[k], bit, count)

time: 121 us -> 123 us (1.017)
  starting transfers between devices: 25.3 us -> 33.2 us
  waiting for transfers between devices: 32.2 us -> 28.1 us
  Pallas kernels: 31.7 us -> 30.1 us
    ppermute x32 -> x36, starting transfers between devices: 25.3 us -> 33.2 us  [swap(): lax.ppermute(values, 'tensor', [(i, i ^ 1 << bit) for i in range(count)])]
    ppermute x32 -> x36, waiting for transfers between devices: 32.2 us -> 28.1 us  [swap(): lax.ppermute(values, 'tensor', [(i, i ^ 1 << bit) for i in range(count)])]
    pallas_call x4 -> x2, Pallas kernels: 6.61 us -> 5.45 us  [finish(): pl.pallas_call(functools.partial(finish_kernel, offsets), grid=(1,), out_...]
  transfers between devices with their start and end apart: 32 -> 36, of which waited for: 12 -> 15; matrix products, arithmetic and copies ran while one was open for 2% -> 2% of each run, Pallas kernels for 7% -> 5%
where the time goes in v7:
time: 123 us
  starting transfers between devices  33.2 us (27%)
  Pallas kernels  30.1 us (24%)
  waiting for transfers between devices  28.1 us (23%)
  blocking collectives  26.2 us (21%)
  other arithmetic  2.85 us (2%)
    ppermute x36, starting transfers between devices, swap(): lax.ppermute(values, 'tensor', [(i, i ^ 1 << bit) for i in range(count)])  33.2 us
    ppermute x36, waiting for transfers between devices, swap(): lax.ppermute(values, 'tensor', [(i, i ^ 1 << bit) for i in range(count)])  28.1 us
    all_to_all x2, blocking collectives, exchange(): lax.all_to_all(blocks, 'tensor', split_axis=0, concat_axis=0, tiled=True)  26.2 us
    pallas_call x1, Pallas kernels, project_in(): pl.pallas_call(functools.partial(input_kernel, count), out_shape=(jax.Sha...  10.3 us
    pallas_call x2, Pallas kernels, project(): pl.pallas_call(functools.partial(project_kernel, count, side), out_shape=...  7.67 us
    pallas_call x1, Pallas kernels, attend(): pl.pallas_call(functools.partial(attend_kernel, count), out_shape=jax.Sha...  6.62 us
    pallas_call x2, Pallas kernels, finish(): pl.pallas_call(functools.partial(finish_kernel, offsets), grid=(1,), out_...  5.45 us
  transfers between devices with their start and end apart: 36, of which 15 were waited for; matrix products, arithmetic and copies ran while one was open for 2% of the time, Pallas kernels for 5%

profile of v7, /device:TPU:0, one launch (start us, length us, event | category | flops | bytes accessed | tf_op | source)
XLA Modules:
  0.0 122.7 jit_solution(8631025486939751518)
XLA Ops:
  0.6 0.7 convert_element_type.283
  1.3 0.3 fusion.4
  1.6 0.7 copy-done.1
  2.4 10.3 %shard_map.113 = (bf16[16,8,640]{2,1,0:T(8,128)(2,1)S(1)}, bf16[128,1024]{1,0:T(8,128)(2,1)S(1)}) custom-call(bf16[128,16384]{1,0:T(8,128)(2,1)} %hidden_ref.1, bf16[16384]{0:T(1024)(128)(2,1)S(1)} %copy-done.1, bf16[16384,512]{1,0:T(8,128)(2,1)} %w_ref.3, bf16[64,16384]{1,0:T(8,128)(2,1)} %bitcast.21, f32[128,128]{1,0:T(8,128)S(1)} %get-tuple-element.177.cosine_ref, ...), custom_call_target="tpu_custom_call" | custom-call | flops 2415919104 | bytes 23068672 | tf_op jit(solution)/shard_map/pallas_call | solution.py:120
  12.7 15.7 %all_to_all.10.refs_0_ = bf16[16,8,640]{2,1,0:T(8,128)(2,1)S(1)} all-to-all(bf16[16,8,640]{2,1,0:T(8,128)(2,1)S(1)} %get-tuple-element.78), channel_id=1, replica_groups=mesh['groups'=2,'tensor'=16] {'tensor'}, dimensions={0} | all-to-all | bytes 327680 | tf_op jit(solution)/shard_map/all_to_all | solution.py:284
  28.4 6.6 %shard_map.114 = bf16[16,8,512]{2,1,0:T(8,128)(2,1)S(1)} custom-call(s32[8]{0:T(128)S(1)} %copy-done.2, f32[128,128]{1,0:T(8,128)S(1)} %get-tuple-element.177.cosine_ref, f32[128,128]{1,0:T(8,128)S(1)} %get-tuple-element.176.sine_ref, bf16[8,1024,512]{2,1,0:T(8,128)(2,1)S(1)} %copy-done, bf16[8,1024,512]{2,1,0:T(8,128)(2,1)} %values_ref.1, ...), custom_call_target="tpu_custom_call" | custom-call | flops 268435456 | bytes 16777216 | tf_op jit(solution)/shard_map/pallas_call | solution.py:259
  35.0 10.5 %all_to_all.11.in_ref = bf16[16,8,512]{2,1,0:T(8,128)(2,1)S(1)} all-to-all(bf16[16,8,512]{2,1,0:T(8,128)(2,1)S(1)} %shard_map.114), channel_id=1, replica_groups=mesh['groups'=2,'tensor'=16] {'tensor'}, dimensions={0} | all-to-all | bytes 262144 | tf_op jit(solution)/shard_map/all_to_all | solution.py:284
  45.5 3.8 %shard_map.115 = (bf16[4,32,1024]{2,1,0:T(8,128)(2,1)S(1)}, bf16[4,32,1024]{2,1,0:T(8,128)(2,1)S(1)}, bf16[4,32,1024]{2,1,0:T(8,128)(2,1)S(1)}, bf16[4,32,1024]{...) custom-call(bf16[16,8,512]{2,1,0:T(8,128)(2,1)S(1)} %all_to_all.11.i, ...), custom_call_target="tpu_custom_call" | custom-call | flops 1073741824 | bytes 10485760 | tf_op jit(solution)/shard_map/pallas_call | solution.py:346
  49.4 0.1 collective-permute-start
  49.4 0.5 collective-permute-start.2
  49.9 0.1 collective-permute-start.4
  50.0 0.4 collective-permute-start.10
  50.5 0.5 collective-permute-done
  51.0 0.1 collective-permute-start.6
  51.1 3.8 %shard_map.116 = (bf16[4,32,1024]{2,1,0:T(8,128)(2,1)S(1)}, bf16[4,32,1024]{2,1,0:T(8,128)(2,1)S(1)}, bf16[4,32,1024]{2,1,0:T(8,128)(2,1)S(1)}, bf16[4,32,1024]{...) custom-call(bf16[16,8,512]{2,1,0:T(8,128)(2,1)S(1)} %all_to_all.11.i, ...), custom_call_target="tpu_custom_call" | custom-call | flops 1073741824 | bytes 10485760 | tf_op jit(solution)/shard_map/pallas_call | solution.py:346
  55.0 0.2 collective-permute-start.1
  55.3 0.1 add_convert_fusion.1
  55.4 0.4 collective-permute-start.5
  55.8 0.1 collective-permute-start.9
  56.0 0.4 collective-permute-start.13
  56.4 0.2 collective-permute-done.1
  56.7 0.4 collective-permute-start.3
  57.2 2.2 %collective-permute-done.6 = bf16[4,32,1024]{2,1,0:T(8,128)(2,1)S(1)} collective-permute-done((bf16[4,32,1024]{2,1,0:T(8,128)(2,1)S(1)}, bf16[4,32,1024]{2,1,0:T(8,128)(2,1)S(1)}, u32[]{:S(2)}, u32[]{:S(2)}) %collective-permute-start.6) | collective-permute-done | bytes 262176 | tf_op jit(solution)/shard_map/ppermute | solution.py:411
  59.5 0.1 collective-permute-start.8
  59.6 1.4 %collective-permute-start.14 = (bf16[4,32,1024]{2,1,0:T(8,128)(2,1)S(1)}, bf16[4,32,1024]{2,1,0:T(8,128)(2,1)S(1)}, u32[]{:S(2)}, u32[]{:S(2)}) collective-permute-start(bf16[4,32,1024]{2,1,0:T(8,128)(2,1)S(1)} %add_convert_fusion.4), channel_id=1, source_target_pairs={{0,2},{1,3},{2,0},{3,1},{4,6},{5,7},{6,4},{7,5},{8,10},{9,11},{10,... | collective-permute-start | bytes 786440 | tf_op jit(solution)/shard_map/ppermute | solution.py:411
  61.3 0.1 add_convert_fusion
  61.3 4.6 %collective-permute-done.3 = bf16[4,32,1024]{2,1,0:T(8,128)(2,1)S(1)} collective-permute-done((bf16[4,32,1024]{2,1,0:T(8,128)(2,1)S(1)}, bf16[4,32,1024]{2,1,0:T(8,128)(2,1)S(1)}, u32[]{:S(2)}, u32[]{:S(2)}) %collective-permute-start.3) | collective-permute-done | bytes 262176 | tf_op jit(solution)/shard_map/ppermute | solution.py:411
  66.0 2.1 %collective-permute-start.7 = (bf16[2,32,1024]{2,1,0:T(8,128)(2,1)S(1)}, bf16[2,32,1024]{2,1,0:T(8,128)(2,1)S(1)}, u32[]{:S(2)}, u32[]{:S(2)}) collective-permute-start(bf16[2,32,1024]{2,1,0:T(8,128)(2,1)S(1)} %get-tuple-element.157), channel_id=1, source_target_pairs={{0,2},{1,3},{2,0},{3,1},{4,6},{5,7},{6,4},{7,5},{8,10},{9,11},{10,... | collective-permute-start | bytes 393224 | tf_op jit(solution)/shard_map/ppermute | solution.py:411
  68.1 1.3 %collective-permute-start.15 = (bf16[1,32,1024]{2,1,0:T(8,128)(2,1)S(1)}, bf16[1,32,1024]{2,1,0:T(8,128)(2,1)S(1)}, u32[]{:S(2)}, u32[]{:S(2)}) collective-permute-start(bf16[1,32,1024]{2,1,0:T(8,128)(2,1)S(1)} %get-tuple-element.166), channel_id=1, source_target_pairs={{0,8},{1,9},{2,10},{3,11},{4,12},{5,13},{6,14},{7,15},{8,0},{9,1},... | collective-permute-start | bytes 196616 | tf_op jit(solution)/shard_map/ppermute | solution.py:411
  69.4 1.6 %collective-permute-done.7 = bf16[2,32,1024]{2,1,0:T(8,128)(2,1)S(1)} collective-permute-done((bf16[2,32,1024]{2,1,0:T(8,128)(2,1)S(1)}, bf16[2,32,1024]{2,1,0:T(8,128)(2,1)S(1)}, u32[]{:S(2)}, u32[]{:S(2)}) %collective-permute-start.7) | collective-permute-done | bytes 131104 | tf_op jit(solution)/shard_map/ppermute | solution.py:411
  71.1 0.7 collective-permute-start.11
  71.8 3.0 %collective-permute-done.15 = bf16[1,32,1024]{2,1,0:T(8,128)(2,1)S(1)} collective-permute-done((bf16[1,32,1024]{2,1,0:T(8,128)(2,1)S(1)}, bf16[1,32,1024]{2,1,0:T(8,128)(2,1)S(1)}, u32[]{:S(2)}, u32[]{:S(2)}) %collective-permute-start.15) | collective-permute-done | bytes 65568 | tf_op jit(solution)/shard_map/ppermute | solution.py:411
  74.8 3.5 %collective-permute-start.18 = (bf16[1,32,1024]{2,1,0:T(8,128)(2,1)S(1)}, bf16[1,32,1024]{2,1,0:T(8,128)(2,1)S(1)}, u32[]{:S(2)}, u32[]{:S(2)}) collective-permute-start(bf16[1,32,1024]{2,1,0:T(8,128)(2,1)S(1)} %bitcast.22), channel_id=1, source_target_pairs={{0,8},{1,9},{2,10},{3,11},{4,12},{5,13},{6,14},{7,15},{8,0},{9,1},... | collective-permute-start | bytes 196616 | tf_op jit(solution)/shard_map/ppermute | solution.py:411
  78.4 0.1 collective-permute-start.16
  78.6 0.8 collective-permute-start.19
  79.4 2.0 %collective-permute-start.17 = (bf16[1,32,1024]{2,1,0:T(8,128)(2,1)S(1)}, bf16[1,32,1024]{2,1,0:T(8,128)(2,1)S(1)}, u32[]{:S(2)}, u32[]{:S(2)}) collective-permute-start(bf16[1,32,1024]{2,1,0:T(8,128)(2,1)S(1)} %bitcast.24), channel_id=1, source_target_pairs={{0,8},{1,9},{2,10},{3,11},{4,12},{5,13},{6,14},{7,15},{8,0},{9,1},... | collective-permute-start | bytes 196616 | tf_op jit(solution)/shard_map/ppermute | solution.py:411
  81.4 2.2 %collective-permute-done.19 = bf16[2,32,1024]{2,1,0:T(8,128)(2,1)S(1)} collective-permute-done((bf16[2,32,1024]{2,1,0:T(8,128)(2,1)S(1)}, bf16[2,32,1024]{2,1,0:T(8,128)(2,1)S(1)}, u32[]{:S(2)}, u32[]{:S(2)}) %collective-permute-start.19) | collective-permute-done | bytes 131104 | tf_op jit(solution)/shard_map/ppermute | solution.py:411
  83.6 1.8 %collective-permute-start.23 = (bf16[1,32,1024]{2,1,0:T(8,128)(2,1)S(1)}, bf16[1,32,1024]{2,1,0:T(8,128)(2,1)S(1)}, u32[]{:S(2)}, u32[]{:S(2)}) collective-permute-start(bf16[1,32,1024]{2,1,0:T(8,128)(2,1)S(1)} %get-tuple-element.162), channel_id=1, source_target_pairs={{0,8},{1,9},{2,10},{3,11},{4,12},{5,13},{6,14},{7,15},{8,0},{9,1},... | collective-permute-start | bytes 196616 | tf_op jit(solution)/shard_map/ppermute | solution.py:411
  85.5 0.7 collective-permute-start.21
  86.2 1.0 collective-permute-start.22
  87.2 2.5 %collective-permute-start.20 = (bf16[1,32,1024]{2,1,0:T(8,128)(2,1)S(1)}, bf16[1,32,1024]{2,1,0:T(8,128)(2,1)S(1)}, u32[]{:S(2)}, u32[]{:S(2)}) collective-permute-start(bf16[1,32,1024]{2,1,0:T(8,128)(2,1)S(1)} %get-tuple-element.161), channel_id=1, source_target_pairs={{0,8},{1,9},{2,10},{3,11},{4,12},{5,13},{6,14},{7,15},{8,0},{9,1},... | collective-permute-start | bytes 196616 | tf_op jit(solution)/shard_map/ppermute | solution.py:411
  89.7 0.1 collective-permute-done.23
  89.9 0.9 collective-permute-start.25
  90.8 1.9 %collective-permute-done.22 = bf16[2,32,1024]{2,1,0:T(8,128)(2,1)S(1)} collective-permute-done((bf16[2,32,1024]{2,1,0:T(8,128)(2,1)S(1)}, bf16[2,32,1024]{2,1,0:T(8,128)(2,1)S(1)}, u32[]{:S(2)}, u32[]{:S(2)}) %collective-permute-start.22) | collective-permute-done | bytes 131104 | tf_op jit(solution)/shard_map/ppermute | solution.py:411
  92.7 1.5 %collective-permute-start.27 = (bf16[4,32,1024]{2,1,0:T(8,128)(2,1)S(1)}, bf16[4,32,1024]{2,1,0:T(8,128)(2,1)S(1)}, u32[]{:S(2)}, u32[]{:S(2)}) collective-permute-start(bf16[4,32,1024]{2,1,0:T(8,128)(2,1)S(1)} %constant_dynamic-update-slice_fusion.4), channel_id=1, source_target_pairs={{0,4},{1,5},{2,6},{3,7},{4,0},{5,1},{6,2},{7,3},{8,12},{9,13},{10,... | collective-permute-start | bytes 786440 | tf_op jit(solution)/shard_map/ppermute | solution.py:411
  94.2 1.0 collective-permute-start.32
  95.2 1.2 collective-permute-start.24
  96.4 0.8 collective-permute-done.25
  97.2 1.0 collective-permute-start.28
  98.2 2.4 %collective-permute-done.24 = bf16[1,32,1024]{2,1,0:T(8,128)(2,1)S(1)} collective-permute-done((bf16[1,32,1024]{2,1,0:T(8,128)(2,1)S(1)}, bf16[1,32,1024]{2,1,0:T(8,128)(2,1)S(1)}, u32[]{:S(2)}, u32[]{:S(2)}) %collective-permute-start.24) | collective-permute-done | bytes 65568 | tf_op jit(solution)/shard_map/ppermute | solution.py:411
  100.6 3.7 %collective-permute-start.26 = (bf16[2,32,1024]{2,1,0:T(8,128)(2,1)S(1)}, bf16[2,32,1024]{2,1,0:T(8,128)(2,1)S(1)}, u32[]{:S(2)}, u32[]{:S(2)}) collective-permute-start(bf16[2,32,1024]{2,1,0:T(8,128)(2,1)S(1)} %constant_dynamic-update-slice_fusion.10), channel_id=1, source_target_pairs={{0,4},{1,5},{2,6},{3,7},{4,0},{5,1},{6,2},{7,3},{8,12},{9,13},{10,... | collective-permute-start | bytes 393224 | tf_op jit(solution)/shard_map/ppermute | solution.py:411
  104.4 2.8 %collective-permute-done.26 = bf16[2,32,1024]{2,1,0:T(8,128)(2,1)S(1)} collective-permute-done((bf16[2,32,1024]{2,1,0:T(8,128)(2,1)S(1)}, bf16[2,32,1024]{2,1,0:T(8,128)(2,1)S(1)}, u32[]{:S(2)}, u32[]{:S(2)}) %collective-permute-start.26) | collective-permute-done | bytes 131104 | tf_op jit(solution)/shard_map/ppermute | solution.py:411
  107.3 0.1 collective-permute-start.33
  107.4 0.5 collective-permute-start.31
  107.9 2.0 %collective-permute-start.30 = (bf16[4,32,1024]{2,1,0:T(8,128)(2,1)S(1)}, bf16[4,32,1024]{2,1,0:T(8,128)(2,1)S(1)}, u32[]{:S(2)}, u32[]{:S(2)}) collective-permute-start(bf16[4,32,1024]{2,1,0:T(8,128)(2,1)S(1)} %constant_dynamic-update-slice_fusion.12), channel_id=1, source_target_pairs={{0,4},{1,5},{2,6},{3,7},{4,0},{5,1},{6,2},{7,3},{8,12},{9,13},{10,... | collective-permute-start | bytes 786440 | tf_op jit(solution)/shard_map/ppermute | solution.py:411
  109.9 0.4 collective-permute-start.29
  110.4 2.7 %shard_map.117.refs_4_ = bf16[128,16384]{1,0:T(8,128)(2,1)} custom-call(f32[16,1024]{1,0:T(8,128)S(1)} %reshape.42.gain_ref, bf16[8,32,1024]{2,1,0:T(8,128)(2,1)S(1)} %constant_dynamic-update-slice_fusion.14.refs_0_, bf16[8,32,1024]{2,1,0:T(8,128)(2,1)S(1)} %collective-permute-done.31.refs_1_, ...), custom_call_target="tpu_custom_call" | custom-call | flops 6291456 | bytes 4194304 | tf_op jit(solution)/shard_map/pallas_call | solution.py:396
  113.1 3.3 %collective-permute-done.30 = bf16[4,32,1024]{2,1,0:T(8,128)(2,1)S(1)} collective-permute-done((bf16[4,32,1024]{2,1,0:T(8,128)(2,1)S(1)}, bf16[4,32,1024]{2,1,0:T(8,128)(2,1)S(1)}, u32[]{:S(2)}, u32[]{:S(2)}) %collective-permute-start.30) | collective-permute-done | bytes 262176 | tf_op jit(solution)/shard_map/ppermute | solution.py:411
  116.5 0.1 collective-permute-start.35
  116.6 1.3 %collective-permute-done.29 = bf16[4,32,1024]{2,1,0:T(8,128)(2,1)S(1)} collective-permute-done((bf16[4,32,1024]{2,1,0:T(8,128)(2,1)S(1)}, bf16[4,32,1024]{2,1,0:T(8,128)(2,1)S(1)}, u32[]{:S(2)}, u32[]{:S(2)}) %collective-permute-start.29) | collective-permute-done | bytes 262176 | tf_op jit(solution)/shard_map/ppermute | solution.py:411
  118.0 0.1 collective-permute-start.34
  118.1 0.7 pad_maximum_fusion.4
  118.8 1.2 collective-permute-done.34.refs_1_
  120.0 2.7 %shard_map.118 = bf16[128,16384]{1,0:T(8,128)(2,1)} custom-call(f32[16,1024]{1,0:T(8,128)S(1)} %reshape.42.gain_ref, bf16[8,32,1024]{2,1,0:T(8,128)(2,1)S(1)} %constant_dynamic-update-slice_fusion.22.refs_0_, bf16[8,32,1024]{2,1,0:T(8,128)(2,1)S(1)} %collective-permute-done.34.refs_1_, ...), custom_call_target="tpu_custom_call", output_to_operand_aliasing={{}: (5, {})} | custom-call | flops 6291456 | bytes 4194304 | tf_op jit(solution)/shard_map/pallas_call | solution.py:396
  (81 shorter events, 1.5 us)
Async XLA Ops:
  1.6 0.8 copy-start.1
  2.4 26.0 %copy-start = (bf16[8,1024,512]{2,1,0:T(8,128)(2,1)S(1)}, bf16[8,1024,512]{2,1,0:T(8,128)(2,1)}, u32[]{:S(2)}) copy-start(bf16[8,1024,512]{2,1,0:T(8,128)(2,1)} %keys_ref.1) | copy-start | bytes 25165828
  2.4 26.0 %copy-start.2 = (s32[8]{0:T(128)S(1)}, s32[8]{0:T(128)}, u32[]{:S(2)}) copy-start(s32[8]{0:T(128)} %lengths_ref.1) | copy-start | bytes 100
  49.4 1.6 %collective-permute-start = (bf16[4,32,1024]{2,1,0:T(8,128)(2,1)S(1)}, bf16[4,32,1024]{2,1,0:T(8,128)(2,1)S(1)}, u32[]{:S(2)}, u32[]{:S(2)}) collective-permute-start(bf16[4,32,1024]{2,1,0:T(8,128)(2,1)S(1)} %get-tuple-element.80), channel_id=1, source_target_pairs={{0,1},{1,0},{2,3},{3,2},{4,5},{5,4},{6,7},{7,6},{8,9},{9,8},{10,11... | collective-permute-start | bytes 786440 | tf_op jit(solution)/shard_map/ppermute | solution.py:411
  49.4 5.7 %collective-permute-start.2 = (bf16[4,32,1024]{2,1,0:T(8,128)(2,1)S(1)}, bf16[4,32,1024]{2,1,0:T(8,128)(2,1)S(1)}, u32[]{:S(2)}, u32[]{:S(2)}) collective-permute-start(bf16[4,32,1024]{2,1,0:T(8,128)(2,1)S(1)} %get-tuple-element.85), channel_id=1, source_target_pairs={{0,1},{1,0},{2,3},{3,2},{4,5},{5,4},{6,7},{7,6},{8,9},{9,8},{10,11... | collective-permute-start | bytes 786440 | tf_op jit(solution)/shard_map/ppermute | solution.py:411
  49.9 6.0 %collective-permute-start.4 = (bf16[4,32,1024]{2,1,0:T(8,128)(2,1)S(1)}, bf16[4,32,1024]{2,1,0:T(8,128)(2,1)S(1)}, u32[]{:S(2)}, u32[]{:S(2)}) collective-permute-start(bf16[4,32,1024]{2,1,0:T(8,128)(2,1)S(1)} %get-tuple-element.89), channel_id=1, source_target_pairs={{0,1},{1,0},{2,3},{3,2},{4,5},{5,4},{6,7},{7,6},{8,9},{9,8},{10,11... | collective-permute-start | bytes 786440 | tf_op jit(solution)/shard_map/ppermute | solution.py:411
  50.0 5.2 %collective-permute-start.10 = (bf16[4,32,1024]{2,1,0:T(8,128)(2,1)S(1)}, bf16[4,32,1024]{2,1,0:T(8,128)(2,1)S(1)}, u32[]{:S(2)}, u32[]{:S(2)}) collective-permute-start(bf16[4,32,1024]{2,1,0:T(8,128)(2,1)S(1)} %get-tuple-element.100), channel_id=1, source_target_pairs={{0,1},{1,0},{2,3},{3,2},{4,5},{5,4},{6,7},{7,6},{8,9},{9,8},{10,11... | collective-permute-start | bytes 786440 | tf_op jit(solution)/shard_map/ppermute | solution.py:411
  51.0 8.4 %collective-permute-start.6 = (bf16[4,32,1024]{2,1,0:T(8,128)(2,1)S(1)}, bf16[4,32,1024]{2,1,0:T(8,128)(2,1)S(1)}, u32[]{:S(2)}, u32[]{:S(2)}) collective-permute-start(bf16[4,32,1024]{2,1,0:T(8,128)(2,1)S(1)} %add_convert_fusion.7), channel_id=1, source_target_pairs={{0,2},{1,3},{2,0},{3,1},{4,6},{5,7},{6,4},{7,5},{8,10},{9,11},{10,... | collective-permute-start | bytes 786440 | tf_op jit(solution)/shard_map/ppermute | solution.py:411
  55.0 1.6 %collective-permute-start.1 = (bf16[4,32,1024]{2,1,0:T(8,128)(2,1)S(1)}, bf16[4,32,1024]{2,1,0:T(8,128)(2,1)S(1)}, u32[]{:S(2)}, u32[]{:S(2)}) collective-permute-start(bf16[4,32,1024]{2,1,0:T(8,128)(2,1)S(1)} %get-tuple-element.83), channel_id=1, source_target_pairs={{0,1},{1,0},{2,3},{3,2},{4,5},{5,4},{6,7},{7,6},{8,9},{9,8},{10,11... | collective-permute-start | bytes 786440 | tf_op jit(solution)/shard_map/ppermute | solution.py:411
  55.4 1.8 %collective-permute-start.5 = (bf16[4,32,1024]{2,1,0:T(8,128)(2,1)S(1)}, bf16[4,32,1024]{2,1,0:T(8,128)(2,1)S(1)}, u32[]{:S(2)}, u32[]{:S(2)}) collective-permute-start(bf16[4,32,1024]{2,1,0:T(8,128)(2,1)S(1)} %get-tuple-element.91), channel_id=1, source_target_pairs={{0,1},{1,0},{2,3},{3,2},{4,5},{5,4},{6,7},{7,6},{8,9},{9,8},{10,11... | collective-permute-start | bytes 786440 | tf_op jit(solution)/shard_map/ppermute | solution.py:411
  55.8 5.2 %collective-permute-start.9 = (bf16[4,32,1024]{2,1,0:T(8,128)(2,1)S(1)}, bf16[4,32,1024]{2,1,0:T(8,128)(2,1)S(1)}, u32[]{:S(2)}, u32[]{:S(2)}) collective-permute-start(bf16[4,32,1024]{2,1,0:T(8,128)(2,1)S(1)} %get-tuple-element.98), channel_id=1, source_target_pairs={{0,1},{1,0},{2,3},{3,2},{4,5},{5,4},{6,7},{7,6},{8,9},{9,8},{10,11... | collective-permute-start | bytes 786440 | tf_op jit(solution)/shard_map/ppermute | solution.py:411
  56.0 5.3 %collective-permute-start.13 = (bf16[4,32,1024]{2,1,0:T(8,128)(2,1)S(1)}, bf16[4,32,1024]{2,1,0:T(8,128)(2,1)S(1)}, u32[]{:S(2)}, u32[]{:S(2)}) collective-permute-start(bf16[4,32,1024]{2,1,0:T(8,128)(2,1)S(1)} %get-tuple-element.107), channel_id=1, source_target_pairs={{0,1},{1,0},{2,3},{3,2},{4,5},{5,4},{6,7},{7,6},{8,9},{9,8},{10,11... | collective-permute-start | bytes 786440 | tf_op jit(solution)/shard_map/ppermute | solution.py:411
  56.6 53.7 %copy-start.3 = (bf16[16384]{0:T(1024)(128)(2,1)S(1)}, bf16[16384]{0:T(1024)(128)(2,1)}, u32[]{:S(2)}) copy-start(bf16[16384]{0:T(1024)(128)(2,1)} %param.17) | copy-start | bytes 98308
  56.7 9.2 %collective-permute-start.3 = (bf16[4,32,1024]{2,1,0:T(8,128)(2,1)S(1)}, bf16[4,32,1024]{2,1,0:T(8,128)(2,1)S(1)}, u32[]{:S(2)}, u32[]{:S(2)}) collective-permute-start(bf16[4,32,1024]{2,1,0:T(8,128)(2,1)S(1)} %pad_maximum_fusion.1), channel_id=1, source_target_pairs={{0,4},{1,5},{2,6},{3,7},{4,0},{5,1},{6,2},{7,3},{8,12},{9,13},{10,... | collective-permute-start | bytes 786440 | tf_op jit(solution)/shard_map/ppermute | solution.py:411
  59.5 8.6 %collective-permute-start.8 = (bf16[2,32,1024]{2,1,0:T(8,128)(2,1)S(1)}, bf16[2,32,1024]{2,1,0:T(8,128)(2,1)S(1)}, u32[]{:S(2)}, u32[]{:S(2)}) collective-permute-start(bf16[2,32,1024]{2,1,0:T(8,128)(2,1)S(1)} %get-tuple-element.159), channel_id=1, source_target_pairs={{0,4},{1,5},{2,6},{3,7},{4,0},{5,1},{6,2},{7,3},{8,12},{9,13},{10,... | collective-permute-start | bytes 393224 | tf_op jit(solution)/shard_map/ppermute | solution.py:411
  59.6 18.7 %collective-permute-start.14 = (bf16[4,32,1024]{2,1,0:T(8,128)(2,1)S(1)}, bf16[4,32,1024]{2,1,0:T(8,128)(2,1)S(1)}, u32[]{:S(2)}, u32[]{:S(2)}) collective-permute-start(bf16[4,32,1024]{2,1,0:T(8,128)(2,1)S(1)} %add_convert_fusion.4), channel_id=1, source_target_pairs={{0,2},{1,3},{2,0},{3,1},{4,6},{5,7},{6,4},{7,5},{8,10},{9,11},{10,... | collective-permute-start | bytes 786440 | tf_op jit(solution)/shard_map/ppermute | solution.py:411
  66.0 5.0 %collective-permute-start.7 = (bf16[2,32,1024]{2,1,0:T(8,128)(2,1)S(1)}, bf16[2,32,1024]{2,1,0:T(8,128)(2,1)S(1)}, u32[]{:S(2)}, u32[]{:S(2)}) collective-permute-start(bf16[2,32,1024]{2,1,0:T(8,128)(2,1)S(1)} %get-tuple-element.157), channel_id=1, source_target_pairs={{0,2},{1,3},{2,0},{3,1},{4,6},{5,7},{6,4},{7,5},{8,10},{9,11},{10,... | collective-permute-start | bytes 393224 | tf_op jit(solution)/shard_map/ppermute | solution.py:411
  68.1 10.4 %collective-permute-start.12 = (bf16[4,32,1024]{2,1,0:T(8,128)(2,1)S(1)}, bf16[4,32,1024]{2,1,0:T(8,128)(2,1)S(1)}, u32[]{:S(2)}, u32[]{:S(2)}) collective-permute-start(bf16[4,32,1024]{2,1,0:T(8,128)(2,1)S(1)} %pad_maximum_fusion.2), channel_id=1, source_target_pairs={{0,4},{1,5},{2,6},{3,7},{4,0},{5,1},{6,2},{7,3},{8,12},{9,13},{10,... | collective-permute-start | bytes 786440 | tf_op jit(solution)/shard_map/ppermute | solution.py:411
  68.1 6.6 %collective-permute-start.15 = (bf16[1,32,1024]{2,1,0:T(8,128)(2,1)S(1)}, bf16[1,32,1024]{2,1,0:T(8,128)(2,1)S(1)}, u32[]{:S(2)}, u32[]{:S(2)}) collective-permute-start(bf16[1,32,1024]{2,1,0:T(8,128)(2,1)S(1)} %get-tuple-element.166), channel_id=1, source_target_pairs={{0,8},{1,9},{2,10},{3,11},{4,12},{5,13},{6,14},{7,15},{8,0},{9,1},... | collective-permute-start | bytes 196616 | tf_op jit(solution)/shard_map/ppermute | solution.py:411
  71.1 8.3 %collective-permute-start.11 = (bf16[1,32,1024]{2,1,0:T(8,128)(2,1)S(1)}, bf16[1,32,1024]{2,1,0:T(8,128)(2,1)S(1)}, u32[]{:S(2)}, u32[]{:S(2)}) collective-permute-start(bf16[1,32,1024]{2,1,0:T(8,128)(2,1)S(1)} %get-tuple-element.165), channel_id=1, source_target_pairs={{0,8},{1,9},{2,10},{3,11},{4,12},{5,13},{6,14},{7,15},{8,0},{9,1},... | collective-permute-start | bytes 196616 | tf_op jit(solution)/shard_map/ppermute | solution.py:411
  74.8 10.7 %collective-permute-start.18 = (bf16[1,32,1024]{2,1,0:T(8,128)(2,1)S(1)}, bf16[1,32,1024]{2,1,0:T(8,128)(2,1)S(1)}, u32[]{:S(2)}, u32[]{:S(2)}) collective-permute-start(bf16[1,32,1024]{2,1,0:T(8,128)(2,1)S(1)} %bitcast.22), channel_id=1, source_target_pairs={{0,8},{1,9},{2,10},{3,11},{4,12},{5,13},{6,14},{7,15},{8,0},{9,1},... | collective-permute-start | bytes 196616 | tf_op jit(solution)/shard_map/ppermute | solution.py:411
  78.4 8.8 %collective-permute-start.16 = (bf16[2,32,1024]{2,1,0:T(8,128)(2,1)S(1)}, bf16[2,32,1024]{2,1,0:T(8,128)(2,1)S(1)}, u32[]{:S(2)}, u32[]{:S(2)}) collective-permute-start(bf16[2,32,1024]{2,1,0:T(8,128)(2,1)S(1)} %get-tuple-element.153), channel_id=1, source_target_pairs={{0,4},{1,5},{2,6},{3,7},{4,0},{5,1},{6,2},{7,3},{8,12},{9,13},{10,... | collective-permute-start | bytes 393224 | tf_op jit(solution)/shard_map/ppermute | solution.py:411
  78.6 5.0 %collective-permute-start.19 = (bf16[2,32,1024]{2,1,0:T(8,128)(2,1)S(1)}, bf16[2,32,1024]{2,1,0:T(8,128)(2,1)S(1)}, u32[]{:S(2)}, u32[]{:S(2)}) collective-permute-start(bf16[2,32,1024]{2,1,0:T(8,128)(2,1)S(1)} %get-tuple-element.154), channel_id=1, source_target_pairs={{0,2},{1,3},{2,0},{3,1},{4,6},{5,7},{6,4},{7,5},{8,10},{9,11},{10,... | collective-permute-start | bytes 393224 | tf_op jit(solution)/shard_map/ppermute | solution.py:411
  79.4 6.8 %collective-permute-start.17 = (bf16[1,32,1024]{2,1,0:T(8,128)(2,1)S(1)}, bf16[1,32,1024]{2,1,0:T(8,128)(2,1)S(1)}, u32[]{:S(2)}, u32[]{:S(2)}) collective-permute-start(bf16[1,32,1024]{2,1,0:T(8,128)(2,1)S(1)} %bitcast.24), channel_id=1, source_target_pairs={{0,8},{1,9},{2,10},{3,11},{4,12},{5,13},{6,14},{7,15},{8,0},{9,1},... | collective-permute-start | bytes 196616 | tf_op jit(solution)/shard_map/ppermute | solution.py:411
  83.6 6.2 %collective-permute-start.23 = (bf16[1,32,1024]{2,1,0:T(8,128)(2,1)S(1)}, bf16[1,32,1024]{2,1,0:T(8,128)(2,1)S(1)}, u32[]{:S(2)}, u32[]{:S(2)}) collective-permute-start(bf16[1,32,1024]{2,1,0:T(8,128)(2,1)S(1)} %get-tuple-element.162), channel_id=1, source_target_pairs={{0,8},{1,9},{2,10},{3,11},{4,12},{5,13},{6,14},{7,15},{8,0},{9,1},... | collective-permute-start | bytes 196616 | tf_op jit(solution)/shard_map/ppermute | solution.py:411
  85.5 8.7 %collective-permute-start.21 = (bf16[2,32,1024]{2,1,0:T(8,128)(2,1)S(1)}, bf16[2,32,1024]{2,1,0:T(8,128)(2,1)S(1)}, u32[]{:S(2)}, u32[]{:S(2)}) collective-permute-start(bf16[2,32,1024]{2,1,0:T(8,128)(2,1)S(1)} %constant_dynamic-update-slice_fusion), channel_id=1, source_target_pairs={{0,4},{1,5},{2,6},{3,7},{4,0},{5,1},{6,2},{7,3},{8,12},{9,13},{10,... | collective-permute-start | bytes 393224 | tf_op jit(solution)/shard_map/ppermute | solution.py:411
  86.2 6.4 %collective-permute-start.22 = (bf16[2,32,1024]{2,1,0:T(8,128)(2,1)S(1)}, bf16[2,32,1024]{2,1,0:T(8,128)(2,1)S(1)}, u32[]{:S(2)}, u32[]{:S(2)}) collective-permute-start(bf16[2,32,1024]{2,1,0:T(8,128)(2,1)S(1)} %constant_dynamic-update-slice_fusion.2), channel_id=1, source_target_pairs={{0,2},{1,3},{2,0},{3,1},{4,6},{5,7},{6,4},{7,5},{8,10},{9,11},{10,... | collective-permute-start | bytes 393224 | tf_op jit(solution)/shard_map/ppermute | solution.py:411
  87.2 8.0 %collective-permute-start.20 = (bf16[1,32,1024]{2,1,0:T(8,128)(2,1)S(1)}, bf16[1,32,1024]{2,1,0:T(8,128)(2,1)S(1)}, u32[]{:S(2)}, u32[]{:S(2)}) collective-permute-start(bf16[1,32,1024]{2,1,0:T(8,128)(2,1)S(1)} %get-tuple-element.161), channel_id=1, source_target_pairs={{0,8},{1,9},{2,10},{3,11},{4,12},{5,13},{6,14},{7,15},{8,0},{9,1},... | collective-permute-start | bytes 196616 | tf_op jit(solution)/shard_map/ppermute | solution.py:411
  89.9 7.3 %collective-permute-start.25 = (bf16[1,32,1024]{2,1,0:T(8,128)(2,1)S(1)}, bf16[1,32,1024]{2,1,0:T(8,128)(2,1)S(1)}, u32[]{:S(2)}, u32[]{:S(2)}) collective-permute-start(bf16[1,32,1024]{2,1,0:T(8,128)(2,1)S(1)} %bitcast.26), channel_id=1, source_target_pairs={{0,8},{1,9},{2,10},{3,11},{4,12},{5,13},{6,14},{7,15},{8,0},{9,1},... | collective-permute-start | bytes 196616 | tf_op jit(solution)/shard_map/ppermute | solution.py:411
  92.7 11.6 %collective-permute-start.27 = (bf16[4,32,1024]{2,1,0:T(8,128)(2,1)S(1)}, bf16[4,32,1024]{2,1,0:T(8,128)(2,1)S(1)}, u32[]{:S(2)}, u32[]{:S(2)}) collective-permute-start(bf16[4,32,1024]{2,1,0:T(8,128)(2,1)S(1)} %constant_dynamic-update-slice_fusion.4), channel_id=1, source_target_pairs={{0,4},{1,5},{2,6},{3,7},{4,0},{5,1},{6,2},{7,3},{8,12},{9,13},{10,... | collective-permute-start | bytes 786440 | tf_op jit(solution)/shard_map/ppermute | solution.py:411
  94.2 13.1 %collective-permute-start.32 = (bf16[4,32,1024]{2,1,0:T(8,128)(2,1)S(1)}, bf16[4,32,1024]{2,1,0:T(8,128)(2,1)S(1)}, u32[]{:S(2)}, u32[]{:S(2)}) collective-permute-start(bf16[4,32,1024]{2,1,0:T(8,128)(2,1)S(1)} %constant_dynamic-update-slice_fusion.6), channel_id=1, source_target_pairs={{0,2},{1,3},{2,0},{3,1},{4,6},{5,7},{6,4},{7,5},{8,10},{9,11},{10,... | collective-permute-start | bytes 786440 | tf_op jit(solution)/shard_map/ppermute | solution.py:411
  95.2 5.3 %collective-permute-start.24 = (bf16[1,32,1024]{2,1,0:T(8,128)(2,1)S(1)}, bf16[1,32,1024]{2,1,0:T(8,128)(2,1)S(1)}, u32[]{:S(2)}, u32[]{:S(2)}) collective-permute-start(bf16[1,32,1024]{2,1,0:T(8,128)(2,1)S(1)} %bitcast.28), channel_id=1, source_target_pairs={{0,8},{1,9},{2,10},{3,11},{4,12},{5,13},{6,14},{7,15},{8,0},{9,1},... | collective-permute-start | bytes 196616 | tf_op jit(solution)/shard_map/ppermute | solution.py:411
  97.2 7.1 %collective-permute-start.28 = (bf16[2,32,1024]{2,1,0:T(8,128)(2,1)S(1)}, bf16[2,32,1024]{2,1,0:T(8,128)(2,1)S(1)}, u32[]{:S(2)}, u32[]{:S(2)}) collective-permute-start(bf16[2,32,1024]{2,1,0:T(8,128)(2,1)S(1)} %constant_dynamic-update-slice_fusion.8), channel_id=1, source_target_pairs={{0,2},{1,3},{2,0},{3,1},{4,6},{5,7},{6,4},{7,5},{8,10},{9,11},{10,... | collective-permute-start | bytes 393224 | tf_op jit(solution)/shard_map/ppermute | solution.py:411
  100.6 6.6 %collective-permute-start.26 = (bf16[2,32,1024]{2,1,0:T(8,128)(2,1)S(1)}, bf16[2,32,1024]{2,1,0:T(8,128)(2,1)S(1)}, u32[]{:S(2)}, u32[]{:S(2)}) collective-permute-start(bf16[2,32,1024]{2,1,0:T(8,128)(2,1)S(1)} %constant_dynamic-update-slice_fusion.10), channel_id=1, source_target_pairs={{0,4},{1,5},{2,6},{3,7},{4,0},{5,1},{6,2},{7,3},{8,12},{9,13},{10,... | collective-permute-start | bytes 393224 | tf_op jit(solution)/shard_map/ppermute | solution.py:411
  107.3 3.1 %collective-permute-start.33 = (bf16[8,32,1024]{2,1,0:T(8,128)(2,1)S(1)}, bf16[8,32,1024]{2,1,0:T(8,128)(2,1)S(1)}, u32[]{:S(2)}, u32[]{:S(2)}) collective-permute-start(bf16[8,32,1024]{2,1,0:T(8,128)(2,1)S(1)} %constant_dynamic-update-slice_fusion.18.refs_2_), channel_id=1, source_target_pairs={{0,1},{1,0},{2,3},{3,2},{4,5},{5,4},{6,7},{7,6},{8,9},{9,8},{10,11... | collective-permute-start | bytes 1572872 | tf_op jit(solution)/shard_map/ppermute | solution.py:411
  107.4 3.0 %collective-permute-start.31 = (bf16[8,32,1024]{2,1,0:T(8,128)(2,1)S(1)}, bf16[8,32,1024]{2,1,0:T(8,128)(2,1)S(1)}, u32[]{:S(2)}, u32[]{:S(2)}) collective-permute-start(bf16[8,32,1024]{2,1,0:T(8,128)(2,1)S(1)} %constant_dynamic-update-slice_fusion.14.refs_0_), channel_id=1, source_target_pairs={{0,1},{1,0},{2,3},{3,2},{4,5},{5,4},{6,7},{7,6},{8,9},{9,8},{10,11... | collective-permute-start | bytes 1572872 | tf_op jit(solution)/shard_map/ppermute | solution.py:411
  107.9 8.6 %collective-permute-start.30 = (bf16[4,32,1024]{2,1,0:T(8,128)(2,1)S(1)}, bf16[4,32,1024]{2,1,0:T(8,128)(2,1)S(1)}, u32[]{:S(2)}, u32[]{:S(2)}) collective-permute-start(bf16[4,32,1024]{2,1,0:T(8,128)(2,1)S(1)} %constant_dynamic-update-slice_fusion.12), channel_id=1, source_target_pairs={{0,4},{1,5},{2,6},{3,7},{4,0},{5,1},{6,2},{7,3},{8,12},{9,13},{10,... | collective-permute-start | bytes 786440 | tf_op jit(solution)/shard_map/ppermute | solution.py:411
  109.9 8.0 %collective-permute-start.29 = (bf16[4,32,1024]{2,1,0:T(8,128)(2,1)S(1)}, bf16[4,32,1024]{2,1,0:T(8,128)(2,1)S(1)}, u32[]{:S(2)}, u32[]{:S(2)}) collective-permute-start(bf16[4,32,1024]{2,1,0:T(8,128)(2,1)S(1)} %constant_dynamic-update-slice_fusion.16), channel_id=1, source_target_pairs={{0,2},{1,3},{2,0},{3,1},{4,6},{5,7},{6,4},{7,5},{8,10},{9,11},{10,... | collective-permute-start | bytes 786440 | tf_op jit(solution)/shard_map/ppermute | solution.py:411
  116.5 2.3 %collective-permute-start.35 = (bf16[8,32,1024]{2,1,0:T(8,128)(2,1)S(1)}, bf16[8,32,1024]{2,1,0:T(8,128)(2,1)S(1)}, u32[]{:S(2)}, u32[]{:S(2)}) collective-permute-start(bf16[8,32,1024]{2,1,0:T(8,128)(2,1)S(1)} %constant_dynamic-update-slice_fusion.20.refs_2_), channel_id=1, source_target_pairs={{0,1},{1,0},{2,3},{3,2},{4,5},{5,4},{6,7},{7,6},{8,9},{9,8},{10,11... | collective-permute-start | bytes 1572872 | tf_op jit(solution)/shard_map/ppermute | solution.py:411
  118.0 2.0 %collective-permute-start.34 = (bf16[8,32,1024]{2,1,0:T(8,128)(2,1)S(1)}, bf16[8,32,1024]{2,1,0:T(8,128)(2,1)S(1)}, u32[]{:S(2)}, u32[]{:S(2)}) collective-permute-start(bf16[8,32,1024]{2,1,0:T(8,128)(2,1)S(1)} %constant_dynamic-update-slice_fusion.22.refs_0_), channel_id=1, source_target_pairs={{0,1},{1,0},{2,3},{3,2},{4,5},{5,4},{6,7},{7,6},{8,9},{9,8},{10,11... | collective-permute-start | bytes 1572872 | tf_op jit(solution)/shard_map/ppermute | solution.py:411

commit v8 on v7

--- a/solution.py
+++ b/solution.py
@@ -11,7 +11,7 @@
 HD = 128
 
 
-TABLE = "101203101230310230123230211323"
+TABLE = "032031032013021320123121302131"
 
 epsilon = 1e-05
 rope_theta = 500000.0
@@ -288,7 +288,8 @@
     bits = list(range(1, count.bit_length() - 1))
     turned = bits[::-1]
     late = bits[1:2] + bits[:1] + bits[2:]
-    return [(late, late[::-1]), (bits, turned), (bits, turned), (late, late[::-1])]
+    crossed = late[::-1]
+    return [(bits, turned), (bits, crossed), (late, turned), (bits, crossed)]
 
 
 def timetable(count):
@@ -367,7 +368,8 @@
     out_ref = refs[-1]
     me = lax.axis_index("tensor")
     half, rows, width = refs[0].shape
-    for k, order in enumerate(offsets):
+
+    def norm(k, order):
         parts = refs[2 * k : 2 * k + 2]
         total = jnp.zeros((rows, width), jnp.float32)
         for ref in parts:
@@ -381,28 +383,31 @@
             index = jnp.bitwise_xor(me, offset)
             column = pl.multiple_of(index * width, width)
             gain = gain_ref[pl.ds(index, 1), :]
-            out_ref[k * rows : (k + 1) * rows, pl.ds(column, width)] = (
-                block * scale * gain
-            ).astype(jnp.bfloat16)
+            out_ref[:, pl.ds(column, width)] = (block * scale * gain).astype(jnp.bfloat16)
+
+    for k, order in enumerate(offsets):
+        pl.when(pl.program_id(0) == k)(functools.partial(norm, k, order))
 
 
 def finish(parts, gain, offsets, which, groups, earlier):
     half, rows, width = parts[0].shape
-    columns, rows = 2 * half * width, rows * len(offsets)
+    columns, count = 2 * half * width, len(offsets)
     operands = [gain, *parts] + ([] if earlier is None else [earlier])
     specs = [pl.BlockSpec(memory_space=pltpu.VMEM)] * (1 + len(parts))
     if earlier is not None:
         specs.append(pl.BlockSpec(memory_space=pl.ANY))
     return pl.pallas_call(
         functools.partial(finish_kernel, offsets),
-        grid=(1,),
-        out_shape=jax.ShapeDtypeStruct((rows * groups, columns), jnp.bfloat16),
+        grid=(count,),
+        out_shape=jax.ShapeDtypeStruct((rows * count * groups, columns), jnp.bfloat16),
         in_specs=specs,
-        out_specs=pl.BlockSpec((rows, columns), lambda i: (which, 0)),
+        out_specs=pl.BlockSpec((rows, columns), lambda i: (which * count + i, 0)),
         input_output_aliases={} if earlier is None else {len(operands) - 1: 0},
         compiler_params=pltpu.CompilerParams(vmem_limit_bytes=24 * 1024 * 1024),
         cost_estimate=pl.CostEstimate(
-            flops=6 * rows * columns, bytes_accessed=4 * rows * columns, transcendentals=0
+            flops=6 * count * rows * columns,
+            bytes_accessed=4 * count * rows * columns,
+            transcendentals=0,
         ),
     )(*operands)
 

time: 123 us -> 118 us (0.959)
  starting transfers between devices: 33.2 us -> 21.6 us
  waiting for transfers between devices: 28.1 us -> 34.9 us
    ppermute x36, starting transfers between devices: 33.2 us -> 21.6 us  [swap(): lax.ppermute(values, 'tensor', [(i, i ^ 1 << bit) for i in range(count)])]
    ppermute x36, waiting for transfers between devices: 28.1 us -> 34.9 us  [swap(): lax.ppermute(values, 'tensor', [(i, i ^ 1 << bit) for i in range(count)])]
  transfers between devices with their start and end apart: 36 -> 36, of which waited for: 15 -> 19; matrix products, arithmetic and copies ran while one was open for 2% -> 2% of each run, Pallas kernels for 5% -> 5%
where the time goes in v8:
time: 118 us
  waiting for transfers between devices  34.9 us (30%)
  Pallas kernels  30 us (25%)
  blocking collectives  26.2 us (22%)
  starting transfers between devices  21.6 us (18%)
  other arithmetic  2.8 us (2%)
    ppermute x36, waiting for transfers between devices, swap(): lax.ppermute(values, 'tensor', [(i, i ^ 1 << bit) for i in range(count)])  34.9 us
    all_to_all x2, blocking collectives, exchange(): lax.all_to_all(blocks, 'tensor', split_axis=0, concat_axis=0, tiled=True)  26.2 us
    ppermute x36, starting transfers between devices, swap(): lax.ppermute(values, 'tensor', [(i, i ^ 1 << bit) for i in range(count)])  21.6 us
    pallas_call x1, Pallas kernels, project_in(): pl.pallas_call(functools.partial(input_kernel, count), out_shape=(jax.Sha...  10.3 us
    pallas_call x2, Pallas kernels, project(): pl.pallas_call(functools.partial(project_kernel, count, side), out_shape=...  7.67 us
    pallas_call x1, Pallas kernels, attend(): pl.pallas_call(functools.partial(attend_kernel, count), out_shape=jax.Sha...  6.62 us
    pallas_call x2, Pallas kernels, finish(): pl.pallas_call(functools.partial(finish_kernel, offsets), grid=(count,),...  5.35 us
  transfers between devices with their start and end apart: 36, of which 19 were waited for; matrix products, arithmetic and copies ran while one was open for 2% of the time, Pallas kernels for 5%

profile of v8, /device:TPU:0, one launch (start us, length us, event | category | flops | bytes accessed | tf_op | source)
XLA Modules:
  0.0 117.6 jit_solution(13378253512865106162)
XLA Ops:
  0.6 0.7 convert_element_type.283
  1.3 0.3 fusion.4
  1.6 0.7 copy-done.1
  2.4 10.3 %shard_map.113 = (bf16[16,8,640]{2,1,0:T(8,128)(2,1)S(1)}, bf16[128,1024]{1,0:T(8,128)(2,1)S(1)}) custom-call(bf16[128,16384]{1,0:T(8,128)(2,1)} %hidden_ref.1, bf16[16384]{0:T(1024)(128)(2,1)S(1)} %copy-done.1, bf16[16384,512]{1,0:T(8,128)(2,1)} %w_ref.3, bf16[64,16384]{1,0:T(8,128)(2,1)} %bitcast.21, f32[128,128]{1,0:T(8,128)S(1)} %get-tuple-element.173.cosine_ref, ...), custom_call_target="tpu_custom_call" | custom-call | flops 2415919104 | bytes 23068672 | tf_op jit(solution)/shard_map/pallas_call | solution.py:120
  12.7 15.7 %all_to_all.10.refs_0_ = bf16[16,8,640]{2,1,0:T(8,128)(2,1)S(1)} all-to-all(bf16[16,8,640]{2,1,0:T(8,128)(2,1)S(1)} %get-tuple-element.78), channel_id=1, replica_groups=mesh['groups'=2,'tensor'=16] {'tensor'}, dimensions={0} | all-to-all | bytes 327680 | tf_op jit(solution)/shard_map/all_to_all | solution.py:284
  28.4 6.6 %shard_map.114 = bf16[16,8,512]{2,1,0:T(8,128)(2,1)S(1)} custom-call(s32[8]{0:T(128)S(1)} %copy-done.2, f32[128,128]{1,0:T(8,128)S(1)} %get-tuple-element.173.cosine_ref, f32[128,128]{1,0:T(8,128)S(1)} %get-tuple-element.172.sine_ref, bf16[8,1024,512]{2,1,0:T(8,128)(2,1)S(1)} %copy-done, bf16[8,1024,512]{2,1,0:T(8,128)(2,1)} %values_ref.1, ...), custom_call_target="tpu_custom_call" | custom-call | flops 268435456 | bytes 16777216 | tf_op jit(solution)/shard_map/pallas_call | solution.py:259
  35.0 10.5 %all_to_all.11.in_ref = bf16[16,8,512]{2,1,0:T(8,128)(2,1)S(1)} all-to-all(bf16[16,8,512]{2,1,0:T(8,128)(2,1)S(1)} %shard_map.114), channel_id=1, replica_groups=mesh['groups'=2,'tensor'=16] {'tensor'}, dimensions={0} | all-to-all | bytes 262144 | tf_op jit(solution)/shard_map/all_to_all | solution.py:284
  45.5 3.8 %shard_map.115 = (bf16[4,32,1024]{2,1,0:T(8,128)(2,1)S(1)}, bf16[4,32,1024]{2,1,0:T(8,128)(2,1)S(1)}, bf16[4,32,1024]{2,1,0:T(8,128)(2,1)S(1)}, bf16[4,32,1024]{...) custom-call(bf16[16,8,512]{2,1,0:T(8,128)(2,1)S(1)} %all_to_all.11.i, ...), custom_call_target="tpu_custom_call" | custom-call | flops 1073741824 | bytes 10485760 | tf_op jit(solution)/shard_map/pallas_call | solution.py:347
  49.4 0.1 collective-permute-start
  49.4 0.5 collective-permute-start.4
  49.9 0.1 collective-permute-start.5
  50.0 0.4 collective-permute-start.7
  50.5 0.5 collective-permute-done
  51.0 0.1 collective-permute-start.2
  51.1 3.8 %shard_map.116 = (bf16[4,32,1024]{2,1,0:T(8,128)(2,1)S(1)}, bf16[4,32,1024]{2,1,0:T(8,128)(2,1)S(1)}, bf16[4,32,1024]{2,1,0:T(8,128)(2,1)S(1)}, bf16[4,32,1024]{...) custom-call(bf16[16,8,512]{2,1,0:T(8,128)(2,1)S(1)} %all_to_all.11.i, ...), custom_call_target="tpu_custom_call" | custom-call | flops 1073741824 | bytes 10485760 | tf_op jit(solution)/shard_map/pallas_call | solution.py:347
  55.0 0.2 collective-permute-start.3
  55.4 2.0 %collective-permute-start.9 = (bf16[4,32,1024]{2,1,0:T(8,128)(2,1)S(1)}, bf16[4,32,1024]{2,1,0:T(8,128)(2,1)S(1)}, u32[]{:S(2)}, u32[]{:S(2)}) collective-permute-start(bf16[4,32,1024]{2,1,0:T(8,128)(2,1)S(1)} %add_convert_fusion.3), channel_id=1, source_target_pairs={{0,2},{1,3},{2,0},{3,1},{4,6},{5,7},{6,4},{7,5},{8,10},{9,11},{10,... | collective-permute-start | bytes 786440 | tf_op jit(solution)/shard_map/ppermute | solution.py:416
  57.3 0.2 collective-permute-start.1
  57.5 0.3 collective-permute-start.8
  57.9 0.3 collective-permute-start.13
  58.3 0.5 collective-permute-done.1
  58.9 1.3 %collective-permute-done.2 = bf16[4,32,1024]{2,1,0:T(8,128)(2,1)S(1)} collective-permute-done((bf16[4,32,1024]{2,1,0:T(8,128)(2,1)S(1)}, bf16[4,32,1024]{2,1,0:T(8,128)(2,1)S(1)}, u32[]{:S(2)}, u32[]{:S(2)}) %collective-permute-start.2) | collective-permute-done | bytes 262176 | tf_op jit(solution)/shard_map/ppermute | solution.py:416
  60.3 0.8 collective-permute-start.6
  61.2 3.9 %collective-permute-done.9 = bf16[4,32,1024]{2,1,0:T(8,128)(2,1)S(1)} collective-permute-done((bf16[4,32,1024]{2,1,0:T(8,128)(2,1)S(1)}, bf16[4,32,1024]{2,1,0:T(8,128)(2,1)S(1)}, u32[]{:S(2)}, u32[]{:S(2)}) %collective-permute-start.9) | collective-permute-done | bytes 262176 | tf_op jit(solution)/shard_map/ppermute | solution.py:416
  65.1 0.1 collective-permute-start.12
  65.2 1.0 collective-permute-start.14
  66.3 4.5 %collective-permute-done.6 = bf16[2,32,1024]{2,1,0:T(8,128)(2,1)S(1)} collective-permute-done((bf16[2,32,1024]{2,1,0:T(8,128)(2,1)S(1)}, bf16[2,32,1024]{2,1,0:T(8,128)(2,1)S(1)}, u32[]{:S(2)}, u32[]{:S(2)}) %collective-permute-start.6) | collective-permute-done | bytes 131104 | tf_op jit(solution)/shard_map/ppermute | solution.py:416
  70.8 0.4 collective-permute-start.10
  71.2 1.7 %collective-permute-done.12 = bf16[2,32,1024]{2,1,0:T(8,128)(2,1)S(1)} collective-permute-done((bf16[2,32,1024]{2,1,0:T(8,128)(2,1)S(1)}, bf16[2,32,1024]{2,1,0:T(8,128)(2,1)S(1)}, u32[]{:S(2)}, u32[]{:S(2)}) %collective-permute-start.12) | collective-permute-done | bytes 131104 | tf_op jit(solution)/shard_map/ppermute | solution.py:416
  72.9 1.0 collective-permute-start.18
  74.0 0.2 collective-permute-start.16
  74.3 3.0 %collective-permute-done.10 = bf16[1,32,1024]{2,1,0:T(8,128)(2,1)S(1)} collective-permute-done((bf16[1,32,1024]{2,1,0:T(8,128)(2,1)S(1)}, bf16[1,32,1024]{2,1,0:T(8,128)(2,1)S(1)}, u32[]{:S(2)}, u32[]{:S(2)}) %collective-permute-start.10) | collective-permute-done | bytes 65568 | tf_op jit(solution)/shard_map/ppermute | solution.py:416
  77.3 0.1 collective-permute-start.17
  77.5 1.8 %collective-permute-start.15 = (bf16[2,32,1024]{2,1,0:T(8,128)(2,1)S(1)}, bf16[2,32,1024]{2,1,0:T(8,128)(2,1)S(1)}, u32[]{:S(2)}, u32[]{:S(2)}) collective-permute-start(bf16[2,32,1024]{2,1,0:T(8,128)(2,1)S(1)} %get-tuple-element.153), channel_id=1, source_target_pairs={{0,4},{1,5},{2,6},{3,7},{4,0},{5,1},{6,2},{7,3},{8,12},{9,13},{10,... | collective-permute-start | bytes 393224 | tf_op jit(solution)/shard_map/ppermute | solution.py:416
  79.2 1.4 %collective-permute-done.18 = bf16[1,32,1024]{2,1,0:T(8,128)(2,1)S(1)} collective-permute-done((bf16[1,32,1024]{2,1,0:T(8,128)(2,1)S(1)}, bf16[1,32,1024]{2,1,0:T(8,128)(2,1)S(1)}, u32[]{:S(2)}, u32[]{:S(2)}) %collective-permute-start.18) | collective-permute-done | bytes 65568 | tf_op jit(solution)/shard_map/ppermute | solution.py:416
  80.7 2.1 %collective-permute-done.17 = bf16[1,32,1024]{2,1,0:T(8,128)(2,1)S(1)} collective-permute-done((bf16[1,32,1024]{2,1,0:T(8,128)(2,1)S(1)}, bf16[1,32,1024]{2,1,0:T(8,128)(2,1)S(1)}, u32[]{:S(2)}, u32[]{:S(2)}) %collective-permute-start.17) | collective-permute-done | bytes 65568 | tf_op jit(solution)/shard_map/ppermute | solution.py:416
  82.8 0.1 collective-permute-start.20
  83.0 3.4 %collective-permute-start.21 = (bf16[1,32,1024]{2,1,0:T(8,128)(2,1)S(1)}, bf16[1,32,1024]{2,1,0:T(8,128)(2,1)S(1)}, u32[]{:S(2)}, u32[]{:S(2)}) collective-permute-start(bf16[1,32,1024]{2,1,0:T(8,128)(2,1)S(1)} %get-tuple-element.162), channel_id=1, source_target_pairs={{0,8},{1,9},{2,10},{3,11},{4,12},{5,13},{6,14},{7,15},{8,0},{9,1},... | collective-permute-start | bytes 196616 | tf_op jit(solution)/shard_map/ppermute | solution.py:416
  86.4 0.1 collective-permute-start.19
  86.5 0.4 collective-permute-done.22
  86.9 1.2 %collective-permute-start.24 = (bf16[2,32,1024]{2,1,0:T(8,128)(2,1)S(1)}, bf16[2,32,1024]{2,1,0:T(8,128)(2,1)S(1)}, u32[]{:S(2)}, u32[]{:S(2)}) collective-permute-start(bf16[2,32,1024]{2,1,0:T(8,128)(2,1)S(1)} %constant_dynamic-update-slice_fusion.2), channel_id=1, source_target_pairs={{0,2},{1,3},{2,0},{3,1},{4,6},{5,7},{6,4},{7,5},{8,10},{9,11},{10,... | collective-permute-start | bytes 393224 | tf_op jit(solution)/shard_map/ppermute | solution.py:416
  88.1 1.4 %collective-permute-done.21 = bf16[1,32,1024]{2,1,0:T(8,128)(2,1)S(1)} collective-permute-done((bf16[1,32,1024]{2,1,0:T(8,128)(2,1)S(1)}, bf16[1,32,1024]{2,1,0:T(8,128)(2,1)S(1)}, u32[]{:S(2)}, u32[]{:S(2)}) %collective-permute-start.21) | collective-permute-done | bytes 65568 | tf_op jit(solution)/shard_map/ppermute | solution.py:416
  89.5 2.1 %collective-permute-start.25 = (bf16[1,32,1024]{2,1,0:T(8,128)(2,1)S(1)}, bf16[1,32,1024]{2,1,0:T(8,128)(2,1)S(1)}, u32[]{:S(2)}, u32[]{:S(2)}) collective-permute-start(bf16[1,32,1024]{2,1,0:T(8,128)(2,1)S(1)} %bitcast.26), channel_id=1, source_target_pairs={{0,8},{1,9},{2,10},{3,11},{4,12},{5,13},{6,14},{7,15},{8,0},{9,1},... | collective-permute-start | bytes 196616 | tf_op jit(solution)/shard_map/ppermute | solution.py:416
  91.7 1.0 collective-permute-start.23
  92.7 0.9 collective-permute-done.19
  93.6 0.1 collective-permute-start.27
  93.7 1.3 %collective-permute-done.25 = bf16[1,32,1024]{2,1,0:T(8,128)(2,1)S(1)} collective-permute-done((bf16[1,32,1024]{2,1,0:T(8,128)(2,1)S(1)}, bf16[1,32,1024]{2,1,0:T(8,128)(2,1)S(1)}, u32[]{:S(2)}, u32[]{:S(2)}) %collective-permute-start.25) | collective-permute-done | bytes 65568 | tf_op jit(solution)/shard_map/ppermute | solution.py:416
  95.0 1.7 %collective-permute-start.29 = (bf16[2,32,1024]{2,1,0:T(8,128)(2,1)S(1)}, bf16[2,32,1024]{2,1,0:T(8,128)(2,1)S(1)}, u32[]{:S(2)}, u32[]{:S(2)}) collective-permute-start(bf16[2,32,1024]{2,1,0:T(8,128)(2,1)S(1)} %constant_dynamic-update-slice_fusion.6), channel_id=1, source_target_pairs={{0,4},{1,5},{2,6},{3,7},{4,0},{5,1},{6,2},{7,3},{8,12},{9,13},{10,... | collective-permute-start | bytes 393224 | tf_op jit(solution)/shard_map/ppermute | solution.py:416
  96.8 0.4 collective-permute-start.26
  97.2 2.2 %collective-permute-done.27 = bf16[1,32,1024]{2,1,0:T(8,128)(2,1)S(1)} collective-permute-done((bf16[1,32,1024]{2,1,0:T(8,128)(2,1)S(1)}, bf16[1,32,1024]{2,1,0:T(8,128)(2,1)S(1)}, u32[]{:S(2)}, u32[]{:S(2)}) %collective-permute-start.27) | collective-permute-done | bytes 65568 | tf_op jit(solution)/shard_map/ppermute | solution.py:416
  99.4 0.5 collective-permute-start.28
  99.9 1.7 %collective-permute-done.29 = bf16[2,32,1024]{2,1,0:T(8,128)(2,1)S(1)} collective-permute-done((bf16[2,32,1024]{2,1,0:T(8,128)(2,1)S(1)}, bf16[2,32,1024]{2,1,0:T(8,128)(2,1)S(1)}, u32[]{:S(2)}, u32[]{:S(2)}) %collective-permute-start.29) | collective-permute-done | bytes 131104 | tf_op jit(solution)/shard_map/ppermute | solution.py:416
  101.6 0.5 collective-permute-start.32
  102.2 2.3 %collective-permute-done.28 = bf16[2,32,1024]{2,1,0:T(8,128)(2,1)S(1)} collective-permute-done((bf16[2,32,1024]{2,1,0:T(8,128)(2,1)S(1)}, bf16[2,32,1024]{2,1,0:T(8,128)(2,1)S(1)}, u32[]{:S(2)}, u32[]{:S(2)}) %collective-permute-start.28) | collective-permute-done | bytes 131104 | tf_op jit(solution)/shard_map/ppermute | solution.py:416
  104.5 0.2 collective-permute-start.31
  104.7 1.7 %collective-permute-done.26 = bf16[4,32,1024]{2,1,0:T(8,128)(2,1)S(1)} collective-permute-done((bf16[4,32,1024]{2,1,0:T(8,128)(2,1)S(1)}, bf16[4,32,1024]{2,1,0:T(8,128)(2,1)S(1)}, u32[]{:S(2)}, u32[]{:S(2)}) %collective-permute-start.26) | collective-permute-done | bytes 262176 | tf_op jit(solution)/shard_map/ppermute | solution.py:416
  106.5 0.1 collective-permute-start.35
  106.6 1.5 %collective-permute-done.32 = bf16[4,32,1024]{2,1,0:T(8,128)(2,1)S(1)} collective-permute-done((bf16[4,32,1024]{2,1,0:T(8,128)(2,1)S(1)}, bf16[4,32,1024]{2,1,0:T(8,128)(2,1)S(1)}, u32[]{:S(2)}, u32[]{:S(2)}) %collective-permute-start.32) | collective-permute-done | bytes 262176 | tf_op jit(solution)/shard_map/ppermute | solution.py:416
  108.2 2.7 %collective-permute-done.31 = bf16[4,32,1024]{2,1,0:T(8,128)(2,1)S(1)} collective-permute-done((bf16[4,32,1024]{2,1,0:T(8,128)(2,1)S(1)}, bf16[4,32,1024]{2,1,0:T(8,128)(2,1)S(1)}, u32[]{:S(2)}, u32[]{:S(2)}) %collective-permute-start.31) | collective-permute-done | bytes 262176 | tf_op jit(solution)/shard_map/ppermute | solution.py:416
  111.0 0.1 collective-permute-start.33
  111.0 0.5 collective-permute-start.30
  111.6 0.7 pad_maximum_fusion.2
  112.3 2.1 %shard_map.117.refs_4_ = bf16[128,16384]{1,0:T(8,128)(2,1)} custom-call(f32[16,1024]{1,0:T(8,128)S(1)} %reshape.42.gain_ref, bf16[8,32,1024]{2,1,0:T(8,128)(2,1)S(1)} %constant_dynamic-update-slice_fusion.20.refs_0_, bf16[8,32,1024]{2,1,0:T(8,128)(2,1)S(1)} %collective-permute-done.34.refs_1_, ...), custom_call_target="tpu_custom_call" | custom-call | flops 6291456 | bytes 4194304 | tf_op jit(solution)/shard_map/pallas_call | solution.py:399
  114.3 3.3 %shard_map.118 = bf16[128,16384]{1,0:T(8,128)(2,1)} custom-call(f32[16,1024]{1,0:T(8,128)S(1)} %reshape.42.gain_ref, bf16[8,32,1024]{2,1,0:T(8,128)(2,1)S(1)} %constant_dynamic-update-slice_fusion.18.refs_0_, bf16[8,32,1024]{2,1,0:T(8,128)(2,1)} %collective-permute-done.30.refs_1_, ...), custom_call_target="tpu_custom_call", output_to_operand_aliasing={{}: (5, {})} | custom-call | flops 6291456 | bytes 4194304 | tf_op jit(solution)/shard_map/pallas_call | solution.py:399
  (77 shorter events, 1.6 us)
Async XLA Ops:
  1.6 0.8 copy-start.1
  2.4 26.0 %copy-start = (bf16[8,1024,512]{2,1,0:T(8,128)(2,1)S(1)}, bf16[8,1024,512]{2,1,0:T(8,128)(2,1)}, u32[]{:S(2)}) copy-start(bf16[8,1024,512]{2,1,0:T(8,128)(2,1)} %keys_ref.1) | copy-start | bytes 25165828
  2.4 26.0 %copy-start.2 = (s32[8]{0:T(128)S(1)}, s32[8]{0:T(128)}, u32[]{:S(2)}) copy-start(s32[8]{0:T(128)} %lengths_ref.1) | copy-start | bytes 100
  49.4 1.6 %collective-permute-start = (bf16[4,32,1024]{2,1,0:T(8,128)(2,1)S(1)}, bf16[4,32,1024]{2,1,0:T(8,128)(2,1)S(1)}, u32[]{:S(2)}, u32[]{:S(2)}) collective-permute-start(bf16[4,32,1024]{2,1,0:T(8,128)(2,1)S(1)} %get-tuple-element.80), channel_id=1, source_target_pairs={{0,1},{1,0},{2,3},{3,2},{4,5},{5,4},{6,7},{7,6},{8,9},{9,8},{10,11... | collective-permute-start | bytes 786440 | tf_op jit(solution)/shard_map/ppermute | solution.py:416
  49.4 5.7 %collective-permute-start.4 = (bf16[4,32,1024]{2,1,0:T(8,128)(2,1)S(1)}, bf16[4,32,1024]{2,1,0:T(8,128)(2,1)S(1)}, u32[]{:S(2)}, u32[]{:S(2)}) collective-permute-start(bf16[4,32,1024]{2,1,0:T(8,128)(2,1)S(1)} %get-tuple-element.88), channel_id=1, source_target_pairs={{0,1},{1,0},{2,3},{3,2},{4,5},{5,4},{6,7},{7,6},{8,9},{9,8},{10,11... | collective-permute-start | bytes 786440 | tf_op jit(solution)/shard_map/ppermute | solution.py:416
  49.9 5.3 %collective-permute-start.5 = (bf16[4,32,1024]{2,1,0:T(8,128)(2,1)S(1)}, bf16[4,32,1024]{2,1,0:T(8,128)(2,1)S(1)}, u32[]{:S(2)}, u32[]{:S(2)}) collective-permute-start(bf16[4,32,1024]{2,1,0:T(8,128)(2,1)S(1)} %get-tuple-element.90), channel_id=1, source_target_pairs={{0,1},{1,0},{2,3},{3,2},{4,5},{5,4},{6,7},{7,6},{8,9},{9,8},{10,11... | collective-permute-start | bytes 786440 | tf_op jit(solution)/shard_map/ppermute | solution.py:416
  50.0 7.5 %collective-permute-start.7 = (bf16[4,32,1024]{2,1,0:T(8,128)(2,1)S(1)}, bf16[4,32,1024]{2,1,0:T(8,128)(2,1)S(1)}, u32[]{:S(2)}, u32[]{:S(2)}) collective-permute-start(bf16[4,32,1024]{2,1,0:T(8,128)(2,1)S(1)} %get-tuple-element.96), channel_id=1, source_target_pairs={{0,1},{1,0},{2,3},{3,2},{4,5},{5,4},{6,7},{7,6},{8,9},{9,8},{10,11... | collective-permute-start | bytes 786440 | tf_op jit(solution)/shard_map/ppermute | solution.py:416
  51.0 9.1 %collective-permute-start.2 = (bf16[4,32,1024]{2,1,0:T(8,128)(2,1)S(1)}, bf16[4,32,1024]{2,1,0:T(8,128)(2,1)S(1)}, u32[]{:S(2)}, u32[]{:S(2)}) collective-permute-start(bf16[4,32,1024]{2,1,0:T(8,128)(2,1)S(1)} %add_convert_fusion.7), channel_id=1, source_target_pairs={{0,2},{1,3},{2,0},{3,1},{4,6},{5,7},{6,4},{7,5},{8,10},{9,11},{10,... | collective-permute-start | bytes 786440 | tf_op jit(solution)/shard_map/ppermute | solution.py:416
  55.0 2.9 %collective-permute-start.3 = (bf16[4,32,1024]{2,1,0:T(8,128)(2,1)S(1)}, bf16[4,32,1024]{2,1,0:T(8,128)(2,1)S(1)}, u32[]{:S(2)}, u32[]{:S(2)}) collective-permute-start(bf16[4,32,1024]{2,1,0:T(8,128)(2,1)S(1)} %get-tuple-element.86), channel_id=1, source_target_pairs={{0,1},{1,0},{2,3},{3,2},{4,5},{5,4},{6,7},{7,6},{8,9},{9,8},{10,11... | collective-permute-start | bytes 786440 | tf_op jit(solution)/shard_map/ppermute | solution.py:416
  55.4 9.7 %collective-permute-start.9 = (bf16[4,32,1024]{2,1,0:T(8,128)(2,1)S(1)}, bf16[4,32,1024]{2,1,0:T(8,128)(2,1)S(1)}, u32[]{:S(2)}, u32[]{:S(2)}) collective-permute-start(bf16[4,32,1024]{2,1,0:T(8,128)(2,1)S(1)} %add_convert_fusion.3), channel_id=1, source_target_pairs={{0,2},{1,3},{2,0},{3,1},{4,6},{5,7},{6,4},{7,5},{8,10},{9,11},{10,... | collective-permute-start | bytes 786440 | tf_op jit(solution)/shard_map/ppermute | solution.py:416
  57.3 1.5 %collective-permute-start.1 = (bf16[4,32,1024]{2,1,0:T(8,128)(2,1)S(1)}, bf16[4,32,1024]{2,1,0:T(8,128)(2,1)S(1)}, u32[]{:S(2)}, u32[]{:S(2)}) collective-permute-start(bf16[4,32,1024]{2,1,0:T(8,128)(2,1)S(1)} %get-tuple-element.83), channel_id=1, source_target_pairs={{0,1},{1,0},{2,3},{3,2},{4,5},{5,4},{6,7},{7,6},{8,9},{9,8},{10,11... | collective-permute-start | bytes 786440 | tf_op jit(solution)/shard_map/ppermute | solution.py:416
  57.5 3.6 %collective-permute-start.8 = (bf16[4,32,1024]{2,1,0:T(8,128)(2,1)S(1)}, bf16[4,32,1024]{2,1,0:T(8,128)(2,1)S(1)}, u32[]{:S(2)}, u32[]{:S(2)}) collective-permute-start(bf16[4,32,1024]{2,1,0:T(8,128)(2,1)S(1)} %get-tuple-element.98), channel_id=1, source_target_pairs={{0,1},{1,0},{2,3},{3,2},{4,5},{5,4},{6,7},{7,6},{8,9},{9,8},{10,11... | collective-permute-start | bytes 786440 | tf_op jit(solution)/shard_map/ppermute | solution.py:416
  57.9 8.3 %collective-permute-start.13 = (bf16[4,32,1024]{2,1,0:T(8,128)(2,1)S(1)}, bf16[4,32,1024]{2,1,0:T(8,128)(2,1)S(1)}, u32[]{:S(2)}, u32[]{:S(2)}) collective-permute-start(bf16[4,32,1024]{2,1,0:T(8,128)(2,1)S(1)} %get-tuple-element.111), channel_id=1, source_target_pairs={{0,1},{1,0},{2,3},{3,2},{4,5},{5,4},{6,7},{7,6},{8,9},{9,8},{10,11... | collective-permute-start | bytes 786440 | tf_op jit(solution)/shard_map/ppermute | solution.py:416
  58.3 53.2 %copy-start.3 = (bf16[16384]{0:T(1024)(128)(2,1)S(1)}, bf16[16384]{0:T(1024)(128)(2,1)}, u32[]{:S(2)}) copy-start(bf16[16384]{0:T(1024)(128)(2,1)} %param.17) | copy-start | bytes 98308
  58.9 15.1 %collective-permute-start.11 = (bf16[4,32,1024]{2,1,0:T(8,128)(2,1)S(1)}, bf16[4,32,1024]{2,1,0:T(8,128)(2,1)S(1)}, u32[]{:S(2)}, u32[]{:S(2)}) collective-permute-start(bf16[4,32,1024]{2,1,0:T(8,128)(2,1)S(1)} %pad_maximum_fusion), channel_id=1, source_target_pairs={{0,4},{1,5},{2,6},{3,7},{4,0},{5,1},{6,2},{7,3},{8,12},{9,13},{10,... | collective-permute-start | bytes 786440 | tf_op jit(solution)/shard_map/ppermute | solution.py:416
  60.3 10.6 %collective-permute-start.6 = (bf16[2,32,1024]{2,1,0:T(8,128)(2,1)S(1)}, bf16[2,32,1024]{2,1,0:T(8,128)(2,1)S(1)}, u32[]{:S(2)}, u32[]{:S(2)}) collective-permute-start(bf16[2,32,1024]{2,1,0:T(8,128)(2,1)S(1)} %get-tuple-element.157), channel_id=1, source_target_pairs={{0,4},{1,5},{2,6},{3,7},{4,0},{5,1},{6,2},{7,3},{8,12},{9,13},{10,... | collective-permute-start | bytes 393224 | tf_op jit(solution)/shard_map/ppermute | solution.py:416
  65.1 7.7 %collective-permute-start.12 = (bf16[2,32,1024]{2,1,0:T(8,128)(2,1)S(1)}, bf16[2,32,1024]{2,1,0:T(8,128)(2,1)S(1)}, u32[]{:S(2)}, u32[]{:S(2)}) collective-permute-start(bf16[2,32,1024]{2,1,0:T(8,128)(2,1)S(1)} %get-tuple-element.158), channel_id=1, source_target_pairs={{0,4},{1,5},{2,6},{3,7},{4,0},{5,1},{6,2},{7,3},{8,12},{9,13},{10,... | collective-permute-start | bytes 393224 | tf_op jit(solution)/shard_map/ppermute | solution.py:416
  65.2 12.1 %collective-permute-start.14 = (bf16[4,32,1024]{2,1,0:T(8,128)(2,1)S(1)}, bf16[4,32,1024]{2,1,0:T(8,128)(2,1)S(1)}, u32[]{:S(2)}, u32[]{:S(2)}) collective-permute-start(bf16[4,32,1024]{2,1,0:T(8,128)(2,1)S(1)} %add_convert_fusion.2), channel_id=1, source_target_pairs={{0,2},{1,3},{2,0},{3,1},{4,6},{5,7},{6,4},{7,5},{8,10},{9,11},{10,... | collective-permute-start | bytes 786440 | tf_op jit(solution)/shard_map/ppermute | solution.py:416
  70.8 6.4 %collective-permute-start.10 = (bf16[1,32,1024]{2,1,0:T(8,128)(2,1)S(1)}, bf16[1,32,1024]{2,1,0:T(8,128)(2,1)S(1)}, u32[]{:S(2)}, u32[]{:S(2)}) collective-permute-start(bf16[1,32,1024]{2,1,0:T(8,128)(2,1)S(1)} %get-tuple-element.169), channel_id=1, source_target_pairs={{0,8},{1,9},{2,10},{3,11},{4,12},{5,13},{6,14},{7,15},{8,0},{9,1},... | collective-permute-start | bytes 196616 | tf_op jit(solution)/shard_map/ppermute | solution.py:416
  72.9 7.7 %collective-permute-start.18 = (bf16[1,32,1024]{2,1,0:T(8,128)(2,1)S(1)}, bf16[1,32,1024]{2,1,0:T(8,128)(2,1)S(1)}, u32[]{:S(2)}, u32[]{:S(2)}) collective-permute-start(bf16[1,32,1024]{2,1,0:T(8,128)(2,1)S(1)} %get-tuple-element.170), channel_id=1, source_target_pairs={{0,8},{1,9},{2,10},{3,11},{4,12},{5,13},{6,14},{7,15},{8,0},{9,1},... | collective-permute-start | bytes 196616 | tf_op jit(solution)/shard_map/ppermute | solution.py:416
  74.0 8.9 %collective-permute-start.16 = (bf16[2,32,1024]{2,1,0:T(8,128)(2,1)S(1)}, bf16[2,32,1024]{2,1,0:T(8,128)(2,1)S(1)}, u32[]{:S(2)}, u32[]{:S(2)}) collective-permute-start(bf16[2,32,1024]{2,1,0:T(8,128)(2,1)S(1)} %get-tuple-element.155), channel_id=1, source_target_pairs={{0,2},{1,3},{2,0},{3,1},{4,6},{5,7},{6,4},{7,5},{8,10},{9,11},{10,... | collective-permute-start | bytes 393224 | tf_op jit(solution)/shard_map/ppermute | solution.py:416
  77.3 5.5 %collective-permute-start.17 = (bf16[1,32,1024]{2,1,0:T(8,128)(2,1)S(1)}, bf16[1,32,1024]{2,1,0:T(8,128)(2,1)S(1)}, u32[]{:S(2)}, u32[]{:S(2)}) collective-permute-start(bf16[1,32,1024]{2,1,0:T(8,128)(2,1)S(1)} %bitcast.22), channel_id=1, source_target_pairs={{0,8},{1,9},{2,10},{3,11},{4,12},{5,13},{6,14},{7,15},{8,0},{9,1},... | collective-permute-start | bytes 196616 | tf_op jit(solution)/shard_map/ppermute | solution.py:416
  77.5 8.9 %collective-permute-start.15 = (bf16[2,32,1024]{2,1,0:T(8,128)(2,1)S(1)}, bf16[2,32,1024]{2,1,0:T(8,128)(2,1)S(1)}, u32[]{:S(2)}, u32[]{:S(2)}) collective-permute-start(bf16[2,32,1024]{2,1,0:T(8,128)(2,1)S(1)} %get-tuple-element.153), channel_id=1, source_target_pairs={{0,4},{1,5},{2,6},{3,7},{4,0},{5,1},{6,2},{7,3},{8,12},{9,13},{10,... | collective-permute-start | bytes 393224 | tf_op jit(solution)/shard_map/ppermute | solution.py:416
  80.6 6.2 %collective-permute-start.22 = (bf16[1,32,1024]{2,1,0:T(8,128)(2,1)S(1)}, bf16[1,32,1024]{2,1,0:T(8,128)(2,1)S(1)}, u32[]{:S(2)}, u32[]{:S(2)}) collective-permute-start(bf16[1,32,1024]{2,1,0:T(8,128)(2,1)S(1)} %bitcast.24), channel_id=1, source_target_pairs={{0,8},{1,9},{2,10},{3,11},{4,12},{5,13},{6,14},{7,15},{8,0},{9,1},... | collective-permute-start | bytes 196616 | tf_op jit(solution)/shard_map/ppermute | solution.py:416
  82.8 8.8 %collective-permute-start.20 = (bf16[2,32,1024]{2,1,0:T(8,128)(2,1)S(1)}, bf16[2,32,1024]{2,1,0:T(8,128)(2,1)S(1)}, u32[]{:S(2)}, u32[]{:S(2)}) collective-permute-start(bf16[2,32,1024]{2,1,0:T(8,128)(2,1)S(1)} %constant_dynamic-update-slice_fusion), channel_id=1, source_target_pairs={{0,4},{1,5},{2,6},{3,7},{4,0},{5,1},{6,2},{7,3},{8,12},{9,13},{10,... | collective-permute-start | bytes 393224 | tf_op jit(solution)/shard_map/ppermute | solution.py:416
  83.0 6.5 %collective-permute-start.21 = (bf16[1,32,1024]{2,1,0:T(8,128)(2,1)S(1)}, bf16[1,32,1024]{2,1,0:T(8,128)(2,1)S(1)}, u32[]{:S(2)}, u32[]{:S(2)}) collective-permute-start(bf16[1,32,1024]{2,1,0:T(8,128)(2,1)S(1)} %get-tuple-element.162), channel_id=1, source_target_pairs={{0,8},{1,9},{2,10},{3,11},{4,12},{5,13},{6,14},{7,15},{8,0},{9,1},... | collective-permute-start | bytes 196616 | tf_op jit(solution)/shard_map/ppermute | solution.py:416
  86.4 7.2 %collective-permute-start.19 = (bf16[1,32,1024]{2,1,0:T(8,128)(2,1)S(1)}, bf16[1,32,1024]{2,1,0:T(8,128)(2,1)S(1)}, u32[]{:S(2)}, u32[]{:S(2)}) collective-permute-start(bf16[1,32,1024]{2,1,0:T(8,128)(2,1)S(1)} %get-tuple-element.161), channel_id=1, source_target_pairs={{0,8},{1,9},{2,10},{3,11},{4,12},{5,13},{6,14},{7,15},{8,0},{9,1},... | collective-permute-start | bytes 196616 | tf_op jit(solution)/shard_map/ppermute | solution.py:416
  86.9 9.9 %collective-permute-start.24 = (bf16[2,32,1024]{2,1,0:T(8,128)(2,1)S(1)}, bf16[2,32,1024]{2,1,0:T(8,128)(2,1)S(1)}, u32[]{:S(2)}, u32[]{:S(2)}) collective-permute-start(bf16[2,32,1024]{2,1,0:T(8,128)(2,1)S(1)} %constant_dynamic-update-slice_fusion.2), channel_id=1, source_target_pairs={{0,2},{1,3},{2,0},{3,1},{4,6},{5,7},{6,4},{7,5},{8,10},{9,11},{10,... | collective-permute-start | bytes 393224 | tf_op jit(solution)/shard_map/ppermute | solution.py:416
  89.5 5.5 %collective-permute-start.25 = (bf16[1,32,1024]{2,1,0:T(8,128)(2,1)S(1)}, bf16[1,32,1024]{2,1,0:T(8,128)(2,1)S(1)}, u32[]{:S(2)}, u32[]{:S(2)}) collective-permute-start(bf16[1,32,1024]{2,1,0:T(8,128)(2,1)S(1)} %bitcast.26), channel_id=1, source_target_pairs={{0,8},{1,9},{2,10},{3,11},{4,12},{5,13},{6,14},{7,15},{8,0},{9,1},... | collective-permute-start | bytes 196616 | tf_op jit(solution)/shard_map/ppermute | solution.py:416
  91.7 14.9 %collective-permute-start.23 = (bf16[4,32,1024]{2,1,0:T(8,128)(2,1)S(1)}, bf16[4,32,1024]{2,1,0:T(8,128)(2,1)S(1)}, u32[]{:S(2)}, u32[]{:S(2)}) collective-permute-start(bf16[4,32,1024]{2,1,0:T(8,128)(2,1)S(1)} %constant_dynamic-update-slice_fusion.4), channel_id=1, source_target_pairs={{0,2},{1,3},{2,0},{3,1},{4,6},{5,7},{6,4},{7,5},{8,10},{9,11},{10,... | collective-permute-start | bytes 786440 | tf_op jit(solution)/shard_map/ppermute | solution.py:416
  93.6 5.8 %collective-permute-start.27 = (bf16[1,32,1024]{2,1,0:T(8,128)(2,1)S(1)}, bf16[1,32,1024]{2,1,0:T(8,128)(2,1)S(1)}, u32[]{:S(2)}, u32[]{:S(2)}) collective-permute-start(bf16[1,32,1024]{2,1,0:T(8,128)(2,1)S(1)} %bitcast.28), channel_id=1, source_target_pairs={{0,8},{1,9},{2,10},{3,11},{4,12},{5,13},{6,14},{7,15},{8,0},{9,1},... | collective-permute-start | bytes 196616 | tf_op jit(solution)/shard_map/ppermute | solution.py:416
  95.0 6.6 %collective-permute-start.29 = (bf16[2,32,1024]{2,1,0:T(8,128)(2,1)S(1)}, bf16[2,32,1024]{2,1,0:T(8,128)(2,1)S(1)}, u32[]{:S(2)}, u32[]{:S(2)}) collective-permute-start(bf16[2,32,1024]{2,1,0:T(8,128)(2,1)S(1)} %constant_dynamic-update-slice_fusion.6), channel_id=1, source_target_pairs={{0,4},{1,5},{2,6},{3,7},{4,0},{5,1},{6,2},{7,3},{8,12},{9,13},{10,... | collective-permute-start | bytes 393224 | tf_op jit(solution)/shard_map/ppermute | solution.py:416
  96.8 9.6 %collective-permute-start.26 = (bf16[4,32,1024]{2,1,0:T(8,128)(2,1)S(1)}, bf16[4,32,1024]{2,1,0:T(8,128)(2,1)S(1)}, u32[]{:S(2)}, u32[]{:S(2)}) collective-permute-start(bf16[4,32,1024]{2,1,0:T(8,128)(2,1)S(1)} %constant_dynamic-update-slice_fusion.8), channel_id=1, source_target_pairs={{0,4},{1,5},{2,6},{3,7},{4,0},{5,1},{6,2},{7,3},{8,12},{9,13},{10,... | collective-permute-start | bytes 786440 | tf_op jit(solution)/shard_map/ppermute | solution.py:416
  99.4 5.0 %collective-permute-start.28 = (bf16[2,32,1024]{2,1,0:T(8,128)(2,1)S(1)}, bf16[2,32,1024]{2,1,0:T(8,128)(2,1)S(1)}, u32[]{:S(2)}, u32[]{:S(2)}) collective-permute-start(bf16[2,32,1024]{2,1,0:T(8,128)(2,1)S(1)} %constant_dynamic-update-slice_fusion.10), channel_id=1, source_target_pairs={{0,2},{1,3},{2,0},{3,1},{4,6},{5,7},{6,4},{7,5},{8,10},{9,11},{10,... | collective-permute-start | bytes 393224 | tf_op jit(solution)/shard_map/ppermute | solution.py:416
  101.6 6.4 %collective-permute-start.32 = (bf16[4,32,1024]{2,1,0:T(8,128)(2,1)S(1)}, bf16[4,32,1024]{2,1,0:T(8,128)(2,1)S(1)}, u32[]{:S(2)}, u32[]{:S(2)}) collective-permute-start(bf16[4,32,1024]{2,1,0:T(8,128)(2,1)S(1)} %constant_dynamic-update-slice_fusion.12), channel_id=1, source_target_pairs={{0,2},{1,3},{2,0},{3,1},{4,6},{5,7},{6,4},{7,5},{8,10},{9,11},{10,... | collective-permute-start | bytes 786440 | tf_op jit(solution)/shard_map/ppermute | solution.py:416
  104.5 6.4 %collective-permute-start.31 = (bf16[4,32,1024]{2,1,0:T(8,128)(2,1)S(1)}, bf16[4,32,1024]{2,1,0:T(8,128)(2,1)S(1)}, u32[]{:S(2)}, u32[]{:S(2)}) collective-permute-start(bf16[4,32,1024]{2,1,0:T(8,128)(2,1)S(1)} %constant_dynamic-update-slice_fusion.14), channel_id=1, source_target_pairs={{0,4},{1,5},{2,6},{3,7},{4,0},{5,1},{6,2},{7,3},{8,12},{9,13},{10,... | collective-permute-start | bytes 786440 | tf_op jit(solution)/shard_map/ppermute | solution.py:416
  106.5 5.8 %collective-permute-start.35 = (bf16[8,32,1024]{2,1,0:T(8,128)(2,1)S(1)}, bf16[8,32,1024]{2,1,0:T(8,128)(2,1)S(1)}, u32[]{:S(2)}, u32[]{:S(2)}) collective-permute-start(bf16[8,32,1024]{2,1,0:T(8,128)(2,1)S(1)} %constant_dynamic-update-slice_fusion.16.refs_2_), channel_id=1, source_target_pairs={{0,1},{1,0},{2,3},{3,2},{4,5},{5,4},{6,7},{7,6},{8,9},{9,8},{10,11... | collective-permute-start | bytes 1572872 | tf_op jit(solution)/shard_map/ppermute | solution.py:416
  108.1 4.2 %collective-permute-start.34 = (bf16[8,32,1024]{2,1,0:T(8,128)(2,1)S(1)}, bf16[8,32,1024]{2,1,0:T(8,128)(2,1)S(1)}, u32[]{:S(2)}, u32[]{:S(2)}) collective-permute-start(bf16[8,32,1024]{2,1,0:T(8,128)(2,1)S(1)} %constant_dynamic-update-slice_fusion.20.refs_0_), channel_id=1, source_target_pairs={{0,1},{1,0},{2,3},{3,2},{4,5},{5,4},{6,7},{7,6},{8,9},{9,8},{10,11... | collective-permute-start | bytes 1572872 | tf_op jit(solution)/shard_map/ppermute | solution.py:416
  111.0 3.4 %collective-permute-start.33 = (bf16[8,32,1024]{2,1,0:T(8,128)(2,1)S(1)}, bf16[8,32,1024]{2,1,0:T(8,128)(2,1)}, u32[]{:S(2)}, u32[]{:S(2)}) collective-permute-start(bf16[8,32,1024]{2,1,0:T(8,128)(2,1)S(1)} %constant_dynamic-update-slice_fusion.22.refs_2_), channel_id=1, source_target_pairs={{0,1},{1,0},{2,3},{3,2},{4,5},{5,4},{6,7},{7,6},{8,9},{9,8},{10,11... | collective-permute-start | bytes 1572872 | tf_op jit(solution)/shard_map/ppermute | solution.py:416
  111.0 3.3 %collective-permute-start.30 = (bf16[8,32,1024]{2,1,0:T(8,128)(2,1)S(1)}, bf16[8,32,1024]{2,1,0:T(8,128)(2,1)}, u32[]{:S(2)}, u32[]{:S(2)}) collective-permute-start(bf16[8,32,1024]{2,1,0:T(8,128)(2,1)S(1)} %constant_dynamic-update-slice_fusion.18.refs_0_), channel_id=1, source_target_pairs={{0,1},{1,0},{2,3},{3,2},{4,5},{5,4},{6,7},{7,6},{8,9},{9,8},{10,11... | collective-permute-start | bytes 1572872 | tf_op jit(solution)/shard_map/ppermute | solution.py:416

commit v9 on v7

--- a/solution.py
+++ b/solution.py
@@ -11,7 +11,7 @@
 HD = 128
 
 
-TABLE = "101203101230310230123230211323"
+TABLE = "03203103201302312012312130320121"
 
 epsilon = 1e-05
 rope_theta = 500000.0
@@ -288,14 +288,14 @@
     bits = list(range(1, count.bit_length() - 1))
     turned = bits[::-1]
     late = bits[1:2] + bits[:1] + bits[2:]
-    return [(late, late[::-1]), (bits, turned), (bits, turned), (late, late[::-1])]
+    crossed = late[::-1]
+    return [(bits, turned), (bits, crossed), (late, turned), (bits, crossed)]
 
 
 def timetable(count):
     if count == 16:
         return [int(c) for c in TABLE]
-    steps = 2 * (count.bit_length() - 2) + 1
-    return [s for _ in range(steps) for s in (1, 0, 2, 3)] + [1, 3]
+    return [s for _ in range(2 * (count.bit_length() - 2) + 2) for s in (1, 0, 2, 3)]
 
 
 def place(offset, order):
@@ -363,43 +363,39 @@
     return outs[0::2], outs[1::2]
 
 
-def finish_kernel(offsets, gain_ref, *refs):
+def finish_kernel(offsets, own_ref, other_ref, gain_ref, *refs):
     out_ref = refs[-1]
     me = lax.axis_index("tensor")
-    half, rows, width = refs[0].shape
-    for k, order in enumerate(offsets):
-        parts = refs[2 * k : 2 * k + 2]
-        total = jnp.zeros((rows, width), jnp.float32)
-        for ref in parts:
-            for spot in range(half):
-                block = ref[spot].astype(jnp.float32)
-                total = total + block * block
-        mean_square = jnp.sum(total, axis=1, keepdims=True) / (2 * half * width)
-        scale = lax.rsqrt(mean_square + epsilon)
-        for spot, offset in enumerate(order):
-            block = parts[spot // half][spot % half].astype(jnp.float32)
-            index = jnp.bitwise_xor(me, offset)
-            column = pl.multiple_of(index * width, width)
-            gain = gain_ref[pl.ds(index, 1), :]
-            out_ref[k * rows : (k + 1) * rows, pl.ds(column, width)] = (
-                block * scale * gain
-            ).astype(jnp.bfloat16)
-
-
-def finish(parts, gain, offsets, which, groups, earlier):
-    half, rows, width = parts[0].shape
-    columns, rows = 2 * half * width, rows * len(offsets)
-    operands = [gain, *parts] + ([] if earlier is None else [earlier])
-    specs = [pl.BlockSpec(memory_space=pltpu.VMEM)] * (1 + len(parts))
-    if earlier is not None:
-        specs.append(pl.BlockSpec(memory_space=pl.ANY))
+    half, _, width = own_ref.shape
+    rows = out_ref.shape[0]
+    here = pl.ds(pl.multiple_of(pl.program_id(0) * rows, rows), rows)
+    total = jnp.zeros((rows, width), jnp.float32)
+    for ref in (own_ref, other_ref):
+        for k in range(half):
+            block = ref[k, here, :].astype(jnp.float32)
+            total = total + block * block
+    mean_square = jnp.sum(total, axis=1, keepdims=True) / (2 * half * width)
+    scale = lax.rsqrt(mean_square + epsilon)
+    for k, offset in enumerate(offsets):
+        block = (own_ref if k < half else other_ref)[k % half, here, :].astype(jnp.float32)
+        index = jnp.bitwise_xor(me, offset)
+        column = pl.multiple_of(index * width, width)
+        gain = gain_ref[pl.ds(index, 1), :]
+        out_ref[:, pl.ds(column, width)] = (block * scale * gain).astype(jnp.bfloat16)
+
+
+def finish(own, other, gain, offsets, which, sets, earlier):
+    half, rows, width = own.shape
+    columns, tiles = 2 * half * width, 2
+    operands = [own, other, gain] + ([] if earlier is None else [earlier])
+    whole = pl.BlockSpec(memory_space=pltpu.VMEM)
     return pl.pallas_call(
         functools.partial(finish_kernel, offsets),
-        grid=(1,),
-        out_shape=jax.ShapeDtypeStruct((rows * groups, columns), jnp.bfloat16),
-        in_specs=specs,
-        out_specs=pl.BlockSpec((rows, columns), lambda i: (which, 0)),
-        input_output_aliases={} if earlier is None else {len(operands) - 1: 0},
+        grid=(tiles,),
+        out_shape=jax.ShapeDtypeStruct((rows * sets, columns), jnp.bfloat16),
+        in_specs=[whole] * 3 + [pl.BlockSpec(memory_space=pl.ANY)] * (len(operands) - 3),
+        out_specs=pl.BlockSpec((rows // tiles, columns), lambda i: (which * tiles + i, 0)),
+        input_output_aliases={} if earlier is None else {3: 0},
         compiler_params=pltpu.CompilerParams(vmem_limit_bytes=24 * 1024 * 1024),
         cost_estimate=pl.CostEstimate(
             flops=6 * rows * columns, bytes_accessed=4 * rows * columns, transcendentals=0
@@ -492,10 +488,7 @@
         elif step <= len(scatter) + len(gather):
             last = held[k] = jnp.concatenate([held[k], arrivals[k]], axis=0)
         else:
-            pair = [k - 1, k]
-            parts = [block for m in pair for block in (held[m], arrivals[m])]
-            lists = [offsets[m] for m in pair]
-            last = normed = finish(parts, gain, lists, k // 2, sets // 2, normed)
+            last = normed = finish(held[k], arrivals[k], gain, offsets[k], k, sets, normed)
             continue
         bit = (gather + [0])[step - len(scatter)]
         arrivals[k] = swap(held[k], bit, count)

time: 123 us -> 122 us (level)
  starting transfers between devices: 33.2 us -> 24.5 us
  waiting for transfers between devices: 28.1 us -> 35 us
    ppermute x36, starting transfers between devices: 33.2 us -> 24.5 us  [swap(): lax.ppermute(values, 'tensor', [(i, i ^ 1 << bit) for i in range(count)])]
    ppermute x36, waiting for transfers between devices: 28.1 us -> 35 us  [swap(): lax.ppermute(values, 'tensor', [(i, i ^ 1 << bit) for i in range(count)])]
    pallas_call x2 -> x4, Pallas kernels: 5.45 us -> 6.19 us  [finish(): pl.pallas_call(functools.partial(finish_kernel, offsets), grid=(tiles,),...]
  transfers between devices with their start and end apart: 36 -> 36, of which waited for: 15 -> 13; matrix products, arithmetic and copies ran while one was open for 2% -> 2% of each run, Pallas kernels for 5% -> 7%
where the time goes in v9:
time: 122 us
  waiting for transfers between devices  35 us (29%)
  Pallas kernels  31.2 us (26%)
  blocking collectives  26.2 us (21%)
  starting transfers between devices  24.5 us (20%)
  other arithmetic  2.81 us (2%)
  local copies, waits for them, and re-layouts  1.26 us (1%)
    ppermute x36, waiting for transfers between devices, swap(): lax.ppermute(values, 'tensor', [(i, i ^ 1 << bit) for i in range(count)])  35 us
    all_to_all x2, blocking collectives, exchange(): lax.all_to_all(blocks, 'tensor', split_axis=0, concat_axis=0, tiled=True)  26.2 us
    ppermute x36, starting transfers between devices, swap(): lax.ppermute(values, 'tensor', [(i, i ^ 1 << bit) for i in range(count)])  24.5 us
    pallas_call x1, Pallas kernels, project_in(): pl.pallas_call(functools.partial(input_kernel, count), out_shape=(jax.Sha...  10.7 us
    pallas_call x2, Pallas kernels, project(): pl.pallas_call(functools.partial(project_kernel, count, side), out_shape=...  7.67 us
    pallas_call x1, Pallas kernels, attend(): pl.pallas_call(functools.partial(attend_kernel, count), out_shape=jax.Sha...  6.62 us
    pallas_call x4, Pallas kernels, finish(): pl.pallas_call(functools.partial(finish_kernel, offsets), grid=(tiles,),...  6.19 us
  transfers between devices with their start and end apart: 36, of which 13 were waited for; matrix products, arithmetic and copies ran while one was open for 2% of the time, Pallas kernels for 7%

profile of v9, /device:TPU:0, one launch (start us, length us, event | category | flops | bytes accessed | tf_op | source)
XLA Modules:
  0.0 122.2 jit_solution(17689710045917147033)
XLA Ops:
  0.6 0.7 convert_element_type.283
  1.3 0.3 fusion.4
  1.6 0.9 copy-done
  2.5 10.7 %shard_map.113 = (bf16[16,8,640]{2,1,0:T(8,128)(2,1)S(1)}, bf16[128,1024]{1,0:T(8,128)(2,1)S(1)}) custom-call(bf16[128,16384]{1,0:T(8,128)(2,1)} %hidden_ref.1, bf16[16384]{0:T(1024)(128)(2,1)S(1)} %copy-done, bf16[16384,512]{1,0:T(8,128)(2,1)} %w_ref.3, bf16[64,16384]{1,0:T(8,128)(2,1)} %bitcast.23, f32[128,128]{1,0:T(8,128)S(1)} %get-tuple-element.181.cosine_ref, ...), custom_call_target="tpu_custom_call" | custom-call | flops 2415919104 | bytes 23068672 | tf_op jit(solution)/shard_map/pallas_call | solution.py:120
  13.3 15.7 %all_to_all.10.refs_0_ = bf16[16,8,640]{2,1,0:T(8,128)(2,1)S(1)} all-to-all(bf16[16,8,640]{2,1,0:T(8,128)(2,1)S(1)} %get-tuple-element.82), channel_id=1, replica_groups=mesh['groups'=2,'tensor'=16] {'tensor'}, dimensions={0} | all-to-all | bytes 327680 | tf_op jit(solution)/shard_map/all_to_all | solution.py:284
  29.0 6.6 %shard_map.114 = bf16[16,8,512]{2,1,0:T(8,128)(2,1)S(1)} custom-call(s32[8]{0:T(128)S(1)} %copy-done.1, f32[128,128]{1,0:T(8,128)S(1)} %get-tuple-element.181.cosine_ref, f32[128,128]{1,0:T(8,128)S(1)} %get-tuple-element.180.sine_ref, bf16[8,1024,512]{2,1,0:T(8,128)(2,1)S(1)} %bitcast.22, bf16[8,1024,512]{2,1,0:T(8,128)(2,1)} %values_ref.1, ...), custom_call_target="tpu_custom_call" | custom-call | flops 268435456 | bytes 16777216 | tf_op jit(solution)/shard_map/pallas_call | solution.py:259
  35.6 10.5 %all_to_all.11.in_ref = bf16[16,8,512]{2,1,0:T(8,128)(2,1)S(1)} all-to-all(bf16[16,8,512]{2,1,0:T(8,128)(2,1)S(1)} %shard_map.114), channel_id=1, replica_groups=mesh['groups'=2,'tensor'=16] {'tensor'}, dimensions={0} | all-to-all | bytes 262144 | tf_op jit(solution)/shard_map/all_to_all | solution.py:284
  46.1 3.8 %shard_map.115 = (bf16[4,32,1024]{2,1,0:T(8,128)(2,1)S(1)}, bf16[4,32,1024]{2,1,0:T(8,128)(2,1)S(1)}, bf16[4,32,1024]{2,1,0:T(8,128)(2,1)S(1)}, bf16[4,32,1024]{...) custom-call(bf16[16,8,512]{2,1,0:T(8,128)(2,1)S(1)} %all_to_all.11.i, ...), custom_call_target="tpu_custom_call" | custom-call | flops 1073741824 | bytes 10485760 | tf_op jit(solution)/shard_map/pallas_call | solution.py:346
  50.0 0.1 collective-permute-start
  50.0 0.5 collective-permute-start.4
  50.5 0.1 collective-permute-start.5
  50.6 0.4 collective-permute-start.7
  51.0 0.5 collective-permute-done
  51.6 3.8 %shard_map.116 = (bf16[4,32,1024]{2,1,0:T(8,128)(2,1)S(1)}, bf16[4,32,1024]{2,1,0:T(8,128)(2,1)S(1)}, bf16[4,32,1024]{2,1,0:T(8,128)(2,1)S(1)}, bf16[4,32,1024]{...) custom-call(bf16[16,8,512]{2,1,0:T(8,128)(2,1)S(1)} %all_to_all.11.i, ...), custom_call_target="tpu_custom_call" | custom-call | flops 1073741824 | bytes 10485760 | tf_op jit(solution)/shard_map/pallas_call | solution.py:346
  55.5 0.2 collective-permute-start.3
  55.8 0.1 collective-permute-start.2
  55.9 0.4 collective-permute-start.1
  56.4 0.1 collective-permute-start.8
  56.5 2.0 %collective-permute-start.9 = (bf16[4,32,1024]{2,1,0:T(8,128)(2,1)S(1)}, bf16[4,32,1024]{2,1,0:T(8,128)(2,1)S(1)}, u32[]{:S(2)}, u32[]{:S(2)}) collective-permute-start(bf16[4,32,1024]{2,1,0:T(8,128)(2,1)S(1)} %add_convert_fusion.3), channel_id=1, source_target_pairs={{0,2},{1,3},{2,0},{3,1},{4,6},{5,7},{6,4},{7,5},{8,10},{9,11},{10,... | collective-permute-start | bytes 786440 | tf_op jit(solution)/shard_map/ppermute | solution.py:407
  58.6 0.1 collective-permute-start.13
  58.7 0.1 add_convert_fusion.5
  58.8 0.1 collective-permute-start.11
  59.0 6.0 %collective-permute-done.2 = bf16[4,32,1024]{2,1,0:T(8,128)(2,1)S(1)} collective-permute-done((bf16[4,32,1024]{2,1,0:T(8,128)(2,1)S(1)}, bf16[4,32,1024]{2,1,0:T(8,128)(2,1)S(1)}, u32[]{:S(2)}, u32[]{:S(2)}) %collective-permute-start.2) | collective-permute-done | bytes 262176 | tf_op jit(solution)/shard_map/ppermute | solution.py:407
  65.1 0.1 collective-permute-start.6
  65.2 4.8 %collective-permute-done.9 = bf16[4,32,1024]{2,1,0:T(8,128)(2,1)S(1)} collective-permute-done((bf16[4,32,1024]{2,1,0:T(8,128)(2,1)S(1)}, bf16[4,32,1024]{2,1,0:T(8,128)(2,1)S(1)}, u32[]{:S(2)}, u32[]{:S(2)}) %collective-permute-start.9) | collective-permute-done | bytes 262176 | tf_op jit(solution)/shard_map/ppermute | solution.py:407
  70.1 0.1 collective-permute-start.12
  70.2 0.4 collective-permute-start.14
  70.7 1.7 %collective-permute-start.10 = (bf16[1,32,1024]{2,1,0:T(8,128)(2,1)S(1)}, bf16[1,32,1024]{2,1,0:T(8,128)(2,1)S(1)}, u32[]{:S(2)}, u32[]{:S(2)}) collective-permute-start(bf16[1,32,1024]{2,1,0:T(8,128)(2,1)S(1)} %get-tuple-element.177), channel_id=1, source_target_pairs={{0,8},{1,9},{2,10},{3,11},{4,12},{5,13},{6,14},{7,15},{8,0},{9,1},... | collective-permute-start | bytes 196616 | tf_op jit(solution)/shard_map/ppermute | solution.py:407
  72.5 4.1 %collective-permute-done.12 = bf16[2,32,1024]{2,1,0:T(8,128)(2,1)S(1)} collective-permute-done((bf16[2,32,1024]{2,1,0:T(8,128)(2,1)S(1)}, bf16[2,32,1024]{2,1,0:T(8,128)(2,1)S(1)}, u32[]{:S(2)}, u32[]{:S(2)}) %collective-permute-start.12) | collective-permute-done | bytes 131104 | tf_op jit(solution)/shard_map/ppermute | solution.py:407
  76.6 0.1 collective-permute-start.16
  76.8 0.1 collective-permute-start.18
  76.9 3.0 %collective-permute-start.19 = (bf16[1,32,1024]{2,1,0:T(8,128)(2,1)S(1)}, bf16[1,32,1024]{2,1,0:T(8,128)(2,1)S(1)}, u32[]{:S(2)}, u32[]{:S(2)}) collective-permute-start(bf16[1,32,1024]{2,1,0:T(8,128)(2,1)S(1)} %bitcast.24), channel_id=1, source_target_pairs={{0,8},{1,9},{2,10},{3,11},{4,12},{5,13},{6,14},{7,15},{8,0},{9,1},... | collective-permute-start | bytes 196616 | tf_op jit(solution)/shard_map/ppermute | solution.py:407
  79.9 1.3 %collective-permute-start.15 = (bf16[2,32,1024]{2,1,0:T(8,128)(2,1)S(1)}, bf16[2,32,1024]{2,1,0:T(8,128)(2,1)S(1)}, u32[]{:S(2)}, u32[]{:S(2)}) collective-permute-start(bf16[2,32,1024]{2,1,0:T(8,128)(2,1)S(1)} %get-tuple-element.161), channel_id=1, source_target_pairs={{0,4},{1,5},{2,6},{3,7},{4,0},{5,1},{6,2},{7,3},{8,12},{9,13},{10,... | collective-permute-start | bytes 393224 | tf_op jit(solution)/shard_map/ppermute | solution.py:407
  81.2 2.5 %collective-permute-done.16 = bf16[1,32,1024]{2,1,0:T(8,128)(2,1)S(1)} collective-permute-done((bf16[1,32,1024]{2,1,0:T(8,128)(2,1)S(1)}, bf16[1,32,1024]{2,1,0:T(8,128)(2,1)S(1)}, u32[]{:S(2)}, u32[]{:S(2)}) %collective-permute-start.16) | collective-permute-done | bytes 65568 | tf_op jit(solution)/shard_map/ppermute | solution.py:407
  83.7 0.1 collective-permute-start.17
  83.8 1.3 %collective-permute-done.19 = bf16[1,32,1024]{2,1,0:T(8,128)(2,1)S(1)} collective-permute-done((bf16[1,32,1024]{2,1,0:T(8,128)(2,1)S(1)}, bf16[1,32,1024]{2,1,0:T(8,128)(2,1)S(1)}, u32[]{:S(2)}, u32[]{:S(2)}) %collective-permute-start.19) | collective-permute-done | bytes 65568 | tf_op jit(solution)/shard_map/ppermute | solution.py:407
  85.1 0.1 collective-permute-start.21
  85.2 1.7 %collective-permute-start.22 = (bf16[1,32,1024]{2,1,0:T(8,128)(2,1)S(1)}, bf16[1,32,1024]{2,1,0:T(8,128)(2,1)S(1)}, u32[]{:S(2)}, u32[]{:S(2)}) collective-permute-start(bf16[1,32,1024]{2,1,0:T(8,128)(2,1)S(1)} %get-tuple-element.170), channel_id=1, source_target_pairs={{0,8},{1,9},{2,10},{3,11},{4,12},{5,13},{6,14},{7,15},{8,0},{9,1},... | collective-permute-start | bytes 196616 | tf_op jit(solution)/shard_map/ppermute | solution.py:407
  86.9 2.1 %collective-permute-done.17 = bf16[1,32,1024]{2,1,0:T(8,128)(2,1)S(1)} collective-permute-done((bf16[1,32,1024]{2,1,0:T(8,128)(2,1)S(1)}, bf16[1,32,1024]{2,1,0:T(8,128)(2,1)S(1)}, u32[]{:S(2)}, u32[]{:S(2)}) %collective-permute-start.17) | collective-permute-done | bytes 65568 | tf_op jit(solution)/shard_map/ppermute | solution.py:407
  89.1 1.8 %collective-permute-start.24 = (bf16[2,32,1024]{2,1,0:T(8,128)(2,1)S(1)}, bf16[2,32,1024]{2,1,0:T(8,128)(2,1)S(1)}, u32[]{:S(2)}, u32[]{:S(2)}) collective-permute-start(bf16[2,32,1024]{2,1,0:T(8,128)(2,1)S(1)} %constant_dynamic-update-slice_fusion.2), channel_id=1, source_target_pairs={{0,2},{1,3},{2,0},{3,1},{4,6},{5,7},{6,4},{7,5},{8,10},{9,11},{10,... | collective-permute-start | bytes 393224 | tf_op jit(solution)/shard_map/ppermute | solution.py:407
  90.9 1.2 collective-permute-start.20
  92.1 1.9 %collective-permute-start.25 = (bf16[1,32,1024]{2,1,0:T(8,128)(2,1)S(1)}, bf16[1,32,1024]{2,1,0:T(8,128)(2,1)S(1)}, u32[]{:S(2)}, u32[]{:S(2)}) collective-permute-start(bf16[1,32,1024]{2,1,0:T(8,128)(2,1)S(1)} %bitcast.28), channel_id=1, source_target_pairs={{0,8},{1,9},{2,10},{3,11},{4,12},{5,13},{6,14},{7,15},{8,0},{9,1},... | collective-permute-start | bytes 196616 | tf_op jit(solution)/shard_map/ppermute | solution.py:407
  94.0 0.4 collective-permute-start.29
  94.4 2.0 %collective-permute-done.20 = bf16[1,32,1024]{2,1,0:T(8,128)(2,1)S(1)} collective-permute-done((bf16[1,32,1024]{2,1,0:T(8,128)(2,1)S(1)}, bf16[1,32,1024]{2,1,0:T(8,128)(2,1)S(1)}, u32[]{:S(2)}, u32[]{:S(2)}) %collective-permute-start.20) | collective-permute-done | bytes 65568 | tf_op jit(solution)/shard_map/ppermute | solution.py:407
  96.4 0.9 collective-permute-start.23
  97.3 0.1 collective-permute-done.25
  97.4 2.0 %collective-permute-start.27 = (bf16[2,32,1024]{2,1,0:T(8,128)(2,1)S(1)}, bf16[2,32,1024]{2,1,0:T(8,128)(2,1)S(1)}, u32[]{:S(2)}, u32[]{:S(2)}) collective-permute-start(bf16[2,32,1024]{2,1,0:T(8,128)(2,1)S(1)} %constant_dynamic-update-slice_fusion.6), channel_id=1, source_target_pairs={{0,4},{1,5},{2,6},{3,7},{4,0},{5,1},{6,2},{7,3},{8,12},{9,13},{10,... | collective-permute-start | bytes 393224 | tf_op jit(solution)/shard_map/ppermute | solution.py:407
  99.4 0.2 collective-permute-start.30
  99.6 2.4 %collective-permute-done.23 = bf16[1,32,1024]{2,1,0:T(8,128)(2,1)S(1)} collective-permute-done((bf16[1,32,1024]{2,1,0:T(8,128)(2,1)S(1)}, bf16[1,32,1024]{2,1,0:T(8,128)(2,1)S(1)}, u32[]{:S(2)}, u32[]{:S(2)}) %collective-permute-start.23) | collective-permute-done | bytes 65568 | tf_op jit(solution)/shard_map/ppermute | solution.py:407
  102.1 1.1 collective-permute-start.26
  103.2 0.2 collective-permute-done.27
  103.5 3.6 %collective-permute-done.26 = bf16[2,32,1024]{2,1,0:T(8,128)(2,1)S(1)} collective-permute-done((bf16[2,32,1024]{2,1,0:T(8,128)(2,1)S(1)}, bf16[2,32,1024]{2,1,0:T(8,128)(2,1)S(1)}, u32[]{:S(2)}, u32[]{:S(2)}) %collective-permute-start.26) | collective-permute-done | bytes 131104 | tf_op jit(solution)/shard_map/ppermute | solution.py:407
  107.2 0.1 collective-permute-start.33
  107.3 0.6 collective-permute-start.31
  107.9 1.1 collective-permute-start.32
  109.0 0.3 collective-permute-start.28
  109.2 1.6 %shard_map.117.refs_0_ = bf16[128,16384]{1,0:T(8,128)(2,1)} custom-call(bf16[8,32,1024]{2,1,0:T(8,128)(2,1)S(1)} %constant_dynamic-update-slice_fusion.16.own_ref, bf16[8,32,1024]{2,1,0:T(8,128)(2,1)S(1)} %collective-permute-done.33.other_ref, f32[16,1024]{1,0:T(8,128)S(1)} %reshape.42.gain_ref), custom_call_target="tpu_custom_call" | custom-call | flops 3145728 | bytes 2097152 | tf_op jit(solution)/shard_map/pallas_call | solution.py:392
  110.8 5.4 %collective-permute-done.32 = bf16[4,32,1024]{2,1,0:T(8,128)(2,1)S(1)} collective-permute-done((bf16[4,32,1024]{2,1,0:T(8,128)(2,1)S(1)}, bf16[4,32,1024]{2,1,0:T(8,128)(2,1)S(1)}, u32[]{:S(2)}, u32[]{:S(2)}) %collective-permute-start.32) | collective-permute-done | bytes 262176 | tf_op jit(solution)/shard_map/ppermute | solution.py:407
  116.2 0.1 collective-permute-start.35
  116.3 1.6 %shard_map.118.refs_0_ = bf16[128,16384]{1,0:T(8,128)(2,1)} custom-call(bf16[8,32,1024]{2,1,0:T(8,128)(2,1)S(1)} %constant_dynamic-update-slice_fusion.18.own_ref, bf16[8,32,1024]{2,1,0:T(8,128)(2,1)S(1)} %collective-permute-done.31.other_ref, f32[16,1024]{1,0:T(8,128)S(1)} %reshape.42.gain_ref, ...), custom_call_target="tpu_custom_call", output_to_operand_aliasing={{}: (3, {})} | custom-call | flops 3145728 | bytes 2097152 | tf_op jit(solution)/shard_map/pallas_call | solution.py:392
  117.9 0.5 collective-permute-start.34
  118.4 0.7 pad_maximum_fusion.2
  119.2 1.5 %shard_map.119.refs_0_ = bf16[128,16384]{1,0:T(8,128)(2,1)} custom-call(bf16[8,32,1024]{2,1,0:T(8,128)(2,1)S(1)} %constant_dynamic-update-slice_fusion.20.own_ref, bf16[8,32,1024]{2,1,0:T(8,128)(2,1)S(1)} %collective-permute-done.35.other_ref, f32[16,1024]{1,0:T(8,128)S(1)} %reshape.42.gain_ref, ...), custom_call_target="tpu_custom_call", output_to_operand_aliasing={{}: (3, {})} | custom-call | flops 3145728 | bytes 2097152 | tf_op jit(solution)/shard_map/pallas_call | solution.py:392
  120.7 1.5 %shard_map.120 = bf16[128,16384]{1,0:T(8,128)(2,1)} custom-call(bf16[8,32,1024]{2,1,0:T(8,128)(2,1)S(1)} %constant_dynamic-update-slice_fusion.22.own_ref, bf16[8,32,1024]{2,1,0:T(8,128)(2,1)S(1)} %collective-permute-done.34.other_ref, f32[16,1024]{1,0:T(8,128)S(1)} %reshape.42.gain_ref, ...), custom_call_target="tpu_custom_call", output_to_operand_aliasing={{}: (3, {})} | custom-call | flops 3145728 | bytes 2097152 | tf_op jit(solution)/shard_map/pallas_call | solution.py:392
  (82 shorter events, 1.5 us)
Async XLA Ops:
  1.6 27.3 %slice-start = ((s8[8388608]{0:T(1024)(128)(4,1)}), s8[4194304]{0:T(1024)(128)(4,1)S(1)}, s32[]{:S(2)}) async-start(s8[8388608]{0:T(1024)(128)(4,1)} %bitcast.21), calls=%async_computation.2 | async-start | bytes 8388608
  1.6 0.9 copy-start
  2.5 26.4 %slice-start.1 = ((s8[8388608]{0:T(1024)(128)(4,1)}), s8[4194304]{0:T(1024)(128)(4,1)S(1)}, s32[]{:S(2)}) async-start(s8[8388608]{0:T(1024)(128)(4,1)} %bitcast.21), calls=%async_computation.3 | async-start | bytes 8388608
  2.5 26.4 %copy-start.1 = (s32[8]{0:T(128)S(1)}, s32[8]{0:T(128)}, u32[]{:S(2)}) copy-start(s32[8]{0:T(128)} %lengths_ref.1) | copy-start | bytes 100
  50.0 1.6 %collective-permute-start = (bf16[4,32,1024]{2,1,0:T(8,128)(2,1)S(1)}, bf16[4,32,1024]{2,1,0:T(8,128)(2,1)S(1)}, u32[]{:S(2)}, u32[]{:S(2)}) collective-permute-start(bf16[4,32,1024]{2,1,0:T(8,128)(2,1)S(1)} %get-tuple-element.84), channel_id=1, source_target_pairs={{0,1},{1,0},{2,3},{3,2},{4,5},{5,4},{6,7},{7,6},{8,9},{9,8},{10,11... | collective-permute-start | bytes 786440 | tf_op jit(solution)/shard_map/ppermute | solution.py:407
  50.0 5.6 %collective-permute-start.4 = (bf16[4,32,1024]{2,1,0:T(8,128)(2,1)S(1)}, bf16[4,32,1024]{2,1,0:T(8,128)(2,1)S(1)}, u32[]{:S(2)}, u32[]{:S(2)}) collective-permute-start(bf16[4,32,1024]{2,1,0:T(8,128)(2,1)S(1)} %get-tuple-element.92), channel_id=1, source_target_pairs={{0,1},{1,0},{2,3},{3,2},{4,5},{5,4},{6,7},{7,6},{8,9},{9,8},{10,11... | collective-permute-start | bytes 786440 | tf_op jit(solution)/shard_map/ppermute | solution.py:407
  50.5 5.3 %collective-permute-start.5 = (bf16[4,32,1024]{2,1,0:T(8,128)(2,1)S(1)}, bf16[4,32,1024]{2,1,0:T(8,128)(2,1)S(1)}, u32[]{:S(2)}, u32[]{:S(2)}) collective-permute-start(bf16[4,32,1024]{2,1,0:T(8,128)(2,1)S(1)} %get-tuple-element.94), channel_id=1, source_target_pairs={{0,1},{1,0},{2,3},{3,2},{4,5},{5,4},{6,7},{7,6},{8,9},{9,8},{10,11... | collective-permute-start | bytes 786440 | tf_op jit(solution)/shard_map/ppermute | solution.py:407
  50.6 5.9 %collective-permute-start.7 = (bf16[4,32,1024]{2,1,0:T(8,128)(2,1)S(1)}, bf16[4,32,1024]{2,1,0:T(8,128)(2,1)S(1)}, u32[]{:S(2)}, u32[]{:S(2)}) collective-permute-start(bf16[4,32,1024]{2,1,0:T(8,128)(2,1)S(1)} %get-tuple-element.100), channel_id=1, source_target_pairs={{0,1},{1,0},{2,3},{3,2},{4,5},{5,4},{6,7},{7,6},{8,9},{9,8},{10,11... | collective-permute-start | bytes 786440 | tf_op jit(solution)/shard_map/ppermute | solution.py:407
  55.5 3.1 %collective-permute-start.3 = (bf16[4,32,1024]{2,1,0:T(8,128)(2,1)S(1)}, bf16[4,32,1024]{2,1,0:T(8,128)(2,1)S(1)}, u32[]{:S(2)}, u32[]{:S(2)}) collective-permute-start(bf16[4,32,1024]{2,1,0:T(8,128)(2,1)S(1)} %get-tuple-element.90), channel_id=1, source_target_pairs={{0,1},{1,0},{2,3},{3,2},{4,5},{5,4},{6,7},{7,6},{8,9},{9,8},{10,11... | collective-permute-start | bytes 786440 | tf_op jit(solution)/shard_map/ppermute | solution.py:407
  55.8 9.2 %collective-permute-start.2 = (bf16[4,32,1024]{2,1,0:T(8,128)(2,1)S(1)}, bf16[4,32,1024]{2,1,0:T(8,128)(2,1)S(1)}, u32[]{:S(2)}, u32[]{:S(2)}) collective-permute-start(bf16[4,32,1024]{2,1,0:T(8,128)(2,1)S(1)} %add_convert_fusion.7), channel_id=1, source_target_pairs={{0,2},{1,3},{2,0},{3,1},{4,6},{5,7},{6,4},{7,5},{8,10},{9,11},{10,... | collective-permute-start | bytes 786440 | tf_op jit(solution)/shard_map/ppermute | solution.py:407
  55.9 2.9 %collective-permute-start.1 = (bf16[4,32,1024]{2,1,0:T(8,128)(2,1)S(1)}, bf16[4,32,1024]{2,1,0:T(8,128)(2,1)S(1)}, u32[]{:S(2)}, u32[]{:S(2)}) collective-permute-start(bf16[4,32,1024]{2,1,0:T(8,128)(2,1)S(1)} %get-tuple-element.87), channel_id=1, source_target_pairs={{0,1},{1,0},{2,3},{3,2},{4,5},{5,4},{6,7},{7,6},{8,9},{9,8},{10,11... | collective-permute-start | bytes 786440 | tf_op jit(solution)/shard_map/ppermute | solution.py:407
  56.4 8.8 %collective-permute-start.8 = (bf16[4,32,1024]{2,1,0:T(8,128)(2,1)S(1)}, bf16[4,32,1024]{2,1,0:T(8,128)(2,1)S(1)}, u32[]{:S(2)}, u32[]{:S(2)}) collective-permute-start(bf16[4,32,1024]{2,1,0:T(8,128)(2,1)S(1)} %get-tuple-element.102), channel_id=1, source_target_pairs={{0,1},{1,0},{2,3},{3,2},{4,5},{5,4},{6,7},{7,6},{8,9},{9,8},{10,11... | collective-permute-start | bytes 786440 | tf_op jit(solution)/shard_map/ppermute | solution.py:407
  56.5 13.5 %collective-permute-start.9 = (bf16[4,32,1024]{2,1,0:T(8,128)(2,1)S(1)}, bf16[4,32,1024]{2,1,0:T(8,128)(2,1)S(1)}, u32[]{:S(2)}, u32[]{:S(2)}) collective-permute-start(bf16[4,32,1024]{2,1,0:T(8,128)(2,1)S(1)} %add_convert_fusion.3), channel_id=1, source_target_pairs={{0,2},{1,3},{2,0},{3,1},{4,6},{5,7},{6,4},{7,5},{8,10},{9,11},{10,... | collective-permute-start | bytes 786440 | tf_op jit(solution)/shard_map/ppermute | solution.py:407
  58.6 12.0 %collective-permute-start.13 = (bf16[4,32,1024]{2,1,0:T(8,128)(2,1)S(1)}, bf16[4,32,1024]{2,1,0:T(8,128)(2,1)S(1)}, u32[]{:S(2)}, u32[]{:S(2)}) collective-permute-start(bf16[4,32,1024]{2,1,0:T(8,128)(2,1)S(1)} %get-tuple-element.115), channel_id=1, source_target_pairs={{0,1},{1,0},{2,3},{3,2},{4,5},{5,4},{6,7},{7,6},{8,9},{9,8},{10,11... | collective-permute-start | bytes 786440 | tf_op jit(solution)/shard_map/ppermute | solution.py:407
  58.8 17.8 %collective-permute-start.11 = (bf16[4,32,1024]{2,1,0:T(8,128)(2,1)S(1)}, bf16[4,32,1024]{2,1,0:T(8,128)(2,1)S(1)}, u32[]{:S(2)}, u32[]{:S(2)}) collective-permute-start(bf16[4,32,1024]{2,1,0:T(8,128)(2,1)S(1)} %pad_maximum_fusion), channel_id=1, source_target_pairs={{0,4},{1,5},{2,6},{3,7},{4,0},{5,1},{6,2},{7,3},{8,12},{9,13},{10,... | collective-permute-start | bytes 786440 | tf_op jit(solution)/shard_map/ppermute | solution.py:407
  65.1 5.6 %collective-permute-start.6 = (bf16[2,32,1024]{2,1,0:T(8,128)(2,1)S(1)}, bf16[2,32,1024]{2,1,0:T(8,128)(2,1)S(1)}, u32[]{:S(2)}, u32[]{:S(2)}) collective-permute-start(bf16[2,32,1024]{2,1,0:T(8,128)(2,1)S(1)} %get-tuple-element.165), channel_id=1, source_target_pairs={{0,4},{1,5},{2,6},{3,7},{4,0},{5,1},{6,2},{7,3},{8,12},{9,13},{10,... | collective-permute-start | bytes 393224 | tf_op jit(solution)/shard_map/ppermute | solution.py:407
  70.1 6.4 %collective-permute-start.12 = (bf16[2,32,1024]{2,1,0:T(8,128)(2,1)S(1)}, bf16[2,32,1024]{2,1,0:T(8,128)(2,1)S(1)}, u32[]{:S(2)}, u32[]{:S(2)}) collective-permute-start(bf16[2,32,1024]{2,1,0:T(8,128)(2,1)S(1)} %get-tuple-element.166), channel_id=1, source_target_pairs={{0,4},{1,5},{2,6},{3,7},{4,0},{5,1},{6,2},{7,3},{8,12},{9,13},{10,... | collective-permute-start | bytes 393224 | tf_op jit(solution)/shard_map/ppermute | solution.py:407
  70.2 9.7 %collective-permute-start.14 = (bf16[4,32,1024]{2,1,0:T(8,128)(2,1)S(1)}, bf16[4,32,1024]{2,1,0:T(8,128)(2,1)S(1)}, u32[]{:S(2)}, u32[]{:S(2)}) collective-permute-start(bf16[4,32,1024]{2,1,0:T(8,128)(2,1)S(1)} %add_convert_fusion.2), channel_id=1, source_target_pairs={{0,2},{1,3},{2,0},{3,1},{4,6},{5,7},{6,4},{7,5},{8,10},{9,11},{10,... | collective-permute-start | bytes 786440 | tf_op jit(solution)/shard_map/ppermute | solution.py:407
  70.7 6.1 %collective-permute-start.10 = (bf16[1,32,1024]{2,1,0:T(8,128)(2,1)S(1)}, bf16[1,32,1024]{2,1,0:T(8,128)(2,1)S(1)}, u32[]{:S(2)}, u32[]{:S(2)}) collective-permute-start(bf16[1,32,1024]{2,1,0:T(8,128)(2,1)S(1)} %get-tuple-element.177), channel_id=1, source_target_pairs={{0,8},{1,9},{2,10},{3,11},{4,12},{5,13},{6,14},{7,15},{8,0},{9,1},... | collective-permute-start | bytes 196616 | tf_op jit(solution)/shard_map/ppermute | solution.py:407
  76.6 32.6 %copy-start.2 = (bf16[16384]{0:T(1024)(128)(2,1)S(1)}, bf16[16384]{0:T(1024)(128)(2,1)}, u32[]{:S(2)}) copy-start(bf16[16384]{0:T(1024)(128)(2,1)} %param.17) | copy-start | bytes 98308
  76.6 7.1 %collective-permute-start.16 = (bf16[1,32,1024]{2,1,0:T(8,128)(2,1)S(1)}, bf16[1,32,1024]{2,1,0:T(8,128)(2,1)S(1)}, u32[]{:S(2)}, u32[]{:S(2)}) collective-permute-start(bf16[1,32,1024]{2,1,0:T(8,128)(2,1)S(1)} %get-tuple-element.178), channel_id=1, source_target_pairs={{0,8},{1,9},{2,10},{3,11},{4,12},{5,13},{6,14},{7,15},{8,0},{9,1},... | collective-permute-start | bytes 196616 | tf_op jit(solution)/shard_map/ppermute | solution.py:407
  76.8 8.4 %collective-permute-start.18 = (bf16[2,32,1024]{2,1,0:T(8,128)(2,1)S(1)}, bf16[2,32,1024]{2,1,0:T(8,128)(2,1)S(1)}, u32[]{:S(2)}, u32[]{:S(2)}) collective-permute-start(bf16[2,32,1024]{2,1,0:T(8,128)(2,1)S(1)} %get-tuple-element.163), channel_id=1, source_target_pairs={{0,2},{1,3},{2,0},{3,1},{4,6},{5,7},{6,4},{7,5},{8,10},{9,11},{10,... | collective-permute-start | bytes 393224 | tf_op jit(solution)/shard_map/ppermute | solution.py:407
  76.9 8.2 %collective-permute-start.19 = (bf16[1,32,1024]{2,1,0:T(8,128)(2,1)S(1)}, bf16[1,32,1024]{2,1,0:T(8,128)(2,1)S(1)}, u32[]{:S(2)}, u32[]{:S(2)}) collective-permute-start(bf16[1,32,1024]{2,1,0:T(8,128)(2,1)S(1)} %bitcast.24), channel_id=1, source_target_pairs={{0,8},{1,9},{2,10},{3,11},{4,12},{5,13},{6,14},{7,15},{8,0},{9,1},... | collective-permute-start | bytes 196616 | tf_op jit(solution)/shard_map/ppermute | solution.py:407
  79.9 10.9 %collective-permute-start.15 = (bf16[2,32,1024]{2,1,0:T(8,128)(2,1)S(1)}, bf16[2,32,1024]{2,1,0:T(8,128)(2,1)S(1)}, u32[]{:S(2)}, u32[]{:S(2)}) collective-permute-start(bf16[2,32,1024]{2,1,0:T(8,128)(2,1)S(1)} %get-tuple-element.161), channel_id=1, source_target_pairs={{0,4},{1,5},{2,6},{3,7},{4,0},{5,1},{6,2},{7,3},{8,12},{9,13},{10,... | collective-permute-start | bytes 393224 | tf_op jit(solution)/shard_map/ppermute | solution.py:407
  83.7 5.3 %collective-permute-start.17 = (bf16[1,32,1024]{2,1,0:T(8,128)(2,1)S(1)}, bf16[1,32,1024]{2,1,0:T(8,128)(2,1)S(1)}, u32[]{:S(2)}, u32[]{:S(2)}) collective-permute-start(bf16[1,32,1024]{2,1,0:T(8,128)(2,1)S(1)} %bitcast.26), channel_id=1, source_target_pairs={{0,8},{1,9},{2,10},{3,11},{4,12},{5,13},{6,14},{7,15},{8,0},{9,1},... | collective-permute-start | bytes 196616 | tf_op jit(solution)/shard_map/ppermute | solution.py:407
  85.1 8.8 %collective-permute-start.21 = (bf16[2,32,1024]{2,1,0:T(8,128)(2,1)S(1)}, bf16[2,32,1024]{2,1,0:T(8,128)(2,1)S(1)}, u32[]{:S(2)}, u32[]{:S(2)}) collective-permute-start(bf16[2,32,1024]{2,1,0:T(8,128)(2,1)S(1)} %constant_dynamic-update-slice_fusion), channel_id=1, source_target_pairs={{0,4},{1,5},{2,6},{3,7},{4,0},{5,1},{6,2},{7,3},{8,12},{9,13},{10,... | collective-permute-start | bytes 393224 | tf_op jit(solution)/shard_map/ppermute | solution.py:407
  85.2 6.8 %collective-permute-start.22 = (bf16[1,32,1024]{2,1,0:T(8,128)(2,1)S(1)}, bf16[1,32,1024]{2,1,0:T(8,128)(2,1)S(1)}, u32[]{:S(2)}, u32[]{:S(2)}) collective-permute-start(bf16[1,32,1024]{2,1,0:T(8,128)(2,1)S(1)} %get-tuple-element.170), channel_id=1, source_target_pairs={{0,8},{1,9},{2,10},{3,11},{4,12},{5,13},{6,14},{7,15},{8,0},{9,1},... | collective-permute-start | bytes 196616 | tf_op jit(solution)/shard_map/ppermute | solution.py:407
  89.1 10.3 %collective-permute-start.24 = (bf16[2,32,1024]{2,1,0:T(8,128)(2,1)S(1)}, bf16[2,32,1024]{2,1,0:T(8,128)(2,1)S(1)}, u32[]{:S(2)}, u32[]{:S(2)}) collective-permute-start(bf16[2,32,1024]{2,1,0:T(8,128)(2,1)S(1)} %constant_dynamic-update-slice_fusion.2), channel_id=1, source_target_pairs={{0,2},{1,3},{2,0},{3,1},{4,6},{5,7},{6,4},{7,5},{8,10},{9,11},{10,... | collective-permute-start | bytes 393224 | tf_op jit(solution)/shard_map/ppermute | solution.py:407
  90.9 5.5 %collective-permute-start.20 = (bf16[1,32,1024]{2,1,0:T(8,128)(2,1)S(1)}, bf16[1,32,1024]{2,1,0:T(8,128)(2,1)S(1)}, u32[]{:S(2)}, u32[]{:S(2)}) collective-permute-start(bf16[1,32,1024]{2,1,0:T(8,128)(2,1)S(1)} %get-tuple-element.169), channel_id=1, source_target_pairs={{0,8},{1,9},{2,10},{3,11},{4,12},{5,13},{6,14},{7,15},{8,0},{9,1},... | collective-permute-start | bytes 196616 | tf_op jit(solution)/shard_map/ppermute | solution.py:407
  92.1 5.3 %collective-permute-start.25 = (bf16[1,32,1024]{2,1,0:T(8,128)(2,1)S(1)}, bf16[1,32,1024]{2,1,0:T(8,128)(2,1)S(1)}, u32[]{:S(2)}, u32[]{:S(2)}) collective-permute-start(bf16[1,32,1024]{2,1,0:T(8,128)(2,1)S(1)} %bitcast.28), channel_id=1, source_target_pairs={{0,8},{1,9},{2,10},{3,11},{4,12},{5,13},{6,14},{7,15},{8,0},{9,1},... | collective-permute-start | bytes 196616 | tf_op jit(solution)/shard_map/ppermute | solution.py:407
  94.0 13.3 %collective-permute-start.29 = (bf16[4,32,1024]{2,1,0:T(8,128)(2,1)S(1)}, bf16[4,32,1024]{2,1,0:T(8,128)(2,1)S(1)}, u32[]{:S(2)}, u32[]{:S(2)}) collective-permute-start(bf16[4,32,1024]{2,1,0:T(8,128)(2,1)S(1)} %constant_dynamic-update-slice_fusion.4), channel_id=1, source_target_pairs={{0,2},{1,3},{2,0},{3,1},{4,6},{5,7},{6,4},{7,5},{8,10},{9,11},{10,... | collective-permute-start | bytes 786440 | tf_op jit(solution)/shard_map/ppermute | solution.py:407
  96.4 5.6 %collective-permute-start.23 = (bf16[1,32,1024]{2,1,0:T(8,128)(2,1)S(1)}, bf16[1,32,1024]{2,1,0:T(8,128)(2,1)S(1)}, u32[]{:S(2)}, u32[]{:S(2)}) collective-permute-start(bf16[1,32,1024]{2,1,0:T(8,128)(2,1)S(1)} %bitcast.30), channel_id=1, source_target_pairs={{0,8},{1,9},{2,10},{3,11},{4,12},{5,13},{6,14},{7,15},{8,0},{9,1},... | collective-permute-start | bytes 196616 | tf_op jit(solution)/shard_map/ppermute | solution.py:407
  97.4 6.0 %collective-permute-start.27 = (bf16[2,32,1024]{2,1,0:T(8,128)(2,1)S(1)}, bf16[2,32,1024]{2,1,0:T(8,128)(2,1)S(1)}, u32[]{:S(2)}, u32[]{:S(2)}) collective-permute-start(bf16[2,32,1024]{2,1,0:T(8,128)(2,1)S(1)} %constant_dynamic-update-slice_fusion.6), channel_id=1, source_target_pairs={{0,4},{1,5},{2,6},{3,7},{4,0},{5,1},{6,2},{7,3},{8,12},{9,13},{10,... | collective-permute-start | bytes 393224 | tf_op jit(solution)/shard_map/ppermute | solution.py:407
  99.4 7.7 %collective-permute-start.30 = (bf16[4,32,1024]{2,1,0:T(8,128)(2,1)S(1)}, bf16[4,32,1024]{2,1,0:T(8,128)(2,1)S(1)}, u32[]{:S(2)}, u32[]{:S(2)}) collective-permute-start(bf16[4,32,1024]{2,1,0:T(8,128)(2,1)S(1)} %constant_dynamic-update-slice_fusion.8), channel_id=1, source_target_pairs={{0,4},{1,5},{2,6},{3,7},{4,0},{5,1},{6,2},{7,3},{8,12},{9,13},{10,... | collective-permute-start | bytes 786440 | tf_op jit(solution)/shard_map/ppermute | solution.py:407
  102.1 5.0 %collective-permute-start.26 = (bf16[2,32,1024]{2,1,0:T(8,128)(2,1)S(1)}, bf16[2,32,1024]{2,1,0:T(8,128)(2,1)S(1)}, u32[]{:S(2)}, u32[]{:S(2)}) collective-permute-start(bf16[2,32,1024]{2,1,0:T(8,128)(2,1)S(1)} %constant_dynamic-update-slice_fusion.10), channel_id=1, source_target_pairs={{0,2},{1,3},{2,0},{3,1},{4,6},{5,7},{6,4},{7,5},{8,10},{9,11},{10,... | collective-permute-start | bytes 393224 | tf_op jit(solution)/shard_map/ppermute | solution.py:407
  107.2 2.0 %collective-permute-start.33 = (bf16[8,32,1024]{2,1,0:T(8,128)(2,1)S(1)}, bf16[8,32,1024]{2,1,0:T(8,128)(2,1)S(1)}, u32[]{:S(2)}, u32[]{:S(2)}) collective-permute-start(bf16[8,32,1024]{2,1,0:T(8,128)(2,1)S(1)} %constant_dynamic-update-slice_fusion.16.own_ref), channel_id=1, source_target_pairs={{0,1},{1,0},{2,3},{3,2},{4,5},{5,4},{6,7},{7,6},{8,9},{9,8},{10,11... | collective-permute-start | bytes 1572872 | tf_op jit(solution)/shard_map/ppermute | solution.py:407
  107.3 9.0 %collective-permute-start.31 = (bf16[8,32,1024]{2,1,0:T(8,128)(2,1)S(1)}, bf16[8,32,1024]{2,1,0:T(8,128)(2,1)S(1)}, u32[]{:S(2)}, u32[]{:S(2)}) collective-permute-start(bf16[8,32,1024]{2,1,0:T(8,128)(2,1)S(1)} %constant_dynamic-update-slice_fusion.18.own_ref), channel_id=1, source_target_pairs={{0,1},{1,0},{2,3},{3,2},{4,5},{5,4},{6,7},{7,6},{8,9},{9,8},{10,11... | collective-permute-start | bytes 1572872 | tf_op jit(solution)/shard_map/ppermute | solution.py:407
  107.9 8.3 %collective-permute-start.32 = (bf16[4,32,1024]{2,1,0:T(8,128)(2,1)S(1)}, bf16[4,32,1024]{2,1,0:T(8,128)(2,1)S(1)}, u32[]{:S(2)}, u32[]{:S(2)}) collective-permute-start(bf16[4,32,1024]{2,1,0:T(8,128)(2,1)S(1)} %constant_dynamic-update-slice_fusion.12), channel_id=1, source_target_pairs={{0,2},{1,3},{2,0},{3,1},{4,6},{5,7},{6,4},{7,5},{8,10},{9,11},{10,... | collective-permute-start | bytes 786440 | tf_op jit(solution)/shard_map/ppermute | solution.py:407
  109.0 8.9 %collective-permute-start.28 = (bf16[4,32,1024]{2,1,0:T(8,128)(2,1)S(1)}, bf16[4,32,1024]{2,1,0:T(8,128)(2,1)S(1)}, u32[]{:S(2)}, u32[]{:S(2)}) collective-permute-start(bf16[4,32,1024]{2,1,0:T(8,128)(2,1)S(1)} %constant_dynamic-update-slice_fusion.14), channel_id=1, source_target_pairs={{0,4},{1,5},{2,6},{3,7},{4,0},{5,1},{6,2},{7,3},{8,12},{9,13},{10,... | collective-permute-start | bytes 786440 | tf_op jit(solution)/shard_map/ppermute | solution.py:407
  116.2 2.9 %collective-permute-start.35 = (bf16[8,32,1024]{2,1,0:T(8,128)(2,1)S(1)}, bf16[8,32,1024]{2,1,0:T(8,128)(2,1)S(1)}, u32[]{:S(2)}, u32[]{:S(2)}) collective-permute-start(bf16[8,32,1024]{2,1,0:T(8,128)(2,1)S(1)} %constant_dynamic-update-slice_fusion.20.own_ref), channel_id=1, source_target_pairs={{0,1},{1,0},{2,3},{3,2},{4,5},{5,4},{6,7},{7,6},{8,9},{9,8},{10,11... | collective-permute-start | bytes 1572872 | tf_op jit(solution)/shard_map/ppermute | solution.py:407
  117.9 2.8 %collective-permute-start.34 = (bf16[8,32,1024]{2,1,0:T(8,128)(2,1)S(1)}, bf16[8,32,1024]{2,1,0:T(8,128)(2,1)S(1)}, u32[]{:S(2)}, u32[]{:S(2)}) collective-permute-start(bf16[8,32,1024]{2,1,0:T(8,128)(2,1)S(1)} %constant_dynamic-update-slice_fusion.22.own_ref), channel_id=1, source_target_pairs={{0,1},{1,0},{2,3},{3,2},{4,5},{5,4},{6,7},{7,6},{8,9},{9,8},{10,11... | collective-permute-start | bytes 1572872 | tf_op jit(solution)/shard_map/ppermute | solution.py:407

commit v10 on v8

--- a/solution.py
+++ b/solution.py
@@ -365,12 +365,13 @@
 
 
 def finish_kernel(offsets, gain_ref, *refs):
-    out_ref = refs[-1]
+    out_ref, own_ref = refs[-2:]
     me = lax.axis_index("tensor")
     half, rows, width = refs[0].shape
 
     def norm(k, order):
         parts = refs[2 * k : 2 * k + 2]
+        own_ref[...] = parts[0][0]
         total = jnp.zeros((rows, width), jnp.float32)
         for ref in parts:
             for spot in range(half):
@@ -392,18 +393,23 @@
 def finish(parts, gain, offsets, which, groups, earlier):
     half, rows, width = parts[0].shape
     columns, count = 2 * half * width, len(offsets)
-    operands = [gain, *parts] + ([] if earlier is None else [earlier])
+    operands = [gain, *parts, *earlier]
     specs = [pl.BlockSpec(memory_space=pltpu.VMEM)] * (1 + len(parts))
-    if earlier is not None:
-        specs.append(pl.BlockSpec(memory_space=pl.ANY))
+    specs += [pl.BlockSpec(memory_space=pl.ANY)] * len(earlier)
     return pl.pallas_call(
         functools.partial(finish_kernel, offsets),
         grid=(count,),
-        out_shape=jax.ShapeDtypeStruct((rows * count * groups, columns), jnp.bfloat16),
+        out_shape=tuple(
+            jax.ShapeDtypeStruct((rows * count * groups, size), jnp.bfloat16)
+            for size in (columns, width)
+        ),
         in_specs=specs,
-        out_specs=pl.BlockSpec((rows, columns), lambda i: (which * count + i, 0)),
-        input_output_aliases={} if earlier is None else {len(operands) - 1: 0},
-        compiler_params=pltpu.CompilerParams(vmem_limit_bytes=24 * 1024 * 1024),
+        out_specs=tuple(
+            pl.BlockSpec((rows, size), lambda i: (which * count + i, 0))
+            for size in (columns, width)
+        ),
+        input_output_aliases={1 + len(parts) + k: k for k in range(len(earlier))},
+        compiler_params=pltpu.CompilerParams(vmem_limit_bytes=12 * 1024 * 1024),
         cost_estimate=pl.CostEstimate(
             flops=6 * count * rows * columns,
             bytes_accessed=4 * count * rows * columns,
@@ -468,10 +474,9 @@
             half = far[k].shape[0] // 2
             held.append(jnp.concatenate([near[k][:half], far[k][:half]], axis=0))
             leaving.append(jnp.concatenate([near[k][half:], far[k][half:]], axis=0))
-    streams = [None] * sets
     offsets = [[0] for _ in range(sets)]
     steps = [0] * sets
-    last = normed = None
+    last, results = None, ()
     arrivals = [None] * sets
     for k in timetable(count):
         scatter, gather = orders[k]
@@ -492,20 +497,21 @@
         if step == len(scatter):
             own_rows = mine[k * set_rows : (k + 1) * set_rows].astype(jnp.float32)
             total = held[k][0].astype(jnp.float32) + arrivals[k][0].astype(jnp.float32)
-            streams[k] = (own_rows + total).astype(jnp.bfloat16)
-            last = held[k] = streams[k][None]
+            last = held[k] = (own_rows + total).astype(jnp.bfloat16)[None]
         elif step <= len(scatter) + len(gather):
             last = held[k] = jnp.concatenate([held[k], arrivals[k]], axis=0)
         else:
             pair = [k - 1, k]
             parts = [block for m in pair for block in (held[m], arrivals[m])]
             lists = [offsets[m] for m in pair]
-            last = normed = finish(parts, gain, lists, k // 2, sets // 2, normed)
+            results = finish(parts, gain, lists, k // 2, sets // 2, results)
+            last = results[0]
             continue
         bit = (gather + [0])[step - len(scatter)]
         arrivals[k] = swap(held[k], bit, count)
         offsets[k] = offsets[k] + [offset ^ (1 << bit) for offset in offsets[k]]
-    return (jnp.concatenate(streams, axis=0), normed)
+    normed, stream = results
+    return (stream, normed)
 
 
 def solution(mesh):

time: 118 us -> 117 us (level)
  transfers between devices with their start and end apart: 36 -> 36, of which waited for: 19 -> 19; matrix products, arithmetic and copies ran while one was open for 2% -> 1% of each run, Pallas kernels for 5% -> 6%
where the time goes in v10:
time: 117 us
  waiting for transfers between devices  34.9 us (30%)
  Pallas kernels  30.1 us (26%)
  blocking collectives  26.2 us (22%)
  starting transfers between devices  21.7 us (19%)
  other arithmetic  2.08 us (2%)
    ppermute x36, waiting for transfers between devices, swap(): lax.ppermute(values, 'tensor', [(i, i ^ 1 << bit) for i in range(count)])  34.9 us
    all_to_all x2, blocking collectives, exchange(): lax.all_to_all(blocks, 'tensor', split_axis=0, concat_axis=0, tiled=True)  26.2 us
    ppermute x36, starting transfers between devices, swap(): lax.ppermute(values, 'tensor', [(i, i ^ 1 << bit) for i in range(count)])  21.7 us
    pallas_call x1, Pallas kernels, project_in(): pl.pallas_call(functools.partial(input_kernel, count), out_shape=(jax.Sha...  10.3 us
    pallas_call x2, Pallas kernels, project(): pl.pallas_call(functools.partial(project_kernel, count, side), out_shape=...  7.67 us
    pallas_call x1, Pallas kernels, attend(): pl.pallas_call(functools.partial(attend_kernel, count), out_shape=jax.Sha...  6.62 us
    pallas_call x2, Pallas kernels, finish(): pl.pallas_call(functools.partial(finish_kernel, offsets), grid=(count,),...  5.44 us
  transfers between devices with their start and end apart: 36, of which 19 were waited for; matrix products, arithmetic and copies ran while one was open for 1% of the time, Pallas kernels for 6%

profile of v10, /device:TPU:0, one launch (start us, length us, event | category | flops | bytes accessed | tf_op | source)
XLA Modules:
  0.0 117.0 jit_solution(8699891511584517456)
XLA Ops:
  0.6 0.7 convert_element_type.283
  1.3 0.3 fusion.4
  1.6 0.7 copy-done.1
  2.4 10.3 %shard_map.113 = (bf16[16,8,640]{2,1,0:T(8,128)(2,1)S(1)}, bf16[128,1024]{1,0:T(8,128)(2,1)S(1)}) custom-call(bf16[128,16384]{1,0:T(8,128)(2,1)} %hidden_ref.1, bf16[16384]{0:T(1024)(128)(2,1)S(1)} %copy-done.1, bf16[16384,512]{1,0:T(8,128)(2,1)} %w_ref.3, bf16[64,16384]{1,0:T(8,128)(2,1)} %bitcast.33, f32[128,128]{1,0:T(8,128)S(1)} %get-tuple-element.181.cosine_ref, ...), custom_call_target="tpu_custom_call" | custom-call | flops 2415919104 | bytes 23068672 | tf_op jit(solution)/shard_map/pallas_call | solution.py:120
  12.7 15.7 %all_to_all.10.refs_0_ = bf16[16,8,640]{2,1,0:T(8,128)(2,1)S(1)} all-to-all(bf16[16,8,640]{2,1,0:T(8,128)(2,1)S(1)} %get-tuple-element.82), channel_id=1, replica_groups=mesh['groups'=2,'tensor'=16] {'tensor'}, dimensions={0} | all-to-all | bytes 327680 | tf_op jit(solution)/shard_map/all_to_all | solution.py:284
  28.4 6.6 %shard_map.114 = bf16[16,8,512]{2,1,0:T(8,128)(2,1)S(1)} custom-call(s32[8]{0:T(128)S(1)} %copy-done.2, f32[128,128]{1,0:T(8,128)S(1)} %get-tuple-element.181.cosine_ref, f32[128,128]{1,0:T(8,128)S(1)} %get-tuple-element.180.sine_ref, bf16[8,1024,512]{2,1,0:T(8,128)(2,1)S(1)} %copy-done, bf16[8,1024,512]{2,1,0:T(8,128)(2,1)} %values_ref.1, ...), custom_call_target="tpu_custom_call" | custom-call | flops 268435456 | bytes 16777216 | tf_op jit(solution)/shard_map/pallas_call | solution.py:259
  35.0 10.5 %all_to_all.11.in_ref = bf16[16,8,512]{2,1,0:T(8,128)(2,1)S(1)} all-to-all(bf16[16,8,512]{2,1,0:T(8,128)(2,1)S(1)} %shard_map.114), channel_id=1, replica_groups=mesh['groups'=2,'tensor'=16] {'tensor'}, dimensions={0} | all-to-all | bytes 262144 | tf_op jit(solution)/shard_map/all_to_all | solution.py:284
  45.5 3.8 %shard_map.115 = (bf16[4,32,1024]{2,1,0:T(8,128)(2,1)S(1)}, bf16[4,32,1024]{2,1,0:T(8,128)(2,1)S(1)}, bf16[4,32,1024]{2,1,0:T(8,128)(2,1)S(1)}, bf16[4,32,1024]{...) custom-call(bf16[16,8,512]{2,1,0:T(8,128)(2,1)S(1)} %all_to_all.11.i, ...), custom_call_target="tpu_custom_call" | custom-call | flops 1073741824 | bytes 10485760 | tf_op jit(solution)/shard_map/pallas_call | solution.py:347
  49.4 0.1 collective-permute-start
  49.4 0.5 collective-permute-start.4
  49.9 0.1 collective-permute-start.5
  50.0 0.4 collective-permute-start.7
  50.5 0.5 collective-permute-done
  51.0 0.1 collective-permute-start.2
  51.1 3.8 %shard_map.116 = (bf16[4,32,1024]{2,1,0:T(8,128)(2,1)S(1)}, bf16[4,32,1024]{2,1,0:T(8,128)(2,1)S(1)}, bf16[4,32,1024]{2,1,0:T(8,128)(2,1)S(1)}, bf16[4,32,1024]{...) custom-call(bf16[16,8,512]{2,1,0:T(8,128)(2,1)S(1)} %all_to_all.11.i, ...), custom_call_target="tpu_custom_call" | custom-call | flops 1073741824 | bytes 10485760 | tf_op jit(solution)/shard_map/pallas_call | solution.py:347
  55.0 0.2 collective-permute-start.3
  55.4 2.0 %collective-permute-start.9 = (bf16[4,32,1024]{2,1,0:T(8,128)(2,1)S(1)}, bf16[4,32,1024]{2,1,0:T(8,128)(2,1)S(1)}, u32[]{:S(2)}, u32[]{:S(2)}) collective-permute-start(bf16[4,32,1024]{2,1,0:T(8,128)(2,1)S(1)} %add_convert_fusion.3), channel_id=1, source_target_pairs={{0,2},{1,3},{2,0},{3,1},{4,6},{5,7},{6,4},{7,5},{8,10},{9,11},{10,... | collective-permute-start | bytes 786440 | tf_op jit(solution)/shard_map/ppermute | solution.py:422
  57.3 0.2 collective-permute-start.1
  57.5 0.3 collective-permute-start.8
  57.9 0.3 collective-permute-start.15
  58.3 0.5 collective-permute-done.1
  58.9 1.3 %collective-permute-done.2 = bf16[4,32,1024]{2,1,0:T(8,128)(2,1)S(1)} collective-permute-done((bf16[4,32,1024]{2,1,0:T(8,128)(2,1)S(1)}, bf16[4,32,1024]{2,1,0:T(8,128)(2,1)S(1)}, u32[]{:S(2)}, u32[]{:S(2)}) %collective-permute-start.2) | collective-permute-done | bytes 262176 | tf_op jit(solution)/shard_map/ppermute | solution.py:422
  60.3 0.8 collective-permute-start.6
  61.2 3.9 %collective-permute-done.9 = bf16[4,32,1024]{2,1,0:T(8,128)(2,1)S(1)} collective-permute-done((bf16[4,32,1024]{2,1,0:T(8,128)(2,1)S(1)}, bf16[4,32,1024]{2,1,0:T(8,128)(2,1)S(1)}, u32[]{:S(2)}, u32[]{:S(2)}) %collective-permute-start.9) | collective-permute-done | bytes 262176 | tf_op jit(solution)/shard_map/ppermute | solution.py:422
  65.1 0.1 collective-permute-start.12
  65.2 1.0 collective-permute-start.16
  66.3 4.5 %collective-permute-done.6 = bf16[2,32,1024]{2,1,0:T(8,128)(2,1)S(1)} collective-permute-done((bf16[2,32,1024]{2,1,0:T(8,128)(2,1)S(1)}, bf16[2,32,1024]{2,1,0:T(8,128)(2,1)S(1)}, u32[]{:S(2)}, u32[]{:S(2)}) %collective-permute-start.6) | collective-permute-done | bytes 131104 | tf_op jit(solution)/shard_map/ppermute | solution.py:422
  70.8 0.4 collective-permute-start.10
  71.2 1.7 %collective-permute-done.12 = bf16[2,32,1024]{2,1,0:T(8,128)(2,1)S(1)} collective-permute-done((bf16[2,32,1024]{2,1,0:T(8,128)(2,1)S(1)}, bf16[2,32,1024]{2,1,0:T(8,128)(2,1)S(1)}, u32[]{:S(2)}, u32[]{:S(2)}) %collective-permute-start.12) | collective-permute-done | bytes 131104 | tf_op jit(solution)/shard_map/ppermute | solution.py:422
  72.9 1.0 collective-permute-start.14
  74.0 0.2 collective-permute-start.18
  74.3 3.0 %collective-permute-done.10 = bf16[1,32,1024]{2,1,0:T(8,128)(2,1)S(1)} collective-permute-done((bf16[1,32,1024]{2,1,0:T(8,128)(2,1)S(1)}, bf16[1,32,1024]{2,1,0:T(8,128)(2,1)S(1)}, u32[]{:S(2)}, u32[]{:S(2)}) %collective-permute-start.10) | collective-permute-done | bytes 65568 | tf_op jit(solution)/shard_map/ppermute | solution.py:422
  77.3 0.1 collective-permute-start.13
  77.5 1.8 %collective-permute-start.21 = (bf16[2,32,1024]{2,1,0:T(8,128)(2,1)S(1)}, bf16[2,32,1024]{2,1,0:T(8,128)(2,1)S(1)}, u32[]{:S(2)}, u32[]{:S(2)}) collective-permute-start(bf16[2,32,1024]{2,1,0:T(8,128)(2,1)S(1)} %get-tuple-element.161), channel_id=1, source_target_pairs={{0,4},{1,5},{2,6},{3,7},{4,0},{5,1},{6,2},{7,3},{8,12},{9,13},{10,... | collective-permute-start | bytes 393224 | tf_op jit(solution)/shard_map/ppermute | solution.py:422
  79.2 1.4 %collective-permute-done.14 = bf16[1,32,1024]{2,1,0:T(8,128)(2,1)S(1)} collective-permute-done((bf16[1,32,1024]{2,1,0:T(8,128)(2,1)S(1)}, bf16[1,32,1024]{2,1,0:T(8,128)(2,1)S(1)}, u32[]{:S(2)}, u32[]{:S(2)}) %collective-permute-start.14) | collective-permute-done | bytes 65568 | tf_op jit(solution)/shard_map/ppermute | solution.py:422
  80.6 0.1 collective-permute-start.20
  80.7 2.1 %collective-permute-done.13 = bf16[1,32,1024]{2,1,0:T(8,128)(2,1)S(1)} collective-permute-done((bf16[1,32,1024]{2,1,0:T(8,128)(2,1)S(1)}, bf16[1,32,1024]{2,1,0:T(8,128)(2,1)S(1)}, u32[]{:S(2)}, u32[]{:S(2)}) %collective-permute-start.13) | collective-permute-done | bytes 65568 | tf_op jit(solution)/shard_map/ppermute | solution.py:422
  82.8 0.1 collective-permute-start.17
  83.0 3.4 %collective-permute-start.19 = (bf16[1,32,1024]{2,1,0:T(8,128)(2,1)S(1)}, bf16[1,32,1024]{2,1,0:T(8,128)(2,1)S(1)}, u32[]{:S(2)}, u32[]{:S(2)}) collective-permute-start(bf16[1,32,1024]{2,1,0:T(8,128)(2,1)S(1)} %get-tuple-element.170), channel_id=1, source_target_pairs={{0,8},{1,9},{2,10},{3,11},{4,12},{5,13},{6,14},{7,15},{8,0},{9,1},... | collective-permute-start | bytes 196616 | tf_op jit(solution)/shard_map/ppermute | solution.py:422
  86.4 0.1 collective-permute-start.25
  86.5 0.4 collective-permute-done.20
  86.9 1.2 %collective-permute-start.23 = (bf16[2,32,1024]{2,1,0:T(8,128)(2,1)S(1)}, bf16[2,32,1024]{2,1,0:T(8,128)(2,1)S(1)}, u32[]{:S(2)}, u32[]{:S(2)}) collective-permute-start(bf16[2,32,1024]{2,1,0:T(8,128)(2,1)S(1)} %constant_dynamic-update-slice_fusion.2), channel_id=1, source_target_pairs={{0,2},{1,3},{2,0},{3,1},{4,6},{5,7},{6,4},{7,5},{8,10},{9,11},{10,... | collective-permute-start | bytes 393224 | tf_op jit(solution)/shard_map/ppermute | solution.py:422
  88.1 1.4 %collective-permute-done.19 = bf16[1,32,1024]{2,1,0:T(8,128)(2,1)S(1)} collective-permute-done((bf16[1,32,1024]{2,1,0:T(8,128)(2,1)S(1)}, bf16[1,32,1024]{2,1,0:T(8,128)(2,1)S(1)}, u32[]{:S(2)}, u32[]{:S(2)}) %collective-permute-start.19) | collective-permute-done | bytes 65568 | tf_op jit(solution)/shard_map/ppermute | solution.py:422
  89.5 2.1 %collective-permute-start.24 = (bf16[1,32,1024]{2,1,0:T(8,128)(2,1)S(1)}, bf16[1,32,1024]{2,1,0:T(8,128)(2,1)S(1)}, u32[]{:S(2)}, u32[]{:S(2)}) collective-permute-start(bf16[1,32,1024]{2,1,0:T(8,128)(2,1)S(1)} %fusion.7), channel_id=1, source_target_pairs={{0,8},{1,9},{2,10},{3,11},{4,12},{5,13},{6,14},{7,15},{8,0},{9,1},... | collective-permute-start | bytes 196616 | tf_op jit(solution)/shard_map/ppermute | solution.py:422
  91.7 1.0 collective-permute-start.22
  92.7 0.9 collective-permute-done.25
  93.6 0.1 collective-permute-start.27
  93.7 1.3 %collective-permute-done.24 = bf16[1,32,1024]{2,1,0:T(8,128)(2,1)S(1)} collective-permute-done((bf16[1,32,1024]{2,1,0:T(8,128)(2,1)S(1)}, bf16[1,32,1024]{2,1,0:T(8,128)(2,1)S(1)}, u32[]{:S(2)}, u32[]{:S(2)}) %collective-permute-start.24) | collective-permute-done | bytes 65568 | tf_op jit(solution)/shard_map/ppermute | solution.py:422
  95.0 1.7 %collective-permute-start.29 = (bf16[2,32,1024]{2,1,0:T(8,128)(2,1)S(1)}, bf16[2,32,1024]{2,1,0:T(8,128)(2,1)S(1)}, u32[]{:S(2)}, u32[]{:S(2)}) collective-permute-start(bf16[2,32,1024]{2,1,0:T(8,128)(2,1)S(1)} %constant_dynamic-update-slice_fusion.6), channel_id=1, source_target_pairs={{0,4},{1,5},{2,6},{3,7},{4,0},{5,1},{6,2},{7,3},{8,12},{9,13},{10,... | collective-permute-start | bytes 393224 | tf_op jit(solution)/shard_map/ppermute | solution.py:422
  96.8 0.4 collective-permute-start.26
  97.2 2.2 %collective-permute-done.27 = bf16[1,32,1024]{2,1,0:T(8,128)(2,1)S(1)} collective-permute-done((bf16[1,32,1024]{2,1,0:T(8,128)(2,1)S(1)}, bf16[1,32,1024]{2,1,0:T(8,128)(2,1)S(1)}, u32[]{:S(2)}, u32[]{:S(2)}) %collective-permute-start.27) | collective-permute-done | bytes 65568 | tf_op jit(solution)/shard_map/ppermute | solution.py:422
  99.4 0.5 collective-permute-start.28
  99.9 1.7 %collective-permute-done.29 = bf16[2,32,1024]{2,1,0:T(8,128)(2,1)S(1)} collective-permute-done((bf16[2,32,1024]{2,1,0:T(8,128)(2,1)S(1)}, bf16[2,32,1024]{2,1,0:T(8,128)(2,1)S(1)}, u32[]{:S(2)}, u32[]{:S(2)}) %collective-permute-start.29) | collective-permute-done | bytes 131104 | tf_op jit(solution)/shard_map/ppermute | solution.py:422
  101.6 0.5 collective-permute-start.32
  102.2 2.3 %collective-permute-done.28 = bf16[2,32,1024]{2,1,0:T(8,128)(2,1)S(1)} collective-permute-done((bf16[2,32,1024]{2,1,0:T(8,128)(2,1)S(1)}, bf16[2,32,1024]{2,1,0:T(8,128)(2,1)S(1)}, u32[]{:S(2)}, u32[]{:S(2)}) %collective-permute-start.28) | collective-permute-done | bytes 131104 | tf_op jit(solution)/shard_map/ppermute | solution.py:422
  104.5 0.2 collective-permute-start.31
  104.7 1.7 %collective-permute-done.26 = bf16[4,32,1024]{2,1,0:T(8,128)(2,1)S(1)} collective-permute-done((bf16[4,32,1024]{2,1,0:T(8,128)(2,1)S(1)}, bf16[4,32,1024]{2,1,0:T(8,128)(2,1)S(1)}, u32[]{:S(2)}, u32[]{:S(2)}) %collective-permute-start.26) | collective-permute-done | bytes 262176 | tf_op jit(solution)/shard_map/ppermute | solution.py:422
  106.5 0.1 collective-permute-start.35
  106.6 1.5 %collective-permute-done.32 = bf16[4,32,1024]{2,1,0:T(8,128)(2,1)S(1)} collective-permute-done((bf16[4,32,1024]{2,1,0:T(8,128)(2,1)S(1)}, bf16[4,32,1024]{2,1,0:T(8,128)(2,1)S(1)}, u32[]{:S(2)}, u32[]{:S(2)}) %collective-permute-start.32) | collective-permute-done | bytes 262176 | tf_op jit(solution)/shard_map/ppermute | solution.py:422
  108.1 0.1 collective-permute-start.34
  108.2 2.7 %collective-permute-done.31 = bf16[4,32,1024]{2,1,0:T(8,128)(2,1)S(1)} collective-permute-done((bf16[4,32,1024]{2,1,0:T(8,128)(2,1)S(1)}, bf16[4,32,1024]{2,1,0:T(8,128)(2,1)S(1)}, u32[]{:S(2)}, u32[]{:S(2)}) %collective-permute-start.31) | collective-permute-done | bytes 262176 | tf_op jit(solution)/shard_map/ppermute | solution.py:422
  111.0 0.5 collective-permute-start.30
  111.6 3.3 %shard_map.117 = (bf16[128,16384]{1,0:T(8,128)(2,1)}, bf16[128,1024]{1,0:T(8,128)(2,1)}) custom-call(f32[16,1024]{1,0:T(8,128)S(1)} %reshape.42.gain_ref, bf16[8,32,1024]{2,1,0:T(8,128)(2,1)S(1)} %constant_dynamic-update-slice_fusion.20.refs_0_, bf16[8,32,1024]{2,1,0:T(8,128)(2,1)} %collective-permute-done.34.refs_1_, ...), custom_call_target="tpu_custom_call" | custom-call | flops 6291456 | bytes 4194304 | tf_op jit(solution)/shard_map/pallas_call | solution.py:399
  114.9 2.1 %shard_map.118 = (bf16[128,16384]{1,0:T(8,128)(2,1)}, bf16[128,1024]{1,0:T(8,128)(2,1)}) custom-call(f32[16,1024]{1,0:T(8,128)S(1)} %reshape.42.gain_ref, bf16[8,32,1024]{2,1,0:T(8,128)(2,1)S(1)} %constant_dynamic-update-slice_fusion.18.refs_0_, ...), custom_call_target="tpu_custom_call", output_to_operand_aliasing={{0}: (5, {}), {1}: (6, {})} | custom-call | flops 6291456 | bytes 4194304 | tf_op jit(solution)/shard_map/pallas_call | solution.py:399
  (76 shorter events, 1.6 us)
Async XLA Ops:
  1.6 0.8 copy-start.1
  2.4 26.0 %copy-start = (bf16[8,1024,512]{2,1,0:T(8,128)(2,1)S(1)}, bf16[8,1024,512]{2,1,0:T(8,128)(2,1)}, u32[]{:S(2)}) copy-start(bf16[8,1024,512]{2,1,0:T(8,128)(2,1)} %keys_ref.1) | copy-start | bytes 25165828
  2.4 26.0 %copy-start.2 = (s32[8]{0:T(128)S(1)}, s32[8]{0:T(128)}, u32[]{:S(2)}) copy-start(s32[8]{0:T(128)} %lengths_ref.1) | copy-start | bytes 100
  49.4 1.6 %collective-permute-start = (bf16[4,32,1024]{2,1,0:T(8,128)(2,1)S(1)}, bf16[4,32,1024]{2,1,0:T(8,128)(2,1)S(1)}, u32[]{:S(2)}, u32[]{:S(2)}) collective-permute-start(bf16[4,32,1024]{2,1,0:T(8,128)(2,1)S(1)} %get-tuple-element.84), channel_id=1, source_target_pairs={{0,1},{1,0},{2,3},{3,2},{4,5},{5,4},{6,7},{7,6},{8,9},{9,8},{10,11... | collective-permute-start | bytes 786440 | tf_op jit(solution)/shard_map/ppermute | solution.py:422
  49.4 5.7 %collective-permute-start.4 = (bf16[4,32,1024]{2,1,0:T(8,128)(2,1)S(1)}, bf16[4,32,1024]{2,1,0:T(8,128)(2,1)S(1)}, u32[]{:S(2)}, u32[]{:S(2)}) collective-permute-start(bf16[4,32,1024]{2,1,0:T(8,128)(2,1)S(1)} %get-tuple-element.92), channel_id=1, source_target_pairs={{0,1},{1,0},{2,3},{3,2},{4,5},{5,4},{6,7},{7,6},{8,9},{9,8},{10,11... | collective-permute-start | bytes 786440 | tf_op jit(solution)/shard_map/ppermute | solution.py:422
  49.9 5.3 %collective-permute-start.5 = (bf16[4,32,1024]{2,1,0:T(8,128)(2,1)S(1)}, bf16[4,32,1024]{2,1,0:T(8,128)(2,1)S(1)}, u32[]{:S(2)}, u32[]{:S(2)}) collective-permute-start(bf16[4,32,1024]{2,1,0:T(8,128)(2,1)S(1)} %get-tuple-element.94), channel_id=1, source_target_pairs={{0,1},{1,0},{2,3},{3,2},{4,5},{5,4},{6,7},{7,6},{8,9},{9,8},{10,11... | collective-permute-start | bytes 786440 | tf_op jit(solution)/shard_map/ppermute | solution.py:422
  50.0 7.5 %collective-permute-start.7 = (bf16[4,32,1024]{2,1,0:T(8,128)(2,1)S(1)}, bf16[4,32,1024]{2,1,0:T(8,128)(2,1)S(1)}, u32[]{:S(2)}, u32[]{:S(2)}) collective-permute-start(bf16[4,32,1024]{2,1,0:T(8,128)(2,1)S(1)} %get-tuple-element.100), channel_id=1, source_target_pairs={{0,1},{1,0},{2,3},{3,2},{4,5},{5,4},{6,7},{7,6},{8,9},{9,8},{10,11... | collective-permute-start | bytes 786440 | tf_op jit(solution)/shard_map/ppermute | solution.py:422
  51.0 9.1 %collective-permute-start.2 = (bf16[4,32,1024]{2,1,0:T(8,128)(2,1)S(1)}, bf16[4,32,1024]{2,1,0:T(8,128)(2,1)S(1)}, u32[]{:S(2)}, u32[]{:S(2)}) collective-permute-start(bf16[4,32,1024]{2,1,0:T(8,128)(2,1)S(1)} %add_convert_fusion.7), channel_id=1, source_target_pairs={{0,2},{1,3},{2,0},{3,1},{4,6},{5,7},{6,4},{7,5},{8,10},{9,11},{10,... | collective-permute-start | bytes 786440 | tf_op jit(solution)/shard_map/ppermute | solution.py:422
  55.0 2.9 %collective-permute-start.3 = (bf16[4,32,1024]{2,1,0:T(8,128)(2,1)S(1)}, bf16[4,32,1024]{2,1,0:T(8,128)(2,1)S(1)}, u32[]{:S(2)}, u32[]{:S(2)}) collective-permute-start(bf16[4,32,1024]{2,1,0:T(8,128)(2,1)S(1)} %get-tuple-element.90), channel_id=1, source_target_pairs={{0,1},{1,0},{2,3},{3,2},{4,5},{5,4},{6,7},{7,6},{8,9},{9,8},{10,11... | collective-permute-start | bytes 786440 | tf_op jit(solution)/shard_map/ppermute | solution.py:422
  55.4 9.7 %collective-permute-start.9 = (bf16[4,32,1024]{2,1,0:T(8,128)(2,1)S(1)}, bf16[4,32,1024]{2,1,0:T(8,128)(2,1)S(1)}, u32[]{:S(2)}, u32[]{:S(2)}) collective-permute-start(bf16[4,32,1024]{2,1,0:T(8,128)(2,1)S(1)} %add_convert_fusion.3), channel_id=1, source_target_pairs={{0,2},{1,3},{2,0},{3,1},{4,6},{5,7},{6,4},{7,5},{8,10},{9,11},{10,... | collective-permute-start | bytes 786440 | tf_op jit(solution)/shard_map/ppermute | solution.py:422
  57.3 1.5 %collective-permute-start.1 = (bf16[4,32,1024]{2,1,0:T(8,128)(2,1)S(1)}, bf16[4,32,1024]{2,1,0:T(8,128)(2,1)S(1)}, u32[]{:S(2)}, u32[]{:S(2)}) collective-permute-start(bf16[4,32,1024]{2,1,0:T(8,128)(2,1)S(1)} %get-tuple-element.87), channel_id=1, source_target_pairs={{0,1},{1,0},{2,3},{3,2},{4,5},{5,4},{6,7},{7,6},{8,9},{9,8},{10,11... | collective-permute-start | bytes 786440 | tf_op jit(solution)/shard_map/ppermute | solution.py:422
  57.5 3.6 %collective-permute-start.8 = (bf16[4,32,1024]{2,1,0:T(8,128)(2,1)S(1)}, bf16[4,32,1024]{2,1,0:T(8,128)(2,1)S(1)}, u32[]{:S(2)}, u32[]{:S(2)}) collective-permute-start(bf16[4,32,1024]{2,1,0:T(8,128)(2,1)S(1)} %get-tuple-element.102), channel_id=1, source_target_pairs={{0,1},{1,0},{2,3},{3,2},{4,5},{5,4},{6,7},{7,6},{8,9},{9,8},{10,11... | collective-permute-start | bytes 786440 | tf_op jit(solution)/shard_map/ppermute | solution.py:422
  57.9 8.3 %collective-permute-start.15 = (bf16[4,32,1024]{2,1,0:T(8,128)(2,1)S(1)}, bf16[4,32,1024]{2,1,0:T(8,128)(2,1)S(1)}, u32[]{:S(2)}, u32[]{:S(2)}) collective-permute-start(bf16[4,32,1024]{2,1,0:T(8,128)(2,1)S(1)} %get-tuple-element.115), channel_id=1, source_target_pairs={{0,1},{1,0},{2,3},{3,2},{4,5},{5,4},{6,7},{7,6},{8,9},{9,8},{10,11... | collective-permute-start | bytes 786440 | tf_op jit(solution)/shard_map/ppermute | solution.py:422
  58.3 53.2 %copy-start.3 = (bf16[16384]{0:T(1024)(128)(2,1)S(1)}, bf16[16384]{0:T(1024)(128)(2,1)}, u32[]{:S(2)}) copy-start(bf16[16384]{0:T(1024)(128)(2,1)} %param.17) | copy-start | bytes 98308
  58.9 15.1 %collective-permute-start.11 = (bf16[4,32,1024]{2,1,0:T(8,128)(2,1)S(1)}, bf16[4,32,1024]{2,1,0:T(8,128)(2,1)S(1)}, u32[]{:S(2)}, u32[]{:S(2)}) collective-permute-start(bf16[4,32,1024]{2,1,0:T(8,128)(2,1)S(1)} %pad_maximum_fusion), channel_id=1, source_target_pairs={{0,4},{1,5},{2,6},{3,7},{4,0},{5,1},{6,2},{7,3},{8,12},{9,13},{10,... | collective-permute-start | bytes 786440 | tf_op jit(solution)/shard_map/ppermute | solution.py:422
  60.3 10.6 %collective-permute-start.6 = (bf16[2,32,1024]{2,1,0:T(8,128)(2,1)S(1)}, bf16[2,32,1024]{2,1,0:T(8,128)(2,1)S(1)}, u32[]{:S(2)}, u32[]{:S(2)}) collective-permute-start(bf16[2,32,1024]{2,1,0:T(8,128)(2,1)S(1)} %get-tuple-element.166), channel_id=1, source_target_pairs={{0,4},{1,5},{2,6},{3,7},{4,0},{5,1},{6,2},{7,3},{8,12},{9,13},{10,... | collective-permute-start | bytes 393224 | tf_op jit(solution)/shard_map/ppermute | solution.py:422
  65.1 7.7 %collective-permute-start.12 = (bf16[2,32,1024]{2,1,0:T(8,128)(2,1)S(1)}, bf16[2,32,1024]{2,1,0:T(8,128)(2,1)S(1)}, u32[]{:S(2)}, u32[]{:S(2)}) collective-permute-start(bf16[2,32,1024]{2,1,0:T(8,128)(2,1)S(1)} %get-tuple-element.165), channel_id=1, source_target_pairs={{0,4},{1,5},{2,6},{3,7},{4,0},{5,1},{6,2},{7,3},{8,12},{9,13},{10,... | collective-permute-start | bytes 393224 | tf_op jit(solution)/shard_map/ppermute | solution.py:422
  65.2 12.1 %collective-permute-start.16 = (bf16[4,32,1024]{2,1,0:T(8,128)(2,1)S(1)}, bf16[4,32,1024]{2,1,0:T(8,128)(2,1)S(1)}, u32[]{:S(2)}, u32[]{:S(2)}) collective-permute-start(bf16[4,32,1024]{2,1,0:T(8,128)(2,1)S(1)} %add_convert_fusion.2), channel_id=1, source_target_pairs={{0,2},{1,3},{2,0},{3,1},{4,6},{5,7},{6,4},{7,5},{8,10},{9,11},{10,... | collective-permute-start | bytes 786440 | tf_op jit(solution)/shard_map/ppermute | solution.py:422
  70.8 6.4 %collective-permute-start.10 = (bf16[1,32,1024]{2,1,0:T(8,128)(2,1)S(1)}, bf16[1,32,1024]{2,1,0:T(8,128)(2,1)S(1)}, u32[]{:S(2)}, u32[]{:S(2)}) collective-permute-start(bf16[1,32,1024]{2,1,0:T(8,128)(2,1)S(1)} %get-tuple-element.178), channel_id=1, source_target_pairs={{0,8},{1,9},{2,10},{3,11},{4,12},{5,13},{6,14},{7,15},{8,0},{9,1},... | collective-permute-start | bytes 196616 | tf_op jit(solution)/shard_map/ppermute | solution.py:422
  72.9 7.7 %collective-permute-start.14 = (bf16[1,32,1024]{2,1,0:T(8,128)(2,1)S(1)}, bf16[1,32,1024]{2,1,0:T(8,128)(2,1)S(1)}, u32[]{:S(2)}, u32[]{:S(2)}) collective-permute-start(bf16[1,32,1024]{2,1,0:T(8,128)(2,1)S(1)} %get-tuple-element.173), channel_id=1, source_target_pairs={{0,8},{1,9},{2,10},{3,11},{4,12},{5,13},{6,14},{7,15},{8,0},{9,1},... | collective-permute-start | bytes 196616 | tf_op jit(solution)/shard_map/ppermute | solution.py:422
  74.0 8.9 %collective-permute-start.18 = (bf16[2,32,1024]{2,1,0:T(8,128)(2,1)S(1)}, bf16[2,32,1024]{2,1,0:T(8,128)(2,1)S(1)}, u32[]{:S(2)}, u32[]{:S(2)}) collective-permute-start(bf16[2,32,1024]{2,1,0:T(8,128)(2,1)S(1)} %get-tuple-element.163), channel_id=1, source_target_pairs={{0,2},{1,3},{2,0},{3,1},{4,6},{5,7},{6,4},{7,5},{8,10},{9,11},{10,... | collective-permute-start | bytes 393224 | tf_op jit(solution)/shard_map/ppermute | solution.py:422
  77.3 5.5 %collective-permute-start.13 = (bf16[1,32,1024]{2,1,0:T(8,128)(2,1)S(1)}, bf16[1,32,1024]{2,1,0:T(8,128)(2,1)S(1)}, u32[]{:S(2)}, u32[]{:S(2)}) collective-permute-start(bf16[1,32,1024]{2,1,0:T(8,128)(2,1)S(1)} %fusion.5), channel_id=1, source_target_pairs={{0,8},{1,9},{2,10},{3,11},{4,12},{5,13},{6,14},{7,15},{8,0},{9,1},... | collective-permute-start | bytes 196616 | tf_op jit(solution)/shard_map/ppermute | solution.py:422
  77.5 8.9 %collective-permute-start.21 = (bf16[2,32,1024]{2,1,0:T(8,128)(2,1)S(1)}, bf16[2,32,1024]{2,1,0:T(8,128)(2,1)S(1)}, u32[]{:S(2)}, u32[]{:S(2)}) collective-permute-start(bf16[2,32,1024]{2,1,0:T(8,128)(2,1)S(1)} %get-tuple-element.161), channel_id=1, source_target_pairs={{0,4},{1,5},{2,6},{3,7},{4,0},{5,1},{6,2},{7,3},{8,12},{9,13},{10,... | collective-permute-start | bytes 393224 | tf_op jit(solution)/shard_map/ppermute | solution.py:422
  80.6 6.2 %collective-permute-start.20 = (bf16[1,32,1024]{2,1,0:T(8,128)(2,1)S(1)}, bf16[1,32,1024]{2,1,0:T(8,128)(2,1)S(1)}, u32[]{:S(2)}, u32[]{:S(2)}) collective-permute-start(bf16[1,32,1024]{2,1,0:T(8,128)(2,1)S(1)} %fusion.6), channel_id=1, source_target_pairs={{0,8},{1,9},{2,10},{3,11},{4,12},{5,13},{6,14},{7,15},{8,0},{9,1},... | collective-permute-start | bytes 196616 | tf_op jit(solution)/shard_map/ppermute | solution.py:422
  82.8 8.8 %collective-permute-start.17 = (bf16[2,32,1024]{2,1,0:T(8,128)(2,1)S(1)}, bf16[2,32,1024]{2,1,0:T(8,128)(2,1)S(1)}, u32[]{:S(2)}, u32[]{:S(2)}) collective-permute-start(bf16[2,32,1024]{2,1,0:T(8,128)(2,1)S(1)} %constant_dynamic-update-slice_fusion), channel_id=1, source_target_pairs={{0,4},{1,5},{2,6},{3,7},{4,0},{5,1},{6,2},{7,3},{8,12},{9,13},{10,... | collective-permute-start | bytes 393224 | tf_op jit(solution)/shard_map/ppermute | solution.py:422
  83.0 6.5 %collective-permute-start.19 = (bf16[1,32,1024]{2,1,0:T(8,128)(2,1)S(1)}, bf16[1,32,1024]{2,1,0:T(8,128)(2,1)S(1)}, u32[]{:S(2)}, u32[]{:S(2)}) collective-permute-start(bf16[1,32,1024]{2,1,0:T(8,128)(2,1)S(1)} %get-tuple-element.170), channel_id=1, source_target_pairs={{0,8},{1,9},{2,10},{3,11},{4,12},{5,13},{6,14},{7,15},{8,0},{9,1},... | collective-permute-start | bytes 196616 | tf_op jit(solution)/shard_map/ppermute | solution.py:422
  86.4 7.2 %collective-permute-start.25 = (bf16[1,32,1024]{2,1,0:T(8,128)(2,1)S(1)}, bf16[1,32,1024]{2,1,0:T(8,128)(2,1)S(1)}, u32[]{:S(2)}, u32[]{:S(2)}) collective-permute-start(bf16[1,32,1024]{2,1,0:T(8,128)(2,1)S(1)} %get-tuple-element.169), channel_id=1, source_target_pairs={{0,8},{1,9},{2,10},{3,11},{4,12},{5,13},{6,14},{7,15},{8,0},{9,1},... | collective-permute-start | bytes 196616 | tf_op jit(solution)/shard_map/ppermute | solution.py:422
  86.9 9.9 %collective-permute-start.23 = (bf16[2,32,1024]{2,1,0:T(8,128)(2,1)S(1)}, bf16[2,32,1024]{2,1,0:T(8,128)(2,1)S(1)}, u32[]{:S(2)}, u32[]{:S(2)}) collective-permute-start(bf16[2,32,1024]{2,1,0:T(8,128)(2,1)S(1)} %constant_dynamic-update-slice_fusion.2), channel_id=1, source_target_pairs={{0,2},{1,3},{2,0},{3,1},{4,6},{5,7},{6,4},{7,5},{8,10},{9,11},{10,... | collective-permute-start | bytes 393224 | tf_op jit(solution)/shard_map/ppermute | solution.py:422
  89.5 5.5 %collective-permute-start.24 = (bf16[1,32,1024]{2,1,0:T(8,128)(2,1)S(1)}, bf16[1,32,1024]{2,1,0:T(8,128)(2,1)S(1)}, u32[]{:S(2)}, u32[]{:S(2)}) collective-permute-start(bf16[1,32,1024]{2,1,0:T(8,128)(2,1)S(1)} %fusion.7), channel_id=1, source_target_pairs={{0,8},{1,9},{2,10},{3,11},{4,12},{5,13},{6,14},{7,15},{8,0},{9,1},... | collective-permute-start | bytes 196616 | tf_op jit(solution)/shard_map/ppermute | solution.py:422
  91.7 14.9 %collective-permute-start.22 = (bf16[4,32,1024]{2,1,0:T(8,128)(2,1)S(1)}, bf16[4,32,1024]{2,1,0:T(8,128)(2,1)S(1)}, u32[]{:S(2)}, u32[]{:S(2)}) collective-permute-start(bf16[4,32,1024]{2,1,0:T(8,128)(2,1)S(1)} %constant_dynamic-update-slice_fusion.4), channel_id=1, source_target_pairs={{0,2},{1,3},{2,0},{3,1},{4,6},{5,7},{6,4},{7,5},{8,10},{9,11},{10,... | collective-permute-start | bytes 786440 | tf_op jit(solution)/shard_map/ppermute | solution.py:422
  93.6 5.8 %collective-permute-start.27 = (bf16[1,32,1024]{2,1,0:T(8,128)(2,1)S(1)}, bf16[1,32,1024]{2,1,0:T(8,128)(2,1)S(1)}, u32[]{:S(2)}, u32[]{:S(2)}) collective-permute-start(bf16[1,32,1024]{2,1,0:T(8,128)(2,1)S(1)} %fusion.8), channel_id=1, source_target_pairs={{0,8},{1,9},{2,10},{3,11},{4,12},{5,13},{6,14},{7,15},{8,0},{9,1},... | collective-permute-start | bytes 196616 | tf_op jit(solution)/shard_map/ppermute | solution.py:422
  95.0 6.6 %collective-permute-start.29 = (bf16[2,32,1024]{2,1,0:T(8,128)(2,1)S(1)}, bf16[2,32,1024]{2,1,0:T(8,128)(2,1)S(1)}, u32[]{:S(2)}, u32[]{:S(2)}) collective-permute-start(bf16[2,32,1024]{2,1,0:T(8,128)(2,1)S(1)} %constant_dynamic-update-slice_fusion.6), channel_id=1, source_target_pairs={{0,4},{1,5},{2,6},{3,7},{4,0},{5,1},{6,2},{7,3},{8,12},{9,13},{10,... | collective-permute-start | bytes 393224 | tf_op jit(solution)/shard_map/ppermute | solution.py:422
  96.8 9.6 %collective-permute-start.26 = (bf16[4,32,1024]{2,1,0:T(8,128)(2,1)S(1)}, bf16[4,32,1024]{2,1,0:T(8,128)(2,1)S(1)}, u32[]{:S(2)}, u32[]{:S(2)}) collective-permute-start(bf16[4,32,1024]{2,1,0:T(8,128)(2,1)S(1)} %constant_dynamic-update-slice_fusion.8), channel_id=1, source_target_pairs={{0,4},{1,5},{2,6},{3,7},{4,0},{5,1},{6,2},{7,3},{8,12},{9,13},{10,... | collective-permute-start | bytes 786440 | tf_op jit(solution)/shard_map/ppermute | solution.py:422
  99.4 5.0 %collective-permute-start.28 = (bf16[2,32,1024]{2,1,0:T(8,128)(2,1)S(1)}, bf16[2,32,1024]{2,1,0:T(8,128)(2,1)S(1)}, u32[]{:S(2)}, u32[]{:S(2)}) collective-permute-start(bf16[2,32,1024]{2,1,0:T(8,128)(2,1)S(1)} %constant_dynamic-update-slice_fusion.10), channel_id=1, source_target_pairs={{0,2},{1,3},{2,0},{3,1},{4,6},{5,7},{6,4},{7,5},{8,10},{9,11},{10,... | collective-permute-start | bytes 393224 | tf_op jit(solution)/shard_map/ppermute | solution.py:422
  101.6 6.4 %collective-permute-start.32 = (bf16[4,32,1024]{2,1,0:T(8,128)(2,1)S(1)}, bf16[4,32,1024]{2,1,0:T(8,128)(2,1)S(1)}, u32[]{:S(2)}, u32[]{:S(2)}) collective-permute-start(bf16[4,32,1024]{2,1,0:T(8,128)(2,1)S(1)} %constant_dynamic-update-slice_fusion.12), channel_id=1, source_target_pairs={{0,2},{1,3},{2,0},{3,1},{4,6},{5,7},{6,4},{7,5},{8,10},{9,11},{10,... | collective-permute-start | bytes 786440 | tf_op jit(solution)/shard_map/ppermute | solution.py:422
  104.5 6.4 %collective-permute-start.31 = (bf16[4,32,1024]{2,1,0:T(8,128)(2,1)S(1)}, bf16[4,32,1024]{2,1,0:T(8,128)(2,1)S(1)}, u32[]{:S(2)}, u32[]{:S(2)}) collective-permute-start(bf16[4,32,1024]{2,1,0:T(8,128)(2,1)S(1)} %constant_dynamic-update-slice_fusion.14), channel_id=1, source_target_pairs={{0,4},{1,5},{2,6},{3,7},{4,0},{5,1},{6,2},{7,3},{8,12},{9,13},{10,... | collective-permute-start | bytes 786440 | tf_op jit(solution)/shard_map/ppermute | solution.py:422
  106.5 5.1 %collective-permute-start.35 = (bf16[8,32,1024]{2,1,0:T(8,128)(2,1)S(1)}, bf16[8,32,1024]{2,1,0:T(8,128)(2,1)}, u32[]{:S(2)}, u32[]{:S(2)}) collective-permute-start(bf16[8,32,1024]{2,1,0:T(8,128)(2,1)S(1)} %constant_dynamic-update-slice_fusion.16.refs_2_), channel_id=1, source_target_pairs={{0,1},{1,0},{2,3},{3,2},{4,5},{5,4},{6,7},{7,6},{8,9},{9,8},{10,11... | collective-permute-start | bytes 1572872 | tf_op jit(solution)/shard_map/ppermute | solution.py:422
  108.1 3.5 %collective-permute-start.34 = (bf16[8,32,1024]{2,1,0:T(8,128)(2,1)S(1)}, bf16[8,32,1024]{2,1,0:T(8,128)(2,1)}, u32[]{:S(2)}, u32[]{:S(2)}) collective-permute-start(bf16[8,32,1024]{2,1,0:T(8,128)(2,1)S(1)} %constant_dynamic-update-slice_fusion.20.refs_0_), channel_id=1, source_target_pairs={{0,1},{1,0},{2,3},{3,2},{4,5},{5,4},{6,7},{7,6},{8,9},{9,8},{10,11... | collective-permute-start | bytes 1572872 | tf_op jit(solution)/shard_map/ppermute | solution.py:422
  111.0 3.9 %collective-permute-start.33 = (bf16[8,32,1024]{2,1,0:T(8,128)(2,1)S(1)}, bf16[8,32,1024]{2,1,0:T(8,128)(2,1)S(1)}, u32[]{:S(2)}, u32[]{:S(2)}) collective-permute-start(bf16[8,32,1024]{2,1,0:T(8,128)(2,1)S(1)} %constant_dynamic-update-slice_fusion.22.refs_2_), channel_id=1, source_target_pairs={{0,1},{1,0},{2,3},{3,2},{4,5},{5,4},{6,7},{7,6},{8,9},{9,8},{10,11... | collective-permute-start | bytes 1572872 | tf_op jit(solution)/shard_map/ppermute | solution.py:422
  111.0 3.9 %collective-permute-start.30 = (bf16[8,32,1024]{2,1,0:T(8,128)(2,1)S(1)}, bf16[8,32,1024]{2,1,0:T(8,128)(2,1)S(1)}, u32[]{:S(2)}, u32[]{:S(2)}) collective-permute-start(bf16[8,32,1024]{2,1,0:T(8,128)(2,1)S(1)} %constant_dynamic-update-slice_fusion.18.refs_0_), channel_id=1, source_target_pairs={{0,1},{1,0},{2,3},{3,2},{4,5},{5,4},{6,7},{7,6},{8,9},{9,8},{10,11... | collective-permute-start | bytes 1572872 | tf_op jit(solution)/shard_map/ppermute | solution.py:422

commit v11 on v10

--- a/solution.py
+++ b/solution.py
@@ -393,6 +393,7 @@
 def finish(parts, gain, offsets, which, groups, earlier):
     half, rows, width = parts[0].shape
     columns, count = 2 * half * width, len(offsets)
+    parts = [pltpu.with_memory_space_constraint(part, pltpu.VMEM) for part in parts]
     operands = [gain, *parts, *earlier]
     specs = [pl.BlockSpec(memory_space=pltpu.VMEM)] * (1 + len(parts))
     specs += [pl.BlockSpec(memory_space=pl.ANY)] * len(earlier)

time: 117 us -> 117 us (level)
  no operation moved by 1% of the time
where the time goes in v11:
time: 117 us
  waiting for transfers between devices  34.9 us (30%)
  Pallas kernels  30.1 us (26%)
  blocking collectives  26.2 us (22%)
  starting transfers between devices  21.7 us (19%)
  other arithmetic  2.08 us (2%)
    ppermute x36, waiting for transfers between devices, swap(): lax.ppermute(values, 'tensor', [(i, i ^ 1 << bit) for i in range(count)])  34.9 us
    all_to_all x2, blocking collectives, exchange(): lax.all_to_all(blocks, 'tensor', split_axis=0, concat_axis=0, tiled=True)  26.2 us
    ppermute x36, starting transfers between devices, swap(): lax.ppermute(values, 'tensor', [(i, i ^ 1 << bit) for i in range(count)])  21.7 us
    pallas_call x1, Pallas kernels, project_in(): pl.pallas_call(functools.partial(input_kernel, count), out_shape=(jax.Sha...  10.3 us
    pallas_call x2, Pallas kernels, project(): pl.pallas_call(functools.partial(project_kernel, count, side), out_shape=...  7.67 us
    pallas_call x1, Pallas kernels, attend(): pl.pallas_call(functools.partial(attend_kernel, count), out_shape=jax.Sha...  6.62 us
    pallas_call x2, Pallas kernels, finish(): pl.pallas_call(functools.partial(finish_kernel, offsets), grid=(count,),...  5.44 us
  transfers between devices with their start and end apart: 36, of which 19 were waited for; matrix products, arithmetic and copies ran while one was open for 1% of the time, Pallas kernels for 6%

profile of v11, /device:TPU:0, one launch (start us, length us, event | category | flops | bytes accessed | tf_op | source)
XLA Modules:
  0.0 117.0 jit_solution(8699891511584517456)
XLA Ops:
  0.6 0.7 convert_element_type.283
  1.3 0.3 fusion.4
  1.6 0.7 copy-done.1
  2.4 10.3 %shard_map.113 = (bf16[16,8,640]{2,1,0:T(8,128)(2,1)S(1)}, bf16[128,1024]{1,0:T(8,128)(2,1)S(1)}) custom-call(bf16[128,16384]{1,0:T(8,128)(2,1)} %hidden_ref.1, bf16[16384]{0:T(1024)(128)(2,1)S(1)} %copy-done.1, bf16[16384,512]{1,0:T(8,128)(2,1)} %w_ref.3, bf16[64,16384]{1,0:T(8,128)(2,1)} %bitcast.33, f32[128,128]{1,0:T(8,128)S(1)} %get-tuple-element.181.cosine_ref, ...), custom_call_target="tpu_custom_call" | custom-call | flops 2415919104 | bytes 23068672 | tf_op jit(solution)/shard_map/pallas_call | solution.py:120
  12.7 15.7 %all_to_all.10.refs_0_ = bf16[16,8,640]{2,1,0:T(8,128)(2,1)S(1)} all-to-all(bf16[16,8,640]{2,1,0:T(8,128)(2,1)S(1)} %get-tuple-element.82), channel_id=1, replica_groups=mesh['groups'=2,'tensor'=16] {'tensor'}, dimensions={0} | all-to-all | bytes 327680 | tf_op jit(solution)/shard_map/all_to_all | solution.py:284
  28.4 6.6 %shard_map.114 = bf16[16,8,512]{2,1,0:T(8,128)(2,1)S(1)} custom-call(s32[8]{0:T(128)S(1)} %copy-done.2, f32[128,128]{1,0:T(8,128)S(1)} %get-tuple-element.181.cosine_ref, f32[128,128]{1,0:T(8,128)S(1)} %get-tuple-element.180.sine_ref, bf16[8,1024,512]{2,1,0:T(8,128)(2,1)S(1)} %copy-done, bf16[8,1024,512]{2,1,0:T(8,128)(2,1)} %values_ref.1, ...), custom_call_target="tpu_custom_call" | custom-call | flops 268435456 | bytes 16777216 | tf_op jit(solution)/shard_map/pallas_call | solution.py:259
  35.0 10.5 %all_to_all.11.in_ref = bf16[16,8,512]{2,1,0:T(8,128)(2,1)S(1)} all-to-all(bf16[16,8,512]{2,1,0:T(8,128)(2,1)S(1)} %shard_map.114), channel_id=1, replica_groups=mesh['groups'=2,'tensor'=16] {'tensor'}, dimensions={0} | all-to-all | bytes 262144 | tf_op jit(solution)/shard_map/all_to_all | solution.py:284
  45.5 3.8 %shard_map.115 = (bf16[4,32,1024]{2,1,0:T(8,128)(2,1)S(1)}, bf16[4,32,1024]{2,1,0:T(8,128)(2,1)S(1)}, bf16[4,32,1024]{2,1,0:T(8,128)(2,1)S(1)}, bf16[4,32,1024]{...) custom-call(bf16[16,8,512]{2,1,0:T(8,128)(2,1)S(1)} %all_to_all.11.i, ...), custom_call_target="tpu_custom_call" | custom-call | flops 1073741824 | bytes 10485760 | tf_op jit(solution)/shard_map/pallas_call | solution.py:347
  49.4 0.1 collective-permute-start
  49.4 0.5 collective-permute-start.4
  49.9 0.1 collective-permute-start.5
  50.0 0.4 collective-permute-start.7
  50.5 0.5 collective-permute-done
  51.0 0.1 collective-permute-start.2
  51.1 3.8 %shard_map.116 = (bf16[4,32,1024]{2,1,0:T(8,128)(2,1)S(1)}, bf16[4,32,1024]{2,1,0:T(8,128)(2,1)S(1)}, bf16[4,32,1024]{2,1,0:T(8,128)(2,1)S(1)}, bf16[4,32,1024]{...) custom-call(bf16[16,8,512]{2,1,0:T(8,128)(2,1)S(1)} %all_to_all.11.i, ...), custom_call_target="tpu_custom_call" | custom-call | flops 1073741824 | bytes 10485760 | tf_op jit(solution)/shard_map/pallas_call | solution.py:347
  55.0 0.2 collective-permute-start.3
  55.4 2.0 %collective-permute-start.9 = (bf16[4,32,1024]{2,1,0:T(8,128)(2,1)S(1)}, bf16[4,32,1024]{2,1,0:T(8,128)(2,1)S(1)}, u32[]{:S(2)}, u32[]{:S(2)}) collective-permute-start(bf16[4,32,1024]{2,1,0:T(8,128)(2,1)S(1)} %add_convert_fusion.3), channel_id=1, source_target_pairs={{0,2},{1,3},{2,0},{3,1},{4,6},{5,7},{6,4},{7,5},{8,10},{9,11},{10,... | collective-permute-start | bytes 786440 | tf_op jit(solution)/shard_map/ppermute | solution.py:423
  57.3 0.2 collective-permute-start.1
  57.5 0.3 collective-permute-start.8
  57.9 0.3 collective-permute-start.15
  58.3 0.5 collective-permute-done.1
  58.9 1.3 %collective-permute-done.2 = bf16[4,32,1024]{2,1,0:T(8,128)(2,1)S(1)} collective-permute-done((bf16[4,32,1024]{2,1,0:T(8,128)(2,1)S(1)}, bf16[4,32,1024]{2,1,0:T(8,128)(2,1)S(1)}, u32[]{:S(2)}, u32[]{:S(2)}) %collective-permute-start.2) | collective-permute-done | bytes 262176 | tf_op jit(solution)/shard_map/ppermute | solution.py:423
  60.3 0.8 collective-permute-start.6
  61.2 3.9 %collective-permute-done.9 = bf16[4,32,1024]{2,1,0:T(8,128)(2,1)S(1)} collective-permute-done((bf16[4,32,1024]{2,1,0:T(8,128)(2,1)S(1)}, bf16[4,32,1024]{2,1,0:T(8,128)(2,1)S(1)}, u32[]{:S(2)}, u32[]{:S(2)}) %collective-permute-start.9) | collective-permute-done | bytes 262176 | tf_op jit(solution)/shard_map/ppermute | solution.py:423
  65.1 0.1 collective-permute-start.12
  65.2 1.0 collective-permute-start.16
  66.3 4.5 %collective-permute-done.6 = bf16[2,32,1024]{2,1,0:T(8,128)(2,1)S(1)} collective-permute-done((bf16[2,32,1024]{2,1,0:T(8,128)(2,1)S(1)}, bf16[2,32,1024]{2,1,0:T(8,128)(2,1)S(1)}, u32[]{:S(2)}, u32[]{:S(2)}) %collective-permute-start.6) | collective-permute-done | bytes 131104 | tf_op jit(solution)/shard_map/ppermute | solution.py:423
  70.8 0.4 collective-permute-start.10
  71.2 1.7 %collective-permute-done.12 = bf16[2,32,1024]{2,1,0:T(8,128)(2,1)S(1)} collective-permute-done((bf16[2,32,1024]{2,1,0:T(8,128)(2,1)S(1)}, bf16[2,32,1024]{2,1,0:T(8,128)(2,1)S(1)}, u32[]{:S(2)}, u32[]{:S(2)}) %collective-permute-start.12) | collective-permute-done | bytes 131104 | tf_op jit(solution)/shard_map/ppermute | solution.py:423
  72.9 1.0 collective-permute-start.14
  74.0 0.2 collective-permute-start.18
  74.3 3.0 %collective-permute-done.10 = bf16[1,32,1024]{2,1,0:T(8,128)(2,1)S(1)} collective-permute-done((bf16[1,32,1024]{2,1,0:T(8,128)(2,1)S(1)}, bf16[1,32,1024]{2,1,0:T(8,128)(2,1)S(1)}, u32[]{:S(2)}, u32[]{:S(2)}) %collective-permute-start.10) | collective-permute-done | bytes 65568 | tf_op jit(solution)/shard_map/ppermute | solution.py:423
  77.3 0.1 collective-permute-start.13
  77.5 1.8 %collective-permute-start.21 = (bf16[2,32,1024]{2,1,0:T(8,128)(2,1)S(1)}, bf16[2,32,1024]{2,1,0:T(8,128)(2,1)S(1)}, u32[]{:S(2)}, u32[]{:S(2)}) collective-permute-start(bf16[2,32,1024]{2,1,0:T(8,128)(2,1)S(1)} %get-tuple-element.161), channel_id=1, source_target_pairs={{0,4},{1,5},{2,6},{3,7},{4,0},{5,1},{6,2},{7,3},{8,12},{9,13},{10,... | collective-permute-start | bytes 393224 | tf_op jit(solution)/shard_map/ppermute | solution.py:423
  79.2 1.4 %collective-permute-done.14 = bf16[1,32,1024]{2,1,0:T(8,128)(2,1)S(1)} collective-permute-done((bf16[1,32,1024]{2,1,0:T(8,128)(2,1)S(1)}, bf16[1,32,1024]{2,1,0:T(8,128)(2,1)S(1)}, u32[]{:S(2)}, u32[]{:S(2)}) %collective-permute-start.14) | collective-permute-done | bytes 65568 | tf_op jit(solution)/shard_map/ppermute | solution.py:423
  80.6 0.1 collective-permute-start.20
  80.7 2.1 %collective-permute-done.13 = bf16[1,32,1024]{2,1,0:T(8,128)(2,1)S(1)} collective-permute-done((bf16[1,32,1024]{2,1,0:T(8,128)(2,1)S(1)}, bf16[1,32,1024]{2,1,0:T(8,128)(2,1)S(1)}, u32[]{:S(2)}, u32[]{:S(2)}) %collective-permute-start.13) | collective-permute-done | bytes 65568 | tf_op jit(solution)/shard_map/ppermute | solution.py:423
  82.8 0.1 collective-permute-start.17
  83.0 3.4 %collective-permute-start.19 = (bf16[1,32,1024]{2,1,0:T(8,128)(2,1)S(1)}, bf16[1,32,1024]{2,1,0:T(8,128)(2,1)S(1)}, u32[]{:S(2)}, u32[]{:S(2)}) collective-permute-start(bf16[1,32,1024]{2,1,0:T(8,128)(2,1)S(1)} %get-tuple-element.170), channel_id=1, source_target_pairs={{0,8},{1,9},{2,10},{3,11},{4,12},{5,13},{6,14},{7,15},{8,0},{9,1},... | collective-permute-start | bytes 196616 | tf_op jit(solution)/shard_map/ppermute | solution.py:423
  86.4 0.1 collective-permute-start.25
  86.5 0.4 collective-permute-done.20
  86.9 1.2 %collective-permute-start.23 = (bf16[2,32,1024]{2,1,0:T(8,128)(2,1)S(1)}, bf16[2,32,1024]{2,1,0:T(8,128)(2,1)S(1)}, u32[]{:S(2)}, u32[]{:S(2)}) collective-permute-start(bf16[2,32,1024]{2,1,0:T(8,128)(2,1)S(1)} %constant_dynamic-update-slice_fusion.2), channel_id=1, source_target_pairs={{0,2},{1,3},{2,0},{3,1},{4,6},{5,7},{6,4},{7,5},{8,10},{9,11},{10,... | collective-permute-start | bytes 393224 | tf_op jit(solution)/shard_map/ppermute | solution.py:423
  88.1 1.4 %collective-permute-done.19 = bf16[1,32,1024]{2,1,0:T(8,128)(2,1)S(1)} collective-permute-done((bf16[1,32,1024]{2,1,0:T(8,128)(2,1)S(1)}, bf16[1,32,1024]{2,1,0:T(8,128)(2,1)S(1)}, u32[]{:S(2)}, u32[]{:S(2)}) %collective-permute-start.19) | collective-permute-done | bytes 65568 | tf_op jit(solution)/shard_map/ppermute | solution.py:423
  89.5 2.1 %collective-permute-start.24 = (bf16[1,32,1024]{2,1,0:T(8,128)(2,1)S(1)}, bf16[1,32,1024]{2,1,0:T(8,128)(2,1)S(1)}, u32[]{:S(2)}, u32[]{:S(2)}) collective-permute-start(bf16[1,32,1024]{2,1,0:T(8,128)(2,1)S(1)} %fusion.7), channel_id=1, source_target_pairs={{0,8},{1,9},{2,10},{3,11},{4,12},{5,13},{6,14},{7,15},{8,0},{9,1},... | collective-permute-start | bytes 196616 | tf_op jit(solution)/shard_map/ppermute | solution.py:423
  91.7 1.0 collective-permute-start.22
  92.7 0.9 collective-permute-done.25
  93.6 0.1 collective-permute-start.27
  93.7 1.3 %collective-permute-done.24 = bf16[1,32,1024]{2,1,0:T(8,128)(2,1)S(1)} collective-permute-done((bf16[1,32,1024]{2,1,0:T(8,128)(2,1)S(1)}, bf16[1,32,1024]{2,1,0:T(8,128)(2,1)S(1)}, u32[]{:S(2)}, u32[]{:S(2)}) %collective-permute-start.24) | collective-permute-done | bytes 65568 | tf_op jit(solution)/shard_map/ppermute | solution.py:423
  95.0 1.7 %collective-permute-start.29 = (bf16[2,32,1024]{2,1,0:T(8,128)(2,1)S(1)}, bf16[2,32,1024]{2,1,0:T(8,128)(2,1)S(1)}, u32[]{:S(2)}, u32[]{:S(2)}) collective-permute-start(bf16[2,32,1024]{2,1,0:T(8,128)(2,1)S(1)} %constant_dynamic-update-slice_fusion.6), channel_id=1, source_target_pairs={{0,4},{1,5},{2,6},{3,7},{4,0},{5,1},{6,2},{7,3},{8,12},{9,13},{10,... | collective-permute-start | bytes 393224 | tf_op jit(solution)/shard_map/ppermute | solution.py:423
  96.8 0.4 collective-permute-start.26
  97.2 2.2 %collective-permute-done.27 = bf16[1,32,1024]{2,1,0:T(8,128)(2,1)S(1)} collective-permute-done((bf16[1,32,1024]{2,1,0:T(8,128)(2,1)S(1)}, bf16[1,32,1024]{2,1,0:T(8,128)(2,1)S(1)}, u32[]{:S(2)}, u32[]{:S(2)}) %collective-permute-start.27) | collective-permute-done | bytes 65568 | tf_op jit(solution)/shard_map/ppermute | solution.py:423
  99.4 0.5 collective-permute-start.28
  99.9 1.7 %collective-permute-done.29 = bf16[2,32,1024]{2,1,0:T(8,128)(2,1)S(1)} collective-permute-done((bf16[2,32,1024]{2,1,0:T(8,128)(2,1)S(1)}, bf16[2,32,1024]{2,1,0:T(8,128)(2,1)S(1)}, u32[]{:S(2)}, u32[]{:S(2)}) %collective-permute-start.29) | collective-permute-done | bytes 131104 | tf_op jit(solution)/shard_map/ppermute | solution.py:423
  101.6 0.5 collective-permute-start.32
  102.2 2.3 %collective-permute-done.28 = bf16[2,32,1024]{2,1,0:T(8,128)(2,1)S(1)} collective-permute-done((bf16[2,32,1024]{2,1,0:T(8,128)(2,1)S(1)}, bf16[2,32,1024]{2,1,0:T(8,128)(2,1)S(1)}, u32[]{:S(2)}, u32[]{:S(2)}) %collective-permute-start.28) | collective-permute-done | bytes 131104 | tf_op jit(solution)/shard_map/ppermute | solution.py:423
  104.5 0.2 collective-permute-start.31
  104.7 1.7 %collective-permute-done.26 = bf16[4,32,1024]{2,1,0:T(8,128)(2,1)S(1)} collective-permute-done((bf16[4,32,1024]{2,1,0:T(8,128)(2,1)S(1)}, bf16[4,32,1024]{2,1,0:T(8,128)(2,1)S(1)}, u32[]{:S(2)}, u32[]{:S(2)}) %collective-permute-start.26) | collective-permute-done | bytes 262176 | tf_op jit(solution)/shard_map/ppermute | solution.py:423
  106.5 0.1 collective-permute-start.35
  106.6 1.5 %collective-permute-done.32 = bf16[4,32,1024]{2,1,0:T(8,128)(2,1)S(1)} collective-permute-done((bf16[4,32,1024]{2,1,0:T(8,128)(2,1)S(1)}, bf16[4,32,1024]{2,1,0:T(8,128)(2,1)S(1)}, u32[]{:S(2)}, u32[]{:S(2)}) %collective-permute-start.32) | collective-permute-done | bytes 262176 | tf_op jit(solution)/shard_map/ppermute | solution.py:423
  108.1 0.1 collective-permute-start.34
  108.2 2.7 %collective-permute-done.31 = bf16[4,32,1024]{2,1,0:T(8,128)(2,1)S(1)} collective-permute-done((bf16[4,32,1024]{2,1,0:T(8,128)(2,1)S(1)}, bf16[4,32,1024]{2,1,0:T(8,128)(2,1)S(1)}, u32[]{:S(2)}, u32[]{:S(2)}) %collective-permute-start.31) | collective-permute-done | bytes 262176 | tf_op jit(solution)/shard_map/ppermute | solution.py:423
  111.0 0.5 collective-permute-start.30
  111.6 3.3 %shard_map.117 = (bf16[128,16384]{1,0:T(8,128)(2,1)}, bf16[128,1024]{1,0:T(8,128)(2,1)}) custom-call(f32[16,1024]{1,0:T(8,128)S(1)} %reshape.42.gain_ref, bf16[8,32,1024]{2,1,0:T(8,128)(2,1)S(1)} %constant_dynamic-update-slice_fusion.20.refs_0_, bf16[8,32,1024]{2,1,0:T(8,128)(2,1)} %collective-permute-done.34.refs_1_, ...), custom_call_target="tpu_custom_call" | custom-call | flops 6291456 | bytes 4194304 | tf_op jit(solution)/shard_map/pallas_call | solution.py:400
  114.9 2.1 %shard_map.118 = (bf16[128,16384]{1,0:T(8,128)(2,1)}, bf16[128,1024]{1,0:T(8,128)(2,1)}) custom-call(f32[16,1024]{1,0:T(8,128)S(1)} %reshape.42.gain_ref, bf16[8,32,1024]{2,1,0:T(8,128)(2,1)S(1)} %constant_dynamic-update-slice_fusion.18.refs_0_, ...), custom_call_target="tpu_custom_call", output_to_operand_aliasing={{0}: (5, {}), {1}: (6, {})} | custom-call | flops 6291456 | bytes 4194304 | tf_op jit(solution)/shard_map/pallas_call | solution.py:400
  (76 shorter events, 1.6 us)
Async XLA Ops:
  1.6 0.8 copy-start.1
  2.4 26.0 %copy-start = (bf16[8,1024,512]{2,1,0:T(8,128)(2,1)S(1)}, bf16[8,1024,512]{2,1,0:T(8,128)(2,1)}, u32[]{:S(2)}) copy-start(bf16[8,1024,512]{2,1,0:T(8,128)(2,1)} %keys_ref.1) | copy-start | bytes 25165828
  2.4 26.0 %copy-start.2 = (s32[8]{0:T(128)S(1)}, s32[8]{0:T(128)}, u32[]{:S(2)}) copy-start(s32[8]{0:T(128)} %lengths_ref.1) | copy-start | bytes 100
  49.4 1.6 %collective-permute-start = (bf16[4,32,1024]{2,1,0:T(8,128)(2,1)S(1)}, bf16[4,32,1024]{2,1,0:T(8,128)(2,1)S(1)}, u32[]{:S(2)}, u32[]{:S(2)}) collective-permute-start(bf16[4,32,1024]{2,1,0:T(8,128)(2,1)S(1)} %get-tuple-element.84), channel_id=1, source_target_pairs={{0,1},{1,0},{2,3},{3,2},{4,5},{5,4},{6,7},{7,6},{8,9},{9,8},{10,11... | collective-permute-start | bytes 786440 | tf_op jit(solution)/shard_map/ppermute | solution.py:423
  49.4 5.7 %collective-permute-start.4 = (bf16[4,32,1024]{2,1,0:T(8,128)(2,1)S(1)}, bf16[4,32,1024]{2,1,0:T(8,128)(2,1)S(1)}, u32[]{:S(2)}, u32[]{:S(2)}) collective-permute-start(bf16[4,32,1024]{2,1,0:T(8,128)(2,1)S(1)} %get-tuple-element.92), channel_id=1, source_target_pairs={{0,1},{1,0},{2,3},{3,2},{4,5},{5,4},{6,7},{7,6},{8,9},{9,8},{10,11... | collective-permute-start | bytes 786440 | tf_op jit(solution)/shard_map/ppermute | solution.py:423
  49.9 5.3 %collective-permute-start.5 = (bf16[4,32,1024]{2,1,0:T(8,128)(2,1)S(1)}, bf16[4,32,1024]{2,1,0:T(8,128)(2,1)S(1)}, u32[]{:S(2)}, u32[]{:S(2)}) collective-permute-start(bf16[4,32,1024]{2,1,0:T(8,128)(2,1)S(1)} %get-tuple-element.94), channel_id=1, source_target_pairs={{0,1},{1,0},{2,3},{3,2},{4,5},{5,4},{6,7},{7,6},{8,9},{9,8},{10,11... | collective-permute-start | bytes 786440 | tf_op jit(solution)/shard_map/ppermute | solution.py:423
  50.0 7.5 %collective-permute-start.7 = (bf16[4,32,1024]{2,1,0:T(8,128)(2,1)S(1)}, bf16[4,32,1024]{2,1,0:T(8,128)(2,1)S(1)}, u32[]{:S(2)}, u32[]{:S(2)}) collective-permute-start(bf16[4,32,1024]{2,1,0:T(8,128)(2,1)S(1)} %get-tuple-element.100), channel_id=1, source_target_pairs={{0,1},{1,0},{2,3},{3,2},{4,5},{5,4},{6,7},{7,6},{8,9},{9,8},{10,11... | collective-permute-start | bytes 786440 | tf_op jit(solution)/shard_map/ppermute | solution.py:423
  51.0 9.1 %collective-permute-start.2 = (bf16[4,32,1024]{2,1,0:T(8,128)(2,1)S(1)}, bf16[4,32,1024]{2,1,0:T(8,128)(2,1)S(1)}, u32[]{:S(2)}, u32[]{:S(2)}) collective-permute-start(bf16[4,32,1024]{2,1,0:T(8,128)(2,1)S(1)} %add_convert_fusion.7), channel_id=1, source_target_pairs={{0,2},{1,3},{2,0},{3,1},{4,6},{5,7},{6,4},{7,5},{8,10},{9,11},{10,... | collective-permute-start | bytes 786440 | tf_op jit(solution)/shard_map/ppermute | solution.py:423
  55.0 2.9 %collective-permute-start.3 = (bf16[4,32,1024]{2,1,0:T(8,128)(2,1)S(1)}, bf16[4,32,1024]{2,1,0:T(8,128)(2,1)S(1)}, u32[]{:S(2)}, u32[]{:S(2)}) collective-permute-start(bf16[4,32,1024]{2,1,0:T(8,128)(2,1)S(1)} %get-tuple-element.90), channel_id=1, source_target_pairs={{0,1},{1,0},{2,3},{3,2},{4,5},{5,4},{6,7},{7,6},{8,9},{9,8},{10,11... | collective-permute-start | bytes 786440 | tf_op jit(solution)/shard_map/ppermute | solution.py:423
  55.4 9.7 %collective-permute-start.9 = (bf16[4,32,1024]{2,1,0:T(8,128)(2,1)S(1)}, bf16[4,32,1024]{2,1,0:T(8,128)(2,1)S(1)}, u32[]{:S(2)}, u32[]{:S(2)}) collective-permute-start(bf16[4,32,1024]{2,1,0:T(8,128)(2,1)S(1)} %add_convert_fusion.3), channel_id=1, source_target_pairs={{0,2},{1,3},{2,0},{3,1},{4,6},{5,7},{6,4},{7,5},{8,10},{9,11},{10,... | collective-permute-start | bytes 786440 | tf_op jit(solution)/shard_map/ppermute | solution.py:423
  57.3 1.5 %collective-permute-start.1 = (bf16[4,32,1024]{2,1,0:T(8,128)(2,1)S(1)}, bf16[4,32,1024]{2,1,0:T(8,128)(2,1)S(1)}, u32[]{:S(2)}, u32[]{:S(2)}) collective-permute-start(bf16[4,32,1024]{2,1,0:T(8,128)(2,1)S(1)} %get-tuple-element.87), channel_id=1, source_target_pairs={{0,1},{1,0},{2,3},{3,2},{4,5},{5,4},{6,7},{7,6},{8,9},{9,8},{10,11... | collective-permute-start | bytes 786440 | tf_op jit(solution)/shard_map/ppermute | solution.py:423
  57.5 3.6 %collective-permute-start.8 = (bf16[4,32,1024]{2,1,0:T(8,128)(2,1)S(1)}, bf16[4,32,1024]{2,1,0:T(8,128)(2,1)S(1)}, u32[]{:S(2)}, u32[]{:S(2)}) collective-permute-start(bf16[4,32,1024]{2,1,0:T(8,128)(2,1)S(1)} %get-tuple-element.102), channel_id=1, source_target_pairs={{0,1},{1,0},{2,3},{3,2},{4,5},{5,4},{6,7},{7,6},{8,9},{9,8},{10,11... | collective-permute-start | bytes 786440 | tf_op jit(solution)/shard_map/ppermute | solution.py:423
  57.9 8.3 %collective-permute-start.15 = (bf16[4,32,1024]{2,1,0:T(8,128)(2,1)S(1)}, bf16[4,32,1024]{2,1,0:T(8,128)(2,1)S(1)}, u32[]{:S(2)}, u32[]{:S(2)}) collective-permute-start(bf16[4,32,1024]{2,1,0:T(8,128)(2,1)S(1)} %get-tuple-element.115), channel_id=1, source_target_pairs={{0,1},{1,0},{2,3},{3,2},{4,5},{5,4},{6,7},{7,6},{8,9},{9,8},{10,11... | collective-permute-start | bytes 786440 | tf_op jit(solution)/shard_map/ppermute | solution.py:423
  58.3 53.2 %copy-start.3 = (bf16[16384]{0:T(1024)(128)(2,1)S(1)}, bf16[16384]{0:T(1024)(128)(2,1)}, u32[]{:S(2)}) copy-start(bf16[16384]{0:T(1024)(128)(2,1)} %param.17) | copy-start | bytes 98308
  58.9 15.1 %collective-permute-start.11 = (bf16[4,32,1024]{2,1,0:T(8,128)(2,1)S(1)}, bf16[4,32,1024]{2,1,0:T(8,128)(2,1)S(1)}, u32[]{:S(2)}, u32[]{:S(2)}) collective-permute-start(bf16[4,32,1024]{2,1,0:T(8,128)(2,1)S(1)} %pad_maximum_fusion), channel_id=1, source_target_pairs={{0,4},{1,5},{2,6},{3,7},{4,0},{5,1},{6,2},{7,3},{8,12},{9,13},{10,... | collective-permute-start | bytes 786440 | tf_op jit(solution)/shard_map/ppermute | solution.py:423
  60.3 10.6 %collective-permute-start.6 = (bf16[2,32,1024]{2,1,0:T(8,128)(2,1)S(1)}, bf16[2,32,1024]{2,1,0:T(8,128)(2,1)S(1)}, u32[]{:S(2)}, u32[]{:S(2)}) collective-permute-start(bf16[2,32,1024]{2,1,0:T(8,128)(2,1)S(1)} %get-tuple-element.166), channel_id=1, source_target_pairs={{0,4},{1,5},{2,6},{3,7},{4,0},{5,1},{6,2},{7,3},{8,12},{9,13},{10,... | collective-permute-start | bytes 393224 | tf_op jit(solution)/shard_map/ppermute | solution.py:423
  65.1 7.7 %collective-permute-start.12 = (bf16[2,32,1024]{2,1,0:T(8,128)(2,1)S(1)}, bf16[2,32,1024]{2,1,0:T(8,128)(2,1)S(1)}, u32[]{:S(2)}, u32[]{:S(2)}) collective-permute-start(bf16[2,32,1024]{2,1,0:T(8,128)(2,1)S(1)} %get-tuple-element.165), channel_id=1, source_target_pairs={{0,4},{1,5},{2,6},{3,7},{4,0},{5,1},{6,2},{7,3},{8,12},{9,13},{10,... | collective-permute-start | bytes 393224 | tf_op jit(solution)/shard_map/ppermute | solution.py:423
  65.2 12.1 %collective-permute-start.16 = (bf16[4,32,1024]{2,1,0:T(8,128)(2,1)S(1)}, bf16[4,32,1024]{2,1,0:T(8,128)(2,1)S(1)}, u32[]{:S(2)}, u32[]{:S(2)}) collective-permute-start(bf16[4,32,1024]{2,1,0:T(8,128)(2,1)S(1)} %add_convert_fusion.2), channel_id=1, source_target_pairs={{0,2},{1,3},{2,0},{3,1},{4,6},{5,7},{6,4},{7,5},{8,10},{9,11},{10,... | collective-permute-start | bytes 786440 | tf_op jit(solution)/shard_map/ppermute | solution.py:423
  70.8 6.4 %collective-permute-start.10 = (bf16[1,32,1024]{2,1,0:T(8,128)(2,1)S(1)}, bf16[1,32,1024]{2,1,0:T(8,128)(2,1)S(1)}, u32[]{:S(2)}, u32[]{:S(2)}) collective-permute-start(bf16[1,32,1024]{2,1,0:T(8,128)(2,1)S(1)} %get-tuple-element.178), channel_id=1, source_target_pairs={{0,8},{1,9},{2,10},{3,11},{4,12},{5,13},{6,14},{7,15},{8,0},{9,1},... | collective-permute-start | bytes 196616 | tf_op jit(solution)/shard_map/ppermute | solution.py:423
  72.9 7.7 %collective-permute-start.14 = (bf16[1,32,1024]{2,1,0:T(8,128)(2,1)S(1)}, bf16[1,32,1024]{2,1,0:T(8,128)(2,1)S(1)}, u32[]{:S(2)}, u32[]{:S(2)}) collective-permute-start(bf16[1,32,1024]{2,1,0:T(8,128)(2,1)S(1)} %get-tuple-element.173), channel_id=1, source_target_pairs={{0,8},{1,9},{2,10},{3,11},{4,12},{5,13},{6,14},{7,15},{8,0},{9,1},... | collective-permute-start | bytes 196616 | tf_op jit(solution)/shard_map/ppermute | solution.py:423
  74.0 8.9 %collective-permute-start.18 = (bf16[2,32,1024]{2,1,0:T(8,128)(2,1)S(1)}, bf16[2,32,1024]{2,1,0:T(8,128)(2,1)S(1)}, u32[]{:S(2)}, u32[]{:S(2)}) collective-permute-start(bf16[2,32,1024]{2,1,0:T(8,128)(2,1)S(1)} %get-tuple-element.163), channel_id=1, source_target_pairs={{0,2},{1,3},{2,0},{3,1},{4,6},{5,7},{6,4},{7,5},{8,10},{9,11},{10,... | collective-permute-start | bytes 393224 | tf_op jit(solution)/shard_map/ppermute | solution.py:423
  77.3 5.5 %collective-permute-start.13 = (bf16[1,32,1024]{2,1,0:T(8,128)(2,1)S(1)}, bf16[1,32,1024]{2,1,0:T(8,128)(2,1)S(1)}, u32[]{:S(2)}, u32[]{:S(2)}) collective-permute-start(bf16[1,32,1024]{2,1,0:T(8,128)(2,1)S(1)} %fusion.5), channel_id=1, source_target_pairs={{0,8},{1,9},{2,10},{3,11},{4,12},{5,13},{6,14},{7,15},{8,0},{9,1},... | collective-permute-start | bytes 196616 | tf_op jit(solution)/shard_map/ppermute | solution.py:423
  77.5 8.9 %collective-permute-start.21 = (bf16[2,32,1024]{2,1,0:T(8,128)(2,1)S(1)}, bf16[2,32,1024]{2,1,0:T(8,128)(2,1)S(1)}, u32[]{:S(2)}, u32[]{:S(2)}) collective-permute-start(bf16[2,32,1024]{2,1,0:T(8,128)(2,1)S(1)} %get-tuple-element.161), channel_id=1, source_target_pairs={{0,4},{1,5},{2,6},{3,7},{4,0},{5,1},{6,2},{7,3},{8,12},{9,13},{10,... | collective-permute-start | bytes 393224 | tf_op jit(solution)/shard_map/ppermute | solution.py:423
  80.6 6.2 %collective-permute-start.20 = (bf16[1,32,1024]{2,1,0:T(8,128)(2,1)S(1)}, bf16[1,32,1024]{2,1,0:T(8,128)(2,1)S(1)}, u32[]{:S(2)}, u32[]{:S(2)}) collective-permute-start(bf16[1,32,1024]{2,1,0:T(8,128)(2,1)S(1)} %fusion.6), channel_id=1, source_target_pairs={{0,8},{1,9},{2,10},{3,11},{4,12},{5,13},{6,14},{7,15},{8,0},{9,1},... | collective-permute-start | bytes 196616 | tf_op jit(solution)/shard_map/ppermute | solution.py:423
  82.8 8.8 %collective-permute-start.17 = (bf16[2,32,1024]{2,1,0:T(8,128)(2,1)S(1)}, bf16[2,32,1024]{2,1,0:T(8,128)(2,1)S(1)}, u32[]{:S(2)}, u32[]{:S(2)}) collective-permute-start(bf16[2,32,1024]{2,1,0:T(8,128)(2,1)S(1)} %constant_dynamic-update-slice_fusion), channel_id=1, source_target_pairs={{0,4},{1,5},{2,6},{3,7},{4,0},{5,1},{6,2},{7,3},{8,12},{9,13},{10,... | collective-permute-start | bytes 393224 | tf_op jit(solution)/shard_map/ppermute | solution.py:423
  83.0 6.5 %collective-permute-start.19 = (bf16[1,32,1024]{2,1,0:T(8,128)(2,1)S(1)}, bf16[1,32,1024]{2,1,0:T(8,128)(2,1)S(1)}, u32[]{:S(2)}, u32[]{:S(2)}) collective-permute-start(bf16[1,32,1024]{2,1,0:T(8,128)(2,1)S(1)} %get-tuple-element.170), channel_id=1, source_target_pairs={{0,8},{1,9},{2,10},{3,11},{4,12},{5,13},{6,14},{7,15},{8,0},{9,1},... | collective-permute-start | bytes 196616 | tf_op jit(solution)/shard_map/ppermute | solution.py:423
  86.4 7.2 %collective-permute-start.25 = (bf16[1,32,1024]{2,1,0:T(8,128)(2,1)S(1)}, bf16[1,32,1024]{2,1,0:T(8,128)(2,1)S(1)}, u32[]{:S(2)}, u32[]{:S(2)}) collective-permute-start(bf16[1,32,1024]{2,1,0:T(8,128)(2,1)S(1)} %get-tuple-element.169), channel_id=1, source_target_pairs={{0,8},{1,9},{2,10},{3,11},{4,12},{5,13},{6,14},{7,15},{8,0},{9,1},... | collective-permute-start | bytes 196616 | tf_op jit(solution)/shard_map/ppermute | solution.py:423
  86.9 9.9 %collective-permute-start.23 = (bf16[2,32,1024]{2,1,0:T(8,128)(2,1)S(1)}, bf16[2,32,1024]{2,1,0:T(8,128)(2,1)S(1)}, u32[]{:S(2)}, u32[]{:S(2)}) collective-permute-start(bf16[2,32,1024]{2,1,0:T(8,128)(2,1)S(1)} %constant_dynamic-update-slice_fusion.2), channel_id=1, source_target_pairs={{0,2},{1,3},{2,0},{3,1},{4,6},{5,7},{6,4},{7,5},{8,10},{9,11},{10,... | collective-permute-start | bytes 393224 | tf_op jit(solution)/shard_map/ppermute | solution.py:423
  89.5 5.5 %collective-permute-start.24 = (bf16[1,32,1024]{2,1,0:T(8,128)(2,1)S(1)}, bf16[1,32,1024]{2,1,0:T(8,128)(2,1)S(1)}, u32[]{:S(2)}, u32[]{:S(2)}) collective-permute-start(bf16[1,32,1024]{2,1,0:T(8,128)(2,1)S(1)} %fusion.7), channel_id=1, source_target_pairs={{0,8},{1,9},{2,10},{3,11},{4,12},{5,13},{6,14},{7,15},{8,0},{9,1},... | collective-permute-start | bytes 196616 | tf_op jit(solution)/shard_map/ppermute | solution.py:423
  91.7 14.9 %collective-permute-start.22 = (bf16[4,32,1024]{2,1,0:T(8,128)(2,1)S(1)}, bf16[4,32,1024]{2,1,0:T(8,128)(2,1)S(1)}, u32[]{:S(2)}, u32[]{:S(2)}) collective-permute-start(bf16[4,32,1024]{2,1,0:T(8,128)(2,1)S(1)} %constant_dynamic-update-slice_fusion.4), channel_id=1, source_target_pairs={{0,2},{1,3},{2,0},{3,1},{4,6},{5,7},{6,4},{7,5},{8,10},{9,11},{10,... | collective-permute-start | bytes 786440 | tf_op jit(solution)/shard_map/ppermute | solution.py:423
  93.6 5.8 %collective-permute-start.27 = (bf16[1,32,1024]{2,1,0:T(8,128)(2,1)S(1)}, bf16[1,32,1024]{2,1,0:T(8,128)(2,1)S(1)}, u32[]{:S(2)}, u32[]{:S(2)}) collective-permute-start(bf16[1,32,1024]{2,1,0:T(8,128)(2,1)S(1)} %fusion.8), channel_id=1, source_target_pairs={{0,8},{1,9},{2,10},{3,11},{4,12},{5,13},{6,14},{7,15},{8,0},{9,1},... | collective-permute-start | bytes 196616 | tf_op jit(solution)/shard_map/ppermute | solution.py:423
  95.0 6.6 %collective-permute-start.29 = (bf16[2,32,1024]{2,1,0:T(8,128)(2,1)S(1)}, bf16[2,32,1024]{2,1,0:T(8,128)(2,1)S(1)}, u32[]{:S(2)}, u32[]{:S(2)}) collective-permute-start(bf16[2,32,1024]{2,1,0:T(8,128)(2,1)S(1)} %constant_dynamic-update-slice_fusion.6), channel_id=1, source_target_pairs={{0,4},{1,5},{2,6},{3,7},{4,0},{5,1},{6,2},{7,3},{8,12},{9,13},{10,... | collective-permute-start | bytes 393224 | tf_op jit(solution)/shard_map/ppermute | solution.py:423
  96.8 9.6 %collective-permute-start.26 = (bf16[4,32,1024]{2,1,0:T(8,128)(2,1)S(1)}, bf16[4,32,1024]{2,1,0:T(8,128)(2,1)S(1)}, u32[]{:S(2)}, u32[]{:S(2)}) collective-permute-start(bf16[4,32,1024]{2,1,0:T(8,128)(2,1)S(1)} %constant_dynamic-update-slice_fusion.8), channel_id=1, source_target_pairs={{0,4},{1,5},{2,6},{3,7},{4,0},{5,1},{6,2},{7,3},{8,12},{9,13},{10,... | collective-permute-start | bytes 786440 | tf_op jit(solution)/shard_map/ppermute | solution.py:423
  99.4 5.0 %collective-permute-start.28 = (bf16[2,32,1024]{2,1,0:T(8,128)(2,1)S(1)}, bf16[2,32,1024]{2,1,0:T(8,128)(2,1)S(1)}, u32[]{:S(2)}, u32[]{:S(2)}) collective-permute-start(bf16[2,32,1024]{2,1,0:T(8,128)(2,1)S(1)} %constant_dynamic-update-slice_fusion.10), channel_id=1, source_target_pairs={{0,2},{1,3},{2,0},{3,1},{4,6},{5,7},{6,4},{7,5},{8,10},{9,11},{10,... | collective-permute-start | bytes 393224 | tf_op jit(solution)/shard_map/ppermute | solution.py:423
  101.6 6.4 %collective-permute-start.32 = (bf16[4,32,1024]{2,1,0:T(8,128)(2,1)S(1)}, bf16[4,32,1024]{2,1,0:T(8,128)(2,1)S(1)}, u32[]{:S(2)}, u32[]{:S(2)}) collective-permute-start(bf16[4,32,1024]{2,1,0:T(8,128)(2,1)S(1)} %constant_dynamic-update-slice_fusion.12), channel_id=1, source_target_pairs={{0,2},{1,3},{2,0},{3,1},{4,6},{5,7},{6,4},{7,5},{8,10},{9,11},{10,... | collective-permute-start | bytes 786440 | tf_op jit(solution)/shard_map/ppermute | solution.py:423
  104.5 6.4 %collective-permute-start.31 = (bf16[4,32,1024]{2,1,0:T(8,128)(2,1)S(1)}, bf16[4,32,1024]{2,1,0:T(8,128)(2,1)S(1)}, u32[]{:S(2)}, u32[]{:S(2)}) collective-permute-start(bf16[4,32,1024]{2,1,0:T(8,128)(2,1)S(1)} %constant_dynamic-update-slice_fusion.14), channel_id=1, source_target_pairs={{0,4},{1,5},{2,6},{3,7},{4,0},{5,1},{6,2},{7,3},{8,12},{9,13},{10,... | collective-permute-start | bytes 786440 | tf_op jit(solution)/shard_map/ppermute | solution.py:423
  106.5 5.1 %collective-permute-start.35 = (bf16[8,32,1024]{2,1,0:T(8,128)(2,1)S(1)}, bf16[8,32,1024]{2,1,0:T(8,128)(2,1)}, u32[]{:S(2)}, u32[]{:S(2)}) collective-permute-start(bf16[8,32,1024]{2,1,0:T(8,128)(2,1)S(1)} %constant_dynamic-update-slice_fusion.16.refs_2_), channel_id=1, source_target_pairs={{0,1},{1,0},{2,3},{3,2},{4,5},{5,4},{6,7},{7,6},{8,9},{9,8},{10,11... | collective-permute-start | bytes 1572872 | tf_op jit(solution)/shard_map/ppermute | solution.py:423
  108.1 3.5 %collective-permute-start.34 = (bf16[8,32,1024]{2,1,0:T(8,128)(2,1)S(1)}, bf16[8,32,1024]{2,1,0:T(8,128)(2,1)}, u32[]{:S(2)}, u32[]{:S(2)}) collective-permute-start(bf16[8,32,1024]{2,1,0:T(8,128)(2,1)S(1)} %constant_dynamic-update-slice_fusion.20.refs_0_), channel_id=1, source_target_pairs={{0,1},{1,0},{2,3},{3,2},{4,5},{5,4},{6,7},{7,6},{8,9},{9,8},{10,11... | collective-permute-start | bytes 1572872 | tf_op jit(solution)/shard_map/ppermute | solution.py:423
  111.0 3.9 %collective-permute-start.33 = (bf16[8,32,1024]{2,1,0:T(8,128)(2,1)S(1)}, bf16[8,32,1024]{2,1,0:T(8,128)(2,1)S(1)}, u32[]{:S(2)}, u32[]{:S(2)}) collective-permute-start(bf16[8,32,1024]{2,1,0:T(8,128)(2,1)S(1)} %constant_dynamic-update-slice_fusion.22.refs_2_), channel_id=1, source_target_pairs={{0,1},{1,0},{2,3},{3,2},{4,5},{5,4},{6,7},{7,6},{8,9},{9,8},{10,11... | collective-permute-start | bytes 1572872 | tf_op jit(solution)/shard_map/ppermute | solution.py:423
  111.0 3.9 %collective-permute-start.30 = (bf16[8,32,1024]{2,1,0:T(8,128)(2,1)S(1)}, bf16[8,32,1024]{2,1,0:T(8,128)(2,1)S(1)}, u32[]{:S(2)}, u32[]{:S(2)}) collective-permute-start(bf16[8,32,1024]{2,1,0:T(8,128)(2,1)S(1)} %constant_dynamic-update-slice_fusion.18.refs_0_), channel_id=1, source_target_pairs={{0,1},{1,0},{2,3},{3,2},{4,5},{5,4},{6,7},{7,6},{8,9},{9,8},{10,11... | collective-permute-start | bytes 1572872 | tf_op jit(solution)/shard_map/ppermute | solution.py:423

commit v12 on v11

--- a/solution.py
+++ b/solution.py
@@ -11,7 +11,7 @@
 HD = 128
 
 
-TABLE = "032031032013021320123121302131"
+TABLE = "032031032013023120123121302131"
 
 epsilon = 1e-05
 rope_theta = 500000.0

time: 117 us -> 119 us (1.017)
  transfers between devices with their start and end apart: 36 -> 36, of which waited for: 19 -> 18; matrix products, arithmetic and copies ran while one was open for 1% -> 1% of each run, Pallas kernels for 6% -> 6%
where the time goes in v12:
time: 119 us; the launch traced here: 118 us
  waiting for transfers between devices  35.5 us (30%)
  Pallas kernels  30.1 us (25%)
  blocking collectives  26.2 us (22%)
  starting transfers between devices  22.3 us (19%)
  other arithmetic  2.08 us (2%)
    ppermute x36, waiting for transfers between devices, swap(): lax.ppermute(values, 'tensor', [(i, i ^ 1 << bit) for i in range(count)])  35.5 us
    all_to_all x2, blocking collectives, exchange(): lax.all_to_all(blocks, 'tensor', split_axis=0, concat_axis=0, tiled=True)  26.2 us
    ppermute x36, starting transfers between devices, swap(): lax.ppermute(values, 'tensor', [(i, i ^ 1 << bit) for i in range(count)])  22.3 us
    pallas_call x1, Pallas kernels, project_in(): pl.pallas_call(functools.partial(input_kernel, count), out_shape=(jax.Sha...  10.3 us
    pallas_call x2, Pallas kernels, project(): pl.pallas_call(functools.partial(project_kernel, count, side), out_shape=...  7.67 us
    pallas_call x1, Pallas kernels, attend(): pl.pallas_call(functools.partial(attend_kernel, count), out_shape=jax.Sha...  6.62 us
    pallas_call x2, Pallas kernels, finish(): pl.pallas_call(functools.partial(finish_kernel, offsets), grid=(count,),...  5.44 us
  transfers between devices with their start and end apart: 36, of which 18 were waited for; matrix products, arithmetic and copies ran while one was open for 1% of the time, Pallas kernels for 6%

profile of v12, /device:TPU:0, one launch (start us, length us, event | category | flops | bytes accessed | tf_op | source)
XLA Modules:
  0.0 118.3 jit_solution(12467109969901991955)
XLA Ops:
  0.6 0.7 convert_element_type.283
  1.3 0.3 fusion.4
  1.6 0.7 copy-done.1
  2.4 10.3 %shard_map.113 = (bf16[16,8,640]{2,1,0:T(8,128)(2,1)S(1)}, bf16[128,1024]{1,0:T(8,128)(2,1)S(1)}) custom-call(bf16[128,16384]{1,0:T(8,128)(2,1)} %hidden_ref.1, bf16[16384]{0:T(1024)(128)(2,1)S(1)} %copy-done.1, bf16[16384,512]{1,0:T(8,128)(2,1)} %w_ref.3, bf16[64,16384]{1,0:T(8,128)(2,1)} %bitcast.33, f32[128,128]{1,0:T(8,128)S(1)} %get-tuple-element.181.cosine_ref, ...), custom_call_target="tpu_custom_call" | custom-call | flops 2415919104 | bytes 23068672 | tf_op jit(solution)/shard_map/pallas_call | solution.py:120
  12.7 15.7 %all_to_all.10.refs_0_ = bf16[16,8,640]{2,1,0:T(8,128)(2,1)S(1)} all-to-all(bf16[16,8,640]{2,1,0:T(8,128)(2,1)S(1)} %get-tuple-element.82), channel_id=1, replica_groups=mesh['groups'=2,'tensor'=16] {'tensor'}, dimensions={0} | all-to-all | bytes 327680 | tf_op jit(solution)/shard_map/all_to_all | solution.py:284
  28.4 6.6 %shard_map.114 = bf16[16,8,512]{2,1,0:T(8,128)(2,1)S(1)} custom-call(s32[8]{0:T(128)S(1)} %copy-done.2, f32[128,128]{1,0:T(8,128)S(1)} %get-tuple-element.181.cosine_ref, f32[128,128]{1,0:T(8,128)S(1)} %get-tuple-element.180.sine_ref, bf16[8,1024,512]{2,1,0:T(8,128)(2,1)S(1)} %copy-done, bf16[8,1024,512]{2,1,0:T(8,128)(2,1)} %values_ref.1, ...), custom_call_target="tpu_custom_call" | custom-call | flops 268435456 | bytes 16777216 | tf_op jit(solution)/shard_map/pallas_call | solution.py:259
  35.0 10.5 %all_to_all.11.in_ref = bf16[16,8,512]{2,1,0:T(8,128)(2,1)S(1)} all-to-all(bf16[16,8,512]{2,1,0:T(8,128)(2,1)S(1)} %shard_map.114), channel_id=1, replica_groups=mesh['groups'=2,'tensor'=16] {'tensor'}, dimensions={0} | all-to-all | bytes 262144 | tf_op jit(solution)/shard_map/all_to_all | solution.py:284
  45.5 3.8 %shard_map.115 = (bf16[4,32,1024]{2,1,0:T(8,128)(2,1)S(1)}, bf16[4,32,1024]{2,1,0:T(8,128)(2,1)S(1)}, bf16[4,32,1024]{2,1,0:T(8,128)(2,1)S(1)}, bf16[4,32,1024]{...) custom-call(bf16[16,8,512]{2,1,0:T(8,128)(2,1)S(1)} %all_to_all.11.i, ...), custom_call_target="tpu_custom_call" | custom-call | flops 1073741824 | bytes 10485760 | tf_op jit(solution)/shard_map/pallas_call | solution.py:347
  49.4 0.1 collective-permute-start
  49.4 0.5 collective-permute-start.4
  49.9 0.1 collective-permute-start.5
  50.0 0.4 collective-permute-start.7
  50.5 0.5 collective-permute-done
  51.0 0.1 collective-permute-start.2
  51.1 3.8 %shard_map.116 = (bf16[4,32,1024]{2,1,0:T(8,128)(2,1)S(1)}, bf16[4,32,1024]{2,1,0:T(8,128)(2,1)S(1)}, bf16[4,32,1024]{2,1,0:T(8,128)(2,1)S(1)}, bf16[4,32,1024]{...) custom-call(bf16[16,8,512]{2,1,0:T(8,128)(2,1)S(1)} %all_to_all.11.i, ...), custom_call_target="tpu_custom_call" | custom-call | flops 1073741824 | bytes 10485760 | tf_op jit(solution)/shard_map/pallas_call | solution.py:347
  55.0 0.2 collective-permute-start.3
  55.4 2.0 %collective-permute-start.9 = (bf16[4,32,1024]{2,1,0:T(8,128)(2,1)S(1)}, bf16[4,32,1024]{2,1,0:T(8,128)(2,1)S(1)}, u32[]{:S(2)}, u32[]{:S(2)}) collective-permute-start(bf16[4,32,1024]{2,1,0:T(8,128)(2,1)S(1)} %add_convert_fusion.3), channel_id=1, source_target_pairs={{0,2},{1,3},{2,0},{3,1},{4,6},{5,7},{6,4},{7,5},{8,10},{9,11},{10,... | collective-permute-start | bytes 786440 | tf_op jit(solution)/shard_map/ppermute | solution.py:423
  57.3 0.2 collective-permute-start.1
  57.5 0.3 collective-permute-start.8
  57.9 0.3 collective-permute-start.15
  58.3 0.5 collective-permute-done.1
  58.9 1.3 %collective-permute-done.2 = bf16[4,32,1024]{2,1,0:T(8,128)(2,1)S(1)} collective-permute-done((bf16[4,32,1024]{2,1,0:T(8,128)(2,1)S(1)}, bf16[4,32,1024]{2,1,0:T(8,128)(2,1)S(1)}, u32[]{:S(2)}, u32[]{:S(2)}) %collective-permute-start.2) | collective-permute-done | bytes 262176 | tf_op jit(solution)/shard_map/ppermute | solution.py:423
  60.3 0.8 collective-permute-start.6
  61.2 3.9 %collective-permute-done.9 = bf16[4,32,1024]{2,1,0:T(8,128)(2,1)S(1)} collective-permute-done((bf16[4,32,1024]{2,1,0:T(8,128)(2,1)S(1)}, bf16[4,32,1024]{2,1,0:T(8,128)(2,1)S(1)}, u32[]{:S(2)}, u32[]{:S(2)}) %collective-permute-start.9) | collective-permute-done | bytes 262176 | tf_op jit(solution)/shard_map/ppermute | solution.py:423
  65.1 0.1 collective-permute-start.12
  65.2 1.0 collective-permute-start.16
  66.3 4.5 %collective-permute-done.6 = bf16[2,32,1024]{2,1,0:T(8,128)(2,1)S(1)} collective-permute-done((bf16[2,32,1024]{2,1,0:T(8,128)(2,1)S(1)}, bf16[2,32,1024]{2,1,0:T(8,128)(2,1)S(1)}, u32[]{:S(2)}, u32[]{:S(2)}) %collective-permute-start.6) | collective-permute-done | bytes 131104 | tf_op jit(solution)/shard_map/ppermute | solution.py:423
  70.8 0.4 collective-permute-start.10
  71.2 1.7 %collective-permute-done.12 = bf16[2,32,1024]{2,1,0:T(8,128)(2,1)S(1)} collective-permute-done((bf16[2,32,1024]{2,1,0:T(8,128)(2,1)S(1)}, bf16[2,32,1024]{2,1,0:T(8,128)(2,1)S(1)}, u32[]{:S(2)}, u32[]{:S(2)}) %collective-permute-start.12) | collective-permute-done | bytes 131104 | tf_op jit(solution)/shard_map/ppermute | solution.py:423
  72.9 1.0 collective-permute-start.14
  74.0 0.2 collective-permute-start.18
  74.3 3.0 %collective-permute-done.10 = bf16[1,32,1024]{2,1,0:T(8,128)(2,1)S(1)} collective-permute-done((bf16[1,32,1024]{2,1,0:T(8,128)(2,1)S(1)}, bf16[1,32,1024]{2,1,0:T(8,128)(2,1)S(1)}, u32[]{:S(2)}, u32[]{:S(2)}) %collective-permute-start.10) | collective-permute-done | bytes 65568 | tf_op jit(solution)/shard_map/ppermute | solution.py:423
  77.3 0.1 collective-permute-start.13
  77.5 1.8 %collective-permute-start.20 = (bf16[2,32,1024]{2,1,0:T(8,128)(2,1)S(1)}, bf16[2,32,1024]{2,1,0:T(8,128)(2,1)S(1)}, u32[]{:S(2)}, u32[]{:S(2)}) collective-permute-start(bf16[2,32,1024]{2,1,0:T(8,128)(2,1)S(1)} %get-tuple-element.161), channel_id=1, source_target_pairs={{0,4},{1,5},{2,6},{3,7},{4,0},{5,1},{6,2},{7,3},{8,12},{9,13},{10,... | collective-permute-start | bytes 393224 | tf_op jit(solution)/shard_map/ppermute | solution.py:423
  79.2 1.4 %collective-permute-done.14 = bf16[1,32,1024]{2,1,0:T(8,128)(2,1)S(1)} collective-permute-done((bf16[1,32,1024]{2,1,0:T(8,128)(2,1)S(1)}, bf16[1,32,1024]{2,1,0:T(8,128)(2,1)S(1)}, u32[]{:S(2)}, u32[]{:S(2)}) %collective-permute-start.14) | collective-permute-done | bytes 65568 | tf_op jit(solution)/shard_map/ppermute | solution.py:423
  80.6 0.1 collective-permute-start.21
  80.7 2.1 %collective-permute-done.13 = bf16[1,32,1024]{2,1,0:T(8,128)(2,1)S(1)} collective-permute-done((bf16[1,32,1024]{2,1,0:T(8,128)(2,1)S(1)}, bf16[1,32,1024]{2,1,0:T(8,128)(2,1)S(1)}, u32[]{:S(2)}, u32[]{:S(2)}) %collective-permute-start.13) | collective-permute-done | bytes 65568 | tf_op jit(solution)/shard_map/ppermute | solution.py:423
  82.8 0.1 collective-permute-start.17
  83.0 3.4 %collective-permute-start.19 = (bf16[1,32,1024]{2,1,0:T(8,128)(2,1)S(1)}, bf16[1,32,1024]{2,1,0:T(8,128)(2,1)S(1)}, u32[]{:S(2)}, u32[]{:S(2)}) collective-permute-start(bf16[1,32,1024]{2,1,0:T(8,128)(2,1)S(1)} %get-tuple-element.170), channel_id=1, source_target_pairs={{0,8},{1,9},{2,10},{3,11},{4,12},{5,13},{6,14},{7,15},{8,0},{9,1},... | collective-permute-start | bytes 196616 | tf_op jit(solution)/shard_map/ppermute | solution.py:423
  86.4 0.9 collective-permute-start.23
  87.3 1.8 %collective-permute-start.25 = (bf16[1,32,1024]{2,1,0:T(8,128)(2,1)S(1)}, bf16[1,32,1024]{2,1,0:T(8,128)(2,1)S(1)}, u32[]{:S(2)}, u32[]{:S(2)}) collective-permute-start(bf16[1,32,1024]{2,1,0:T(8,128)(2,1)S(1)} %get-tuple-element.169), channel_id=1, source_target_pairs={{0,8},{1,9},{2,10},{3,11},{4,12},{5,13},{6,14},{7,15},{8,0},{9,1},... | collective-permute-start | bytes 196616 | tf_op jit(solution)/shard_map/ppermute | solution.py:423
  89.2 1.6 %collective-permute-done.19 = bf16[1,32,1024]{2,1,0:T(8,128)(2,1)S(1)} collective-permute-done((bf16[1,32,1024]{2,1,0:T(8,128)(2,1)S(1)}, bf16[1,32,1024]{2,1,0:T(8,128)(2,1)S(1)}, u32[]{:S(2)}, u32[]{:S(2)}) %collective-permute-start.19) | collective-permute-done | bytes 65568 | tf_op jit(solution)/shard_map/ppermute | solution.py:423
  90.8 0.9 collective-permute-start.24
  91.7 0.9 collective-permute-start.22
  92.7 2.1 %collective-permute-done.25 = bf16[1,32,1024]{2,1,0:T(8,128)(2,1)S(1)} collective-permute-done((bf16[1,32,1024]{2,1,0:T(8,128)(2,1)S(1)}, bf16[1,32,1024]{2,1,0:T(8,128)(2,1)S(1)}, u32[]{:S(2)}, u32[]{:S(2)}) %collective-permute-start.25) | collective-permute-done | bytes 65568 | tf_op jit(solution)/shard_map/ppermute | solution.py:423
  94.8 0.2 collective-permute-start.27
  95.0 1.4 %collective-permute-done.24 = bf16[1,32,1024]{2,1,0:T(8,128)(2,1)S(1)} collective-permute-done((bf16[1,32,1024]{2,1,0:T(8,128)(2,1)S(1)}, bf16[1,32,1024]{2,1,0:T(8,128)(2,1)S(1)}, u32[]{:S(2)}, u32[]{:S(2)}) %collective-permute-start.24) | collective-permute-done | bytes 65568 | tf_op jit(solution)/shard_map/ppermute | solution.py:423
  96.5 0.4 collective-permute-start.29
  96.9 1.8 %collective-permute-start.26 = (bf16[4,32,1024]{2,1,0:T(8,128)(2,1)S(1)}, bf16[4,32,1024]{2,1,0:T(8,128)(2,1)S(1)}, u32[]{:S(2)}, u32[]{:S(2)}) collective-permute-start(bf16[4,32,1024]{2,1,0:T(8,128)(2,1)S(1)} %constant_dynamic-update-slice_fusion.8), channel_id=1, source_target_pairs={{0,4},{1,5},{2,6},{3,7},{4,0},{5,1},{6,2},{7,3},{8,12},{9,13},{10,... | collective-permute-start | bytes 786440 | tf_op jit(solution)/shard_map/ppermute | solution.py:423
  98.6 2.0 %collective-permute-done.27 = bf16[1,32,1024]{2,1,0:T(8,128)(2,1)S(1)} collective-permute-done((bf16[1,32,1024]{2,1,0:T(8,128)(2,1)S(1)}, bf16[1,32,1024]{2,1,0:T(8,128)(2,1)S(1)}, u32[]{:S(2)}, u32[]{:S(2)}) %collective-permute-start.27) | collective-permute-done | bytes 65568 | tf_op jit(solution)/shard_map/ppermute | solution.py:423
  100.7 0.1 collective-permute-start.28
  100.8 1.1 collective-permute-done.29
  101.9 1.1 collective-permute-start.32
  103.0 2.7 %collective-permute-done.28 = bf16[2,32,1024]{2,1,0:T(8,128)(2,1)S(1)} collective-permute-done((bf16[2,32,1024]{2,1,0:T(8,128)(2,1)S(1)}, bf16[2,32,1024]{2,1,0:T(8,128)(2,1)S(1)}, u32[]{:S(2)}, u32[]{:S(2)}) %collective-permute-start.28) | collective-permute-done | bytes 131104 | tf_op jit(solution)/shard_map/ppermute | solution.py:423
  105.7 0.4 collective-permute-start.31
  106.1 0.8 collective-permute-done.26
  106.9 0.1 collective-permute-start.35
  107.1 1.5 %collective-permute-done.32 = bf16[4,32,1024]{2,1,0:T(8,128)(2,1)S(1)} collective-permute-done((bf16[4,32,1024]{2,1,0:T(8,128)(2,1)S(1)}, bf16[4,32,1024]{2,1,0:T(8,128)(2,1)S(1)}, u32[]{:S(2)}, u32[]{:S(2)}) %collective-permute-start.32) | collective-permute-done | bytes 262176 | tf_op jit(solution)/shard_map/ppermute | solution.py:423
  108.6 0.1 collective-permute-start.34
  108.7 3.5 %collective-permute-done.31 = bf16[4,32,1024]{2,1,0:T(8,128)(2,1)S(1)} collective-permute-done((bf16[4,32,1024]{2,1,0:T(8,128)(2,1)S(1)}, bf16[4,32,1024]{2,1,0:T(8,128)(2,1)S(1)}, u32[]{:S(2)}, u32[]{:S(2)}) %collective-permute-start.31) | collective-permute-done | bytes 262176 | tf_op jit(solution)/shard_map/ppermute | solution.py:423
  112.2 0.1 collective-permute-start.33
  112.3 0.5 collective-permute-start.30
  112.9 3.3 %shard_map.117 = (bf16[128,16384]{1,0:T(8,128)(2,1)}, bf16[128,1024]{1,0:T(8,128)(2,1)}) custom-call(f32[16,1024]{1,0:T(8,128)S(1)} %reshape.42.gain_ref, bf16[8,32,1024]{2,1,0:T(8,128)(2,1)S(1)} %constant_dynamic-update-slice_fusion.20.refs_0_, bf16[8,32,1024]{2,1,0:T(8,128)(2,1)} %collective-permute-done.34.refs_1_, ...), custom_call_target="tpu_custom_call" | custom-call | flops 6291456 | bytes 4194304 | tf_op jit(solution)/shard_map/pallas_call | solution.py:400
  116.2 2.1 %shard_map.118 = (bf16[128,16384]{1,0:T(8,128)(2,1)}, bf16[128,1024]{1,0:T(8,128)(2,1)}) custom-call(f32[16,1024]{1,0:T(8,128)S(1)} %reshape.42.gain_ref, bf16[8,32,1024]{2,1,0:T(8,128)(2,1)S(1)} %constant_dynamic-update-slice_fusion.18.refs_0_, ...), custom_call_target="tpu_custom_call", output_to_operand_aliasing={{0}: (5, {}), {1}: (6, {})} | custom-call | flops 6291456 | bytes 4194304 | tf_op jit(solution)/shard_map/pallas_call | solution.py:400
  (76 shorter events, 1.5 us)
Async XLA Ops:
  1.6 0.8 copy-start.1
  2.4 26.0 %copy-start = (bf16[8,1024,512]{2,1,0:T(8,128)(2,1)S(1)}, bf16[8,1024,512]{2,1,0:T(8,128)(2,1)}, u32[]{:S(2)}) copy-start(bf16[8,1024,512]{2,1,0:T(8,128)(2,1)} %keys_ref.1) | copy-start | bytes 25165828
  2.4 26.0 %copy-start.2 = (s32[8]{0:T(128)S(1)}, s32[8]{0:T(128)}, u32[]{:S(2)}) copy-start(s32[8]{0:T(128)} %lengths_ref.1) | copy-start | bytes 100
  49.4 1.6 %collective-permute-start = (bf16[4,32,1024]{2,1,0:T(8,128)(2,1)S(1)}, bf16[4,32,1024]{2,1,0:T(8,128)(2,1)S(1)}, u32[]{:S(2)}, u32[]{:S(2)}) collective-permute-start(bf16[4,32,1024]{2,1,0:T(8,128)(2,1)S(1)} %get-tuple-element.84), channel_id=1, source_target_pairs={{0,1},{1,0},{2,3},{3,2},{4,5},{5,4},{6,7},{7,6},{8,9},{9,8},{10,11... | collective-permute-start | bytes 786440 | tf_op jit(solution)/shard_map/ppermute | solution.py:423
  49.4 5.7 %collective-permute-start.4 = (bf16[4,32,1024]{2,1,0:T(8,128)(2,1)S(1)}, bf16[4,32,1024]{2,1,0:T(8,128)(2,1)S(1)}, u32[]{:S(2)}, u32[]{:S(2)}) collective-permute-start(bf16[4,32,1024]{2,1,0:T(8,128)(2,1)S(1)} %get-tuple-element.92), channel_id=1, source_target_pairs={{0,1},{1,0},{2,3},{3,2},{4,5},{5,4},{6,7},{7,6},{8,9},{9,8},{10,11... | collective-permute-start | bytes 786440 | tf_op jit(solution)/shard_map/ppermute | solution.py:423
  49.9 5.3 %collective-permute-start.5 = (bf16[4,32,1024]{2,1,0:T(8,128)(2,1)S(1)}, bf16[4,32,1024]{2,1,0:T(8,128)(2,1)S(1)}, u32[]{:S(2)}, u32[]{:S(2)}) collective-permute-start(bf16[4,32,1024]{2,1,0:T(8,128)(2,1)S(1)} %get-tuple-element.94), channel_id=1, source_target_pairs={{0,1},{1,0},{2,3},{3,2},{4,5},{5,4},{6,7},{7,6},{8,9},{9,8},{10,11... | collective-permute-start | bytes 786440 | tf_op jit(solution)/shard_map/ppermute | solution.py:423
  50.0 7.5 %collective-permute-start.7 = (bf16[4,32,1024]{2,1,0:T(8,128)(2,1)S(1)}, bf16[4,32,1024]{2,1,0:T(8,128)(2,1)S(1)}, u32[]{:S(2)}, u32[]{:S(2)}) collective-permute-start(bf16[4,32,1024]{2,1,0:T(8,128)(2,1)S(1)} %get-tuple-element.100), channel_id=1, source_target_pairs={{0,1},{1,0},{2,3},{3,2},{4,5},{5,4},{6,7},{7,6},{8,9},{9,8},{10,11... | collective-permute-start | bytes 786440 | tf_op jit(solution)/shard_map/ppermute | solution.py:423
  51.0 9.1 %collective-permute-start.2 = (bf16[4,32,1024]{2,1,0:T(8,128)(2,1)S(1)}, bf16[4,32,1024]{2,1,0:T(8,128)(2,1)S(1)}, u32[]{:S(2)}, u32[]{:S(2)}) collective-permute-start(bf16[4,32,1024]{2,1,0:T(8,128)(2,1)S(1)} %add_convert_fusion.7), channel_id=1, source_target_pairs={{0,2},{1,3},{2,0},{3,1},{4,6},{5,7},{6,4},{7,5},{8,10},{9,11},{10,... | collective-permute-start | bytes 786440 | tf_op jit(solution)/shard_map/ppermute | solution.py:423
  55.0 2.9 %collective-permute-start.3 = (bf16[4,32,1024]{2,1,0:T(8,128)(2,1)S(1)}, bf16[4,32,1024]{2,1,0:T(8,128)(2,1)S(1)}, u32[]{:S(2)}, u32[]{:S(2)}) collective-permute-start(bf16[4,32,1024]{2,1,0:T(8,128)(2,1)S(1)} %get-tuple-element.90), channel_id=1, source_target_pairs={{0,1},{1,0},{2,3},{3,2},{4,5},{5,4},{6,7},{7,6},{8,9},{9,8},{10,11... | collective-permute-start | bytes 786440 | tf_op jit(solution)/shard_map/ppermute | solution.py:423
  55.4 9.7 %collective-permute-start.9 = (bf16[4,32,1024]{2,1,0:T(8,128)(2,1)S(1)}, bf16[4,32,1024]{2,1,0:T(8,128)(2,1)S(1)}, u32[]{:S(2)}, u32[]{:S(2)}) collective-permute-start(bf16[4,32,1024]{2,1,0:T(8,128)(2,1)S(1)} %add_convert_fusion.3), channel_id=1, source_target_pairs={{0,2},{1,3},{2,0},{3,1},{4,6},{5,7},{6,4},{7,5},{8,10},{9,11},{10,... | collective-permute-start | bytes 786440 | tf_op jit(solution)/shard_map/ppermute | solution.py:423
  57.3 1.5 %collective-permute-start.1 = (bf16[4,32,1024]{2,1,0:T(8,128)(2,1)S(1)}, bf16[4,32,1024]{2,1,0:T(8,128)(2,1)S(1)}, u32[]{:S(2)}, u32[]{:S(2)}) collective-permute-start(bf16[4,32,1024]{2,1,0:T(8,128)(2,1)S(1)} %get-tuple-element.87), channel_id=1, source_target_pairs={{0,1},{1,0},{2,3},{3,2},{4,5},{5,4},{6,7},{7,6},{8,9},{9,8},{10,11... | collective-permute-start | bytes 786440 | tf_op jit(solution)/shard_map/ppermute | solution.py:423
  57.5 3.6 %collective-permute-start.8 = (bf16[4,32,1024]{2,1,0:T(8,128)(2,1)S(1)}, bf16[4,32,1024]{2,1,0:T(8,128)(2,1)S(1)}, u32[]{:S(2)}, u32[]{:S(2)}) collective-permute-start(bf16[4,32,1024]{2,1,0:T(8,128)(2,1)S(1)} %get-tuple-element.102), channel_id=1, source_target_pairs={{0,1},{1,0},{2,3},{3,2},{4,5},{5,4},{6,7},{7,6},{8,9},{9,8},{10,11... | collective-permute-start | bytes 786440 | tf_op jit(solution)/shard_map/ppermute | solution.py:423
  57.9 8.3 %collective-permute-start.15 = (bf16[4,32,1024]{2,1,0:T(8,128)(2,1)S(1)}, bf16[4,32,1024]{2,1,0:T(8,128)(2,1)S(1)}, u32[]{:S(2)}, u32[]{:S(2)}) collective-permute-start(bf16[4,32,1024]{2,1,0:T(8,128)(2,1)S(1)} %get-tuple-element.115), channel_id=1, source_target_pairs={{0,1},{1,0},{2,3},{3,2},{4,5},{5,4},{6,7},{7,6},{8,9},{9,8},{10,11... | collective-permute-start | bytes 786440 | tf_op jit(solution)/shard_map/ppermute | solution.py:423
  58.3 54.5 %copy-start.3 = (bf16[16384]{0:T(1024)(128)(2,1)S(1)}, bf16[16384]{0:T(1024)(128)(2,1)}, u32[]{:S(2)}) copy-start(bf16[16384]{0:T(1024)(128)(2,1)} %param.17) | copy-start | bytes 98308
  58.9 15.1 %collective-permute-start.11 = (bf16[4,32,1024]{2,1,0:T(8,128)(2,1)S(1)}, bf16[4,32,1024]{2,1,0:T(8,128)(2,1)S(1)}, u32[]{:S(2)}, u32[]{:S(2)}) collective-permute-start(bf16[4,32,1024]{2,1,0:T(8,128)(2,1)S(1)} %pad_maximum_fusion), channel_id=1, source_target_pairs={{0,4},{1,5},{2,6},{3,7},{4,0},{5,1},{6,2},{7,3},{8,12},{9,13},{10,... | collective-permute-start | bytes 786440 | tf_op jit(solution)/shard_map/ppermute | solution.py:423
  60.3 10.6 %collective-permute-start.6 = (bf16[2,32,1024]{2,1,0:T(8,128)(2,1)S(1)}, bf16[2,32,1024]{2,1,0:T(8,128)(2,1)S(1)}, u32[]{:S(2)}, u32[]{:S(2)}) collective-permute-start(bf16[2,32,1024]{2,1,0:T(8,128)(2,1)S(1)} %get-tuple-element.166), channel_id=1, source_target_pairs={{0,4},{1,5},{2,6},{3,7},{4,0},{5,1},{6,2},{7,3},{8,12},{9,13},{10,... | collective-permute-start | bytes 393224 | tf_op jit(solution)/shard_map/ppermute | solution.py:423
  65.1 7.7 %collective-permute-start.12 = (bf16[2,32,1024]{2,1,0:T(8,128)(2,1)S(1)}, bf16[2,32,1024]{2,1,0:T(8,128)(2,1)S(1)}, u32[]{:S(2)}, u32[]{:S(2)}) collective-permute-start(bf16[2,32,1024]{2,1,0:T(8,128)(2,1)S(1)} %get-tuple-element.165), channel_id=1, source_target_pairs={{0,4},{1,5},{2,6},{3,7},{4,0},{5,1},{6,2},{7,3},{8,12},{9,13},{10,... | collective-permute-start | bytes 393224 | tf_op jit(solution)/shard_map/ppermute | solution.py:423
  65.2 12.1 %collective-permute-start.16 = (bf16[4,32,1024]{2,1,0:T(8,128)(2,1)S(1)}, bf16[4,32,1024]{2,1,0:T(8,128)(2,1)S(1)}, u32[]{:S(2)}, u32[]{:S(2)}) collective-permute-start(bf16[4,32,1024]{2,1,0:T(8,128)(2,1)S(1)} %add_convert_fusion.2), channel_id=1, source_target_pairs={{0,2},{1,3},{2,0},{3,1},{4,6},{5,7},{6,4},{7,5},{8,10},{9,11},{10,... | collective-permute-start | bytes 786440 | tf_op jit(solution)/shard_map/ppermute | solution.py:423
  70.8 6.4 %collective-permute-start.10 = (bf16[1,32,1024]{2,1,0:T(8,128)(2,1)S(1)}, bf16[1,32,1024]{2,1,0:T(8,128)(2,1)S(1)}, u32[]{:S(2)}, u32[]{:S(2)}) collective-permute-start(bf16[1,32,1024]{2,1,0:T(8,128)(2,1)S(1)} %get-tuple-element.178), channel_id=1, source_target_pairs={{0,8},{1,9},{2,10},{3,11},{4,12},{5,13},{6,14},{7,15},{8,0},{9,1},... | collective-permute-start | bytes 196616 | tf_op jit(solution)/shard_map/ppermute | solution.py:423
  72.9 7.7 %collective-permute-start.14 = (bf16[1,32,1024]{2,1,0:T(8,128)(2,1)S(1)}, bf16[1,32,1024]{2,1,0:T(8,128)(2,1)S(1)}, u32[]{:S(2)}, u32[]{:S(2)}) collective-permute-start(bf16[1,32,1024]{2,1,0:T(8,128)(2,1)S(1)} %get-tuple-element.173), channel_id=1, source_target_pairs={{0,8},{1,9},{2,10},{3,11},{4,12},{5,13},{6,14},{7,15},{8,0},{9,1},... | collective-permute-start | bytes 196616 | tf_op jit(solution)/shard_map/ppermute | solution.py:423
  74.0 8.9 %collective-permute-start.18 = (bf16[2,32,1024]{2,1,0:T(8,128)(2,1)S(1)}, bf16[2,32,1024]{2,1,0:T(8,128)(2,1)S(1)}, u32[]{:S(2)}, u32[]{:S(2)}) collective-permute-start(bf16[2,32,1024]{2,1,0:T(8,128)(2,1)S(1)} %get-tuple-element.163), channel_id=1, source_target_pairs={{0,2},{1,3},{2,0},{3,1},{4,6},{5,7},{6,4},{7,5},{8,10},{9,11},{10,... | collective-permute-start | bytes 393224 | tf_op jit(solution)/shard_map/ppermute | solution.py:423
  77.3 5.5 %collective-permute-start.13 = (bf16[1,32,1024]{2,1,0:T(8,128)(2,1)S(1)}, bf16[1,32,1024]{2,1,0:T(8,128)(2,1)S(1)}, u32[]{:S(2)}, u32[]{:S(2)}) collective-permute-start(bf16[1,32,1024]{2,1,0:T(8,128)(2,1)S(1)} %fusion.5), channel_id=1, source_target_pairs={{0,8},{1,9},{2,10},{3,11},{4,12},{5,13},{6,14},{7,15},{8,0},{9,1},... | collective-permute-start | bytes 196616 | tf_op jit(solution)/shard_map/ppermute | solution.py:423
  77.5 9.8 %collective-permute-start.20 = (bf16[2,32,1024]{2,1,0:T(8,128)(2,1)S(1)}, bf16[2,32,1024]{2,1,0:T(8,128)(2,1)S(1)}, u32[]{:S(2)}, u32[]{:S(2)}) collective-permute-start(bf16[2,32,1024]{2,1,0:T(8,128)(2,1)S(1)} %get-tuple-element.161), channel_id=1, source_target_pairs={{0,4},{1,5},{2,6},{3,7},{4,0},{5,1},{6,2},{7,3},{8,12},{9,13},{10,... | collective-permute-start | bytes 393224 | tf_op jit(solution)/shard_map/ppermute | solution.py:423
  80.6 5.7 %collective-permute-start.21 = (bf16[1,32,1024]{2,1,0:T(8,128)(2,1)S(1)}, bf16[1,32,1024]{2,1,0:T(8,128)(2,1)S(1)}, u32[]{:S(2)}, u32[]{:S(2)}) collective-permute-start(bf16[1,32,1024]{2,1,0:T(8,128)(2,1)S(1)} %fusion.6), channel_id=1, source_target_pairs={{0,8},{1,9},{2,10},{3,11},{4,12},{5,13},{6,14},{7,15},{8,0},{9,1},... | collective-permute-start | bytes 196616 | tf_op jit(solution)/shard_map/ppermute | solution.py:423
  82.8 8.9 %collective-permute-start.17 = (bf16[2,32,1024]{2,1,0:T(8,128)(2,1)S(1)}, bf16[2,32,1024]{2,1,0:T(8,128)(2,1)S(1)}, u32[]{:S(2)}, u32[]{:S(2)}) collective-permute-start(bf16[2,32,1024]{2,1,0:T(8,128)(2,1)S(1)} %constant_dynamic-update-slice_fusion), channel_id=1, source_target_pairs={{0,4},{1,5},{2,6},{3,7},{4,0},{5,1},{6,2},{7,3},{8,12},{9,13},{10,... | collective-permute-start | bytes 393224 | tf_op jit(solution)/shard_map/ppermute | solution.py:423
  83.0 7.8 %collective-permute-start.19 = (bf16[1,32,1024]{2,1,0:T(8,128)(2,1)S(1)}, bf16[1,32,1024]{2,1,0:T(8,128)(2,1)S(1)}, u32[]{:S(2)}, u32[]{:S(2)}) collective-permute-start(bf16[1,32,1024]{2,1,0:T(8,128)(2,1)S(1)} %get-tuple-element.170), channel_id=1, source_target_pairs={{0,8},{1,9},{2,10},{3,11},{4,12},{5,13},{6,14},{7,15},{8,0},{9,1},... | collective-permute-start | bytes 196616 | tf_op jit(solution)/shard_map/ppermute | solution.py:423
  86.4 10.5 %collective-permute-start.23 = (bf16[2,32,1024]{2,1,0:T(8,128)(2,1)S(1)}, bf16[2,32,1024]{2,1,0:T(8,128)(2,1)S(1)}, u32[]{:S(2)}, u32[]{:S(2)}) collective-permute-start(bf16[2,32,1024]{2,1,0:T(8,128)(2,1)S(1)} %constant_dynamic-update-slice_fusion.2), channel_id=1, source_target_pairs={{0,2},{1,3},{2,0},{3,1},{4,6},{5,7},{6,4},{7,5},{8,10},{9,11},{10,... | collective-permute-start | bytes 393224 | tf_op jit(solution)/shard_map/ppermute | solution.py:423
  87.3 7.4 %collective-permute-start.25 = (bf16[1,32,1024]{2,1,0:T(8,128)(2,1)S(1)}, bf16[1,32,1024]{2,1,0:T(8,128)(2,1)S(1)}, u32[]{:S(2)}, u32[]{:S(2)}) collective-permute-start(bf16[1,32,1024]{2,1,0:T(8,128)(2,1)S(1)} %get-tuple-element.169), channel_id=1, source_target_pairs={{0,8},{1,9},{2,10},{3,11},{4,12},{5,13},{6,14},{7,15},{8,0},{9,1},... | collective-permute-start | bytes 196616 | tf_op jit(solution)/shard_map/ppermute | solution.py:423
  90.8 5.7 %collective-permute-start.24 = (bf16[1,32,1024]{2,1,0:T(8,128)(2,1)S(1)}, bf16[1,32,1024]{2,1,0:T(8,128)(2,1)S(1)}, u32[]{:S(2)}, u32[]{:S(2)}) collective-permute-start(bf16[1,32,1024]{2,1,0:T(8,128)(2,1)S(1)} %fusion.7), channel_id=1, source_target_pairs={{0,8},{1,9},{2,10},{3,11},{4,12},{5,13},{6,14},{7,15},{8,0},{9,1},... | collective-permute-start | bytes 196616 | tf_op jit(solution)/shard_map/ppermute | solution.py:423
  91.7 15.3 %collective-permute-start.22 = (bf16[4,32,1024]{2,1,0:T(8,128)(2,1)S(1)}, bf16[4,32,1024]{2,1,0:T(8,128)(2,1)S(1)}, u32[]{:S(2)}, u32[]{:S(2)}) collective-permute-start(bf16[4,32,1024]{2,1,0:T(8,128)(2,1)S(1)} %constant_dynamic-update-slice_fusion.4), channel_id=1, source_target_pairs={{0,2},{1,3},{2,0},{3,1},{4,6},{5,7},{6,4},{7,5},{8,10},{9,11},{10,... | collective-permute-start | bytes 786440 | tf_op jit(solution)/shard_map/ppermute | solution.py:423
  94.8 5.9 %collective-permute-start.27 = (bf16[1,32,1024]{2,1,0:T(8,128)(2,1)S(1)}, bf16[1,32,1024]{2,1,0:T(8,128)(2,1)S(1)}, u32[]{:S(2)}, u32[]{:S(2)}) collective-permute-start(bf16[1,32,1024]{2,1,0:T(8,128)(2,1)S(1)} %fusion.8), channel_id=1, source_target_pairs={{0,8},{1,9},{2,10},{3,11},{4,12},{5,13},{6,14},{7,15},{8,0},{9,1},... | collective-permute-start | bytes 196616 | tf_op jit(solution)/shard_map/ppermute | solution.py:423
  96.5 5.4 %collective-permute-start.29 = (bf16[2,32,1024]{2,1,0:T(8,128)(2,1)S(1)}, bf16[2,32,1024]{2,1,0:T(8,128)(2,1)S(1)}, u32[]{:S(2)}, u32[]{:S(2)}) collective-permute-start(bf16[2,32,1024]{2,1,0:T(8,128)(2,1)S(1)} %constant_dynamic-update-slice_fusion.6), channel_id=1, source_target_pairs={{0,4},{1,5},{2,6},{3,7},{4,0},{5,1},{6,2},{7,3},{8,12},{9,13},{10,... | collective-permute-start | bytes 393224 | tf_op jit(solution)/shard_map/ppermute | solution.py:423
  96.9 10.0 %collective-permute-start.26 = (bf16[4,32,1024]{2,1,0:T(8,128)(2,1)S(1)}, bf16[4,32,1024]{2,1,0:T(8,128)(2,1)S(1)}, u32[]{:S(2)}, u32[]{:S(2)}) collective-permute-start(bf16[4,32,1024]{2,1,0:T(8,128)(2,1)S(1)} %constant_dynamic-update-slice_fusion.8), channel_id=1, source_target_pairs={{0,4},{1,5},{2,6},{3,7},{4,0},{5,1},{6,2},{7,3},{8,12},{9,13},{10,... | collective-permute-start | bytes 786440 | tf_op jit(solution)/shard_map/ppermute | solution.py:423
  100.7 5.0 %collective-permute-start.28 = (bf16[2,32,1024]{2,1,0:T(8,128)(2,1)S(1)}, bf16[2,32,1024]{2,1,0:T(8,128)(2,1)S(1)}, u32[]{:S(2)}, u32[]{:S(2)}) collective-permute-start(bf16[2,32,1024]{2,1,0:T(8,128)(2,1)S(1)} %constant_dynamic-update-slice_fusion.10), channel_id=1, source_target_pairs={{0,2},{1,3},{2,0},{3,1},{4,6},{5,7},{6,4},{7,5},{8,10},{9,11},{10,... | collective-permute-start | bytes 393224 | tf_op jit(solution)/shard_map/ppermute | solution.py:423
  101.9 6.6 %collective-permute-start.32 = (bf16[4,32,1024]{2,1,0:T(8,128)(2,1)S(1)}, bf16[4,32,1024]{2,1,0:T(8,128)(2,1)S(1)}, u32[]{:S(2)}, u32[]{:S(2)}) collective-permute-start(bf16[4,32,1024]{2,1,0:T(8,128)(2,1)S(1)} %constant_dynamic-update-slice_fusion.12), channel_id=1, source_target_pairs={{0,2},{1,3},{2,0},{3,1},{4,6},{5,7},{6,4},{7,5},{8,10},{9,11},{10,... | collective-permute-start | bytes 786440 | tf_op jit(solution)/shard_map/ppermute | solution.py:423
  105.7 6.4 %collective-permute-start.31 = (bf16[4,32,1024]{2,1,0:T(8,128)(2,1)S(1)}, bf16[4,32,1024]{2,1,0:T(8,128)(2,1)S(1)}, u32[]{:S(2)}, u32[]{:S(2)}) collective-permute-start(bf16[4,32,1024]{2,1,0:T(8,128)(2,1)S(1)} %constant_dynamic-update-slice_fusion.14), channel_id=1, source_target_pairs={{0,4},{1,5},{2,6},{3,7},{4,0},{5,1},{6,2},{7,3},{8,12},{9,13},{10,... | collective-permute-start | bytes 786440 | tf_op jit(solution)/shard_map/ppermute | solution.py:423
  106.9 5.9 %collective-permute-start.35 = (bf16[8,32,1024]{2,1,0:T(8,128)(2,1)S(1)}, bf16[8,32,1024]{2,1,0:T(8,128)(2,1)}, u32[]{:S(2)}, u32[]{:S(2)}) collective-permute-start(bf16[8,32,1024]{2,1,0:T(8,128)(2,1)S(1)} %constant_dynamic-update-slice_fusion.16.refs_2_), channel_id=1, source_target_pairs={{0,1},{1,0},{2,3},{3,2},{4,5},{5,4},{6,7},{7,6},{8,9},{9,8},{10,11... | collective-permute-start | bytes 1572872 | tf_op jit(solution)/shard_map/ppermute | solution.py:423
  108.6 4.3 %collective-permute-start.34 = (bf16[8,32,1024]{2,1,0:T(8,128)(2,1)S(1)}, bf16[8,32,1024]{2,1,0:T(8,128)(2,1)}, u32[]{:S(2)}, u32[]{:S(2)}) collective-permute-start(bf16[8,32,1024]{2,1,0:T(8,128)(2,1)S(1)} %constant_dynamic-update-slice_fusion.20.refs_0_), channel_id=1, source_target_pairs={{0,1},{1,0},{2,3},{3,2},{4,5},{5,4},{6,7},{7,6},{8,9},{9,8},{10,11... | collective-permute-start | bytes 1572872 | tf_op jit(solution)/shard_map/ppermute | solution.py:423
  112.2 3.9 %collective-permute-start.33 = (bf16[8,32,1024]{2,1,0:T(8,128)(2,1)S(1)}, bf16[8,32,1024]{2,1,0:T(8,128)(2,1)S(1)}, u32[]{:S(2)}, u32[]{:S(2)}) collective-permute-start(bf16[8,32,1024]{2,1,0:T(8,128)(2,1)S(1)} %constant_dynamic-update-slice_fusion.22.refs_2_), channel_id=1, source_target_pairs={{0,1},{1,0},{2,3},{3,2},{4,5},{5,4},{6,7},{7,6},{8,9},{9,8},{10,11... | collective-permute-start | bytes 1572872 | tf_op jit(solution)/shard_map/ppermute | solution.py:423
  112.3 3.9 %collective-permute-start.30 = (bf16[8,32,1024]{2,1,0:T(8,128)(2,1)S(1)}, bf16[8,32,1024]{2,1,0:T(8,128)(2,1)S(1)}, u32[]{:S(2)}, u32[]{:S(2)}) collective-permute-start(bf16[8,32,1024]{2,1,0:T(8,128)(2,1)S(1)} %constant_dynamic-update-slice_fusion.18.refs_0_), channel_id=1, source_target_pairs={{0,1},{1,0},{2,3},{3,2},{4,5},{5,4},{6,7},{7,6},{8,9},{9,8},{10,11... | collective-permute-start | bytes 1572872 | tf_op jit(solution)/shard_map/ppermute | solution.py:423
